TPU v7x, 32 devices: a whole 2x2x4 slice. The times are simulated.
32 devices in a mesh: ga: 8 (over z, y), pair: 4 (over x, core).
Axes of the slice: x: 2, y: 2, z: 4, core: 2. Of those that a mesh axis runs over, the one named last changes fastest.
Arguments:
- val_density: bfloat16 [256, 3, 2, 8192], P('pair', None, None, 'ga'), may hold values from -0.0625 to 0.0625
- con_density: bfloat16 [576, 3, 2, 8192], P('ga', None, None, 'pair'), may hold values from -6 to 6
- screened: bfloat16 [3, 2, 8192, 8192], P(None, None, 'ga', 'pair'), may hold values from -0.0625 to 0.0625
- coulomb: float32 [3, 8192], P(None, 'ga'), may hold values from 0.2 to 2
- trans_here: bfloat16 [384, 2, 8192], P('pair', None, 'ga'), may hold values from -6 to 6
- trans_there: bfloat16 [384, 3, 2, 8192], P('pair', None, None, 'ga'), may hold values from -0.0625 to 0.0625
- shift_map: int32 [3, 8192], P(None, 'pair'), may hold values from 0 to 8191, as said below
- ordering: int32 [384], replicated, may hold values from 0 to 383, each once
Outputs:
- kernel: float32 [3, 2, 384, 384], P(None, None, 'pair', 'ga')
Inputs may be any that keep to these rules, and one draw needn't show every extreme that they name: `shift_map`: each aligned block of 128 entries of a row is a permutation of that block's own G-vector indices.
All inputs are finite; a program needn't handle non-finite values.
Results may differ from a plain program's by a relative error of at most 0.0003.
Values may be sent and summed in bfloat16 or wider, within the bound.
No kernel may reach another device: no remote copies, remote signals or barrier semaphores. Data moves between devices by JAX's collectives and lax.ppermute only.
A program may use at most 192 MiB of HBM per device.

v0:
```python
import jax
import jax.numpy as jnp
from jax import lax
from jax.sharding import PartitionSpec as P

NV = 16
NC = 24
GBLK = 128
NT = 384


def contract_float(left, right):
    high = lax.Precision.HIGHEST
    real_part = jnp.einsum(
        "nkg,mkg->nkm", left[:, :, 0], right[:, :, 0], precision=high
    ) - jnp.einsum("nkg,mkg->nkm", left[:, :, 1], right[:, :, 1], precision=high)
    imag_part = jnp.einsum(
        "nkg,mkg->nkm", left[:, :, 0], right[:, :, 1], precision=high
    ) + jnp.einsum("nkg,mkg->nkm", left[:, :, 1], right[:, :, 0], precision=high)
    return jnp.stack([real_part, imag_part], axis=2)


def times_cols(rows, weights):
    first = jnp.einsum(
        "nkh,kgh->nkg", rows[:, :, 0], weights[:, 0], preferred_element_type=jnp.float32
    ) - jnp.einsum("nkh,kgh->nkg", rows[:, :, 1], weights[:, 1], preferred_element_type=jnp.float32)
    second = jnp.einsum(
        "nkh,kgh->nkg", rows[:, :, 0], weights[:, 1], preferred_element_type=jnp.float32
    ) + jnp.einsum("nkh,kgh->nkg", rows[:, :, 1], weights[:, 0], preferred_element_type=jnp.float32)
    return jnp.stack([first, second], axis=2)


def on_device(
    val_density, con_density, screened, coulomb, trans_here, trans_there, shift_map, ordering
):
    con_count = con_density.shape[0]
    points = con_density.shape[1]
    slab_cols = con_density.shape[3]
    blocks = slab_cols // GBLK
    within = (shift_map % GBLK).reshape(points, blocks, GBLK)
    onehot = (
        within[:, :, :, None] == jnp.arange(GBLK, dtype=jnp.int32)[None, None, None, :]
    ).astype(jnp.bfloat16)
    con_blocks = con_density.reshape(con_count, points, 2, blocks, GBLK)
    shifted = (
        jnp.einsum("bkpnh,kngh->bkpng", con_blocks, onehot, preferred_element_type=jnp.float32)
        .astype(jnp.bfloat16)
        .reshape(con_density.shape)
    )
    whole_here = lax.all_gather(trans_here, "pair", axis=0, tiled=True).astype(jnp.float32)
    weighted = trans_there.astype(jnp.float32) * coulomb[None, :, None, :]
    high = lax.Precision.HIGHEST
    exch_real = jnp.einsum(
        "tg,skg->tks", whole_here[:, 0], weighted[:, :, 0], precision=high
    ) - jnp.einsum("tg,skg->tks", whole_here[:, 1], weighted[:, :, 1], precision=high)
    exch_imag = jnp.einsum(
        "tg,skg->tks", whole_here[:, 0], weighted[:, :, 1], precision=high
    ) + jnp.einsum("tg,skg->tks", whole_here[:, 1], weighted[:, :, 0], precision=high)
    exch_part = jnp.stack([exch_real, exch_imag], axis=2)
    whole_con = lax.all_gather(shifted, "ga", axis=0, tiled=True)
    screened_rows = lax.psum_scatter(
        times_cols(whole_con, screened), "pair", scatter_dimension=0, tiled=True
    )
    direct_part = contract_float(
        lax.all_gather(val_density, "pair", axis=0, tiled=True).astype(jnp.float32), screened_rows
    )
    direct_sum, exch_sum = lax.psum((direct_part, exch_part), "ga")
    direct_full, exch_full = (
        lax.all_gather(direct_sum, "pair", axis=3, tiled=True),
        lax.all_gather(exch_sum, "pair", axis=3, tiled=True),
    )
    row_count = NT // lax.axis_size("pair")
    col_count = NT // lax.axis_size("ga")
    row_trans = lax.dynamic_slice_in_dim(ordering, lax.axis_index("pair") * row_count, row_count, 0)
    col_trans = lax.dynamic_slice_in_dim(ordering, lax.axis_index("ga") * col_count, col_count, 0)
    row_pairs = (row_trans // NC)[:, None] * NV + (col_trans // NC)[None, :]
    col_pairs = (row_trans % NC)[:, None] * NC + (col_trans % NC)[None, :]
    picked = direct_full[row_pairs.reshape(-1)]
    col_mask = (
        col_pairs.reshape(-1)[:, None] == jnp.arange(direct_full.shape[3], dtype=jnp.int32)[None, :]
    ).astype(jnp.float32)
    direct_flat = jnp.sum(picked * col_mask[:, None, None, :], axis=3)
    direct_sel = jnp.transpose(direct_flat.reshape(row_count, col_count, points, 2), (2, 3, 0, 1))
    exch_picked = exch_full[row_trans]
    col_hot = (jnp.arange(NT, dtype=jnp.int32)[:, None] == col_trans[None, :]).astype(jnp.float32)
    exch_sel = jnp.einsum("rkpt,tc->kprc", exch_picked, col_hot, precision=high)
    return 2.0 * exch_sel - direct_sel


def solution(mesh):
    in_specs = (
        P("pair", None, None, "ga"),
        P("ga", None, None, "pair"),
        P(None, None, "ga", "pair"),
        P(None, "ga"),
        P("pair", None, "ga"),
        P("pair", None, None, "ga"),
        P(None, "pair"),
        P(),
    )
    out_specs = P(None, None, "pair", "ga")
    return jax.shard_map(
        on_device, mesh=mesh, in_specs=in_specs, out_specs=out_specs, check_vma=False
    )
```

profile of v0, /device:TPU:0, one launch (start us, length us, event | category | flops | bytes accessed | tf_op | source)
XLA Modules:
  0.0 777.4 jit_solution(17481288712702647545)
XLA Ops:
  7.3 4.3 reshape.80
  11.6 2.4 convert_bitcast_fusion
  14.5 2.2 reshape.104
  19.1 196.1 %all-gather.10.cloned.1.call-done = bf16[576,3,2,2048]{3,0,1,2:T(8,128)(2,1)} async-done(((bf16[72,3,2,2048]{3,0,1,2:T(8,128)(2,1)}), bf16[576,3,2,2048]{3,0,1,2:T(8,128)(2,1)}) %all-gather.10.cloned.1.call-update) | async-done | bytes 14155792 | tf_op jit(solution)/shard_map/all_gather | solution.py:60
  215.2 14.3 %fusion = f32[3,576,1024]{2,1,0:T(8,128)} fusion(bf16[3,2,1024,2048]{3,2,1,0:T(8,128)(2,1)} %param.10, bf16[576,3,2,2048]{3,0,1,2:T(8,128)(2,1)} %all-gather.10.cloned.1.call-done), kind=kOutput, calls=%fused_computation.4 | convolution fusion | flops 7247757312 | bytes 26738688 | tf_op jit(solution)/shard_map/nkh,kgh->nkg/dot_general | solution.py:27
  229.5 14.4 %fusion.2 = f32[3,576,1024]{2,1,0:T(8,128)} fusion(bf16[3,2,1024,2048]{3,2,1,0:T(8,128)(2,1)} %param.10, bf16[576,3,2,2048]{3,0,1,2:T(8,128)(2,1)} %all-gather.10.cloned.1.call-done), kind=kOutput, calls=%fused_computation.6 | convolution fusion | flops 7247757312 | bytes 26738688 | tf_op jit(solution)/shard_map/nkh,kgh->nkg/dot_general | solution.py:26
  243.9 15.8 %add_bitcast_fusion = f32[576,3,1,1024]{3,0,1,2:T(8,128)} fusion(f32[3,576,1024]{2,1,0:T(8,128)} %fusion, bf16[3,2,1024,2048]{3,2,1,0:T(8,128)(2,1)} %param.10, bf16[576,3,2,2048]{3,0,1,2:T(8,128)(2,1)} %all-gather.10.cloned.1.call-done), kind=kOutput, calls=%fused_computation.20 | convolution fusion | flops 7249526784 | bytes 33816576 | tf_op jit(solution)/shard_map/nkh,kgh->nkg/dot_general | solution.py:29
  259.7 15.8 %subtract_bitcast_fusion = f32[576,3,1,1024]{3,0,1,2:T(8,128)} fusion(f32[3,576,1024]{2,1,0:T(8,128)} %fusion.2, bf16[3,2,1024,2048]{3,2,1,0:T(8,128)(2,1)} %param.10, bf16[576,3,2,2048]{3,0,1,2:T(8,128)(2,1)} %all-gather.10.cloned.1.call-done), kind=kOutput, calls=%fused_computation.21 | convolution fusion | flops 7249526784 | bytes 33816576 | tf_op jit(solution)/shard_map/nkh,kgh->nkg/dot_general | solution.py:24
  275.5 13.2 %pad_maximum_fusion = f32[576,3,2,1024]{3,0,1,2:T(8,128)} fusion(f32[576,3,1,1024]{3,0,1,2:T(8,128)} %add_bitcast_fusion, f32[576,3,1,1024]{3,0,1,2:T(8,128)} %subtract_bitcast_fusion), kind=kLoop, calls=%fused_computation.3 | loop fusion | flops 3538944 | bytes 28311552 | tf_op jit(solution)/shard_map/stack | solution.py:30
  290.4 2.3 fusion.39
  292.7 2.4 fusion.34
  298.4 98.5 %reduce-scatter.2.cloned.1.call-done = f32[144,3,2,1024]{3,0,1,2:T(8,128)} async-done(((f32[576,3,2,1024]{3,0,1,2:T(8,128)}), f32[144,3,2,1024]{3,0,1,2:T(8,128)}) %reduce-scatter.2.cloned.1.call-update) | async-done | bytes 3538960 | tf_op jit(solution)/shard_map/reduce_scatter | solution.py:61
  396.9 3.8 fusion.25
  400.7 3.2 fusion.26
  408.5 94.0 %all-reduce.3.cloned.1.call-done = (f32[384,3,2,96]{0,3,1,2:T(8,128)}, f32[256,3,2,144]{0,3,1,2:T(8,128)}) async-done(((f32[384,3,2,96]{0,3,1,2:T(8,128)}, f32[256,3,2,144]{0,3,1,2:T(8,128)}), (f32[384,3,2,96]{0,3,1,2:T(8,128)}, f32[256,3,2,144]{0,3,1,2:T(8,128)})) %all-reduce.3.cloned.1.call-update) | async-done | bytes 1769488 | tf_op jit(solution)/shard_map/psum | solution.py:67
  503.4 5.3 fusion.8
  508.7 25.7 %all-gather.14.cloned.1.call-done = f32[256,3,2,576]{0,3,1,2:T(8,128)} async-done(((f32[256,3,2,144]{0,3,1,2:T(8,128)}), f32[256,3,2,576]{0,3,1,2:T(8,128)}) %all-gather.14.cloned.1.call-update) | async-done | bytes 3538960 | tf_op jit(solution)/shard_map/all_gather | solution.py:69
  534.4 7.5 copy.38
  541.8 158.0 %gather_fusion.1 = f32[4608,3,2,576]{3,2,1,0:T(2,128)} fusion(f32[256,3,2,576]{3,2,1,0:T(2,128)} %copy.38, s32[5120]{0:T(1024)S(1)} %pad_clamp_fusion), kind=kCustom, calls=%fused_computation.1 | custom fusion | bytes 127420416 | tf_op jit(solution)/shard_map/gather | solution.py:78
  699.8 51.6 %multiply_reduce_fusion = f32[4608,3,2]{2,1,0:T(4,128)} fusion(f32[4608,3,2,576]{3,2,1,0:T(2,128)} %gather_fusion.1, f32[4608,576]{1,0:T(8,128)} %fusion.8), kind=kLoop, calls=%fused_computation.2 | loop fusion | flops 31822848 | bytes 74428416 | tf_op jit(solution)/shard_map/reduce_sum | solution.py:82
  751.4 7.6 copy.40
  759.0 6.2 copy.30
  765.2 2.5 gather_fusion
  767.7 2.6 fusion.37
  (54 shorter events, 13.8 us)
Async XLA Ops:
  6.5 208.6 %all-gather.10.cloned.1.call-start = ((), (), s32[]{:S(2)}) async-start(), calls=%async_computation.3 | async-start | bytes 15925248 | tf_op jit(solution)/shard_map/all_gather | solution.py:60
  14.5 2.3 copy-start.5
  14.5 3.2 copy-start.4
  16.7 273.7 %all-gather.6.cloned.1.call-start = ((), (), s32[]{:S(2)}) async-start(), calls=%async_computation.1 | async-start | bytes 1966080 | tf_op jit(solution)/shard_map/all_gather | solution.py:50
  17.6 280.7 %all-gather.12.cloned.1.call-start = ((), (), s32[]{:S(2)}) async-start(), calls=%async_computation.5 | async-start | bytes 3932160 | tf_op jit(solution)/shard_map/all_gather | solution.py:65
  18.8 378.0 %reduce-scatter.2.cloned.1.call-start = ((), (), s32[]{:S(2)}) async-start(), calls=%async_computation.4 | async-start | bytes 17694720 | tf_op jit(solution)/shard_map/reduce_scatter | solution.py:61
  288.7 1.3 copy-start.3
  288.7 1.3 copy-start.6
  288.7 213.8 %all-reduce.3.cloned.1.call-start = ((), (), s32[]{:S(2)}) async-start(), calls=%async_computation.7 | async-start | bytes 3538944 | tf_op jit(solution)/shard_map/psum | solution.py:67
  290.4 4.8 copy-start.2
  396.9 3.8 copy-start
  396.9 7.0 copy-start.1
  405.7 97.1 %copy-start.7 = (s32[384]{0:T(512)S(1)}, s32[384]{0:T(512)}, u32[]{:S(2)}) copy-start(s32[384]{0:T(512)} %param.15) | copy-start | bytes 4612
  408.5 125.9 %all-gather.14.cloned.1.call-start = ((), (), s32[]{:S(2)}) async-start(), calls=%async_computation.6 | async-start | bytes 4423680 | tf_op jit(solution)/shard_map/all_gather | solution.py:69
  502.6 256.5 %all-gather.8.cloned.1.call-start = ((), (), s32[]{:S(2)}) async-start(), calls=%async_computation.2 | async-start | bytes 4423680 | tf_op jit(solution)/shard_map/all_gather | solution.py:70
Sparse Core Ops, SparseCore 0:
  16.8 198.3 all-gather.9
  216.7 17.8 all-gather.5
  236.2 28.5 all-gather.11
  288.8 107.9 reduce-scatter.1
  408.6 93.8 all-reduce.2
  504.0 30.2 all-gather.13
  536.0 30.7 all-gather.7
where the time goes:
time: 787 us; the launch traced here: 777 us
  waiting for transfers between devices  414 us (53%)
  local copies, waits for them, and re-layouts  192 us (24%)
  matrix products  82.7 us (11%)
  other arithmetic  73.6 us (9%)
  between operations  13.9 us (2%)
    all_gather x1, waiting for transfers between devices, on_device(): whole_con = lax.all_gather(shifted, 'ga', axis=0, tiled=True)  196 us
    gather x1, local copies, waits for them, and re-layouts, on_device(): picked = direct_full[row_pairs.reshape(-1)]  158 us
    reduce_scatter x1, waiting for transfers between devices, on_device(): lax.psum_scatter(times_cols(whole_con, screened), 'pair', scatter_dimensi...  98.5 us
    psum x1, waiting for transfers between devices, on_device(): direct_sum, exch_sum = lax.psum((direct_part, exch_part), 'ga')  94 us
    reduce_sum x1, other arithmetic, on_device(): direct_flat = jnp.sum(picked * col_mask[:, None, None, :], axis=3)  51.6 us
    all_gather x1, waiting for transfers between devices, on_device(): lax.all_gather(direct_sum, 'pair', axis=3, tiled=True)  25.7 us
    dot_general x1, matrix products, times_cols(): jnp.einsum('nkh,kgh->nkg', rows[:, :, 1], weights[:, 0], preferred_elemen...  15.8 us
    dot_general x1, matrix products, times_cols(): jnp.einsum('nkh,kgh->nkg', rows[:, :, 0], weights[:, 0], preferred_elemen...  15.8 us
  transfers between devices with their start and end apart: 7, of which 4 were waited for; matrix products, arithmetic and copies ran while one was open for 40% of the time, Pallas kernels for 0%

commit v1 on v0

--- a/solution.py
+++ b/solution.py
@@ -1,12 +1,442 @@
+import math
+
 import jax
 import jax.numpy as jnp
 from jax import lax
+from jax.experimental import pallas as pl
+from jax.experimental.pallas import tpu as pltpu
 from jax.sharding import PartitionSpec as P
 
 NV = 16
 NC = 24
 GBLK = 128
 NT = 384
+
+GROUP = 64
+EXP_ROWS = 16
+STEPS = 128.0
+TOP = 32700.0
+NT_DIMS = (((1,), (1,)), ((), ()))
+VMEM = 56 * 1024 * 1024
+
+
+def params():
+    return pltpu.CompilerParams(vmem_limit_bytes=VMEM)
+
+
+def cost(flops, moved):
+    return pl.CostEstimate(flops=int(flops), bytes_accessed=int(moved), transcendentals=0)
+
+
+def mm(left, right):
+    return jnp.dot(left, right, preferred_element_type=jnp.float32)
+
+
+def mm_nt(left, right):
+    return lax.dot_general(left, right, NT_DIMS, preferred_element_type=jnp.float32)
+
+
+def halves(value):
+    high = value.astype(jnp.bfloat16)
+    low = (value - high.astype(jnp.float32)).astype(jnp.bfloat16)
+    return high, low
+
+
+def encode(value, out_ref):
+    rows, width = value.shape
+    groups = rows // GROUP
+    parts = value.reshape(groups, GROUP, width)
+    largest = jnp.maximum(jnp.max(jnp.abs(parts), axis=1), 1e-30)
+    level = jnp.ceil(jnp.log2(largest) * STEPS) + 1.0
+    factor = TOP * jnp.exp2(level * (-1.0 / STEPS))
+    coded = jnp.round(parts * factor[:, None, :]).astype(jnp.int32)
+    out_ref[0:rows, :] = coded.reshape(rows, width).astype(jnp.int16)
+    pad = jnp.zeros((EXP_ROWS - groups, width), jnp.int32)
+    out_ref[rows : rows + EXP_ROWS, :] = jnp.concatenate(
+        [level.astype(jnp.int32), pad], axis=0
+    ).astype(jnp.int16)
+
+
+def decode(ref):
+    rows = ref.shape[0] - EXP_ROWS
+    width = ref.shape[1]
+    groups = rows // GROUP
+    level = ref[rows : rows + EXP_ROWS, :].astype(jnp.int32).astype(jnp.float32)[0:groups]
+    factor = jnp.exp2(level * (1.0 / STEPS)) * (1.0 / TOP)
+    parts = ref[0:rows, :].astype(jnp.int32).astype(jnp.float32).reshape(groups, GROUP, width)
+    return (parts * factor[:, None, :]).reshape(rows, width)
+
+
+def shift_kernel(dest_ref, con_ref, map_ref, out_ref):
+    rows, width = con_ref.shape[2], con_ref.shape[3]
+    for block in range(width // GBLK):
+        cols = slice(block * GBLK, (block + 1) * GBLK)
+        within = jnp.bitwise_and(map_ref[0, 0:1, cols], GBLK - 1)
+        source = lax.broadcasted_iota(jnp.int32, (GBLK, GBLK), 0)
+        pick = (source == within).astype(jnp.float32).astype(jnp.bfloat16)
+        for part in range(2):
+            out_ref[0, 0, part, :, cols] = mm(con_ref[0, part, :, cols], pick).astype(jnp.bfloat16)
+
+
+def shift_call(con, shift_map, dests, width):
+    points, _, rows, _ = con.shape
+    slots = dests.shape[0]
+    grid_spec = pltpu.PrefetchScalarGridSpec(
+        num_scalar_prefetch=1,
+        grid=(points, slots),
+        in_specs=[
+            pl.BlockSpec((1, 2, rows, width), lambda q, k, dest: (q, 0, 0, dest[k])),
+            pl.BlockSpec((1, 1, width), lambda q, k, dest: (q, 0, dest[k])),
+        ],
+        out_specs=pl.BlockSpec((1, 1, 2, rows, width), lambda q, k, dest: (k, q, 0, 0, 0)),
+    )
+    return pl.pallas_call(
+        shift_kernel,
+        grid_spec=grid_spec,
+        out_shape=jax.ShapeDtypeStruct((slots, points, 2, rows, width), jnp.bfloat16),
+        compiler_params=params(),
+        cost_estimate=cost(2 * con.size * GBLK, 4 * con.size),
+    )(dests, con, shift_map.reshape(points, 1, -1))
+
+
+def x_kernel(coded, slots, base_ref, *refs):
+    val_refs, (weight_ref, out_ref, left_ref) = refs[:slots], refs[slots:]
+    rows, depth = val_refs[0].shape[1], val_refs[0].shape[2]
+    half = slots * rows
+
+    @pl.when(pl.program_id(0) == 0)
+    def _():
+        for slot in range(slots):
+            real, imag = val_refs[slot][0], val_refs[slot][1]
+            top = slice(slot * rows, (slot + 1) * rows)
+            low = slice(half + slot * rows, half + (slot + 1) * rows)
+            left_ref[top, 0:depth] = real
+            left_ref[top, depth : 2 * depth] = -imag
+            left_ref[low, 0:depth] = imag
+            left_ref[low, depth : 2 * depth] = real
+
+    weight = weight_ref[0].reshape(2 * depth, weight_ref.shape[3])
+    product = mm(left_ref[...], weight)
+    if coded:
+        encode(product, out_ref)
+    else:
+        out_ref[...] = product
+
+
+def x_call(vals, screened, point, base, width, tiles, coded):
+    slots = len(vals)
+    rows, depth = vals[0].shape[1], vals[0].shape[2]
+    height = 2 * slots * rows
+    out_rows, kind = (height + EXP_ROWS, jnp.int16) if coded else (height, jnp.float32)
+    grid_spec = pltpu.PrefetchScalarGridSpec(
+        num_scalar_prefetch=1,
+        grid=(tiles,),
+        in_specs=[pl.BlockSpec(v.shape, lambda j, b: (0, 0, 0)) for v in vals]
+        + [pl.BlockSpec((1, 2, depth, width), lambda j, b: (point, 0, 0, b[0] + j))],
+        out_specs=pl.BlockSpec((out_rows, width), lambda j, b: (0, j)),
+        scratch_shapes=[pltpu.VMEM((height, 2 * depth), jnp.bfloat16)],
+    )
+    return pl.pallas_call(
+        lambda *refs: x_kernel(coded, slots, *refs),
+        grid_spec=grid_spec,
+        out_shape=jax.ShapeDtypeStruct((out_rows, width * tiles), kind),
+        compiler_params=params(),
+        cost_estimate=cost(
+            2 * height * 2 * depth * width * tiles,
+            4 * depth * width * tiles + out_rows * width * tiles * 3,
+        ),
+    )(base, *vals, screened)
+
+
+def hop_kernel(have, index_ref, *refs):
+    if have:
+        keep_up, near_up, got_up, keep_down, near_down, got_down, out_up, out_down = refs
+    else:
+        keep_up, near_up, keep_down, near_down, out_up, out_down = refs
+        got_up = got_down = None
+    for keep, near, got, out in (
+        (keep_up, near_up, got_up, out_up),
+        (keep_down, near_down, got_down, out_down),
+    ):
+        total = keep[...] + decode(near)
+        if got is not None:
+            total = total + decode(got)
+        encode(total, out)
+
+
+def hop_call(keep, near, got, index, width):
+    height, tall = keep.shape[0], near.shape[0]
+    in_specs, operands = [], []
+    for way in range(2):
+        in_specs += [
+            pl.BlockSpec((height, width), lambda i, at, way=way: (0, at[way])),
+            pl.BlockSpec((tall, width), lambda i, at, way=way: (0, at[way])),
+        ]
+        operands += [keep, near]
+        if got is not None:
+            in_specs.append(pl.BlockSpec((tall, width), lambda i, at: (0, 0)))
+            operands.append(got[way])
+    grid_spec = pltpu.PrefetchScalarGridSpec(
+        num_scalar_prefetch=1,
+        grid=(1,),
+        in_specs=in_specs,
+        out_specs=[pl.BlockSpec((tall, width), lambda i, at: (0, 0))] * 2,
+    )
+    return pl.pallas_call(
+        lambda *refs: hop_kernel(got is not None, *refs),
+        grid_spec=grid_spec,
+        out_shape=[jax.ShapeDtypeStruct((tall, width), jnp.int16)] * 2,
+        compiler_params=params(),
+        cost_estimate=cost(40 * height * width, 16 * height * width),
+    )(index, *operands)
+
+
+def exchange_kernel(slots, *refs):
+    here_refs, (there_ref, coulomb_ref, out_ref, left_ref) = refs[:slots], refs[slots:]
+    rows, depth = here_refs[0].shape[1], here_refs[0].shape[2]
+
+    @pl.when(pl.program_id(0) == 0)
+    def _():
+        for slot in range(slots):
+            for part in range(2):
+                left_ref[
+                    slot * rows : (slot + 1) * rows, part * depth : (part + 1) * depth
+                ] = here_refs[slot][part]
+
+    factor = coulomb_ref[0]
+    real = there_ref[0, 0].astype(jnp.float32) * factor
+    imag = there_ref[0, 1].astype(jnp.float32) * factor
+    right = jnp.concatenate(
+        [jnp.concatenate([real, -imag], axis=1), jnp.concatenate([imag, real], axis=1)], axis=0
+    )
+    high, low = halves(right)
+    left = left_ref[...]
+    out_ref[0] = mm_nt(left, high) + mm_nt(left, low)
+
+
+def exchange_call(heres, there, coulomb):
+    slots = len(heres)
+    points, _, cols, depth = there.shape
+    rows = heres[0].shape[1]
+    height = slots * rows
+    return pl.pallas_call(
+        lambda *refs: exchange_kernel(slots, *refs),
+        grid=(points,),
+        in_specs=[pl.BlockSpec(h.shape, lambda q: (0, 0, 0)) for h in heres]
+        + [
+            pl.BlockSpec((1, 2, cols, depth), lambda q: (q, 0, 0, 0)),
+            pl.BlockSpec((1, 1, depth), lambda q: (q, 0, 0)),
+        ],
+        out_specs=pl.BlockSpec((1, height, 2 * cols), lambda q: (q, 0, 0)),
+        out_shape=jax.ShapeDtypeStruct((points, height, 2 * cols), jnp.float32),
+        scratch_shapes=[pltpu.VMEM((height, 2 * depth), jnp.bfloat16)],
+        compiler_params=params(),
+        cost_estimate=cost(2 * points * height * 2 * cols * 2 * depth * 2, 8 * points * cols * depth),
+    )(*heres, there, coulomb.reshape(points, 1, depth))
+
+
+def tile_kernel(slots, index_ref, *refs):
+    con_refs = refs[:slots]
+    (keep_ref, near_ref, up_ref, down_ref, exch_ref, row_ref, col_direct_ref, col_exch_ref) = refs[
+        slots : slots + 8
+    ]
+    out_ref, con_all, direct_ref, natural_ref = refs[slots + 8 :]
+    total = keep_ref[...] + decode(near_ref) + decode(up_ref) + decode(down_ref)
+    pairs, width = total.shape[0] // 2, total.shape[1]
+    rows = con_refs[0].shape[2]
+    pitch = con_all.shape[0] // slots
+    for slot in range(slots):
+        for part in range(2):
+            con_all[
+                slot * pitch : slot * pitch + rows, part * width : (part + 1) * width
+            ] = con_refs[slot][0, part]
+    real, imag = total[:pairs], total[pairs:]
+    right = jnp.concatenate(
+        [jnp.concatenate([real, -imag], axis=1), jnp.concatenate([imag, real], axis=1)], axis=0
+    )
+    high, low = halves(right)
+    left = con_all[...]
+    direct = mm_nt(left, high) + mm_nt(left, low)
+    lanes = direct_ref.shape[0]
+    for slot in range(slots):
+        start = pl.multiple_of(index_ref[1 + slot] * rows, 8)
+        for lane in range(lanes):
+            direct_ref[lane, pl.ds(start, rows), :] = direct[
+                slot * pitch : slot * pitch + rows, lane * 128 : (lane + 1) * 128
+            ]
+    group = 128 // NV
+    place = lax.broadcasted_iota(jnp.int32, (NC, 128), 1) // NV
+    per_part = lanes // 2
+    for part in range(2):
+        for chunk in range(NC // group):
+            for band in range(NV):
+                block = jnp.zeros((NC, 128), jnp.float32)
+                for step in range(group):
+                    e = chunk * group + step
+                    piece = direct_ref[part * per_part + band // group, pl.ds(e, NC, stride=NC), :]
+                    turn = (NV * (step - band)) % 128
+                    if turn:
+                        piece = pltpu.roll(piece, turn, 1)
+                    block = jnp.where(place == step, piece, block)
+                at = part * NC * NV + chunk * 128
+                natural_ref[band * NC : (band + 1) * NC, at : at + 128] = block
+    pick_rows = row_ref[...]
+    result = None
+    for source, pick_cols in ((natural_ref[...], col_direct_ref), (exch_ref[0], col_exch_ref)):
+        for piece in halves(source):
+            moved = mm(pick_rows, piece).astype(jnp.bfloat16)
+            term = mm(moved, pick_cols[...])
+            result = term if result is None else result + term
+    out_ref[...] = result
+
+
+def tile_call(cons, point, keep, near, got, exch, index, pick_rows, col_direct, col_exch):
+    slots = len(cons)
+    _, _, rows, width = cons[0].shape
+    height, tall = keep.shape[0], near.shape[0]
+    pitch = -(-rows // 16) * 16
+    out_cols = col_direct.shape[1]
+    whole = lambda a: pl.BlockSpec(a.shape, lambda i, at: (0,) * a.ndim)
+    grid_spec = pltpu.PrefetchScalarGridSpec(
+        num_scalar_prefetch=1,
+        grid=(1,),
+        in_specs=[pl.BlockSpec((1, 2, rows, width), lambda i, at: (point, 0, 0, 0))] * slots
+        + [
+            pl.BlockSpec((height, width), lambda i, at: (0, at[0])),
+            pl.BlockSpec((tall, width), lambda i, at: (0, at[0])),
+            whole(got[0]),
+            whole(got[1]),
+            pl.BlockSpec((1,) + exch.shape[1:], lambda i, at: (point, 0, 0)),
+            whole(pick_rows),
+            whole(col_direct),
+            whole(col_exch),
+        ],
+        out_specs=pl.BlockSpec((NT, out_cols), lambda i, at: (0, 0)),
+        scratch_shapes=[
+            pltpu.VMEM((slots * pitch, 2 * width), jnp.bfloat16),
+            pltpu.VMEM((height // 128, NC * NC, 128), jnp.float32),
+            pltpu.VMEM((NT, 2 * NT), jnp.float32),
+        ],
+    )
+    return pl.pallas_call(
+        lambda *refs: tile_kernel(slots, *refs),
+        grid_spec=grid_spec,
+        out_shape=jax.ShapeDtypeStruct((NT, out_cols), jnp.float32),
+        compiler_params=params(),
+        cost_estimate=cost(2.8e9, 8e6),
+    )(index, *cons, keep, near, got[0], got[1], exch, pick_rows, col_direct, col_exch)
+
+
+def swap(value, axis, size, bit):
+    return lax.ppermute(value, axis, [(i, i ^ bit) for i in range(size)])
+
+
+def gather_slots(value, axis, size):
+    slots = [value]
+    bit = size // 2
+    found = {0: value}
+    while bit:
+        for known in sorted(found):
+            found[known ^ bit] = swap(found[known], axis, size, bit)
+        bit //= 2
+    return [found[r] for r in range(size)]
+
+
+def halving_order(bits):
+    order = [0]
+    for bit in reversed(bits):
+        order = order + [o ^ bit for o in order]
+    return order
+
+
+def on_device(outer, inner, *args):
+    (val_density, con_density, screened, coulomb, trans_here, trans_there, shift_map, ordering) = args
+    ga, pair = outer * inner, lax.axis_size("pair")
+    points = con_density.shape[1]
+    slab = con_density.shape[3]
+    width = slab // ga
+    me_ga, me_pair = lax.axis_index("ga"), lax.axis_index("pair")
+    me_outer, me_inner = me_ga // inner, me_ga % inner
+    as_index = lambda *items: jnp.stack([jnp.asarray(i, jnp.int32) for i in items])
+
+    val = jnp.transpose(val_density, (1, 2, 0, 3))
+    vals = [gather_slots(val[q], "pair", pair) for q in range(points)]
+
+    con = jnp.transpose(con_density, (1, 2, 0, 3))
+    dests = me_ga ^ jnp.arange(ga, dtype=jnp.int32)
+    dest_blocks = (dests % inner) * outer + dests // inner
+    sends = shift_call(con, shift_map, dest_blocks, width)
+    cons = [sends[0]] + [swap(sends[k], "ga", ga, k) for k in range(1, ga)]
+
+    other, mine = as_index((1 - me_inner) * outer), as_index(me_inner * outer)
+    gone = [x_call(vals[q], screened, q, other, width, outer, True) for q in range(points)]
+    near = [swap(gone[q], "ga", ga, 1) for q in range(points)]
+    keep = [x_call(vals[q], screened, q, mine, width, outer, False) for q in range(points)]
+
+    here = jnp.transpose(trans_here, (1, 0, 2))
+    heres = gather_slots(here, "pair", pair)
+    there = jnp.transpose(trans_there, (1, 2, 0, 3))
+    exch = exchange_call(heres, there, coulomb)
+
+    row_bits, col_bits = [1 << b for b in range(pair.bit_length() - 1)], [1]
+    col_bits += [1 << b for b in reversed(range(1, ga.bit_length() - 1))]
+    row_count, col_count = NT // pair, NT // ga
+    row_slots = jnp.asarray(halving_order(row_bits), jnp.int32)
+    col_slots = jnp.asarray(halving_order(col_bits), jnp.int32)
+    row_trans = ordering.reshape(pair, row_count)[me_pair ^ row_slots].reshape(-1)
+    at_row = ((row_trans // row_count) ^ me_pair) * row_count + row_trans % row_count
+    pick_rows = (at_row[:, None] == jnp.arange(NT, dtype=jnp.int32)[None, :]).astype(jnp.bfloat16)
+    col_trans = ordering.reshape(ga, col_count)[me_ga ^ col_slots]
+    fill = jnp.full((ga, 64 - col_count), -1, jnp.int32)
+    at_direct = (col_trans % NC) * NV + col_trans // NC
+    at_exch = jnp.where(col_trans // row_count == me_pair, col_trans % row_count, -1)
+
+    def pick_cols(at, size, scale):
+        real = jnp.concatenate([at, fill], axis=1)
+        imag = jnp.where(real >= 0, real + size, -1)
+        lanes = jnp.stack([real, imag], axis=1).reshape(1, -1)
+        hot = lanes == jnp.arange(2 * size, dtype=jnp.int32)[:, None]
+        return jnp.where(hot, scale, 0.0).astype(jnp.bfloat16)
+
+    col_direct, col_exch = pick_cols(at_direct, NT, -1.0), pick_cols(at_exch, row_count, 2.0)
+
+    up_pairs = [
+        [(p * inner + y, (p + 1) * inner + y) for p in range(step) for y in range(inner)]
+        for step in range(outer)
+    ]
+    last = outer - 1
+    down_pairs = [
+        [((last - p) * inner + y, (last - p - 1) * inner + y) for p in range(step) for y in range(inner)]
+        for step in range(outer)
+    ]
+    hop_index = [
+        as_index(
+            jnp.clip(outer - step + me_outer, 0, last), jnp.clip(step - outer + me_outer, 0, last)
+        )
+        for step in range(outer)
+    ]
+    got = [None] * points
+    for step in range(1, outer):
+        for q in range(points):
+            up, down = hop_call(keep[q], near[q], got[q], hop_index[step], width)
+            got[q] = (
+                lax.ppermute(up, "ga", up_pairs[step]),
+                lax.ppermute(down, "ga", down_pairs[step]),
+            )
+    tile_index = jnp.concatenate([as_index(me_outer), dests])
+    outs = []
+    for q in range(points):
+        part = tile_call(
+            cons, q, keep[q], near[q], got[q], exch, tile_index, pick_rows, col_direct, col_exch
+        )
+        for bit in row_bits:
+            half = part.shape[0] // 2
+            part = part[:half] + swap(part[half:], "pair", pair, bit)
+        for bit in col_bits:
+            half = part.shape[1] // 2
+            part = part[:, :half] + swap(part[:, half:], "ga", ga, bit)
+        outs.append(jnp.stack([part[:, :col_count], part[:, 64 : 64 + col_count]]))
+    return jnp.stack(outs)
 
 
 def contract_float(left, right):
@@ -30,7 +460,7 @@
     return jnp.stack([first, second], axis=2)
 
 
-def on_device(
+def on_any_device(
     val_density, con_density, screened, coulomb, trans_here, trans_there, shift_map, ordering
 ):
     con_count = con_density.shape[0]
@@ -99,6 +529,24 @@
         P(),
     )
     out_specs = P(None, None, "pair", "ga")
-    return jax.shard_map(
-        on_device, mesh=mesh, in_specs=in_specs, out_specs=out_specs, check_vma=False
-    )
+
+    def run(*args):
+        ga, pair = mesh.shape["ga"], mesh.shape["pair"]
+        inner = 1 << (int(math.log2(ga)) // 2)
+        con_count, h_count = args[1].shape[0], args[1].shape[3]
+        suits = (
+            ga & (ga - 1) == 0
+            and pair & (pair - 1) == 0
+            and inner == 2
+            and h_count % (ga * pair * GBLK) == 0
+            and con_count % (8 * ga) == 0
+            and args[0].shape[0] % (16 * pair) == 0
+            and NT % (16 * pair) == 0
+            and NT // ga <= 64
+        )
+        body = (lambda *a: on_device(ga // inner, inner, *a)) if suits else on_any_device
+        return jax.shard_map(
+            body, mesh=mesh, in_specs=in_specs, out_specs=out_specs, check_vma=False
+        )(*args)
+
+    return run

time: 787 us -> 291 us (0.37)
  waiting for transfers between devices: 414 us -> 54.3 us
  local copies, waits for them, and re-layouts: 192 us -> 24.8 us
  Pallas kernels: 0 us -> 119 us
  matrix products: 82.7 us -> 0 us
  starting transfers between devices: 0.6 us -> 82.2 us
  other arithmetic: 73.6 us -> 7.25 us
  between operations: 13.9 us -> 1.05 us
    all_gather x5 -> x0, waiting for transfers between devices: 222 us -> none  [the longest x1 196 us: on_device(): whole_con = lax.all_gather(shifted, 'ga', axis=0, tiled=True)]
    gather x2, local copies, waits for them, and re-layouts: 161 us -> 1.12 us  [the longest x1 0.56 us: on_device(): ordering.reshape(pair, row_count)[me_pair ^ row_slots].reshape(-1)]
    pallas_call x0 -> x20, Pallas kernels: none -> 119 us  [the longest x6 37 us: x_call(): pl.pallas_call(lambda *refs: x_kernel(coded, slots, *refs), grid_spec=gri...]
    reduce_scatter x1 -> x0, waiting for transfers between devices: 98.5 us -> none  [on_device(): lax.psum_scatter(times_cols(whole_con, screened), 'pair', scatter_dimensi...]
    psum x1 -> x0, waiting for transfers between devices: 94 us -> none  [on_device(): direct_sum, exch_sum = lax.psum((direct_part, exch_part), 'ga')]
    dot_general x14 -> x0, matrix products: 82.7 us -> none  [the longest x1 15.8 us: times_cols(): jnp.einsum('nkh,kgh->nkg', rows[:, :, 1], weights[:, 0], preferred_elemen...]
    ppermute x0 -> x55, starting transfers between devices: none -> 82.2 us  [the longest x37 43.8 us: swap(): return lax.ppermute(value, axis, [(i, i ^ bit) for i in range(size)])]
    ppermute x0 -> x55, waiting for transfers between devices: none -> 54.3 us  [the longest x37 54.2 us: swap(): return lax.ppermute(value, axis, [(i, i ^ bit) for i in range(size)])]
  transfers between devices with their start and end apart: 7 -> 55, of which waited for: 4 -> 13; matrix products, arithmetic and copies ran while one was open for 40% -> 8% of each run, Pallas kernels for 0% -> 41%
where the time goes in v1:
time: 291 us; the launch traced here: 288 us
  Pallas kernels  119 us (41%)
  starting transfers between devices  82.2 us (28%)
  waiting for transfers between devices  54.3 us (19%)
  local copies, waits for them, and re-layouts  24.8 us (9%)
  other arithmetic  7.25 us (2%)
    ppermute x37, waiting for transfers between devices, swap(): return lax.ppermute(value, axis, [(i, i ^ bit) for i in range(size)])  54.2 us
    ppermute x37, starting transfers between devices, swap(): return lax.ppermute(value, axis, [(i, i ^ bit) for i in range(size)])  43.8 us
    pallas_call x6, Pallas kernels, x_call(): pl.pallas_call(lambda *refs: x_kernel(coded, slots, *refs), grid_spec=gri...  37 us
    pallas_call x9, Pallas kernels, hop_call(): pl.pallas_call(lambda *refs: hop_kernel(got is not None, *refs), grid_spe...  30.7 us
    ppermute x9, starting transfers between devices, on_device(): lax.ppermute(up, 'ga', up_pairs[step])  30.1 us
    pallas_call x3, Pallas kernels, tile_call(): pl.pallas_call(lambda *refs: tile_kernel(slots, *refs), grid_spec=grid_sp...  30 us
    pallas_call x1, Pallas kernels, shift_call(): pl.pallas_call(shift_kernel, grid_spec=grid_spec, out_shape=jax.ShapeDtyp...  15.5 us
    unnamed x112, local copies, waits for them, and re-layouts  14.1 us
  transfers between devices with their start and end apart: 55, of which 13 were waited for; matrix products, arithmetic and copies ran while one was open for 8% of the time, Pallas kernels for 41%

profile of v1, /device:TPU:0, one launch (start us, length us, event | category | flops | bytes accessed | tf_op | source)
XLA Modules:
  0.0 288.3 jit_solution(18093383559437045689)
XLA Ops:
  10.3 15.5 %shard_map.100 = bf16[8,3,2,72,256]{4,3,2,1,0:T(8,128)(2,1)} custom-call(s32[8]{0:T(128)} %get-tuple-element.67.dest_ref, bf16[3,2,72,2048]{3,2,1,0:T(8,128)(2,1)} %bitcast.69, s32[3,1,2048]{2,1,0:T(1,128)} %reshape.49.map_ref), custom_call_target="tpu_custom_call" | custom-call | flops 226492416 | bytes 3538944 | tf_op jit(solution)/shard_map/pallas_call | solution.py:93
  33.1 6.1 %shard_map.115 = s16[528,1024]{1,0:T(8,128)(2,1)} custom-call(s32[1]{0:T(128)} %bitcast.13.refs_0_, bf16[2,64,1024]{2,1,0:T(8,128)(2,1)} %copy-done.8, bf16[2,64,1024]{2,1,0:T(8,128)(2,1)} %copy-done.17, bf16[2,64,1024]{2,1,0:T(8,128)(2,1)} %copy-done.19, bf16[2,64,1024]{2,1,0:T(8,128)(2,1)} %copy-done.21, bf16[3,2,1024,2048]{3,2,1,0:T(8,128)(2,1)} %refs_5_.11), custom_call_target="tpu_custom_call" | custom-call | flops 2147483648 | bytes 5816320 | tf_op jit(solution)/shard_map/pallas_call | solution.py:139
  40.7 6.1 %shard_map.109 = s16[528,1024]{1,0:T(8,128)(2,1)} custom-call(s32[1]{0:T(128)} %bitcast.13.refs_0_, bf16[2,64,1024]{2,1,0:T(8,128)(2,1)} %copy-done.7, bf16[2,64,1024]{2,1,0:T(8,128)(2,1)} %collective-permute-done.25.refs_2_, bf16[2,64,1024]{2,1,0:T(8,128)(2,1)} %collective-permute-done.26.refs_3_, bf16[2,64,1024]{2,1,0:T(8,128)(2,1)} %copy-done.20, ...), custom_call_target="tpu_custom_call" | custom-call | flops 2147483648 | bytes 5816320 | tf_op jit(solution)/shard_map/pallas_call | solution.py:139
  51.3 6.1 %shard_map.102 = s16[528,1024]{1,0:T(8,128)(2,1)} custom-call(s32[1]{0:T(128)} %bitcast.13.refs_0_, bf16[2,64,1024]{2,1,0:T(8,128)(2,1)} %copy-done.6, bf16[2,64,1024]{2,1,0:T(8,128)(2,1)} %copy-done.16, bf16[2,64,1024]{2,1,0:T(8,128)(2,1)} %collective-permute-done.8.refs_3_, bf16[2,64,1024]{2,1,0:T(8,128)(2,1)} %copy-done.18, ...), custom_call_target="tpu_custom_call" | custom-call | flops 2147483648 | bytes 5816320 | tf_op jit(solution)/shard_map/pallas_call | solution.py:139
  61.6 4.6 %collective-permute-done.43.refs_2_.refs_4_.refs_5_.refs_10_ = s16[528,1024]{1,0:T(8,128)(2,1)S(1)} collective-permute-done((s16[528,1024]{1,0:T(8,128)(2,1)}, s16[528,1024]{1,0:T(8,128)(2,1)S(1)}, u32[]{:S(2)}, u32[]{:S(2)}) %collective-permute-start.43) | collective-permute-done | bytes 1081376 | tf_op jit(solution)/shard_map/ppermute | solution.py:331
  67.9 6.2 %shard_map.114.refs_1_.refs_3_.refs_4_.refs_9_ = f32[512,1024]{1,0:T(8,128)} custom-call(s32[1]{0:T(128)} %bitcast.10.refs_0_, bf16[2,64,1024]{2,1,0:T(8,128)(2,1)} %copy-done.8, bf16[2,64,1024]{2,1,0:T(8,128)(2,1)} %copy-done.17, bf16[2,64,1024]{2,1,0:T(8,128)(2,1)} %copy-done.19, bf16[2,64,1024]{2,1,0:T(8,128)(2,1)} %copy-done.21, ...), custom_call_target="tpu_custom_call" | custom-call | flops 2147483648 | bytes 5767168 | tf_op jit(solution)/shard_map/pallas_call | solution.py:139
  80.1 13.9 %collective-permute-done.28.refs_2_.refs_4_.refs_5_.refs_10_ = s16[528,1024]{1,0:T(8,128)(2,1)S(1)} collective-permute-done((s16[528,1024]{1,0:T(8,128)(2,1)}, s16[528,1024]{1,0:T(8,128)(2,1)S(1)}, u32[]{:S(2)}, u32[]{:S(2)}) %collective-permute-start.28) | collective-permute-done | bytes 1081376 | tf_op jit(solution)/shard_map/ppermute | solution.py:331
  94.7 6.2 %shard_map.108.refs_1_.refs_3_.refs_4_.refs_9_ = f32[512,1024]{1,0:T(8,128)} custom-call(s32[1]{0:T(128)} %bitcast.10.refs_0_, bf16[2,64,1024]{2,1,0:T(8,128)(2,1)} %copy-done.7, bf16[2,64,1024]{2,1,0:T(8,128)(2,1)} %collective-permute-done.25.refs_2_, bf16[2,64,1024]{2,1,0:T(8,128)(2,1)} %collective-permute-done.26.refs_3_, ...), custom_call_target="tpu_custom_call" | custom-call | flops 2147483648 | bytes 5767168 | tf_op jit(solution)/shard_map/pallas_call | solution.py:139
  120.8 6.3 %shard_map.101.refs_1_.refs_3_.refs_4_.refs_9_ = f32[512,1024]{1,0:T(8,128)} custom-call(s32[1]{0:T(128)} %bitcast.10.refs_0_, bf16[2,64,1024]{2,1,0:T(8,128)(2,1)} %copy-done.6, bf16[2,64,1024]{2,1,0:T(8,128)(2,1)} %copy-done.16, bf16[2,64,1024]{2,1,0:T(8,128)(2,1)} %collective-permute-done.8.refs_3_, bf16[2,64,1024]{2,1,0:T(8,128)(2,1)} %copy-done.18, ...), custom_call_target="tpu_custom_call" | custom-call | flops 2147483648 | bytes 5767168 | tf_op jit(solution)/shard_map/pallas_call | solution.py:139
  147.0 5.5 %collective-permute-start.4 = (bf16[3,2,72,256]{3,2,1,0:T(8,128)(2,1)S(1)}, bf16[3,2,72,256]{3,2,1,0:T(8,128)(2,1)S(1)}, u32[]{:S(2)}, u32[]{:S(2)}) collective-permute-start(bf16[3,2,72,256]{3,2,1,0:T(8,128)(2,1)S(1)} %copy-done.42), channel_id=1, source_target_pairs={{0,20},{4,16},{8,28},{12,24},{16,4},{20,0},{24,12},{28,8},{1,21},{... | collective-permute-start | bytes 663560 | tf_op jit(solution)/shard_map/ppermute | solution.py:331
  152.9 4.4 %collective-permute-start.6 = (bf16[3,2,72,256]{3,2,1,0:T(8,128)(2,1)S(1)}, bf16[3,2,72,256]{3,2,1,0:T(8,128)(2,1)S(1)}, u32[]{:S(2)}, u32[]{:S(2)}) collective-permute-start(bf16[3,2,72,256]{3,2,1,0:T(8,128)(2,1)S(1)} %copy-done.40), channel_id=1, source_target_pairs={{0,28},{4,24},{8,20},{12,16},{16,12},{20,8},{24,4},{28,0},{1,29},{... | collective-permute-start | bytes 663560 | tf_op jit(solution)/shard_map/ppermute | solution.py:331
  162.4 5.5 %shard_map.106.refs_13_ = f32[3,384,192]{2,1,0:T(8,128)} custom-call(bf16[2,96,1024]{2,1,0:T(8,128)(2,1)} %bitcast.68.refs_0_, bf16[2,96,1024]{2,1,0:T(8,128)(2,1)} %copy-done.48, bf16[2,96,1024]{2,1,0:T(8,128)(2,1)} %collective-permute-done.18.refs_2_, bf16[2,96,1024]{2,1,0:T(8,128)(2,1)} %collective-permute-done.19.refs_3_, ...), custom_call_target="tpu_custom_call" | custom-call | flops 1811939328 | bytes 2359296 | tf_op jit(solution)/shard_map/pallas_call | solution.py:222
  175.1 4.6 %collective-permute-start.13 = (s16[528,256]{1,0:T(8,128)(2,1)S(1)}, s16[528,256]{1,0:T(8,128)(2,1)S(1)}, u32[]{:S(2)}, u32[]{:S(2)}) collective-permute-start(s16[528,256]{1,0:T(8,128)(2,1)S(1)} %copy-done.52), channel_id=1, source_target_pairs={{0,8},{4,12},{8,16},{12,20},{1,9},{5,13},{9,17},{13,21},{2,10},{6,... | collective-permute-start | bytes 811016 | tf_op jit(solution)/shard_map/ppermute | solution.py:423
  180.4 4.6 %collective-permute-start.33 = (s16[528,256]{1,0:T(8,128)(2,1)}, s16[528,256]{1,0:T(8,128)(2,1)S(1)}, u32[]{:S(2)}, u32[]{:S(2)}) collective-permute-start(s16[528,256]{1,0:T(8,128)(2,1)} %get-tuple-element.33), channel_id=1, source_target_pairs={{0,8},{4,12},{8,16},{12,20},{16,24},{20,28},{1,9},{5,13},{9,17},{1... | collective-permute-start | bytes 811016 | tf_op jit(solution)/shard_map/ppermute | solution.py:423
  187.0 10.0 %shard_map.119 = f32[384,1024]{1,0:T(8,128)} custom-call(s32[9]{0:T(128)} %pad_add_fusion.2.refs_0_, bf16[3,2,72,256]{3,2,1,0:T(8,128)(2,1)} %get-tuple-element.48.refs_1_, bf16[3,2,72,256]{3,2,1,0:T(8,128)(2,1)} %collective-permute-done.refs_2_, bf16[3,2,72,256]{3,2,1,0:T(8,128)(2,1)} %copy-done.9, bf16[3,2,72,256]{3,2,1,0:T(8,128)(2,1)} %collective-permute-done.2.refs_4_, ...), custom_call_target="tpu_custom_call" | custom-call | flops 2800000000 | bytes 8000000 | tf_op jit(solution)/shard_map/pallas_call | solution.py:321
  203.2 4.9 %collective-permute-start.15 = (s16[528,256]{1,0:T(8,128)(2,1)}, s16[528,256]{1,0:T(8,128)(2,1)S(1)}, u32[]{:S(2)}, u32[]{:S(2)}) collective-permute-start(s16[528,256]{1,0:T(8,128)(2,1)} %get-tuple-element.27), channel_id=1, source_target_pairs={{0,8},{4,12},{8,16},{12,20},{16,24},{20,28},{1,9},{5,13},{9,17},{1... | collective-permute-start | bytes 811016 | tf_op jit(solution)/shard_map/ppermute | solution.py:423
  211.0 10.0 %shard_map.113 = f32[384,1024]{1,0:T(8,128)} custom-call(s32[9]{0:T(128)} %pad_add_fusion.2.refs_0_, bf16[3,2,72,256]{3,2,1,0:T(8,128)(2,1)} %get-tuple-element.48.refs_1_, bf16[3,2,72,256]{3,2,1,0:T(8,128)(2,1)} %collective-permute-done.refs_2_, bf16[3,2,72,256]{3,2,1,0:T(8,128)(2,1)} %copy-done.9, bf16[3,2,72,256]{3,2,1,0:T(8,128)(2,1)} %collective-permute-done.2.refs_4_, ...), custom_call_target="tpu_custom_call" | custom-call | flops 2800000000 | bytes 8000000 | tf_op jit(solution)/shard_map/pallas_call | solution.py:321
  223.9 10.0 %shard_map.107 = f32[384,1024]{1,0:T(8,128)} custom-call(s32[9]{0:T(128)} %pad_add_fusion.2.refs_0_, bf16[3,2,72,256]{3,2,1,0:T(8,128)(2,1)} %get-tuple-element.48.refs_1_, bf16[3,2,72,256]{3,2,1,0:T(8,128)(2,1)} %collective-permute-done.refs_2_, bf16[3,2,72,256]{3,2,1,0:T(8,128)(2,1)} %copy-done.9, bf16[3,2,72,256]{3,2,1,0:T(8,128)(2,1)} %collective-permute-done.2.refs_4_, ...), custom_call_target="tpu_custom_call" | custom-call | flops 2800000000 | bytes 8000000 | tf_op jit(solution)/shard_map/pallas_call | solution.py:321
  239.2 8.6 %collective-permute-done.51 = f32[96,1024]{1,0:T(8,128)S(1)} collective-permute-done((f32[96,1024]{1,0:T(8,128)S(1)}, f32[96,1024]{1,0:T(8,128)S(1)}, u32[]{:S(2)}, u32[]{:S(2)}) %collective-permute-start.51) | collective-permute-done | bytes 393248 | tf_op jit(solution)/shard_map/ppermute | solution.py:331
  249.3 7.0 %collective-permute-done.36 = f32[96,1024]{1,0:T(8,128)S(1)} collective-permute-done((f32[96,1024]{1,0:T(8,128)S(1)}, f32[96,1024]{1,0:T(8,128)S(1)}, u32[]{:S(2)}, u32[]{:S(2)}) %collective-permute-start.36) | collective-permute-done | bytes 393248 | tf_op jit(solution)/shard_map/ppermute | solution.py:331
  257.7 6.3 %collective-permute-done.21 = f32[96,1024]{1,0:T(8,128)S(1)} collective-permute-done((f32[96,1024]{1,0:T(8,128)S(1)}, f32[96,1024]{1,0:T(8,128)S(1)}, u32[]{:S(2)}, u32[]{:S(2)}) %collective-permute-start.21) | collective-permute-done | bytes 393248 | tf_op jit(solution)/shard_map/ppermute | solution.py:331
  265.5 4.5 %collective-permute-start.53 = (f32[96,256]{1,0:T(8,128)S(1)}, f32[96,256]{1,0:T(8,128)S(1)}, u32[]{:S(2)}, u32[]{:S(2)}) collective-permute-start(f32[96,256]{1,0:T(8,128)S(1)} %slice.234), channel_id=1, source_target_pairs={{0,16},{4,20},{8,24},{12,28},{16,0},{20,4},{24,8},{28,12},{1,17},{... | collective-permute-start | bytes 294920 | tf_op jit(solution)/shard_map/ppermute | solution.py:331
  270.4 4.5 %collective-permute-start.23 = (f32[96,256]{1,0:T(8,128)S(1)}, f32[96,256]{1,0:T(8,128)S(1)}, u32[]{:S(2)}, u32[]{:S(2)}) collective-permute-start(f32[96,256]{1,0:T(8,128)S(1)} %slice.208), channel_id=1, source_target_pairs={{0,16},{4,20},{8,24},{12,28},{16,0},{20,4},{24,8},{28,12},{1,17},{... | collective-permute-start | bytes 294920 | tf_op jit(solution)/shard_map/ppermute | solution.py:331
  274.9 4.9 %collective-permute-done.53 = f32[96,256]{1,0:T(8,128)S(1)} collective-permute-done((f32[96,256]{1,0:T(8,128)S(1)}, f32[96,256]{1,0:T(8,128)S(1)}, u32[]{:S(2)}, u32[]{:S(2)}) %collective-permute-start.53) | collective-permute-done | bytes 98336 | tf_op jit(solution)/shard_map/ppermute | solution.py:331
  (291 shorter events, 121.1 us)
Async XLA Ops:
  1.6 29.1 %collective-permute-start.40 = (bf16[2,64,1024]{2,1,0:T(8,128)(2,1)S(1)}, bf16[2,64,1024]{2,1,0:T(8,128)(2,1)S(1)}, u32[]{:S(2)}, u32[]{:S(2)}) collective-permute-start(bf16[2,64,1024]{2,1,0:T(8,128)(2,1)S(1)} %get-tuple-element.50.refs_1_), channel_id=1, source_target_pairs={{0,1},{1,0},{2,3},{3,2},{4,5},{5,4},{6,7},{7,6},{8,9},{9,8},{10,11... | collective-permute-start | bytes 786440 | tf_op jit(solution)/shard_map/ppermute | solution.py:331
  2.1 27.9 %collective-permute-start.41 = (bf16[2,64,1024]{2,1,0:T(8,128)(2,1)S(1)}, bf16[2,64,1024]{2,1,0:T(8,128)(2,1)S(1)}, u32[]{:S(2)}, u32[]{:S(2)}) collective-permute-start(bf16[2,64,1024]{2,1,0:T(8,128)(2,1)S(1)} %get-tuple-element.50.refs_1_), channel_id=1, source_target_pairs={{0,2},{1,3},{2,0},{3,1},{4,6},{5,7},{6,4},{7,5},{8,10},{9,11},{10,... | collective-permute-start | bytes 786440 | tf_op jit(solution)/shard_map/ppermute | solution.py:331
  4.7 34.5 %collective-permute-start.25 = (bf16[2,64,1024]{2,1,0:T(8,128)(2,1)S(1)}, bf16[2,64,1024]{2,1,0:T(8,128)(2,1)}, u32[]{:S(2)}, u32[]{:S(2)}) collective-permute-start(bf16[2,64,1024]{2,1,0:T(8,128)(2,1)S(1)} %get-tuple-element.51.refs_1_), channel_id=1, source_target_pairs={{0,1},{1,0},{2,3},{3,2},{4,5},{5,4},{6,7},{7,6},{8,9},{9,8},{10,11... | collective-permute-start | bytes 786440 | tf_op jit(solution)/shard_map/ppermute | solution.py:331
  4.8 25.3 %collective-permute-start.26 = (bf16[2,64,1024]{2,1,0:T(8,128)(2,1)S(1)}, bf16[2,64,1024]{2,1,0:T(8,128)(2,1)}, u32[]{:S(2)}, u32[]{:S(2)}) collective-permute-start(bf16[2,64,1024]{2,1,0:T(8,128)(2,1)S(1)} %get-tuple-element.51.refs_1_), channel_id=1, source_target_pairs={{0,2},{1,3},{2,0},{3,1},{4,6},{5,7},{6,4},{7,5},{8,10},{9,11},{10,... | collective-permute-start | bytes 786440 | tf_op jit(solution)/shard_map/ppermute | solution.py:331
  5.1 25.7 %collective-permute-start.8 = (bf16[2,64,1024]{2,1,0:T(8,128)(2,1)S(1)}, bf16[2,64,1024]{2,1,0:T(8,128)(2,1)}, u32[]{:S(2)}, u32[]{:S(2)}) collective-permute-start(bf16[2,64,1024]{2,1,0:T(8,128)(2,1)S(1)} %get-tuple-element.49.refs_1_), channel_id=1, source_target_pairs={{0,2},{1,3},{2,0},{3,1},{4,6},{5,7},{6,4},{7,5},{8,10},{9,11},{10,... | collective-permute-start | bytes 786440 | tf_op jit(solution)/shard_map/ppermute | solution.py:331
  30.8 46.4 %collective-permute-start = (bf16[3,2,72,256]{3,2,1,0:T(8,128)(2,1)}, bf16[3,2,72,256]{3,2,1,0:T(8,128)(2,1)}, u32[]{:S(2)}, u32[]{:S(2)}) collective-permute-start(bf16[3,2,72,256]{3,2,1,0:T(8,128)(2,1)} %get-tuple-element.47), channel_id=1, source_target_pairs={{0,4},{4,0},{8,12},{12,8},{16,20},{20,16},{24,28},{28,24},{1,5},{5... | collective-permute-start | bytes 663560 | tf_op jit(solution)/shard_map/ppermute | solution.py:331
  39.2 26.9 %collective-permute-start.43 = (s16[528,1024]{1,0:T(8,128)(2,1)}, s16[528,1024]{1,0:T(8,128)(2,1)S(1)}, u32[]{:S(2)}, u32[]{:S(2)}) collective-permute-start(s16[528,1024]{1,0:T(8,128)(2,1)} %shard_map.115), channel_id=1, source_target_pairs={{0,4},{4,0},{8,12},{12,8},{16,20},{20,16},{24,28},{28,24},{1,5},{5... | collective-permute-start | bytes 3244040 | tf_op jit(solution)/shard_map/ppermute | solution.py:331
  46.8 47.2 %collective-permute-start.28 = (s16[528,1024]{1,0:T(8,128)(2,1)}, s16[528,1024]{1,0:T(8,128)(2,1)S(1)}, u32[]{:S(2)}, u32[]{:S(2)}) collective-permute-start(s16[528,1024]{1,0:T(8,128)(2,1)} %shard_map.109), channel_id=1, source_target_pairs={{0,4},{4,0},{8,12},{12,8},{16,20},{20,16},{24,28},{28,24},{1,5},{5... | collective-permute-start | bytes 3244040 | tf_op jit(solution)/shard_map/ppermute | solution.py:331
  49.0 28.8 %collective-permute-start.1 = (bf16[3,2,72,256]{3,2,1,0:T(8,128)(2,1)}, bf16[3,2,72,256]{3,2,1,0:T(8,128)(2,1)S(1)}, u32[]{:S(2)}, u32[]{:S(2)}) collective-permute-start(bf16[3,2,72,256]{3,2,1,0:T(8,128)(2,1)} %get-tuple-element.46), channel_id=1, source_target_pairs={{0,8},{4,12},{8,0},{12,4},{16,24},{20,28},{24,16},{28,20},{1,9},{5... | collective-permute-start | bytes 663560 | tf_op jit(solution)/shard_map/ppermute | solution.py:331
  57.4 59.0 %collective-permute-start.10 = (s16[528,1024]{1,0:T(8,128)(2,1)}, s16[528,1024]{1,0:T(8,128)(2,1)S(1)}, u32[]{:S(2)}, u32[]{:S(2)}) collective-permute-start(s16[528,1024]{1,0:T(8,128)(2,1)} %shard_map.102), channel_id=1, source_target_pairs={{0,4},{4,0},{8,12},{12,8},{16,20},{20,16},{24,28},{28,24},{1,5},{5... | collective-permute-start | bytes 3244040 | tf_op jit(solution)/shard_map/ppermute | solution.py:331
  66.1 38.0 %collective-permute-start.2 = (bf16[3,2,72,256]{3,2,1,0:T(8,128)(2,1)}, bf16[3,2,72,256]{3,2,1,0:T(8,128)(2,1)}, u32[]{:S(2)}, u32[]{:S(2)}) collective-permute-start(bf16[3,2,72,256]{3,2,1,0:T(8,128)(2,1)} %get-tuple-element.45), channel_id=1, source_target_pairs={{0,12},{4,8},{8,4},{12,0},{16,28},{20,24},{24,20},{28,16},{1,13},{... | collective-permute-start | bytes 663560 | tf_op jit(solution)/shard_map/ppermute | solution.py:331
  77.2 35.4 %collective-permute-start.18 = (bf16[2,96,1024]{2,1,0:T(8,128)(2,1)}, bf16[2,96,1024]{2,1,0:T(8,128)(2,1)}, u32[]{:S(2)}, u32[]{:S(2)}) collective-permute-start(bf16[2,96,1024]{2,1,0:T(8,128)(2,1)} %bitcast.68.refs_0_), channel_id=1, source_target_pairs={{0,2},{1,3},{2,0},{3,1},{4,6},{5,7},{6,4},{7,5},{8,10},{9,11},{10,... | collective-permute-start | bytes 1179656 | tf_op jit(solution)/shard_map/ppermute | solution.py:331
  77.8 29.8 %collective-permute-start.44 = (s16[528,256]{1,0:T(8,128)(2,1)}, s16[528,256]{1,0:T(8,128)(2,1)S(1)}, u32[]{:S(2)}, u32[]{:S(2)}) collective-permute-start(s16[528,256]{1,0:T(8,128)(2,1)} %get-tuple-element.35), channel_id=1, source_target_pairs={{0,8},{4,12},{1,9},{5,13},{2,10},{6,14},{3,11},{7,15}} | collective-permute-start | bytes 811016 | tf_op jit(solution)/shard_map/ppermute | solution.py:423
  108.3 29.6 %collective-permute-start.17 = (bf16[2,96,1024]{2,1,0:T(8,128)(2,1)}, bf16[2,96,1024]{2,1,0:T(8,128)(2,1)S(1)}, u32[]{:S(2)}, u32[]{:S(2)}) collective-permute-start(bf16[2,96,1024]{2,1,0:T(8,128)(2,1)} %bitcast.68.refs_0_), channel_id=1, source_target_pairs={{0,1},{1,0},{2,3},{3,2},{4,5},{5,4},{6,7},{7,6},{8,9},{9,8},{10,11... | collective-permute-start | bytes 1179656 | tf_op jit(solution)/shard_map/ppermute | solution.py:331
  120.7 26.3 %collective-permute-start.19 = (bf16[2,96,1024]{2,1,0:T(8,128)(2,1)}, bf16[2,96,1024]{2,1,0:T(8,128)(2,1)}, u32[]{:S(2)}, u32[]{:S(2)}) collective-permute-start(bf16[2,96,1024]{2,1,0:T(8,128)(2,1)} %collective-permute-done.18.refs_2_), channel_id=1, source_target_pairs={{0,1},{1,0},{2,3},{3,2},{4,5},{5,4},{6,7},{7,6},{8,9},{9,8},{10,11... | collective-permute-start | bytes 1179656 | tf_op jit(solution)/shard_map/ppermute | solution.py:331
  147.0 28.1 %collective-permute-start.4 = (bf16[3,2,72,256]{3,2,1,0:T(8,128)(2,1)S(1)}, bf16[3,2,72,256]{3,2,1,0:T(8,128)(2,1)S(1)}, u32[]{:S(2)}, u32[]{:S(2)}) collective-permute-start(bf16[3,2,72,256]{3,2,1,0:T(8,128)(2,1)S(1)} %copy-done.42), channel_id=1, source_target_pairs={{0,20},{4,16},{8,28},{12,24},{16,4},{20,0},{24,12},{28,8},{1,21},{... | collective-permute-start | bytes 663560 | tf_op jit(solution)/shard_map/ppermute | solution.py:331
  152.5 27.1 %collective-permute-start.5 = (bf16[3,2,72,256]{3,2,1,0:T(8,128)(2,1)S(1)}, bf16[3,2,72,256]{3,2,1,0:T(8,128)(2,1)S(1)}, u32[]{:S(2)}, u32[]{:S(2)}) collective-permute-start(bf16[3,2,72,256]{3,2,1,0:T(8,128)(2,1)S(1)} %copy-done.41), channel_id=1, source_target_pairs={{0,24},{4,28},{8,16},{12,20},{16,8},{20,12},{24,0},{28,4},{1,25},{... | collective-permute-start | bytes 663560 | tf_op jit(solution)/shard_map/ppermute | solution.py:331
  152.9 27.5 %collective-permute-start.6 = (bf16[3,2,72,256]{3,2,1,0:T(8,128)(2,1)S(1)}, bf16[3,2,72,256]{3,2,1,0:T(8,128)(2,1)S(1)}, u32[]{:S(2)}, u32[]{:S(2)}) collective-permute-start(bf16[3,2,72,256]{3,2,1,0:T(8,128)(2,1)S(1)} %copy-done.40), channel_id=1, source_target_pairs={{0,28},{4,24},{8,20},{12,16},{16,12},{20,8},{24,4},{28,0},{1,29},{... | collective-permute-start | bytes 663560 | tf_op jit(solution)/shard_map/ppermute | solution.py:331
  157.2 27.8 %collective-permute-start.48 = (s16[528,256]{1,0:T(8,128)(2,1)}, s16[528,256]{1,0:T(8,128)(2,1)S(1)}, u32[]{:S(2)}, u32[]{:S(2)}) collective-permute-start(s16[528,256]{1,0:T(8,128)(2,1)} %get-tuple-element.39), channel_id=1, source_target_pairs={{0,8},{4,12},{8,16},{12,20},{16,24},{20,28},{1,9},{5,13},{9,17},{1... | collective-permute-start | bytes 811016 | tf_op jit(solution)/shard_map/ppermute | solution.py:423
  158.5 27.8 %collective-permute-start.49 = (s16[528,256]{1,0:T(8,128)(2,1)}, s16[528,256]{1,0:T(8,128)(2,1)S(1)}, u32[]{:S(2)}, u32[]{:S(2)}) collective-permute-start(s16[528,256]{1,0:T(8,128)(2,1)} %get-tuple-element.40), channel_id=1, source_target_pairs={{24,16},{28,20},{16,8},{20,12},{8,0},{12,4},{25,17},{29,21},{17,9}... | collective-permute-start | bytes 811016 | tf_op jit(solution)/shard_map/ppermute | solution.py:424
  180.4 29.2 %collective-permute-start.33 = (s16[528,256]{1,0:T(8,128)(2,1)}, s16[528,256]{1,0:T(8,128)(2,1)S(1)}, u32[]{:S(2)}, u32[]{:S(2)}) collective-permute-start(s16[528,256]{1,0:T(8,128)(2,1)} %get-tuple-element.33), channel_id=1, source_target_pairs={{0,8},{4,12},{8,16},{12,20},{16,24},{20,28},{1,9},{5,13},{9,17},{1... | collective-permute-start | bytes 811016 | tf_op jit(solution)/shard_map/ppermute | solution.py:423
  185.0 24.6 %collective-permute-start.34 = (s16[528,256]{1,0:T(8,128)(2,1)}, s16[528,256]{1,0:T(8,128)(2,1)S(1)}, u32[]{:S(2)}, u32[]{:S(2)}) collective-permute-start(s16[528,256]{1,0:T(8,128)(2,1)} %get-tuple-element.34), channel_id=1, source_target_pairs={{24,16},{28,20},{16,8},{20,12},{8,0},{12,4},{25,17},{29,21},{17,9}... | collective-permute-start | bytes 811016 | tf_op jit(solution)/shard_map/ppermute | solution.py:424
  198.2 37.4 %collective-permute-start.50 = (f32[192,1024]{1,0:T(8,128)S(1)}, f32[192,1024]{1,0:T(8,128)S(1)}, u32[]{:S(2)}, u32[]{:S(2)}) collective-permute-start(f32[192,1024]{1,0:T(8,128)S(1)} %slice.228), channel_id=1, source_target_pairs={{0,1},{1,0},{2,3},{3,2},{4,5},{5,4},{6,7},{7,6},{8,9},{9,8},{10,11... | collective-permute-start | bytes 2359304 | tf_op jit(solution)/shard_map/ppermute | solution.py:331
  238.3 25.7 %collective-permute-start.21 = (f32[96,1024]{1,0:T(8,128)S(1)}, f32[96,1024]{1,0:T(8,128)S(1)}, u32[]{:S(2)}, u32[]{:S(2)}) collective-permute-start(f32[96,1024]{1,0:T(8,128)S(1)} %slice.204), channel_id=1, source_target_pairs={{0,2},{1,3},{2,0},{3,1},{4,6},{5,7},{6,4},{7,5},{8,10},{9,11},{10,... | collective-permute-start | bytes 1179656 | tf_op jit(solution)/shard_map/ppermute | solution.py:331
  (85 other events, 775.2 us)

commit v2 on v1

v2 whole, which is shorter than its diff:
```python
import jax
import jax.numpy as jnp
from jax import lax
from jax.experimental import pallas as pl
from jax.experimental.pallas import tpu as pltpu
from jax.sharding import PartitionSpec as P

NV = 16
NC = 24
GBLK = 128
NT = 384

GROUP = 64
EXP_ROWS = 16
STEPS = 128.0
TOP = 32700.0
MAGIC = 1.5 * 2.0**23
NT_DIMS = (((1,), (1,)), ((), ()))
VMEM = 56 * 1024 * 1024


def params():
    return pltpu.CompilerParams(vmem_limit_bytes=VMEM)


def cost(flops, moved):
    return pl.CostEstimate(flops=int(flops), bytes_accessed=int(moved), transcendentals=0)


def mm(left, right):
    return jnp.dot(left, right, preferred_element_type=jnp.float32)


def mm_nt(left, right):
    return lax.dot_general(left, right, NT_DIMS, preferred_element_type=jnp.float32)


def halves(value):
    high = value.astype(jnp.bfloat16)
    low = (value - high.astype(jnp.float32)).astype(jnp.bfloat16)
    return high, low


def encode(value, out_ref):
    rows, width = value.shape
    groups = rows // GROUP
    parts = value.reshape(groups, GROUP, width)
    largest = jnp.maximum(jnp.max(jnp.abs(parts), axis=1), 1e-30)
    level = jnp.ceil(jnp.log2(largest) * STEPS) + 1.0
    factor = TOP * jnp.exp2(level * (-1.0 / STEPS))
    coded = ((parts * factor[:, None, :] + MAGIC) - MAGIC).astype(jnp.int32)
    out_ref[0:rows, :] = coded.reshape(rows, width).astype(jnp.int16)
    pad = jnp.zeros((EXP_ROWS - groups, width), jnp.int32)
    out_ref[rows : rows + EXP_ROWS, :] = jnp.concatenate(
        [level.astype(jnp.int32), pad], axis=0
    ).astype(jnp.int16)


def decode(ref):
    rows = ref.shape[0] - EXP_ROWS
    width = ref.shape[1]
    groups = rows // GROUP
    level = ref[rows : rows + EXP_ROWS, :].astype(jnp.int32).astype(jnp.float32)[0:groups]
    factor = jnp.exp2(level * (1.0 / STEPS)) * (1.0 / TOP)
    parts = ref[0:rows, :].astype(jnp.int32).astype(jnp.float32).reshape(groups, GROUP, width)
    return (parts * factor[:, None, :]).reshape(rows, width)


def shift_kernel(dest_ref, con_ref, map_ref, stay_ref, go_ref):
    slots, _, _, rows, width = stay_ref.shape
    for which, out_ref in enumerate((stay_ref, go_ref)):
        for slot in range(slots):
            first = dest_ref[which * slots + slot] * width
            for block in range(width // GBLK):
                cols = pl.ds(pl.multiple_of(first + block * GBLK, GBLK), GBLK)
                within = jnp.bitwise_and(map_ref[0, 0:1, cols], GBLK - 1)
                within = jnp.broadcast_to(within, (rows, GBLK))
                for part in range(2):
                    values = con_ref[0, part, :, cols].astype(jnp.float32)
                    moved = jnp.take_along_axis(values, within, axis=1)
                    out_ref[slot, 0, part, :, block * GBLK : (block + 1) * GBLK] = moved.astype(
                        jnp.bfloat16
                    )


def shift_call(con, shift_map, dests, width):
    points, _, rows, slab = con.shape
    slots = dests.shape[0] // 2
    grid_spec = pltpu.PrefetchScalarGridSpec(
        num_scalar_prefetch=1,
        grid=(points,),
        in_specs=[
            pl.BlockSpec((1, 2, rows, slab), lambda q, dest: (q, 0, 0, 0)),
            pl.BlockSpec((1, 1, slab), lambda q, dest: (q, 0, 0)),
        ],
        out_specs=[pl.BlockSpec((slots, 1, 2, rows, width), lambda q, dest: (0, q, 0, 0, 0))] * 2,
    )
    return pl.pallas_call(
        shift_kernel,
        grid_spec=grid_spec,
        out_shape=[jax.ShapeDtypeStruct((slots, points, 2, rows, width), jnp.bfloat16)] * 2,
        compiler_params=params(),
        cost_estimate=cost(8 * con.size, 4 * con.size),
    )(dests, con, shift_map.reshape(points, 1, slab))


def x_kernel(slots, at_once, table_ref, *refs):
    val_refs, weight_refs = refs[:slots], refs[slots : slots + at_once]
    go_ref, keep_ref, left_ref = refs[slots + at_once :]
    rows, depth = val_refs[0].shape[2], val_refs[0].shape[3]
    half = slots * rows
    step = pl.program_id(0)
    halfway = pl.num_programs(0) // 2

    @pl.when(step == 0)
    def _():
        for slot in range(slots):
            real, imag = val_refs[slot][0, 0], val_refs[slot][0, 1]
            top = slice(slot * rows, (slot + 1) * rows)
            low = slice(half + slot * rows, half + (slot + 1) * rows)
            left_ref[top, 0:depth] = real
            left_ref[top, depth : 2 * depth] = -imag
            left_ref[low, 0:depth] = imag
            left_ref[low, depth : 2 * depth] = real

    width = weight_refs[0].shape[3]
    for place, weight_ref in enumerate(weight_refs):
        product = mm(left_ref[...], weight_ref[0].reshape(2 * depth, width))
        cols = slice(place * width, (place + 1) * width)

        @pl.when(step < halfway)
        def _():
            encode(product, go_ref.at[:, cols])

        @pl.when(step >= halfway)
        def _():
            keep_ref[:, cols] = product


def x_call(vals, screened, point, table, width, at_once):
    slots = len(vals)
    _, _, rows, depth = vals[0].shape
    height = 2 * slots * rows
    steps = table.shape[0] // at_once
    half = steps // 2
    columns = width * at_once * half
    weights = [
        pl.BlockSpec(
            (1, 2, depth, width), lambda j, t, place=place: (point, 0, 0, t[j * at_once + place])
        )
        for place in range(at_once)
    ]
    grid_spec = pltpu.PrefetchScalarGridSpec(
        num_scalar_prefetch=1,
        grid=(steps,),
        in_specs=[
            pl.BlockSpec((1, 2, rows, depth), lambda j, t: (point, 0, 0, 0)) for _ in vals
        ]
        + weights,
        out_specs=[
            pl.BlockSpec(
                (height + EXP_ROWS, width * at_once), lambda j, t: (0, jnp.minimum(j, half - 1))
            ),
            pl.BlockSpec((height, width * at_once), lambda j, t: (0, jnp.maximum(j - half, 0))),
        ],
        scratch_shapes=[pltpu.VMEM((height, 2 * depth), jnp.bfloat16)],
    )
    return pl.pallas_call(
        lambda *refs: x_kernel(slots, at_once, *refs),
        grid_spec=grid_spec,
        out_shape=[
            jax.ShapeDtypeStruct((height + EXP_ROWS, columns), jnp.int16),
            jax.ShapeDtypeStruct((height, columns), jnp.float32),
        ],
        compiler_params=params(),
        cost_estimate=cost(
            2 * height * 2 * depth * 2 * columns, 8 * depth * columns + 6 * height * columns
        ),
    )(table, *vals, *([screened] * at_once))


def hop_kernel(keep_ref, *refs):
    total = keep_ref[...]
    for ref in refs[:-1]:
        total = total + decode(ref)
    encode(total, refs[-1])


def hop_call(keep, others, block, width):
    height, tall = keep.shape[0], others[0].shape[0]
    return pl.pallas_call(
        hop_kernel,
        grid=(1,),
        in_specs=[pl.BlockSpec((height, width), lambda i: (0, block))]
        + [pl.BlockSpec((tall, width), lambda i: (0, block)) for _ in others],
        out_specs=pl.BlockSpec((tall, width), lambda i: (0, 0)),
        out_shape=jax.ShapeDtypeStruct((tall, width), jnp.int16),
        compiler_params=params(),
        cost_estimate=cost(20 * height * width, 8 * height * width),
    )(keep, *others)


def exchange_kernel(slots, *refs):
    here_refs, (there_ref, coulomb_ref, out_ref, left_ref) = refs[:slots], refs[slots:]
    rows, depth = here_refs[0].shape[1], here_refs[0].shape[2]

    @pl.when(pl.program_id(0) == 0)
    def _():
        for slot in range(slots):
            for part in range(2):
                left_ref[
                    slot * rows : (slot + 1) * rows, part * depth : (part + 1) * depth
                ] = here_refs[slot][part]

    factor = coulomb_ref[0]
    real = there_ref[0, 0].astype(jnp.float32) * factor
    imag = there_ref[0, 1].astype(jnp.float32) * factor
    right = jnp.concatenate(
        [jnp.concatenate([real, -imag], axis=1), jnp.concatenate([imag, real], axis=1)], axis=0
    )
    high, low = halves(right)
    left = left_ref[...]
    both = mm_nt(left, high) + mm_nt(left, low)
    cols = both.shape[1] // 2
    for part in range(2):
        out_ref[0, part] = both[:, part * cols : (part + 1) * cols]


def exchange_call(heres, there, coulomb):
    slots = len(heres)
    points, _, cols, depth = there.shape
    rows = heres[0].shape[1]
    height = slots * rows
    return pl.pallas_call(
        lambda *refs: exchange_kernel(slots, *refs),
        grid=(points,),
        in_specs=[pl.BlockSpec(h.shape, lambda q: (0, 0, 0)) for h in heres]
        + [
            pl.BlockSpec((1, 2, cols, depth), lambda q: (q, 0, 0, 0)),
            pl.BlockSpec((1, 1, depth), lambda q: (q, 0, 0)),
        ],
        out_specs=pl.BlockSpec((1, 2, height, cols), lambda q: (q, 0, 0, 0)),
        out_shape=jax.ShapeDtypeStruct((points, 2, height, cols), jnp.float32),
        scratch_shapes=[pltpu.VMEM((height, 2 * depth), jnp.bfloat16)],
        compiler_params=params(),
        cost_estimate=cost(2 * points * height * 2 * cols * 2 * depth * 2, 8 * points * cols * depth),
    )(*heres, there, coulomb.reshape(points, 1, depth))


def tile_kernel(slots, heard, chunks, index_ref, *refs):
    con_refs, keep_ref = refs[:slots], refs[slots]
    heard_refs = refs[slots + 1 : slots + 1 + heard]
    exch_ref, row_ref, col_direct_ref, col_exch_ref = refs[slots + 1 + heard : slots + 5 + heard]
    out_ref, con_all, direct_ref, natural_ref = refs[slots + 5 + heard :]
    total = keep_ref[...]
    for ref in heard_refs:
        total = total + decode(ref)
    pairs, width = total.shape[0] // 2, total.shape[1]
    rows = con_refs[0].shape[3]
    pitch = con_all.shape[0] // slots
    for slot in range(slots):
        for part in range(2):
            con_all[
                slot * pitch : slot * pitch + rows, part * width : (part + 1) * width
            ] = con_refs[slot][0, 0, part]
    real, imag = total[:pairs], total[pairs:]
    right = jnp.concatenate(
        [jnp.concatenate([real, -imag], axis=1), jnp.concatenate([imag, real], axis=1)], axis=0
    )
    high, low = halves(right)
    left = con_all[...]
    direct = mm_nt(left, high) + mm_nt(left, low)
    lanes = direct_ref.shape[0]
    for slot in range(slots):
        start = pl.multiple_of(index_ref[slot] * rows, 8)
        for lane in range(lanes):
            direct_ref[lane, pl.ds(start, rows), :] = direct[
                slot * pitch : slot * pitch + rows, lane * 128 : (lane + 1) * 128
            ]
    group = 128 // NV
    place = lax.broadcasted_iota(jnp.int32, (NC, 128), 1) // NV
    per_part = lanes // 2
    for part in range(2):
        for chunk in range(NC // group):
            for band in range(NV):
                block = jnp.zeros((NC, 128), jnp.float32)
                for step in range(group):
                    e = chunk * group + step
                    piece = direct_ref[part * per_part + band // group, pl.ds(e, NC, stride=NC), :]
                    turn = (NV * (step - band)) % 128
                    if turn:
                        piece = pltpu.roll(piece, turn, 1)
                    block = jnp.where(place == step, piece, block)
                natural_ref[
                    part, band * NC : (band + 1) * NC, chunk * 128 : (chunk + 1) * 128
                ] = block
    pick_rows = row_ref[...]
    count = NT // chunks
    for part in range(2):
        result = None
        for source, pick_cols in (
            (natural_ref[part], col_direct_ref),
            (exch_ref[0, part], col_exch_ref),
        ):
            for piece in halves(source):
                moved = mm(pick_rows, piece).astype(jnp.bfloat16)
                term = mm(moved, pick_cols[...])
                result = term if result is None else result + term
        for chunk in range(chunks):
            at = (2 * chunk + part) * count
            out_ref[at : at + count, :] = result[chunk * count : (chunk + 1) * count]


def tile_call(cons, point, keep, heard, exch, index, pick_rows, col_direct, col_exch, chunks):
    slots = len(cons)
    _, _, _, rows, width = cons[0][0].shape
    height, tall = keep.shape[0], heard[0].shape[0]
    pitch = -(-rows // 16) * 16
    out_cols = col_direct.shape[1]
    whole = lambda a: pl.BlockSpec(a.shape, lambda i, at: (0,) * a.ndim)
    grid_spec = pltpu.PrefetchScalarGridSpec(
        num_scalar_prefetch=1,
        grid=(1,),
        in_specs=[
            pl.BlockSpec((1, 1, 2, rows, width), lambda i, at, place=place: (place, point, 0, 0, 0))
            for _, place in cons
        ]
        + [pl.BlockSpec((height, width), lambda i, at: (0, 0))]
        + [pl.BlockSpec((tall, width), lambda i, at: (0, 0)) for _ in heard]
        + [
            pl.BlockSpec((1,) + exch.shape[1:], lambda i, at: (point, 0, 0, 0)),
            whole(pick_rows),
            whole(col_direct),
            whole(col_exch),
        ],
        out_specs=pl.BlockSpec((2 * NT, out_cols), lambda i, at: (0, 0)),
        scratch_shapes=[
            pltpu.VMEM((slots * pitch, 2 * width), jnp.bfloat16),
            pltpu.VMEM((height // 128, NC * NC, 128), jnp.float32),
            pltpu.VMEM((2, NT, NT), jnp.float32),
        ],
    )
    return pl.pallas_call(
        lambda *refs: tile_kernel(slots, len(heard), chunks, *refs),
        grid_spec=grid_spec,
        out_shape=jax.ShapeDtypeStruct((2 * NT, out_cols), jnp.float32),
        compiler_params=params(),
        cost_estimate=cost(2.8e9, 8e6),
    )(index, *[c for c, _ in cons], keep, *heard, exch, pick_rows, col_direct, col_exch)


def swap(value, axis, size, bit):
    return lax.ppermute(value, axis, [(i, i ^ bit) for i in range(size)])


def gather_slots(value, axis, size):
    found = {0: value}
    bit = size // 2
    while bit:
        for known in sorted(found):
            found[known ^ bit] = swap(found[known], axis, size, bit)
        bit //= 2
    return [found[r] for r in range(size)]


def halving_order(bits):
    order = [0]
    for bit in reversed(bits):
        order = order + [o ^ bit for o in order]
    return order


def on_device(*args):
    (val_density, con_density, screened, coulomb, trans_here, trans_there, shift_map, ordering) = args
    ga, pair = lax.axis_size("ga"), lax.axis_size("pair")
    points = con_density.shape[1]
    slab = con_density.shape[3]
    width = slab // ga
    me_ga, me_pair = lax.axis_index("ga"), lax.axis_index("pair")
    ga_bits = [1 << b for b in range(ga.bit_length() - 1)]
    pair_bits = [1 << b for b in range(pair.bit_length() - 1)]
    ga_order = halving_order(ga_bits)
    half = ga // 2
    dests = me_ga ^ jnp.asarray(ga_order, jnp.int32)

    vals = gather_slots(jnp.transpose(val_density, (1, 2, 0, 3)), "pair", pair)

    con = jnp.transpose(con_density, (1, 2, 0, 3))
    stay, go = shift_call(con, shift_map, dests, width)
    cons = {}
    for p, slot in enumerate(ga_order):
        cons[slot] = (stay, p) if p < half else (go, p - half)
    for bit in ga_bits:
        moving = [slot for slot in ga_order if slot & bit]
        if bit == ga_bits[0]:
            sent = go
        else:
            sent = jnp.stack([cons[slot][0][cons[slot][1]] for slot in moving])
        got = swap(sent, "ga", ga, bit)
        for place, slot in enumerate(moving):
            cons[slot] = (got, place)
    cons = [cons[slot] for slot in ga_order]

    table = jnp.concatenate([dests[half:], dests[:half]])
    gone, keep = [], []
    for q in range(points):
        coded, own = x_call(vals, screened, q, table, width, 2)
        gone.append(coded)
        keep.append(own)

    heres = gather_slots(jnp.transpose(trans_here, (1, 0, 2)), "pair", pair)
    exch = exchange_call(heres, jnp.transpose(trans_there, (1, 2, 0, 3)), coulomb)

    row_count, col_count = NT // pair, NT // ga
    row_slots = jnp.asarray(halving_order(pair_bits), jnp.int32)
    row_trans = ordering.reshape(pair, row_count)[me_pair ^ row_slots].reshape(-1)
    at_row = ((row_trans // row_count) ^ me_pair) * row_count + row_trans % row_count
    pick_rows = (at_row[:, None] == jnp.arange(NT, dtype=jnp.int32)[None, :]).astype(jnp.bfloat16)
    col_trans = ordering.reshape(ga, col_count)[dests]
    col_trans = jnp.pad(col_trans, ((0, 0), (0, 64 - col_count)), constant_values=-1).reshape(1, -1)
    real_col = col_trans >= 0
    at_direct = jnp.where(real_col, (col_trans % NC) * NV + col_trans // NC, -1)
    own_col = real_col & (col_trans // row_count == me_pair)
    at_exch = jnp.where(own_col, col_trans % row_count, -1)

    def pick_cols(at, size, scale):
        hot = at == jnp.arange(size, dtype=jnp.int32)[:, None]
        return jnp.where(hot, scale, 0.0).astype(jnp.bfloat16)

    col_direct, col_exch = pick_cols(at_direct, NT, -1.0), pick_cols(at_exch, row_count, 2.0)

    heard = [[swap(gone[q], "ga", ga, ga_bits[0])] for q in range(points)]
    part = half
    for bit in ga_bits[1:]:
        part //= 2
        for q in range(points):
            heard[q].append(swap(hop_call(keep[q], heard[q], 1, part * width), "ga", ga, bit))
    outs = []
    for q in range(points):
        tile = tile_call(
            cons, q, keep[q], heard[q], exch, dests, pick_rows, col_direct, col_exch, pair
        )
        for bit in pair_bits:
            rows = tile.shape[0] // 2
            tile = tile[:rows] + swap(tile[rows:], "pair", pair, bit)
        for bit in ga_bits:
            cols = tile.shape[1] // 2
            tile = tile[:, :cols] + swap(tile[:, cols:], "ga", ga, bit)
        outs.append(tile[:, :col_count].reshape(2, row_count, col_count))
    return jnp.stack(outs)


def contract_float(left, right):
    high = lax.Precision.HIGHEST
    real_part = jnp.einsum(
        "nkg,mkg->nkm", left[:, :, 0], right[:, :, 0], precision=high
    ) - jnp.einsum("nkg,mkg->nkm", left[:, :, 1], right[:, :, 1], precision=high)
    imag_part = jnp.einsum(
        "nkg,mkg->nkm", left[:, :, 0], right[:, :, 1], precision=high
    ) + jnp.einsum("nkg,mkg->nkm", left[:, :, 1], right[:, :, 0], precision=high)
    return jnp.stack([real_part, imag_part], axis=2)


def times_cols(rows, weights):
    first = jnp.einsum(
        "nkh,kgh->nkg", rows[:, :, 0], weights[:, 0], preferred_element_type=jnp.float32
    ) - jnp.einsum("nkh,kgh->nkg", rows[:, :, 1], weights[:, 1], preferred_element_type=jnp.float32)
    second = jnp.einsum(
        "nkh,kgh->nkg", rows[:, :, 0], weights[:, 1], preferred_element_type=jnp.float32
    ) + jnp.einsum("nkh,kgh->nkg", rows[:, :, 1], weights[:, 0], preferred_element_type=jnp.float32)
    return jnp.stack([first, second], axis=2)


def on_any_device(
    val_density, con_density, screened, coulomb, trans_here, trans_there, shift_map, ordering
):
    con_count = con_density.shape[0]
    points = con_density.shape[1]
    slab_cols = con_density.shape[3]
    blocks = slab_cols // GBLK
    within = (shift_map % GBLK).reshape(points, blocks, GBLK)
    onehot = (
        within[:, :, :, None] == jnp.arange(GBLK, dtype=jnp.int32)[None, None, None, :]
    ).astype(jnp.bfloat16)
    con_blocks = con_density.reshape(con_count, points, 2, blocks, GBLK)
    shifted = (
        jnp.einsum("bkpnh,kngh->bkpng", con_blocks, onehot, preferred_element_type=jnp.float32)
        .astype(jnp.bfloat16)
        .reshape(con_density.shape)
    )
    whole_here = lax.all_gather(trans_here, "pair", axis=0, tiled=True).astype(jnp.float32)
    weighted = trans_there.astype(jnp.float32) * coulomb[None, :, None, :]
    high = lax.Precision.HIGHEST
    exch_real = jnp.einsum(
        "tg,skg->tks", whole_here[:, 0], weighted[:, :, 0], precision=high
    ) - jnp.einsum("tg,skg->tks", whole_here[:, 1], weighted[:, :, 1], precision=high)
    exch_imag = jnp.einsum(
        "tg,skg->tks", whole_here[:, 0], weighted[:, :, 1], precision=high
    ) + jnp.einsum("tg,skg->tks", whole_here[:, 1], weighted[:, :, 0], precision=high)
    exch_part = jnp.stack([exch_real, exch_imag], axis=2)
    whole_con = lax.all_gather(shifted, "ga", axis=0, tiled=True)
    screened_rows = lax.psum_scatter(
        times_cols(whole_con, screened), "pair", scatter_dimension=0, tiled=True
    )
    direct_part = contract_float(
        lax.all_gather(val_density, "pair", axis=0, tiled=True).astype(jnp.float32), screened_rows
    )
    direct_sum, exch_sum = lax.psum((direct_part, exch_part), "ga")
    direct_full, exch_full = (
        lax.all_gather(direct_sum, "pair", axis=3, tiled=True),
        lax.all_gather(exch_sum, "pair", axis=3, tiled=True),
    )
    row_count = NT // lax.axis_size("pair")
    col_count = NT // lax.axis_size("ga")
    row_trans = lax.dynamic_slice_in_dim(ordering, lax.axis_index("pair") * row_count, row_count, 0)
    col_trans = lax.dynamic_slice_in_dim(ordering, lax.axis_index("ga") * col_count, col_count, 0)
    row_pairs = (row_trans // NC)[:, None] * NV + (col_trans // NC)[None, :]
    col_pairs = (row_trans % NC)[:, None] * NC + (col_trans % NC)[None, :]
    picked = direct_full[row_pairs.reshape(-1)]
    col_mask = (
        col_pairs.reshape(-1)[:, None] == jnp.arange(direct_full.shape[3], dtype=jnp.int32)[None, :]
    ).astype(jnp.float32)
    direct_flat = jnp.sum(picked * col_mask[:, None, None, :], axis=3)
    direct_sel = jnp.transpose(direct_flat.reshape(row_count, col_count, points, 2), (2, 3, 0, 1))
    exch_picked = exch_full[row_trans]
    col_hot = (jnp.arange(NT, dtype=jnp.int32)[:, None] == col_trans[None, :]).astype(jnp.float32)
    exch_sel = jnp.einsum("rkpt,tc->kprc", exch_picked, col_hot, precision=high)
    return 2.0 * exch_sel - direct_sel


def solution(mesh):
    in_specs = (
        P("pair", None, None, "ga"),
        P("ga", None, None, "pair"),
        P(None, None, "ga", "pair"),
        P(None, "ga"),
        P("pair", None, "ga"),
        P("pair", None, None, "ga"),
        P(None, "pair"),
        P(),
    )
    out_specs = P(None, None, "pair", "ga")

    def run(*args):
        ga, pair = mesh.shape["ga"], mesh.shape["pair"]
        con_count, h_count = args[1].shape[0], args[1].shape[3]
        suits = (
            ga & (ga - 1) == 0
            and pair & (pair - 1) == 0
            and ga >= 4
            and pair >= 2
            and h_count % (ga * pair * GBLK) == 0
            and con_count % (8 * ga) == 0
            and args[0].shape[0] % (16 * pair) == 0
            and NT % (16 * pair) == 0
            and NT // ga <= 64
        )
        body = on_device if suits else on_any_device
        return jax.shard_map(
            body, mesh=mesh, in_specs=in_specs, out_specs=out_specs, check_vma=False
        )(*args)

    return run
```

time: 291 us -> 250 us (0.86)
  starting transfers between devices: 82.2 us -> 39.5 us
  waiting for transfers between devices: 54.3 us -> 85.6 us
  Pallas kernels: 119 us -> 95.2 us
    ppermute x18 -> x0, starting transfers between devices: 38.4 us -> none  [the longest x9 30.1 us: on_device(): lax.ppermute(up, 'ga', up_pairs[step])]
    ppermute x37 -> x33, waiting for transfers between devices: 54.2 us -> 85.6 us  [swap(): return lax.ppermute(value, axis, [(i, i ^ bit) for i in range(size)])]
    pallas_call x19 -> x13, Pallas kernels: 113 us -> 89.6 us  [the longest x3 44.1 us: x_call(): pl.pallas_call(lambda *refs: x_kernel(slots, at_once, *refs), grid_spec=g...]
    ppermute x37 -> x33, starting transfers between devices: 43.8 us -> 39.5 us  [swap(): return lax.ppermute(value, axis, [(i, i ^ bit) for i in range(size)])]
    slice x15 -> x21, local copies, waits for them, and re-layouts: 3.88 us -> 6.22 us  [the longest x6 3.75 us: on_device(): tile = tile[:rows] + swap(tile[rows:], 'pair', pair, bit)]
    unnamed x112 -> x56, local copies, waits for them, and re-layouts: 14.1 us -> 13.5 us
  transfers between devices with their start and end apart: 55 -> 33, of which waited for: 13 -> 15; matrix products, arithmetic and copies ran while one was open for 8% -> 8% of each run, Pallas kernels for 41% -> 38%
where the time goes in v2:
time: 250 us; the launch traced here: 249 us
  Pallas kernels  95.2 us (38%)
  waiting for transfers between devices  85.6 us (34%)
  starting transfers between devices  39.5 us (16%)
  local copies, waits for them, and re-layouts  23.1 us (9%)
  other arithmetic  5.18 us (2%)
    ppermute x33, waiting for transfers between devices, swap(): return lax.ppermute(value, axis, [(i, i ^ bit) for i in range(size)])  85.6 us
    pallas_call x3, Pallas kernels, x_call(): pl.pallas_call(lambda *refs: x_kernel(slots, at_once, *refs), grid_spec=g...  44.1 us
    ppermute x33, starting transfers between devices, swap(): return lax.ppermute(value, axis, [(i, i ^ bit) for i in range(size)])  39.5 us
    pallas_call x3, Pallas kernels, tile_call(): pl.pallas_call(lambda *refs: tile_kernel(slots, len(heard), chunks, *refs...  26.1 us
    pallas_call x6, Pallas kernels, hop_call(): pl.pallas_call(hop_kernel, grid=(1,), in_specs=[pl.BlockSpec((height, wid...  14.6 us
    unnamed x56, local copies, waits for them, and re-layouts  13.5 us
    pallas_call x1, Pallas kernels, exchange_call(): pl.pallas_call(lambda *refs: exchange_kernel(slots, *refs), grid=(points,...  5.65 us
  transfers between devices with their start and end apart: 33, of which 15 were waited for; matrix products, arithmetic and copies ran while one was open for 8% of the time, Pallas kernels for 38%

profile of v2, /device:TPU:0, one launch (start us, length us, event | category | flops | bytes accessed | tf_op | source)
XLA Modules:
  0.0 249.2 jit_solution(17562295110908472073)
XLA Ops:
  4.4 3.5 %copy.22 = bf16[72,3,2,2048]{3,0,2,1:T(8,128)(2,1)} copy(bf16[72,3,2,2048]{3,2,1,0:T(2,128)(2,1)} %param.11) | data formatting | bytes 3538944 | tf_op args[1]
  9.1 4.8 %shard_map.100 = (bf16[4,3,2,72,256]{4,3,2,1,0:T(8,128)(2,1)}, bf16[4,3,2,72,256]{4,3,2,1,0:T(8,128)(2,1)}) custom-call(s32[8]{0:T(128)} %get-tuple-element.40.dest_ref.refs_0_, bf16[3,2,72,2048]{3,2,1,0:T(8,128)(2,1)} %bitcast.20, s32[3,1,2048]{2,1,0:T(1,128)} %reshape.162.map_ref), custom_call_target="tpu_custom_call" | custom-call | flops 7077888 | bytes 3538944 | tf_op jit(solution)/shard_map/pallas_call | solution.py:98
  18.4 4.5 %collective-permute-done.4.refs_3_ = bf16[3,2,64,1024]{3,2,1,0:T(8,128)(2,1)} collective-permute-done((bf16[3,2,64,1024]{3,2,1,0:T(8,128)(2,1)S(1)}, bf16[3,2,64,1024]{3,2,1,0:T(8,128)(2,1)}, u32[]{:S(2)}, u32[]{:S(2)}) %collective-permute-start.4) | collective-permute-done | bytes 786464 | tf_op jit(solution)/shard_map/ppermute | solution.py:353
  24.2 11.6 %collective-permute-done.refs_5_ = bf16[4,3,2,72,256]{4,3,2,1,0:T(8,128)(2,1)S(1)} collective-permute-done((bf16[4,3,2,72,256]{4,3,2,1,0:T(8,128)(2,1)}, bf16[4,3,2,72,256]{4,3,2,1,0:T(8,128)(2,1)S(1)}, u32[]{:S(2)}, u32[]{:S(2)}) %collective-permute-start) | collective-permute-done | bytes 884768 | tf_op jit(solution)/shard_map/ppermute | solution.py:353
  38.5 14.7 %shard_map.110 = (s16[528,1024]{1,0:T(8,128)(2,1)}, f32[512,1024]{1,0:T(8,128)}) custom-call(s32[8]{0:T(128)} %pad_add_fusion.refs_0_, bf16[3,2,64,1024]{3,2,1,0:T(8,128)(2,1)} %bitcast.17, bf16[3,2,64,1024]{3,2,1,0:T(8,128)(2,1)} %copy-done.5, bf16[3,2,64,1024]{3,2,1,0:T(8,128)(2,1)} %collective-permute-done.4.refs_3_, ...), custom_call_target="tpu_custom_call" | custom-call | flops 4294967296 | bytes 11534336 | tf_op jit(solution)/shard_map/pallas_call | solution.py:168
  54.7 14.7 %shard_map.106 = (s16[528,1024]{1,0:T(8,128)(2,1)}, f32[512,1024]{1,0:T(8,128)}) custom-call(s32[8]{0:T(128)} %pad_add_fusion.refs_0_, bf16[3,2,64,1024]{3,2,1,0:T(8,128)(2,1)} %bitcast.18, bf16[3,2,64,1024]{3,2,1,0:T(8,128)(2,1)} %copy-done.5, bf16[3,2,64,1024]{3,2,1,0:T(8,128)(2,1)} %collective-permute-done.4.refs_3_, ...), custom_call_target="tpu_custom_call" | custom-call | flops 4294967296 | bytes 11534336 | tf_op jit(solution)/shard_map/pallas_call | solution.py:168
  69.9 14.7 %shard_map.101 = (s16[528,1024]{1,0:T(8,128)(2,1)}, f32[512,1024]{1,0:T(8,128)}) custom-call(s32[8]{0:T(128)} %pad_add_fusion.refs_0_, bf16[3,2,64,1024]{3,2,1,0:T(8,128)(2,1)} %bitcast.19, bf16[3,2,64,1024]{3,2,1,0:T(8,128)(2,1)} %copy-done.5, bf16[3,2,64,1024]{3,2,1,0:T(8,128)(2,1)} %collective-permute-done.4.refs_3_, ...), custom_call_target="tpu_custom_call" | custom-call | flops 4294967296 | bytes 11534336 | tf_op jit(solution)/shard_map/pallas_call | solution.py:168
  88.2 2.7 %collective-permute-start.2 = (bf16[4,3,2,72,256]{4,3,2,1,0:T(8,128)(2,1)S(1)}, bf16[4,3,2,72,256]{4,3,2,1,0:T(8,128)(2,1)S(1)}, u32[]{:S(2)}, u32[]{:S(2)}) collective-permute-start(bf16[4,3,2,72,256]{4,3,2,1,0:T(8,128)(2,1)S(1)} %pad_maximum_fusion.1), channel_id=1, source_target_pairs={{0,16},{4,20},{8,24},{12,28},{16,0},{20,4},{24,8},{28,12},{1,17},{... | collective-permute-start | bytes 2654216 | tf_op jit(solution)/shard_map/ppermute | solution.py:353
  91.9 2.7 %shard_map.111 = s16[528,512]{1,0:T(8,128)(2,1)} custom-call(f32[512,1024]{1,0:T(8,128)} %get-tuple-element.19.keep_ref.refs_9_, s16[528,1024]{1,0:T(8,128)(2,1)} %copy-done.4), custom_call_target="tpu_custom_call" | custom-call | flops 5242880 | bytes 2097152 | tf_op jit(solution)/shard_map/pallas_call | solution.py:191
  95.4 8.2 %collective-permute-done.17.refs_0_.refs_10_ = s16[528,1024]{1,0:T(8,128)(2,1)} collective-permute-done((s16[528,1024]{1,0:T(8,128)(2,1)}, s16[528,1024]{1,0:T(8,128)(2,1)}, u32[]{:S(2)}, u32[]{:S(2)}) %collective-permute-start.17) | collective-permute-done | bytes 1081376 | tf_op jit(solution)/shard_map/ppermute | solution.py:353
  103.5 2.6 %shard_map.107 = s16[528,512]{1,0:T(8,128)(2,1)} custom-call(f32[512,1024]{1,0:T(8,128)} %get-tuple-element.17.keep_ref.refs_9_, s16[528,1024]{1,0:T(8,128)(2,1)} %collective-permute-done.17.refs_0_.refs_10_), custom_call_target="tpu_custom_call" | custom-call | flops 5242880 | bytes 2097152 | tf_op jit(solution)/shard_map/pallas_call | solution.py:191
  106.2 18.5 %collective-permute-done.6.refs_0_.refs_10_ = s16[528,1024]{1,0:T(8,128)(2,1)} collective-permute-done((s16[528,1024]{1,0:T(8,128)(2,1)}, s16[528,1024]{1,0:T(8,128)(2,1)}, u32[]{:S(2)}, u32[]{:S(2)}) %collective-permute-start.6) | collective-permute-done | bytes 1081376 | tf_op jit(solution)/shard_map/ppermute | solution.py:353
  132.5 2.7 %collective-permute-start.27 = (s16[528,256]{1,0:T(8,128)(2,1)}, s16[528,256]{1,0:T(8,128)(2,1)S(1)}, u32[]{:S(2)}, u32[]{:S(2)}) collective-permute-start(s16[528,256]{1,0:T(8,128)(2,1)} %shard_map.112), channel_id=1, source_target_pairs={{0,16},{4,20},{8,24},{12,28},{16,0},{20,4},{24,8},{28,12},{1,17},{... | collective-permute-start | bytes 811016 | tf_op jit(solution)/shard_map/ppermute | solution.py:353
  138.6 5.7 %shard_map.104.refs_13_ = f32[3,2,384,96]{3,2,1,0:T(8,128)} custom-call(bf16[2,96,1024]{2,1,0:T(8,128)(2,1)} %bitcast.24, bf16[2,96,1024]{2,1,0:T(8,128)(2,1)} %copy-done.23, bf16[2,96,1024]{2,1,0:T(8,128)(2,1)} %collective-permute-done.10.refs_2_, bf16[2,96,1024]{2,1,0:T(8,128)(2,1)} %copy-done.24, bf16[3,2,96,1024]{3,2,1,0:T(8,128)(2,1)} %bitcast.21, ...), custom_call_target="tpu_custom_call" | custom-call | flops 1811939328 | bytes 2359296 | tf_op jit(solution)/shard_map/pallas_call | solution.py:234
  149.6 6.0 %collective-permute-done.27.refs_12_ = s16[528,256]{1,0:T(8,128)(2,1)S(1)} collective-permute-done((s16[528,256]{1,0:T(8,128)(2,1)}, s16[528,256]{1,0:T(8,128)(2,1)S(1)}, u32[]{:S(2)}, u32[]{:S(2)}) %collective-permute-start.27) | collective-permute-done | bytes 270368 | tf_op jit(solution)/shard_map/ppermute | solution.py:353
  156.3 8.7 %shard_map.113 = f32[768,512]{1,0:T(8,128)} custom-call(s32[8]{0:T(128)} %get-tuple-element.40.dest_ref.refs_0_, bf16[4,3,2,72,256]{4,3,2,1,0:T(8,128)(2,1)} %get-tuple-element.13.refs_1_, bf16[4,3,2,72,256]{4,3,2,1,0:T(8,128)(2,1)} %copy-done, bf16[4,3,2,72,256]{4,3,2,1,0:T(8,128)(2,1)} %copy-done.1, bf16[4,3,2,72,256]{4,3,2,1,0:T(8,128)(2,1)} %copy-done, ...), custom_call_target="tpu_custom_call" | custom-call | flops 2800000000 | bytes 8000000 | tf_op jit(solution)/shard_map/pallas_call | solution.py:343
  169.3 3.3 %collective-permute-start.8 = (s16[528,256]{1,0:T(8,128)(2,1)}, s16[528,256]{1,0:T(8,128)(2,1)S(1)}, u32[]{:S(2)}, u32[]{:S(2)}) collective-permute-start(s16[528,256]{1,0:T(8,128)(2,1)} %shard_map.103), channel_id=1, source_target_pairs={{0,16},{4,20},{8,24},{12,28},{16,0},{20,4},{24,8},{28,12},{1,17},{... | collective-permute-start | bytes 811016 | tf_op jit(solution)/shard_map/ppermute | solution.py:353
  173.3 8.6 %shard_map.109 = f32[768,512]{1,0:T(8,128)} custom-call(s32[8]{0:T(128)} %get-tuple-element.40.dest_ref.refs_0_, bf16[4,3,2,72,256]{4,3,2,1,0:T(8,128)(2,1)} %get-tuple-element.13.refs_1_, bf16[4,3,2,72,256]{4,3,2,1,0:T(8,128)(2,1)} %copy-done, bf16[4,3,2,72,256]{4,3,2,1,0:T(8,128)(2,1)} %copy-done.1, bf16[4,3,2,72,256]{4,3,2,1,0:T(8,128)(2,1)} %copy-done, ...), custom_call_target="tpu_custom_call" | custom-call | flops 2800000000 | bytes 8000000 | tf_op jit(solution)/shard_map/pallas_call | solution.py:343
  186.5 8.8 %shard_map.105 = f32[768,512]{1,0:T(8,128)} custom-call(s32[8]{0:T(128)} %get-tuple-element.40.dest_ref.refs_0_, bf16[4,3,2,72,256]{4,3,2,1,0:T(8,128)(2,1)} %get-tuple-element.13.refs_1_, bf16[4,3,2,72,256]{4,3,2,1,0:T(8,128)(2,1)} %copy-done, bf16[4,3,2,72,256]{4,3,2,1,0:T(8,128)(2,1)} %copy-done.1, bf16[4,3,2,72,256]{4,3,2,1,0:T(8,128)(2,1)} %copy-done, ...), custom_call_target="tpu_custom_call" | custom-call | flops 2800000000 | bytes 8000000 | tf_op jit(solution)/shard_map/pallas_call | solution.py:343
  200.6 8.5 %collective-permute-done.29 = f32[192,512]{1,0:T(8,128)S(1)} collective-permute-done((f32[192,512]{1,0:T(8,128)S(1)}, f32[192,512]{1,0:T(8,128)S(1)}, u32[]{:S(2)}, u32[]{:S(2)}) %collective-permute-start.29) | collective-permute-done | bytes 393248 | tf_op jit(solution)/shard_map/ppermute | solution.py:353
  210.8 6.8 %collective-permute-done.21 = f32[192,512]{1,0:T(8,128)S(1)} collective-permute-done((f32[192,512]{1,0:T(8,128)S(1)}, f32[192,512]{1,0:T(8,128)S(1)}, u32[]{:S(2)}, u32[]{:S(2)}) %collective-permute-start.21) | collective-permute-done | bytes 393248 | tf_op jit(solution)/shard_map/ppermute | solution.py:353
  219.2 6.1 %collective-permute-done.13 = f32[192,512]{1,0:T(8,128)S(1)} collective-permute-done((f32[192,512]{1,0:T(8,128)S(1)}, f32[192,512]{1,0:T(8,128)S(1)}, u32[]{:S(2)}, u32[]{:S(2)}) %collective-permute-start.13) | collective-permute-done | bytes 393248 | tf_op jit(solution)/shard_map/ppermute | solution.py:353
  232.8 3.3 %collective-permute-start.32 = (f32[192,64]{1,0:T(8,128)S(1)}, f32[192,64]{1,0:T(8,128)S(1)}, u32[]{:S(2)}, u32[]{:S(2)}) collective-permute-start(f32[192,64]{1,0:T(8,128)S(1)} %get-tuple-element.28), channel_id=1, source_target_pairs={{0,16},{4,20},{8,24},{12,28},{16,0},{20,4},{24,8},{28,12},{1,17},{... | collective-permute-start | bytes 147464 | tf_op jit(solution)/shard_map/ppermute | solution.py:353
  239.8 5.3 %collective-permute-done.32 = f32[192,64]{1,0:T(8,128)S(1)} collective-permute-done((f32[192,64]{1,0:T(8,128)S(1)}, f32[192,64]{1,0:T(8,128)S(1)}, u32[]{:S(2)}, u32[]{:S(2)}) %collective-permute-start.32) | collective-permute-done | bytes 49184 | tf_op jit(solution)/shard_map/ppermute | solution.py:353
  (183 shorter events, 71.8 us)
Async XLA Ops:
  1.4 36.2 %collective-permute-start.3 = (bf16[3,2,64,1024]{3,2,1,0:T(8,128)(2,1)S(1)}, bf16[3,2,64,1024]{3,2,1,0:T(8,128)(2,1)S(1)}, u32[]{:S(2)}, u32[]{:S(2)}) collective-permute-start(bf16[3,2,64,1024]{3,2,1,0:T(8,128)(2,1)S(1)} %bitcast.15), channel_id=1, source_target_pairs={{0,1},{1,0},{2,3},{3,2},{4,5},{5,4},{6,7},{7,6},{8,9},{9,8},{10,11... | collective-permute-start | bytes 2359304 | tf_op jit(solution)/shard_map/ppermute | solution.py:353
  1.9 21.1 %collective-permute-start.4 = (bf16[3,2,64,1024]{3,2,1,0:T(8,128)(2,1)S(1)}, bf16[3,2,64,1024]{3,2,1,0:T(8,128)(2,1)}, u32[]{:S(2)}, u32[]{:S(2)}) collective-permute-start(bf16[3,2,64,1024]{3,2,1,0:T(8,128)(2,1)S(1)} %bitcast.16), channel_id=1, source_target_pairs={{0,2},{1,3},{2,0},{3,1},{4,6},{5,7},{6,4},{7,5},{8,10},{9,11},{10,... | collective-permute-start | bytes 2359304 | tf_op jit(solution)/shard_map/ppermute | solution.py:353
  13.9 21.9 %collective-permute-start = (bf16[4,3,2,72,256]{4,3,2,1,0:T(8,128)(2,1)}, bf16[4,3,2,72,256]{4,3,2,1,0:T(8,128)(2,1)S(1)}, u32[]{:S(2)}, u32[]{:S(2)}) collective-permute-start(bf16[4,3,2,72,256]{4,3,2,1,0:T(8,128)(2,1)} %get-tuple-element.14), channel_id=1, source_target_pairs={{0,4},{4,0},{8,12},{12,8},{16,20},{20,16},{24,28},{28,24},{1,5},{5... | collective-permute-start | bytes 2654216 | tf_op jit(solution)/shard_map/ppermute | solution.py:353
  15.5 79.7 %collective-permute-start.10 = (bf16[2,96,1024]{2,1,0:T(8,128)(2,1)S(1)}, bf16[2,96,1024]{2,1,0:T(8,128)(2,1)}, u32[]{:S(2)}, u32[]{:S(2)}) collective-permute-start(bf16[2,96,1024]{2,1,0:T(8,128)(2,1)S(1)} %bitcast.22), channel_id=1, source_target_pairs={{0,2},{1,3},{2,0},{3,1},{4,6},{5,7},{6,4},{7,5},{8,10},{9,11},{10,... | collective-permute-start | bytes 1179656 | tf_op jit(solution)/shard_map/ppermute | solution.py:353
  22.9 14.7 %collective-permute-start.5 = (bf16[3,2,64,1024]{3,2,1,0:T(8,128)(2,1)}, bf16[3,2,64,1024]{3,2,1,0:T(8,128)(2,1)}, u32[]{:S(2)}, u32[]{:S(2)}) collective-permute-start(bf16[3,2,64,1024]{3,2,1,0:T(8,128)(2,1)} %collective-permute-done.4.refs_3_), channel_id=1, source_target_pairs={{0,1},{1,0},{2,3},{3,2},{4,5},{5,4},{6,7},{7,6},{8,9},{9,8},{10,11... | collective-permute-start | bytes 2359304 | tf_op jit(solution)/shard_map/ppermute | solution.py:353
  36.0 52.0 %collective-permute-start.1 = (bf16[4,3,2,72,256]{4,3,2,1,0:T(8,128)(2,1)S(1)}, bf16[4,3,2,72,256]{4,3,2,1,0:T(8,128)(2,1)S(1)}, u32[]{:S(2)}, u32[]{:S(2)}) collective-permute-start(bf16[4,3,2,72,256]{4,3,2,1,0:T(8,128)(2,1)S(1)} %pad_maximum_fusion), channel_id=1, source_target_pairs={{0,8},{4,12},{8,0},{12,4},{16,24},{20,28},{24,16},{28,20},{1,9},{5... | collective-permute-start | bytes 2654216 | tf_op jit(solution)/shard_map/ppermute | solution.py:353
  53.2 37.6 %collective-permute-start.25 = (s16[528,1024]{1,0:T(8,128)(2,1)}, s16[528,1024]{1,0:T(8,128)(2,1)S(1)}, u32[]{:S(2)}, u32[]{:S(2)}) collective-permute-start(s16[528,1024]{1,0:T(8,128)(2,1)} %get-tuple-element.20), channel_id=1, source_target_pairs={{0,4},{4,0},{8,12},{12,8},{16,20},{20,16},{24,28},{28,24},{1,5},{5... | collective-permute-start | bytes 3244040 | tf_op jit(solution)/shard_map/ppermute | solution.py:353
  69.4 34.1 %collective-permute-start.17 = (s16[528,1024]{1,0:T(8,128)(2,1)}, s16[528,1024]{1,0:T(8,128)(2,1)}, u32[]{:S(2)}, u32[]{:S(2)}) collective-permute-start(s16[528,1024]{1,0:T(8,128)(2,1)} %get-tuple-element.18), channel_id=1, source_target_pairs={{0,4},{4,0},{8,12},{12,8},{16,20},{20,16},{24,28},{28,24},{1,5},{5... | collective-permute-start | bytes 3244040 | tf_op jit(solution)/shard_map/ppermute | solution.py:353
  84.6 40.1 %collective-permute-start.6 = (s16[528,1024]{1,0:T(8,128)(2,1)}, s16[528,1024]{1,0:T(8,128)(2,1)}, u32[]{:S(2)}, u32[]{:S(2)}) collective-permute-start(s16[528,1024]{1,0:T(8,128)(2,1)} %get-tuple-element.16), channel_id=1, source_target_pairs={{0,4},{4,0},{8,12},{12,8},{16,20},{20,16},{24,28},{28,24},{1,5},{5... | collective-permute-start | bytes 3244040 | tf_op jit(solution)/shard_map/ppermute | solution.py:353
  88.2 61.4 %collective-permute-start.2 = (bf16[4,3,2,72,256]{4,3,2,1,0:T(8,128)(2,1)S(1)}, bf16[4,3,2,72,256]{4,3,2,1,0:T(8,128)(2,1)S(1)}, u32[]{:S(2)}, u32[]{:S(2)}) collective-permute-start(bf16[4,3,2,72,256]{4,3,2,1,0:T(8,128)(2,1)S(1)} %pad_maximum_fusion.1), channel_id=1, source_target_pairs={{0,16},{4,20},{8,24},{12,28},{16,0},{20,4},{24,8},{28,12},{1,17},{... | collective-permute-start | bytes 2654216 | tf_op jit(solution)/shard_map/ppermute | solution.py:353
  94.5 34.1 %collective-permute-start.26 = (s16[528,512]{1,0:T(8,128)(2,1)}, s16[528,512]{1,0:T(8,128)(2,1)S(1)}, u32[]{:S(2)}, u32[]{:S(2)}) collective-permute-start(s16[528,512]{1,0:T(8,128)(2,1)} %shard_map.111), channel_id=1, source_target_pairs={{0,8},{4,12},{8,0},{12,4},{16,24},{20,28},{24,16},{28,20},{1,9},{5... | collective-permute-start | bytes 1622024 | tf_op jit(solution)/shard_map/ppermute | solution.py:353
  95.3 37.2 %collective-permute-start.9 = (bf16[2,96,1024]{2,1,0:T(8,128)(2,1)S(1)}, bf16[2,96,1024]{2,1,0:T(8,128)(2,1)S(1)}, u32[]{:S(2)}, u32[]{:S(2)}) collective-permute-start(bf16[2,96,1024]{2,1,0:T(8,128)(2,1)S(1)} %bitcast.23), channel_id=1, source_target_pairs={{0,1},{1,0},{2,3},{3,2},{4,5},{5,4},{6,7},{7,6},{8,9},{9,8},{10,11... | collective-permute-start | bytes 1179656 | tf_op jit(solution)/shard_map/ppermute | solution.py:353
  103.5 34.3 %collective-permute-start.11 = (bf16[2,96,1024]{2,1,0:T(8,128)(2,1)}, bf16[2,96,1024]{2,1,0:T(8,128)(2,1)S(1)}, u32[]{:S(2)}, u32[]{:S(2)}) collective-permute-start(bf16[2,96,1024]{2,1,0:T(8,128)(2,1)} %collective-permute-done.10.refs_2_), channel_id=1, source_target_pairs={{0,1},{1,0},{2,3},{3,2},{4,5},{5,4},{6,7},{7,6},{8,9},{9,8},{10,11... | collective-permute-start | bytes 1179656 | tf_op jit(solution)/shard_map/ppermute | solution.py:353
  124.7 21.2 %collective-permute-start.18 = (s16[528,512]{1,0:T(8,128)(2,1)}, s16[528,512]{1,0:T(8,128)(2,1)S(1)}, u32[]{:S(2)}, u32[]{:S(2)}) collective-permute-start(s16[528,512]{1,0:T(8,128)(2,1)} %shard_map.107), channel_id=1, source_target_pairs={{0,8},{4,12},{8,0},{12,4},{16,24},{20,28},{24,16},{28,20},{1,9},{5... | collective-permute-start | bytes 1622024 | tf_op jit(solution)/shard_map/ppermute | solution.py:353
  128.6 37.6 %collective-permute-start.7 = (s16[528,512]{1,0:T(8,128)(2,1)}, s16[528,512]{1,0:T(8,128)(2,1)S(1)}, u32[]{:S(2)}, u32[]{:S(2)}) collective-permute-start(s16[528,512]{1,0:T(8,128)(2,1)} %shard_map.102), channel_id=1, source_target_pairs={{0,8},{4,12},{8,0},{12,4},{16,24},{20,28},{24,16},{28,20},{1,9},{5... | collective-permute-start | bytes 1622024 | tf_op jit(solution)/shard_map/ppermute | solution.py:353
  132.5 23.1 %collective-permute-start.27 = (s16[528,256]{1,0:T(8,128)(2,1)}, s16[528,256]{1,0:T(8,128)(2,1)S(1)}, u32[]{:S(2)}, u32[]{:S(2)}) collective-permute-start(s16[528,256]{1,0:T(8,128)(2,1)} %shard_map.112), channel_id=1, source_target_pairs={{0,16},{4,20},{8,24},{12,28},{16,0},{20,4},{24,8},{28,12},{1,17},{... | collective-permute-start | bytes 811016 | tf_op jit(solution)/shard_map/ppermute | solution.py:353
  149.0 23.7 %collective-permute-start.19 = (s16[528,256]{1,0:T(8,128)(2,1)}, s16[528,256]{1,0:T(8,128)(2,1)S(1)}, u32[]{:S(2)}, u32[]{:S(2)}) collective-permute-start(s16[528,256]{1,0:T(8,128)(2,1)} %shard_map.108), channel_id=1, source_target_pairs={{0,16},{4,20},{8,24},{12,28},{16,0},{20,4},{24,8},{28,12},{1,17},{... | collective-permute-start | bytes 811016 | tf_op jit(solution)/shard_map/ppermute | solution.py:353
  166.2 30.5 %collective-permute-start.28 = (f32[384,512]{1,0:T(8,128)S(1)}, f32[384,512]{1,0:T(8,128)S(1)}, u32[]{:S(2)}, u32[]{:S(2)}) collective-permute-start(f32[384,512]{1,0:T(8,128)S(1)} %slice.201), channel_id=1, source_target_pairs={{0,1},{1,0},{2,3},{3,2},{4,5},{5,4},{6,7},{7,6},{8,9},{9,8},{10,11... | collective-permute-start | bytes 2359304 | tf_op jit(solution)/shard_map/ppermute | solution.py:353
  169.3 16.5 %collective-permute-start.8 = (s16[528,256]{1,0:T(8,128)(2,1)}, s16[528,256]{1,0:T(8,128)(2,1)S(1)}, u32[]{:S(2)}, u32[]{:S(2)}) collective-permute-start(s16[528,256]{1,0:T(8,128)(2,1)} %shard_map.103), channel_id=1, source_target_pairs={{0,16},{4,20},{8,24},{12,28},{16,0},{20,4},{24,8},{28,12},{1,17},{... | collective-permute-start | bytes 811016 | tf_op jit(solution)/shard_map/ppermute | solution.py:353
  183.2 14.5 %collective-permute-start.20 = (f32[384,512]{1,0:T(8,128)S(1)}, f32[384,512]{1,0:T(8,128)S(1)}, u32[]{:S(2)}, u32[]{:S(2)}) collective-permute-start(f32[384,512]{1,0:T(8,128)S(1)} %slice.189), channel_id=1, source_target_pairs={{0,1},{1,0},{2,3},{3,2},{4,5},{5,4},{6,7},{7,6},{8,9},{9,8},{10,11... | collective-permute-start | bytes 2359304 | tf_op jit(solution)/shard_map/ppermute | solution.py:353
  198.3 19.3 %collective-permute-start.21 = (f32[192,512]{1,0:T(8,128)S(1)}, f32[192,512]{1,0:T(8,128)S(1)}, u32[]{:S(2)}, u32[]{:S(2)}) collective-permute-start(f32[192,512]{1,0:T(8,128)S(1)} %slice.191), channel_id=1, source_target_pairs={{0,2},{1,3},{2,0},{3,1},{4,6},{5,7},{6,4},{7,5},{8,10},{9,11},{10,... | collective-permute-start | bytes 1179656 | tf_op jit(solution)/shard_map/ppermute | solution.py:353
  199.7 25.7 %collective-permute-start.13 = (f32[192,512]{1,0:T(8,128)S(1)}, f32[192,512]{1,0:T(8,128)S(1)}, u32[]{:S(2)}, u32[]{:S(2)}) collective-permute-start(f32[192,512]{1,0:T(8,128)S(1)} %slice.179), channel_id=1, source_target_pairs={{0,2},{1,3},{2,0},{3,1},{4,6},{5,7},{6,4},{7,5},{8,10},{9,11},{10,... | collective-permute-start | bytes 1179656 | tf_op jit(solution)/shard_map/ppermute | solution.py:353
  209.2 17.8 %collective-permute-start.30 = (f32[192,256]{1,0:T(8,128)S(1)}, f32[192,256]{1,0:T(8,128)S(1)}, u32[]{:S(2)}, u32[]{:S(2)}) collective-permute-start(f32[192,256]{1,0:T(8,128)S(1)} %slice.205), channel_id=1, source_target_pairs={{0,4},{4,0},{8,12},{12,8},{16,20},{20,16},{24,28},{28,24},{1,5},{5... | collective-permute-start | bytes 589832 | tf_op jit(solution)/shard_map/ppermute | solution.py:353
  232.8 12.4 %collective-permute-start.32 = (f32[192,64]{1,0:T(8,128)S(1)}, f32[192,64]{1,0:T(8,128)S(1)}, u32[]{:S(2)}, u32[]{:S(2)}) collective-permute-start(f32[192,64]{1,0:T(8,128)S(1)} %get-tuple-element.28), channel_id=1, source_target_pairs={{0,16},{4,20},{8,24},{12,28},{16,0},{20,4},{24,8},{28,12},{1,17},{... | collective-permute-start | bytes 147464 | tf_op jit(solution)/shard_map/ppermute | solution.py:353
  (35 other events, 301.7 us)

commit v3 on v2

--- a/solution.py
+++ b/solution.py
@@ -104,9 +104,8 @@
     )(dests, con, shift_map.reshape(points, 1, slab))
 
 
-def x_kernel(slots, at_once, table_ref, *refs):
-    val_refs, weight_refs = refs[:slots], refs[slots : slots + at_once]
-    go_ref, keep_ref, left_ref = refs[slots + at_once :]
+def x_kernel(slots, base_ref, *refs):
+    val_refs, (weight_ref, go_ref, keep_ref, left_ref) = refs[:slots], refs[slots:]
     rows, depth = val_refs[0].shape[2], val_refs[0].shape[3]
     half = slots * rows
     step = pl.program_id(0)
@@ -123,50 +122,43 @@
             left_ref[low, 0:depth] = imag
             left_ref[low, depth : 2 * depth] = real
 
-    width = weight_refs[0].shape[3]
-    for place, weight_ref in enumerate(weight_refs):
-        product = mm(left_ref[...], weight_ref[0].reshape(2 * depth, width))
-        cols = slice(place * width, (place + 1) * width)
-
-        @pl.when(step < halfway)
-        def _():
-            encode(product, go_ref.at[:, cols])
-
-        @pl.when(step >= halfway)
-        def _():
-            keep_ref[:, cols] = product
-
-
-def x_call(vals, screened, point, table, width, at_once):
+    weight = weight_ref[0].reshape(2 * depth, weight_ref.shape[3])
+
+    @pl.when(step < halfway)
+    def _():
+        encode(mm(left_ref[...], weight), go_ref)
+
+    @pl.when(step >= halfway)
+    def _():
+        keep_ref[...] = mm(left_ref[...], weight)
+
+
+def x_call(vals, screened, place, point, side, steps):
     slots = len(vals)
     _, _, rows, depth = vals[0].shape
     height = 2 * slots * rows
-    steps = table.shape[0] // at_once
+    columns = screened.shape[3] // 2
     half = steps // 2
-    columns = width * at_once * half
-    weights = [
-        pl.BlockSpec(
-            (1, 2, depth, width), lambda j, t, place=place: (point, 0, 0, t[j * at_once + place])
-        )
-        for place in range(at_once)
-    ]
+    width = columns // half
     grid_spec = pltpu.PrefetchScalarGridSpec(
         num_scalar_prefetch=1,
         grid=(steps,),
         in_specs=[
-            pl.BlockSpec((1, 2, rows, depth), lambda j, t: (point, 0, 0, 0)) for _ in vals
+            pl.BlockSpec((1, 2, rows, depth), lambda j, t: (place, 0, 0, 0)) for _ in vals
         ]
-        + weights,
+        + [
+            pl.BlockSpec(
+                (1, 2, depth, width), lambda j, t: (point, 0, 0, t[j // half] * half + j % half)
+            )
+        ],
         out_specs=[
-            pl.BlockSpec(
-                (height + EXP_ROWS, width * at_once), lambda j, t: (0, jnp.minimum(j, half - 1))
-            ),
-            pl.BlockSpec((height, width * at_once), lambda j, t: (0, jnp.maximum(j - half, 0))),
+            pl.BlockSpec((height + EXP_ROWS, width), lambda j, t: (0, jnp.minimum(j, half - 1))),
+            pl.BlockSpec((height, width), lambda j, t: (0, jnp.maximum(j - half, 0))),
         ],
         scratch_shapes=[pltpu.VMEM((height, 2 * depth), jnp.bfloat16)],
     )
     return pl.pallas_call(
-        lambda *refs: x_kernel(slots, at_once, *refs),
+        lambda *refs: x_kernel(slots, *refs),
         grid_spec=grid_spec,
         out_shape=[
             jax.ShapeDtypeStruct((height + EXP_ROWS, columns), jnp.int16),
@@ -176,28 +168,36 @@
         cost_estimate=cost(
             2 * height * 2 * depth * 2 * columns, 8 * depth * columns + 6 * height * columns
         ),
-    )(table, *vals, *([screened] * at_once))
-
-
-def hop_kernel(keep_ref, *refs):
+    )(side, *vals, screened)
+
+
+def hop_kernel(heard, at_ref, keep_ref, *refs):
     total = keep_ref[...]
-    for ref in refs[:-1]:
+    for ref in refs[:heard]:
         total = total + decode(ref)
     encode(total, refs[-1])
 
 
-def hop_call(keep, others, block, width):
+def hop_call(keep, others, at, width, after):
     height, tall = keep.shape[0], others[0].shape[0]
+    grid_spec = pltpu.PrefetchScalarGridSpec(
+        num_scalar_prefetch=1,
+        grid=(1,),
+        in_specs=[pl.BlockSpec((height, width), lambda i, at: (0, at[0]))]
+        + [
+            pl.BlockSpec((tall, width), lambda i, at, n=n: (0, at[n + 1]))
+            for n in range(len(others))
+        ]
+        + [pl.BlockSpec(memory_space=pl.ANY) for _ in after],
+        out_specs=pl.BlockSpec((tall, width), lambda i, at: (0, 0)),
+    )
     return pl.pallas_call(
-        hop_kernel,
-        grid=(1,),
-        in_specs=[pl.BlockSpec((height, width), lambda i: (0, block))]
-        + [pl.BlockSpec((tall, width), lambda i: (0, block)) for _ in others],
-        out_specs=pl.BlockSpec((tall, width), lambda i: (0, 0)),
+        lambda *refs: hop_kernel(len(others), *refs),
+        grid_spec=grid_spec,
         out_shape=jax.ShapeDtypeStruct((tall, width), jnp.int16),
         compiler_params=params(),
         cost_estimate=cost(20 * height * width, 8 * height * width),
-    )(keep, *others)
+    )(at, keep, *others, *after)
 
 
 def exchange_kernel(slots, *refs):
@@ -247,11 +247,11 @@
     )(*heres, there, coulomb.reshape(points, 1, depth))
 
 
-def tile_kernel(slots, heard, chunks, index_ref, *refs):
+def tile_kernel(slots, heard, chunks, waits, index_ref, at_ref, *refs):
     con_refs, keep_ref = refs[:slots], refs[slots]
     heard_refs = refs[slots + 1 : slots + 1 + heard]
     exch_ref, row_ref, col_direct_ref, col_exch_ref = refs[slots + 1 + heard : slots + 5 + heard]
-    out_ref, con_all, direct_ref, natural_ref = refs[slots + 5 + heard :]
+    keep_out, go_out, con_all, direct_ref, natural_ref = refs[slots + 5 + heard + waits :]
     total = keep_ref[...]
     for ref in heard_refs:
         total = total + decode(ref)
@@ -307,33 +307,42 @@
                 term = mm(moved, pick_cols[...])
                 result = term if result is None else result + term
         for chunk in range(chunks):
-            at = (2 * chunk + part) * count
+            out_ref = keep_out if chunk < chunks // 2 else go_out
+            at = (2 * (chunk % (chunks // 2)) + part) * count
             out_ref[at : at + count, :] = result[chunk * count : (chunk + 1) * count]
 
 
-def tile_call(cons, point, keep, heard, exch, index, pick_rows, col_direct, col_exch, chunks):
+def tile_call(
+    cons, point, keep, heard, exch, index, at, pick_rows, col_direct, col_exch, chunks, after
+):
     slots = len(cons)
     _, _, _, rows, width = cons[0][0].shape
     height, tall = keep.shape[0], heard[0].shape[0]
     pitch = -(-rows // 16) * 16
     out_cols = col_direct.shape[1]
-    whole = lambda a: pl.BlockSpec(a.shape, lambda i, at: (0,) * a.ndim)
+    whole = lambda a: pl.BlockSpec(a.shape, lambda i, index, at: (0,) * a.ndim)
     grid_spec = pltpu.PrefetchScalarGridSpec(
-        num_scalar_prefetch=1,
+        num_scalar_prefetch=2,
         grid=(1,),
         in_specs=[
-            pl.BlockSpec((1, 1, 2, rows, width), lambda i, at, place=place: (place, point, 0, 0, 0))
+            pl.BlockSpec(
+                (1, 1, 2, rows, width), lambda i, index, at, place=place: (place, point, 0, 0, 0)
+            )
             for _, place in cons
         ]
-        + [pl.BlockSpec((height, width), lambda i, at: (0, 0))]
-        + [pl.BlockSpec((tall, width), lambda i, at: (0, 0)) for _ in heard]
+        + [pl.BlockSpec((height, width), lambda i, index, at: (0, at[0]))]
         + [
-            pl.BlockSpec((1,) + exch.shape[1:], lambda i, at: (point, 0, 0, 0)),
+            pl.BlockSpec((tall, width), lambda i, index, at, n=n: (0, at[n + 1]))
+            for n in range(len(heard))
+        ]
+        + [
+            pl.BlockSpec((1,) + exch.shape[1:], lambda i, index, at: (point, 0, 0, 0)),
             whole(pick_rows),
             whole(col_direct),
             whole(col_exch),
-        ],
-        out_specs=pl.BlockSpec((2 * NT, out_cols), lambda i, at: (0, 0)),
+        ]
+        + [pl.BlockSpec(memory_space=pl.ANY) for _ in after],
+        out_specs=[pl.BlockSpec((NT, out_cols), lambda i, index, at: (0, 0))] * 2,
         scratch_shapes=[
             pltpu.VMEM((slots * pitch, 2 * width), jnp.bfloat16),
             pltpu.VMEM((height // 128, NC * NC, 128), jnp.float32),
@@ -341,12 +350,14 @@
         ],
     )
     return pl.pallas_call(
-        lambda *refs: tile_kernel(slots, len(heard), chunks, *refs),
+        lambda *refs: tile_kernel(slots, len(heard), chunks, len(after), *refs),
         grid_spec=grid_spec,
-        out_shape=jax.ShapeDtypeStruct((2 * NT, out_cols), jnp.float32),
+        out_shape=[jax.ShapeDtypeStruct((NT, out_cols), jnp.float32)] * 2,
         compiler_params=params(),
         cost_estimate=cost(2.8e9, 8e6),
-    )(index, *[c for c, _ in cons], keep, *heard, exch, pick_rows, col_direct, col_exch)
+    )(
+        index, at, *[c for c, _ in cons], keep, *heard, exch, pick_rows, col_direct, col_exch, *after
+    )
 
 
 def swap(value, axis, size, bit):
@@ -382,11 +393,21 @@
     ga_order = halving_order(ga_bits)
     half = ga // 2
     dests = me_ga ^ jnp.asarray(ga_order, jnp.int32)
-
-    vals = gather_slots(jnp.transpose(val_density, (1, 2, 0, 3)), "pair", pair)
+    flags = [(me_ga // bit) % 2 for bit in ga_bits]
+    blocks = sum(((dests // bit) % 2) * (half // bit) for bit in ga_bits)
+    as_index = lambda items: jnp.stack([jnp.asarray(i, jnp.int32) for i in items])
+
+    def block_at(known, chosen):
+        number = jnp.int32(0)
+        for flag in flags[known : len(flags) if chosen is None else chosen]:
+            number = 2 * number + flag
+        return number if chosen is None else 2 * number + 1 - flags[chosen]
+
+    val = jnp.transpose(val_density, (1, 2, 0, 3))
+    first, others = gather_slots(val[:1], "pair", pair), gather_slots(val[1:], "pair", pair)
 
     con = jnp.transpose(con_density, (1, 2, 0, 3))
-    stay, go = shift_call(con, shift_map, dests, width)
+    stay, go = shift_call(con, shift_map, blocks, width)
     cons = {}
     for p, slot in enumerate(ga_order):
         cons[slot] = (stay, p) if p < half else (go, p - half)
@@ -401,10 +422,11 @@
             cons[slot] = (got, place)
     cons = [cons[slot] for slot in ga_order]
 
-    table = jnp.concatenate([dests[half:], dests[:half]])
+    side = as_index([1 - flags[0], flags[0]])
     gone, keep = [], []
     for q in range(points):
-        coded, own = x_call(vals, screened, q, table, width, 2)
+        vals, place = (first, 0) if q == 0 else (others, q - 1)
+        coded, own = x_call(vals, screened, place, q, side, 4)
         gone.append(coded)
         keep.append(own)
 
@@ -430,23 +452,33 @@
     col_direct, col_exch = pick_cols(at_direct, NT, -1.0), pick_cols(at_exch, row_count, 2.0)
 
     heard = [[swap(gone[q], "ga", ga, ga_bits[0])] for q in range(points)]
-    part = half
-    for bit in ga_bits[1:]:
-        part //= 2
-        for q in range(points):
-            heard[q].append(swap(hop_call(keep[q], heard[q], 1, part * width), "ga", ga, bit))
-    outs = []
-    for q in range(points):
-        tile = tile_call(
-            cons, q, keep[q], heard[q], exch, dests, pick_rows, col_direct, col_exch, pair
-        )
-        for bit in pair_bits:
-            rows = tile.shape[0] // 2
-            tile = tile[:rows] + swap(tile[rows:], "pair", pair, bit)
-        for bit in ga_bits:
-            cols = tile.shape[1] // 2
-            tile = tile[:, :cols] + swap(tile[:, cols:], "ga", ga, bit)
-        outs.append(tile[:, :col_count].reshape(2, row_count, col_count))
+    outs = [None] * points
+    stages = len(ga_bits)
+    after = []
+    for wave in range(2 * points + stages):
+        for q in reversed(range(points)):
+            stage = wave - 2 * q
+            if 1 <= stage < stages:
+                columns = ga >> (stage + 1)
+                at = as_index([block_at(k, stage) for k in [1] + list(range(1, stage + 1))])
+                coded = hop_call(keep[q], heard[q], at, columns * width, after)
+                after = [coded]
+                heard[q].append(swap(coded, "ga", ga, ga_bits[stage]))
+            elif stage == stages:
+                at = as_index([block_at(k, None) for k in [1] + list(range(1, stages + 1))])
+                tile, sent = tile_call(
+                    cons, q, keep[q], heard[q], exch, dests, at, pick_rows, col_direct, col_exch,
+                    pair, after,
+                )
+                after = [sent]
+                tile = tile + swap(sent, "pair", pair, pair_bits[0])
+                for bit in pair_bits[1:]:
+                    rows = tile.shape[0] // 2
+                    tile = tile[:rows] + swap(tile[rows:], "pair", pair, bit)
+                for bit in ga_bits:
+                    cols = tile.shape[1] // 2
+                    tile = tile[:, :cols] + swap(tile[:, cols:], "ga", ga, bit)
+                outs[q] = tile[:, :col_count].reshape(2, row_count, col_count)
     return jnp.stack(outs)
 
 

time: 250 us -> 243 us (0.972)
  Pallas kernels: 95.2 us -> 85.8 us
  starting transfers between devices: 39.5 us -> 35.4 us
  other arithmetic: 5.18 us -> 8.14 us
    pallas_call x12, Pallas kernels: 84.8 us -> 75.3 us  [the longest x3 30.6 us: x_call(): pl.pallas_call(lambda *refs: x_kernel(slots, *refs), grid_spec=grid_spec,...]
    ppermute x33 -> x36, starting transfers between devices: 39.5 us -> 35.4 us  [swap(): return lax.ppermute(value, axis, [(i, i ^ bit) for i in range(size)])]
    unnamed x56 -> x66, local copies, waits for them, and re-layouts: 13.5 us -> 17.3 us
    slice x6 -> x3, local copies, waits for them, and re-layouts: 3.75 us -> 0.08 us  [on_device(): tile = tile[:rows] + swap(tile[rows:], 'pair', pair, bit)]
    ppermute x33 -> x36, waiting for transfers between devices: 85.6 us -> 87.9 us  [swap(): return lax.ppermute(value, axis, [(i, i ^ bit) for i in range(size)])]
  transfers between devices with their start and end apart: 33 -> 36, of which waited for: 15 -> 16; matrix products, arithmetic and copies ran while one was open for 8% -> 8% of each run, Pallas kernels for 38% -> 36%
where the time goes in v3:
time: 243 us; the launch traced here: 242 us
  waiting for transfers between devices  87.9 us (36%)
  Pallas kernels  85.8 us (35%)
  starting transfers between devices  35.4 us (15%)
  local copies, waits for them, and re-layouts  23.9 us (10%)
  other arithmetic  8.14 us (3%)
    ppermute x36, waiting for transfers between devices, swap(): return lax.ppermute(value, axis, [(i, i ^ bit) for i in range(size)])  87.9 us
    ppermute x36, starting transfers between devices, swap(): return lax.ppermute(value, axis, [(i, i ^ bit) for i in range(size)])  35.4 us
    pallas_call x3, Pallas kernels, x_call(): pl.pallas_call(lambda *refs: x_kernel(slots, *refs), grid_spec=grid_spec,...  30.6 us
    pallas_call x3, Pallas kernels, tile_call(): pl.pallas_call(lambda *refs: tile_kernel(slots, len(heard), chunks, len(a...  26 us
    pallas_call x6, Pallas kernels, hop_call(): pl.pallas_call(lambda *refs: hop_kernel(len(others), *refs), grid_spec=gr...  18.7 us
    unnamed x66, local copies, waits for them, and re-layouts  17.3 us
    pallas_call x1, Pallas kernels, exchange_call(): pl.pallas_call(lambda *refs: exchange_kernel(slots, *refs), grid=(points,...  5.7 us
  transfers between devices with their start and end apart: 36, of which 16 were waited for; matrix products, arithmetic and copies ran while one was open for 8% of the time, Pallas kernels for 36%

profile of v3, /device:TPU:0, one launch (start us, length us, event | category | flops | bytes accessed | tf_op | source)
XLA Modules:
  0.0 241.7 jit_solution(16407541398589093134)
XLA Ops:
  1.5 3.0 %collective-permute-start.4 = (bf16[1,2,64,1024]{3,2,1,0:T(8,128)(2,1)S(1)}, bf16[1,2,64,1024]{3,2,1,0:T(8,128)(2,1)S(1)}, u32[]{:S(2)}, u32[]{:S(2)}) collective-permute-start(bf16[1,2,64,1024]{3,2,1,0:T(8,128)(2,1)S(1)} %slice.152.refs_1_), channel_id=1, source_target_pairs={{0,2},{1,3},{2,0},{3,1},{4,6},{5,7},{6,4},{7,5},{8,10},{9,11},{10,... | collective-permute-start | bytes 786440 | tf_op jit(solution)/shard_map/ppermute | solution.py:364
  8.4 4.8 %shard_map.100 = (bf16[4,3,2,72,256]{4,3,2,1,0:T(8,128)(2,1)}, bf16[4,3,2,72,256]{4,3,2,1,0:T(8,128)(2,1)}) custom-call(s32[8]{0:T(128)} %get-tuple-element.52.dest_ref, bf16[3,2,72,2048]{3,2,1,0:T(8,128)(2,1)} %bitcast.22, s32[3,1,2048]{2,1,0:T(1,128)} %reshape.162.map_ref), custom_call_target="tpu_custom_call" | custom-call | flops 7077888 | bytes 3538944 | tf_op jit(solution)/shard_map/pallas_call | solution.py:98
  22.5 10.2 %shard_map.101 = (s16[528,1024]{1,0:T(8,128)(2,1)}, f32[512,1024]{1,0:T(8,128)}) custom-call(s32[2]{0:T(128)} %pad_add_fusion.1.refs_0_, bf16[1,2,64,1024]{3,2,1,0:T(8,128)(2,1)} %copy-done.12, bf16[1,2,64,1024]{3,2,1,0:T(8,128)(2,1)} %copy-done.22, bf16[1,2,64,1024]{3,2,1,0:T(8,128)(2,1)} %copy-done.21, bf16[1,2,64,1024]{3,2,1,0:T(8,128)(2,1)} %copy-done.23, ...), custom_call_target="tpu_custom_call" | custom-call | flops 4294967296 | bytes 11534336 | tf_op jit(solution)/shard_map/pallas_call | solution.py:160
  45.8 10.3 %shard_map.105 = (s16[528,1024]{1,0:T(8,128)(2,1)}, f32[512,1024]{1,0:T(8,128)}) custom-call(s32[2]{0:T(128)} %pad_add_fusion.1.refs_0_, bf16[2,2,64,1024]{3,2,1,0:T(8,128)(2,1)} %copy-done.6, bf16[2,2,64,1024]{3,2,1,0:T(8,128)(2,1)} %collective-permute-done.12.refs_2_, bf16[2,2,64,1024]{3,2,1,0:T(8,128)(2,1)} %collective-permute-done.13.refs_3_, ...), custom_call_target="tpu_custom_call" | custom-call | flops 4294967296 | bytes 11534336 | tf_op jit(solution)/shard_map/pallas_call | solution.py:160
  59.9 3.4 %shard_map.102.refs_4_ = s16[528,512]{1,0:T(8,128)(2,1)} custom-call(s32[2]{0:T(128)} %pad_add_fusion.2.refs_0_, f32[512,1024]{1,0:T(8,128)} %get-tuple-element.21.refs_1_.refs_10_, s16[528,1024]{1,0:T(8,128)(2,1)} %copy-done.3), custom_call_target="tpu_custom_call" | custom-call | flops 5242880 | bytes 2097152 | tf_op jit(solution)/shard_map/pallas_call | solution.py:194
  71.3 5.7 %shard_map.104.refs_14_ = f32[3,2,384,96]{3,2,1,0:T(8,128)} custom-call(bf16[2,96,1024]{2,1,0:T(8,128)(2,1)} %bitcast.21.refs_0_, bf16[2,96,1024]{2,1,0:T(8,128)(2,1)} %copy-done.28, bf16[2,96,1024]{2,1,0:T(8,128)(2,1)} %collective-permute-done.10.refs_2_, bf16[2,96,1024]{2,1,0:T(8,128)(2,1)} %copy-done.29, bf16[3,2,96,1024]{3,2,1,0:T(8,128)(2,1)} %bitcast.25, ...), custom_call_target="tpu_custom_call" | custom-call | flops 1811939328 | bytes 2359296 | tf_op jit(solution)/shard_map/pallas_call | solution.py:234
  77.0 10.9 %collective-permute-done.7.refs_3_.refs_12_ = s16[528,512]{1,0:T(8,128)(2,1)S(1)} collective-permute-done((s16[528,512]{1,0:T(8,128)(2,1)}, s16[528,512]{1,0:T(8,128)(2,1)S(1)}, u32[]{:S(2)}, u32[]{:S(2)}) %collective-permute-start.7) | collective-permute-done | bytes 540704 | tf_op jit(solution)/shard_map/ppermute | solution.py:364
  88.7 2.9 %shard_map.103.refs_3_ = s16[528,256]{1,0:T(8,128)(2,1)} custom-call(s32[3]{0:T(128)} %pad_add_fusion.3.refs_0_, f32[512,1024]{1,0:T(8,128)} %get-tuple-element.21.refs_1_.refs_10_, s16[528,1024]{1,0:T(8,128)(2,1)} %copy-done.3, s16[528,512]{1,0:T(8,128)(2,1)} %copy-done.7, s16[528,512]{1,0:T(8,128)(2,1)} %shard_map.102.refs_4_), custom_call_target="tpu_custom_call" | custom-call | flops 2621440 | bytes 1048576 | tf_op jit(solution)/shard_map/pallas_call | solution.py:194
  92.2 10.2 %shard_map.109 = (s16[528,1024]{1,0:T(8,128)(2,1)}, f32[512,1024]{1,0:T(8,128)}) custom-call(s32[2]{0:T(128)} %pad_add_fusion.1.refs_0_, bf16[2,2,64,1024]{3,2,1,0:T(8,128)(2,1)} %copy-done.6, bf16[2,2,64,1024]{3,2,1,0:T(8,128)(2,1)} %collective-permute-done.12.refs_2_, bf16[2,2,64,1024]{3,2,1,0:T(8,128)(2,1)} %collective-permute-done.13.refs_3_, ...), custom_call_target="tpu_custom_call" | custom-call | flops 4294967296 | bytes 11534336 | tf_op jit(solution)/shard_map/pallas_call | solution.py:160
  104.9 3.3 %shard_map.106.refs_18_ = s16[528,512]{1,0:T(8,128)(2,1)} custom-call(s32[2]{0:T(128)} %pad_add_fusion.2.refs_0_, f32[512,1024]{1,0:T(8,128)} %get-tuple-element.23.refs_1_.refs_10_, s16[528,1024]{1,0:T(8,128)(2,1)} %copy-done.4, s16[528,256]{1,0:T(8,128)(2,1)} %shard_map.103.refs_3_), custom_call_target="tpu_custom_call" | custom-call | flops 5242880 | bytes 2097152 | tf_op jit(solution)/shard_map/pallas_call | solution.py:194
  108.2 9.8 %collective-permute-done.8.refs_13_ = s16[528,256]{1,0:T(8,128)(2,1)S(1)} collective-permute-done((s16[528,256]{1,0:T(8,128)(2,1)}, s16[528,256]{1,0:T(8,128)(2,1)S(1)}, u32[]{:S(2)}, u32[]{:S(2)}) %collective-permute-start.8) | collective-permute-done | bytes 270368 | tf_op jit(solution)/shard_map/ppermute | solution.py:364
  119.0 8.7 %shard_map.107 = (f32[384,512]{1,0:T(8,128)}, f32[384,512]{1,0:T(8,128)}) custom-call(s32[8]{0:T(128)} %get-tuple-element.53.refs_0_, s32[4]{0:T(128)} %pad_add_fusion.refs_1_, bf16[4,3,2,72,256]{4,3,2,1,0:T(8,128)(2,1)} %get-tuple-element.19.refs_2_, bf16[4,3,2,72,256]{4,3,2,1,0:T(8,128)(2,1)} %copy-done, bf16[4,3,2,72,256]{4,3,2,1,0:T(8,128)(2,1)} %copy-done.1, ...), custom_call_target="tpu_custom_call" | custom-call | flops 2800000000 | bytes 8000000 | tf_op jit(solution)/shard_map/pallas_call | solution.py:352
  127.8 14.6 %collective-permute-done.21.refs_3_.refs_12_ = s16[528,512]{1,0:T(8,128)(2,1)S(1)} collective-permute-done((s16[528,512]{1,0:T(8,128)(2,1)S(1)}, s16[528,512]{1,0:T(8,128)(2,1)S(1)}, u32[]{:S(2)}, u32[]{:S(2)}) %collective-permute-start.21) | collective-permute-done | bytes 540704 | tf_op jit(solution)/shard_map/ppermute | solution.py:364
  143.2 2.9 %shard_map.108.refs_3_ = s16[528,256]{1,0:T(8,128)(2,1)} custom-call(s32[3]{0:T(128)} %pad_add_fusion.3.refs_0_, f32[512,1024]{1,0:T(8,128)} %get-tuple-element.23.refs_1_.refs_10_, s16[528,1024]{1,0:T(8,128)(2,1)} %copy-done.4, s16[528,512]{1,0:T(8,128)(2,1)} %copy-done.8, f32[384,512]{1,0:T(8,128)} %get-tuple-element.26.refs_4_), custom_call_target="tpu_custom_call" | custom-call | flops 2621440 | bytes 1048576 | tf_op jit(solution)/shard_map/pallas_call | solution.py:194
  150.4 3.3 %shard_map.110.refs_18_ = s16[528,512]{1,0:T(8,128)(2,1)} custom-call(s32[2]{0:T(128)} %pad_add_fusion.2.refs_0_, f32[512,1024]{1,0:T(8,128)} %get-tuple-element.27.refs_1_.refs_10_, s16[528,1024]{1,0:T(8,128)(2,1)} %copy-done.5, s16[528,256]{1,0:T(8,128)(2,1)} %shard_map.108.refs_3_), custom_call_target="tpu_custom_call" | custom-call | flops 5242880 | bytes 2097152 | tf_op jit(solution)/shard_map/pallas_call | solution.py:194
  155.4 5.6 %collective-permute-done.22.refs_13_ = s16[528,256]{1,0:T(8,128)(2,1)S(1)} collective-permute-done((s16[528,256]{1,0:T(8,128)(2,1)}, s16[528,256]{1,0:T(8,128)(2,1)S(1)}, u32[]{:S(2)}, u32[]{:S(2)}) %collective-permute-start.22) | collective-permute-done | bytes 270368 | tf_op jit(solution)/shard_map/ppermute | solution.py:364
  161.7 8.6 %shard_map.111 = (f32[384,512]{1,0:T(8,128)}, f32[384,512]{1,0:T(8,128)}) custom-call(s32[8]{0:T(128)} %get-tuple-element.53.refs_0_, s32[4]{0:T(128)} %pad_add_fusion.refs_1_, bf16[4,3,2,72,256]{4,3,2,1,0:T(8,128)(2,1)} %get-tuple-element.19.refs_2_, bf16[4,3,2,72,256]{4,3,2,1,0:T(8,128)(2,1)} %copy-done, bf16[4,3,2,72,256]{4,3,2,1,0:T(8,128)(2,1)} %copy-done.1, ...), custom_call_target="tpu_custom_call" | custom-call | flops 2800000000 | bytes 8000000 | tf_op jit(solution)/shard_map/pallas_call | solution.py:352
  173.3 2.9 %shard_map.112.refs_18_ = s16[528,256]{1,0:T(8,128)(2,1)} custom-call(s32[3]{0:T(128)} %pad_add_fusion.3.refs_0_, f32[512,1024]{1,0:T(8,128)} %get-tuple-element.27.refs_1_.refs_10_, s16[528,1024]{1,0:T(8,128)(2,1)} %copy-done.5, s16[528,512]{1,0:T(8,128)(2,1)} %copy-done.10, f32[384,512]{1,0:T(8,128)} %get-tuple-element.30.refs_4_), custom_call_target="tpu_custom_call" | custom-call | flops 2621440 | bytes 1048576 | tf_op jit(solution)/shard_map/pallas_call | solution.py:194
  178.8 12.2 %collective-permute-done.30.refs_13_ = s16[528,256]{1,0:T(8,128)(2,1)S(1)} collective-permute-done((s16[528,256]{1,0:T(8,128)(2,1)}, s16[528,256]{1,0:T(8,128)(2,1)S(1)}, u32[]{:S(2)}, u32[]{:S(2)}) %collective-permute-start.30) | collective-permute-done | bytes 270368 | tf_op jit(solution)/shard_map/ppermute | solution.py:364
  191.6 8.7 %shard_map.113 = (f32[384,512]{1,0:T(8,128)}, f32[384,512]{1,0:T(8,128)}) custom-call(s32[8]{0:T(128)} %get-tuple-element.53.refs_0_, s32[4]{0:T(128)} %pad_add_fusion.refs_1_, bf16[4,3,2,72,256]{4,3,2,1,0:T(8,128)(2,1)} %get-tuple-element.19.refs_2_, bf16[4,3,2,72,256]{4,3,2,1,0:T(8,128)(2,1)} %copy-done, bf16[4,3,2,72,256]{4,3,2,1,0:T(8,128)(2,1)} %copy-done.1, ...), custom_call_target="tpu_custom_call" | custom-call | flops 2800000000 | bytes 8000000 | tf_op jit(solution)/shard_map/pallas_call | solution.py:352
  202.4 9.8 %collective-permute-done.25 = f32[192,512]{1,0:T(8,128)S(1)} collective-permute-done((f32[192,512]{1,0:T(8,128)S(1)}, f32[192,512]{1,0:T(8,128)S(1)}, u32[]{:S(2)}, u32[]{:S(2)}) %collective-permute-start.25) | collective-permute-done | bytes 393248 | tf_op jit(solution)/shard_map/ppermute | solution.py:364
  215.0 3.8 %collective-permute-done.26 = f32[192,256]{1,0:T(8,128)S(1)} collective-permute-done((f32[192,256]{1,0:T(8,128)S(1)}, f32[192,256]{1,0:T(8,128)S(1)}, u32[]{:S(2)}, u32[]{:S(2)}) %collective-permute-start.26) | collective-permute-done | bytes 196640 | tf_op jit(solution)/shard_map/ppermute | solution.py:364
  218.9 5.1 %collective-permute-done.32 = f32[192,512]{1,0:T(8,128)S(1)} collective-permute-done((f32[192,512]{1,0:T(8,128)S(1)}, f32[192,512]{1,0:T(8,128)S(1)}, u32[]{:S(2)}, u32[]{:S(2)}) %collective-permute-start.32) | collective-permute-done | bytes 393248 | tf_op jit(solution)/shard_map/ppermute | solution.py:364
  225.2 4.7 %collective-permute-done.33 = f32[192,256]{1,0:T(8,128)S(1)} collective-permute-done((f32[192,256]{1,0:T(8,128)S(1)}, f32[192,256]{1,0:T(8,128)S(1)}, u32[]{:S(2)}, u32[]{:S(2)}) %collective-permute-start.33) | collective-permute-done | bytes 196640 | tf_op jit(solution)/shard_map/ppermute | solution.py:364
  (201 shorter events, 76.1 us)
Async XLA Ops:
  1.5 15.9 %collective-permute-start.4 = (bf16[1,2,64,1024]{3,2,1,0:T(8,128)(2,1)S(1)}, bf16[1,2,64,1024]{3,2,1,0:T(8,128)(2,1)S(1)}, u32[]{:S(2)}, u32[]{:S(2)}) collective-permute-start(bf16[1,2,64,1024]{3,2,1,0:T(8,128)(2,1)S(1)} %slice.152.refs_1_), channel_id=1, source_target_pairs={{0,2},{1,3},{2,0},{3,1},{4,6},{5,7},{6,4},{7,5},{8,10},{9,11},{10,... | collective-permute-start | bytes 786440 | tf_op jit(solution)/shard_map/ppermute | solution.py:364
  4.5 15.7 %collective-permute-start.3 = (bf16[1,2,64,1024]{3,2,1,0:T(8,128)(2,1)S(1)}, bf16[1,2,64,1024]{3,2,1,0:T(8,128)(2,1)S(1)}, u32[]{:S(2)}, u32[]{:S(2)}) collective-permute-start(bf16[1,2,64,1024]{3,2,1,0:T(8,128)(2,1)S(1)} %slice.152.refs_1_), channel_id=1, source_target_pairs={{0,1},{1,0},{2,3},{3,2},{4,5},{5,4},{6,7},{7,6},{8,9},{9,8},{10,11... | collective-permute-start | bytes 786440 | tf_op jit(solution)/shard_map/ppermute | solution.py:364
  4.6 28.6 %collective-permute-start.13 = (bf16[2,2,64,1024]{3,2,1,0:T(8,128)(2,1)S(1)}, bf16[2,2,64,1024]{3,2,1,0:T(8,128)(2,1)}, u32[]{:S(2)}, u32[]{:S(2)}) collective-permute-start(bf16[2,2,64,1024]{3,2,1,0:T(8,128)(2,1)S(1)} %slice.153.refs_1_), channel_id=1, source_target_pairs={{0,2},{1,3},{2,0},{3,1},{4,6},{5,7},{6,4},{7,5},{8,10},{9,11},{10,... | collective-permute-start | bytes 1572872 | tf_op jit(solution)/shard_map/ppermute | solution.py:364
  4.7 40.5 %collective-permute-start.12 = (bf16[2,2,64,1024]{3,2,1,0:T(8,128)(2,1)S(1)}, bf16[2,2,64,1024]{3,2,1,0:T(8,128)(2,1)}, u32[]{:S(2)}, u32[]{:S(2)}) collective-permute-start(bf16[2,2,64,1024]{3,2,1,0:T(8,128)(2,1)S(1)} %slice.153.refs_1_), channel_id=1, source_target_pairs={{0,1},{1,0},{2,3},{3,2},{4,5},{5,4},{6,7},{7,6},{8,9},{9,8},{10,11... | collective-permute-start | bytes 1572872 | tf_op jit(solution)/shard_map/ppermute | solution.py:364
  13.2 22.0 %collective-permute-start = (bf16[4,3,2,72,256]{4,3,2,1,0:T(8,128)(2,1)}, bf16[4,3,2,72,256]{4,3,2,1,0:T(8,128)(2,1)S(1)}, u32[]{:S(2)}, u32[]{:S(2)}) collective-permute-start(bf16[4,3,2,72,256]{4,3,2,1,0:T(8,128)(2,1)} %get-tuple-element.20), channel_id=1, source_target_pairs={{0,4},{4,0},{8,12},{12,8},{16,20},{20,16},{24,28},{28,24},{1,5},{5... | collective-permute-start | bytes 2654216 | tf_op jit(solution)/shard_map/ppermute | solution.py:364
  20.2 25.0 %collective-permute-start.10 = (bf16[2,96,1024]{2,1,0:T(8,128)(2,1)}, bf16[2,96,1024]{2,1,0:T(8,128)(2,1)}, u32[]{:S(2)}, u32[]{:S(2)}) collective-permute-start(bf16[2,96,1024]{2,1,0:T(8,128)(2,1)} %bitcast.21.refs_0_), channel_id=1, source_target_pairs={{0,2},{1,3},{2,0},{3,1},{4,6},{5,7},{6,4},{7,5},{8,10},{9,11},{10,... | collective-permute-start | bytes 1179656 | tf_op jit(solution)/shard_map/ppermute | solution.py:364
  32.6 26.2 %collective-permute-start.6 = (s16[528,1024]{1,0:T(8,128)(2,1)}, s16[528,1024]{1,0:T(8,128)(2,1)S(1)}, u32[]{:S(2)}, u32[]{:S(2)}) collective-permute-start(s16[528,1024]{1,0:T(8,128)(2,1)} %get-tuple-element.22), channel_id=1, source_target_pairs={{0,4},{4,0},{8,12},{12,8},{16,20},{20,16},{24,28},{28,24},{1,5},{5... | collective-permute-start | bytes 3244040 | tf_op jit(solution)/shard_map/ppermute | solution.py:364
  36.4 29.0 %collective-permute-start.1 = (bf16[4,3,2,72,256]{4,3,2,1,0:T(8,128)(2,1)}, bf16[4,3,2,72,256]{4,3,2,1,0:T(8,128)(2,1)S(1)}, u32[]{:S(2)}, u32[]{:S(2)}) collective-permute-start(bf16[4,3,2,72,256]{4,3,2,1,0:T(8,128)(2,1)} %pad_maximum_fusion), channel_id=1, source_target_pairs={{0,8},{4,12},{8,0},{12,4},{16,24},{20,28},{24,16},{28,20},{1,9},{5... | collective-permute-start | bytes 2654216 | tf_op jit(solution)/shard_map/ppermute | solution.py:364
  45.2 25.1 %collective-permute-start.9 = (bf16[2,96,1024]{2,1,0:T(8,128)(2,1)}, bf16[2,96,1024]{2,1,0:T(8,128)(2,1)S(1)}, u32[]{:S(2)}, u32[]{:S(2)}) collective-permute-start(bf16[2,96,1024]{2,1,0:T(8,128)(2,1)} %bitcast.21.refs_0_), channel_id=1, source_target_pairs={{0,1},{1,0},{2,3},{3,2},{4,5},{5,4},{6,7},{7,6},{8,9},{9,8},{10,11... | collective-permute-start | bytes 1179656 | tf_op jit(solution)/shard_map/ppermute | solution.py:364
  45.3 25.1 %collective-permute-start.11 = (bf16[2,96,1024]{2,1,0:T(8,128)(2,1)}, bf16[2,96,1024]{2,1,0:T(8,128)(2,1)S(1)}, u32[]{:S(2)}, u32[]{:S(2)}) collective-permute-start(bf16[2,96,1024]{2,1,0:T(8,128)(2,1)} %collective-permute-done.10.refs_2_), channel_id=1, source_target_pairs={{0,1},{1,0},{2,3},{3,2},{4,5},{5,4},{6,7},{7,6},{8,9},{9,8},{10,11... | collective-permute-start | bytes 1179656 | tf_op jit(solution)/shard_map/ppermute | solution.py:364
  56.0 47.9 %collective-permute-start.15 = (s16[528,1024]{1,0:T(8,128)(2,1)}, s16[528,1024]{1,0:T(8,128)(2,1)S(1)}, u32[]{:S(2)}, u32[]{:S(2)}) collective-permute-start(s16[528,1024]{1,0:T(8,128)(2,1)} %get-tuple-element.24), channel_id=1, source_target_pairs={{0,4},{4,0},{8,12},{12,8},{16,20},{20,16},{24,28},{28,24},{1,5},{5... | collective-permute-start | bytes 3244040 | tf_op jit(solution)/shard_map/ppermute | solution.py:364
  63.3 24.5 %collective-permute-start.7 = (s16[528,512]{1,0:T(8,128)(2,1)}, s16[528,512]{1,0:T(8,128)(2,1)S(1)}, u32[]{:S(2)}, u32[]{:S(2)}) collective-permute-start(s16[528,512]{1,0:T(8,128)(2,1)} %shard_map.102.refs_4_), channel_id=1, source_target_pairs={{0,8},{4,12},{8,0},{12,4},{16,24},{20,28},{24,16},{28,20},{1,9},{5... | collective-permute-start | bytes 1622024 | tf_op jit(solution)/shard_map/ppermute | solution.py:364
  66.4 51.6 %collective-permute-start.2 = (bf16[4,3,2,72,256]{4,3,2,1,0:T(8,128)(2,1)S(1)}, bf16[4,3,2,72,256]{4,3,2,1,0:T(8,128)(2,1)S(1)}, u32[]{:S(2)}, u32[]{:S(2)}) collective-permute-start(bf16[4,3,2,72,256]{4,3,2,1,0:T(8,128)(2,1)S(1)} %pad_maximum_fusion.1), channel_id=1, source_target_pairs={{0,16},{4,20},{8,24},{12,28},{16,0},{20,4},{24,8},{28,12},{1,17},{... | collective-permute-start | bytes 2654216 | tf_op jit(solution)/shard_map/ppermute | solution.py:364
  91.5 26.4 %collective-permute-start.8 = (s16[528,256]{1,0:T(8,128)(2,1)}, s16[528,256]{1,0:T(8,128)(2,1)S(1)}, u32[]{:S(2)}, u32[]{:S(2)}) collective-permute-start(s16[528,256]{1,0:T(8,128)(2,1)} %shard_map.103.refs_3_), channel_id=1, source_target_pairs={{0,16},{4,20},{8,24},{12,28},{16,0},{20,4},{24,8},{28,12},{1,17},{... | collective-permute-start | bytes 811016 | tf_op jit(solution)/shard_map/ppermute | solution.py:364
  102.4 47.0 %collective-permute-start.23 = (s16[528,1024]{1,0:T(8,128)(2,1)}, s16[528,1024]{1,0:T(8,128)(2,1)S(1)}, u32[]{:S(2)}, u32[]{:S(2)}) collective-permute-start(s16[528,1024]{1,0:T(8,128)(2,1)} %get-tuple-element.28), channel_id=1, source_target_pairs={{0,4},{4,0},{8,12},{12,8},{16,20},{20,16},{24,28},{28,24},{1,5},{5... | collective-permute-start | bytes 3244040 | tf_op jit(solution)/shard_map/ppermute | solution.py:364
  127.7 19.7 %collective-permute-start.16 = (f32[384,512]{1,0:T(8,128)}, f32[384,512]{1,0:T(8,128)S(1)}, u32[]{:S(2)}, u32[]{:S(2)}) collective-permute-start(f32[384,512]{1,0:T(8,128)} %get-tuple-element.26.refs_4_), channel_id=1, source_target_pairs={{0,1},{1,0},{2,3},{3,2},{4,5},{5,4},{6,7},{7,6},{8,9},{9,8},{10,11... | collective-permute-start | bytes 2359304 | tf_op jit(solution)/shard_map/ppermute | solution.py:364
  127.7 14.7 %collective-permute-start.21 = (s16[528,512]{1,0:T(8,128)(2,1)S(1)}, s16[528,512]{1,0:T(8,128)(2,1)S(1)}, u32[]{:S(2)}, u32[]{:S(2)}) collective-permute-start(s16[528,512]{1,0:T(8,128)(2,1)S(1)} %copy-done.9), channel_id=1, source_target_pairs={{0,8},{4,12},{8,0},{12,4},{16,24},{20,28},{24,16},{28,20},{1,9},{5... | collective-permute-start | bytes 1622024 | tf_op jit(solution)/shard_map/ppermute | solution.py:364
  146.1 14.9 %collective-permute-start.22 = (s16[528,256]{1,0:T(8,128)(2,1)}, s16[528,256]{1,0:T(8,128)(2,1)S(1)}, u32[]{:S(2)}, u32[]{:S(2)}) collective-permute-start(s16[528,256]{1,0:T(8,128)(2,1)} %shard_map.108.refs_3_), channel_id=1, source_target_pairs={{0,16},{4,20},{8,24},{12,28},{16,0},{20,4},{24,8},{28,12},{1,17},{... | collective-permute-start | bytes 811016 | tf_op jit(solution)/shard_map/ppermute | solution.py:364
  147.5 22.8 %collective-permute-start.17 = (f32[192,512]{1,0:T(8,128)S(1)}, f32[192,512]{1,0:T(8,128)S(1)}, u32[]{:S(2)}, u32[]{:S(2)}) collective-permute-start(f32[192,512]{1,0:T(8,128)S(1)} %slice.155), channel_id=1, source_target_pairs={{0,2},{1,3},{2,0},{3,1},{4,6},{5,7},{6,4},{7,5},{8,10},{9,11},{10,... | collective-permute-start | bytes 1179656 | tf_op jit(solution)/shard_map/ppermute | solution.py:364
  153.7 18.8 %collective-permute-start.29 = (s16[528,512]{1,0:T(8,128)(2,1)}, s16[528,512]{1,0:T(8,128)(2,1)S(1)}, u32[]{:S(2)}, u32[]{:S(2)}) collective-permute-start(s16[528,512]{1,0:T(8,128)(2,1)} %shard_map.110.refs_18_), channel_id=1, source_target_pairs={{0,8},{4,12},{8,0},{12,4},{16,24},{20,28},{24,16},{28,20},{1,9},{5... | collective-permute-start | bytes 1622024 | tf_op jit(solution)/shard_map/ppermute | solution.py:364
  170.3 30.1 %collective-permute-start.24 = (f32[384,512]{1,0:T(8,128)}, f32[384,512]{1,0:T(8,128)S(1)}, u32[]{:S(2)}, u32[]{:S(2)}) collective-permute-start(f32[384,512]{1,0:T(8,128)} %get-tuple-element.30.refs_4_), channel_id=1, source_target_pairs={{0,1},{1,0},{2,3},{3,2},{4,5},{5,4},{6,7},{7,6},{8,9},{9,8},{10,11... | collective-permute-start | bytes 2359304 | tf_op jit(solution)/shard_map/ppermute | solution.py:364
  176.2 14.8 %collective-permute-start.30 = (s16[528,256]{1,0:T(8,128)(2,1)}, s16[528,256]{1,0:T(8,128)(2,1)S(1)}, u32[]{:S(2)}, u32[]{:S(2)}) collective-permute-start(s16[528,256]{1,0:T(8,128)(2,1)} %shard_map.112.refs_18_), channel_id=1, source_target_pairs={{0,16},{4,20},{8,24},{12,28},{16,0},{20,4},{24,8},{28,12},{1,17},{... | collective-permute-start | bytes 811016 | tf_op jit(solution)/shard_map/ppermute | solution.py:364
  177.8 24.3 %collective-permute-start.19 = (f32[192,128]{1,0:T(8,128)S(1)}, f32[192,128]{1,0:T(8,128)S(1)}, u32[]{:S(2)}, u32[]{:S(2)}) collective-permute-start(f32[192,128]{1,0:T(8,128)S(1)} %slice.159), channel_id=1, source_target_pairs={{0,8},{4,12},{8,0},{12,4},{16,24},{20,28},{24,16},{28,20},{1,9},{5... | collective-permute-start | bytes 294920 | tf_op jit(solution)/shard_map/ppermute | solution.py:364
  200.4 13.0 %collective-permute-start.31 = (f32[384,512]{1,0:T(8,128)}, f32[384,512]{1,0:T(8,128)S(1)}, u32[]{:S(2)}, u32[]{:S(2)}) collective-permute-start(f32[384,512]{1,0:T(8,128)} %get-tuple-element.32), channel_id=1, source_target_pairs={{0,1},{1,0},{2,3},{3,2},{4,5},{5,4},{6,7},{7,6},{8,9},{9,8},{10,11... | collective-permute-start | bytes 2359304 | tf_op jit(solution)/shard_map/ppermute | solution.py:364
  (44 other events, 248.1 us)

commit v4 on v3

--- a/solution.py
+++ b/solution.py
@@ -17,6 +17,9 @@
 MAGIC = 1.5 * 2.0**23
 NT_DIMS = (((1,), (1,)), ((), ()))
 VMEM = 56 * 1024 * 1024
+
+
+TOKEN = jax.ShapeDtypeStruct((8, 128), jnp.float32)
 
 
 def params():
@@ -104,17 +107,18 @@
     )(dests, con, shift_map.reshape(points, 1, slab))
 
 
-def x_kernel(slots, base_ref, *refs):
-    val_refs, (weight_ref, go_ref, keep_ref, left_ref) = refs[:slots], refs[slots:]
-    rows, depth = val_refs[0].shape[2], val_refs[0].shape[3]
+def x_kernel(waits, base_ref, val_ref, weight_ref, *refs):
+    go_ref, keep_ref, token_ref, left_ref = refs[waits:]
+    slots, _, _, rows, depth = val_ref.shape
     half = slots * rows
+    token_ref[...] = jnp.zeros_like(token_ref)
     step = pl.program_id(0)
     halfway = pl.num_programs(0) // 2
 
     @pl.when(step == 0)
     def _():
         for slot in range(slots):
-            real, imag = val_refs[slot][0, 0], val_refs[slot][0, 1]
+            real, imag = val_ref[slot, 0, 0], val_ref[slot, 0, 1]
             top = slice(slot * rows, (slot + 1) * rows)
             low = slice(half + slot * rows, half + (slot + 1) * rows)
             left_ref[top, 0:depth] = real
@@ -133,9 +137,8 @@
         keep_ref[...] = mm(left_ref[...], weight)
 
 
-def x_call(vals, screened, place, point, side, steps):
-    slots = len(vals)
-    _, _, rows, depth = vals[0].shape
+def x_call(val, screened, place, point, side, steps, after):
+    slots, _, _, rows, depth = val.shape
     height = 2 * slots * rows
     columns = screened.shape[3] // 2
     half = steps // 2
@@ -144,38 +147,41 @@
         num_scalar_prefetch=1,
         grid=(steps,),
         in_specs=[
-            pl.BlockSpec((1, 2, rows, depth), lambda j, t: (place, 0, 0, 0)) for _ in vals
-        ]
-        + [
+            pl.BlockSpec((slots, 1, 2, rows, depth), lambda j, t: (0, place, 0, 0, 0)),
             pl.BlockSpec(
                 (1, 2, depth, width), lambda j, t: (point, 0, 0, t[j // half] * half + j % half)
-            )
-        ],
+            ),
+        ]
+        + [pl.BlockSpec(memory_space=pl.ANY) for _ in after],
         out_specs=[
             pl.BlockSpec((height + EXP_ROWS, width), lambda j, t: (0, jnp.minimum(j, half - 1))),
             pl.BlockSpec((height, width), lambda j, t: (0, jnp.maximum(j - half, 0))),
+            pl.BlockSpec(TOKEN.shape, lambda j, t: (0, 0)),
         ],
         scratch_shapes=[pltpu.VMEM((height, 2 * depth), jnp.bfloat16)],
     )
     return pl.pallas_call(
-        lambda *refs: x_kernel(slots, *refs),
+        lambda *refs: x_kernel(len(after), *refs),
         grid_spec=grid_spec,
         out_shape=[
             jax.ShapeDtypeStruct((height + EXP_ROWS, columns), jnp.int16),
             jax.ShapeDtypeStruct((height, columns), jnp.float32),
+            TOKEN,
         ],
         compiler_params=params(),
         cost_estimate=cost(
             2 * height * 2 * depth * 2 * columns, 8 * depth * columns + 6 * height * columns
         ),
-    )(side, *vals, screened)
+    )(side, val, screened, *after)
 
 
 def hop_kernel(heard, at_ref, keep_ref, *refs):
     total = keep_ref[...]
     for ref in refs[:heard]:
         total = total + decode(ref)
-    encode(total, refs[-1])
+    out_ref, token_ref = refs[-2:]
+    encode(total, out_ref)
+    token_ref[...] = jnp.zeros_like(token_ref)
 
 
 def hop_call(keep, others, at, width, after):
@@ -189,20 +195,24 @@
             for n in range(len(others))
         ]
         + [pl.BlockSpec(memory_space=pl.ANY) for _ in after],
-        out_specs=pl.BlockSpec((tall, width), lambda i, at: (0, 0)),
+        out_specs=[
+            pl.BlockSpec((tall, width), lambda i, at: (0, 0)),
+            pl.BlockSpec(TOKEN.shape, lambda i, at: (0, 0)),
+        ],
     )
     return pl.pallas_call(
         lambda *refs: hop_kernel(len(others), *refs),
         grid_spec=grid_spec,
-        out_shape=jax.ShapeDtypeStruct((tall, width), jnp.int16),
+        out_shape=[jax.ShapeDtypeStruct((tall, width), jnp.int16), TOKEN],
         compiler_params=params(),
         cost_estimate=cost(20 * height * width, 8 * height * width),
     )(at, keep, *others, *after)
 
 
-def exchange_kernel(slots, *refs):
-    here_refs, (there_ref, coulomb_ref, out_ref, left_ref) = refs[:slots], refs[slots:]
-    rows, depth = here_refs[0].shape[1], here_refs[0].shape[2]
+def exchange_kernel(waits, here_ref, there_ref, coulomb_ref, *refs):
+    out_ref, token_ref, left_ref = refs[waits:]
+    slots, _, rows, depth = here_ref.shape
+    token_ref[...] = jnp.zeros_like(token_ref)
 
     @pl.when(pl.program_id(0) == 0)
     def _():
@@ -210,7 +220,7 @@
             for part in range(2):
                 left_ref[
                     slot * rows : (slot + 1) * rows, part * depth : (part + 1) * depth
-                ] = here_refs[slot][part]
+                ] = here_ref[slot, part]
 
     factor = coulomb_ref[0]
     real = there_ref[0, 0].astype(jnp.float32) * factor
@@ -226,32 +236,36 @@
         out_ref[0, part] = both[:, part * cols : (part + 1) * cols]
 
 
-def exchange_call(heres, there, coulomb):
-    slots = len(heres)
+def exchange_call(here, there, coulomb, after):
+    slots, _, rows, _ = here.shape
     points, _, cols, depth = there.shape
-    rows = heres[0].shape[1]
     height = slots * rows
     return pl.pallas_call(
-        lambda *refs: exchange_kernel(slots, *refs),
+        lambda *refs: exchange_kernel(len(after), *refs),
         grid=(points,),
-        in_specs=[pl.BlockSpec(h.shape, lambda q: (0, 0, 0)) for h in heres]
-        + [
+        in_specs=[
+            pl.BlockSpec(here.shape, lambda q: (0, 0, 0, 0)),
             pl.BlockSpec((1, 2, cols, depth), lambda q: (q, 0, 0, 0)),
             pl.BlockSpec((1, 1, depth), lambda q: (q, 0, 0)),
+        ]
+        + [pl.BlockSpec(memory_space=pl.ANY) for _ in after],
+        out_specs=[
+            pl.BlockSpec((1, 2, height, cols), lambda q: (q, 0, 0, 0)),
+            pl.BlockSpec(TOKEN.shape, lambda q: (0, 0)),
         ],
-        out_specs=pl.BlockSpec((1, 2, height, cols), lambda q: (q, 0, 0, 0)),
-        out_shape=jax.ShapeDtypeStruct((points, 2, height, cols), jnp.float32),
+        out_shape=[jax.ShapeDtypeStruct((points, 2, height, cols), jnp.float32), TOKEN],
         scratch_shapes=[pltpu.VMEM((height, 2 * depth), jnp.bfloat16)],
         compiler_params=params(),
         cost_estimate=cost(2 * points * height * 2 * cols * 2 * depth * 2, 8 * points * cols * depth),
-    )(*heres, there, coulomb.reshape(points, 1, depth))
+    )(here, there, coulomb.reshape(points, 1, depth), *after)
 
 
 def tile_kernel(slots, heard, chunks, waits, index_ref, at_ref, *refs):
     con_refs, keep_ref = refs[:slots], refs[slots]
     heard_refs = refs[slots + 1 : slots + 1 + heard]
     exch_ref, row_ref, col_direct_ref, col_exch_ref = refs[slots + 1 + heard : slots + 5 + heard]
-    keep_out, go_out, con_all, direct_ref, natural_ref = refs[slots + 5 + heard + waits :]
+    keep_out, go_out, token_ref, con_all, direct_ref, natural_ref = refs[slots + 5 + heard + waits :]
+    token_ref[...] = jnp.zeros_like(token_ref)
     total = keep_ref[...]
     for ref in heard_refs:
         total = total + decode(ref)
@@ -342,7 +356,8 @@
             whole(col_exch),
         ]
         + [pl.BlockSpec(memory_space=pl.ANY) for _ in after],
-        out_specs=[pl.BlockSpec((NT, out_cols), lambda i, index, at: (0, 0))] * 2,
+        out_specs=[pl.BlockSpec((NT, out_cols), lambda i, index, at: (0, 0))] * 2
+        + [pl.BlockSpec(TOKEN.shape, lambda i, index, at: (0, 0))],
         scratch_shapes=[
             pltpu.VMEM((slots * pitch, 2 * width), jnp.bfloat16),
             pltpu.VMEM((height // 128, NC * NC, 128), jnp.float32),
@@ -352,7 +367,7 @@
     return pl.pallas_call(
         lambda *refs: tile_kernel(slots, len(heard), chunks, len(after), *refs),
         grid_spec=grid_spec,
-        out_shape=[jax.ShapeDtypeStruct((NT, out_cols), jnp.float32)] * 2,
+        out_shape=[jax.ShapeDtypeStruct((NT, out_cols), jnp.float32)] * 2 + [TOKEN],
         compiler_params=params(),
         cost_estimate=cost(2.8e9, 8e6),
     )(
@@ -362,16 +377,6 @@
 
 def swap(value, axis, size, bit):
     return lax.ppermute(value, axis, [(i, i ^ bit) for i in range(size)])
-
-
-def gather_slots(value, axis, size):
-    found = {0: value}
-    bit = size // 2
-    while bit:
-        for known in sorted(found):
-            found[known ^ bit] = swap(found[known], axis, size, bit)
-        bit //= 2
-    return [found[r] for r in range(size)]
 
 
 def halving_order(bits):
@@ -404,7 +409,9 @@
         return number if chosen is None else 2 * number + 1 - flags[chosen]
 
     val = jnp.transpose(val_density, (1, 2, 0, 3))
-    first, others = gather_slots(val[:1], "pair", pair), gather_slots(val[1:], "pair", pair)
+    first, others = lax.all_gather(val[:1], "pair"), lax.all_gather(val[1:], "pair")
+    here = lax.all_gather(jnp.transpose(trans_here, (1, 0, 2)), "pair")
+    there = jnp.transpose(trans_there, (1, 2, 0, 3))
 
     con = jnp.transpose(con_density, (1, 2, 0, 3))
     stay, go = shift_call(con, shift_map, blocks, width)
@@ -423,21 +430,18 @@
     cons = [cons[slot] for slot in ga_order]
 
     side = as_index([1 - flags[0], flags[0]])
-    gone, keep = [], []
+    gone, keep, after = [], [], []
     for q in range(points):
         vals, place = (first, 0) if q == 0 else (others, q - 1)
-        coded, own = x_call(vals, screened, place, q, side, 4)
+        coded, own, token = x_call(vals, screened, place, q, side, 4, after)
+        after = [token]
         gone.append(coded)
         keep.append(own)
-
-    heres = gather_slots(jnp.transpose(trans_here, (1, 0, 2)), "pair", pair)
-    exch = exchange_call(heres, jnp.transpose(trans_there, (1, 2, 0, 3)), coulomb)
 
     row_count, col_count = NT // pair, NT // ga
     row_slots = jnp.asarray(halving_order(pair_bits), jnp.int32)
     row_trans = ordering.reshape(pair, row_count)[me_pair ^ row_slots].reshape(-1)
-    at_row = ((row_trans // row_count) ^ me_pair) * row_count + row_trans % row_count
-    pick_rows = (at_row[:, None] == jnp.arange(NT, dtype=jnp.int32)[None, :]).astype(jnp.bfloat16)
+    pick_rows = (row_trans[:, None] == jnp.arange(NT, dtype=jnp.int32)[None, :]).astype(jnp.bfloat16)
     col_trans = ordering.reshape(ga, col_count)[dests]
     col_trans = jnp.pad(col_trans, ((0, 0), (0, 64 - col_count)), constant_values=-1).reshape(1, -1)
     real_col = col_trans >= 0
@@ -452,34 +456,41 @@
     col_direct, col_exch = pick_cols(at_direct, NT, -1.0), pick_cols(at_exch, row_count, 2.0)
 
     heard = [[swap(gone[q], "ga", ga, ga_bits[0])] for q in range(points)]
-    outs = [None] * points
+    tiles = [None] * points
     stages = len(ga_bits)
-    after = []
+    exch = None
     for wave in range(2 * points + stages):
         for q in reversed(range(points)):
             stage = wave - 2 * q
             if 1 <= stage < stages:
                 columns = ga >> (stage + 1)
                 at = as_index([block_at(k, stage) for k in [1] + list(range(1, stage + 1))])
-                coded = hop_call(keep[q], heard[q], at, columns * width, after)
-                after = [coded]
+                coded, token = hop_call(keep[q], heard[q], at, columns * width, after)
+                after = [token]
                 heard[q].append(swap(coded, "ga", ga, ga_bits[stage]))
+                if exch is None:
+                    exch, token = exchange_call(here, there, coulomb, after)
+                    after = [token]
             elif stage == stages:
                 at = as_index([block_at(k, None) for k in [1] + list(range(1, stages + 1))])
-                tile, sent = tile_call(
+                tile, sent, token = tile_call(
                     cons, q, keep[q], heard[q], exch, dests, at, pick_rows, col_direct, col_exch,
                     pair, after,
                 )
-                after = [sent]
-                tile = tile + swap(sent, "pair", pair, pair_bits[0])
-                for bit in pair_bits[1:]:
-                    rows = tile.shape[0] // 2
-                    tile = tile[:rows] + swap(tile[rows:], "pair", pair, bit)
-                for bit in ga_bits:
-                    cols = tile.shape[1] // 2
-                    tile = tile[:, :cols] + swap(tile[:, cols:], "ga", ga, bit)
-                outs[q] = tile[:, :col_count].reshape(2, row_count, col_count)
-    return jnp.stack(outs)
+                after = [token]
+                tiles[q] = tile + swap(sent, "pair", pair, pair_bits[0])
+    halved = []
+    for group in (tiles[:-1], tiles[-1:]):
+        tile = jnp.stack(group)
+        for bit in pair_bits[1:]:
+            rows = tile.shape[1] // 2
+            tile = tile[:, :rows] + swap(tile[:, rows:], "pair", pair, bit)
+        halved.append(tile)
+    tile = jnp.concatenate(halved)
+    for bit in ga_bits:
+        cols = tile.shape[2] // 2
+        tile = tile[:, :, :cols] + swap(tile[:, :, cols:], "ga", ga, bit)
+    return tile[:, :, :col_count].reshape(points, 2, row_count, col_count)
 
 
 def contract_float(left, right):

time: 243 us -> 277 us (1.14)
  waiting for transfers between devices: 87.9 us -> 127 us
  between operations: 0.49 us -> 13.4 us
  starting transfers between devices: 35.4 us -> 22.9 us
  local copies, waits for them, and re-layouts: 23.9 us -> 18.3 us
    ppermute x36 -> x20, waiting for transfers between devices: 87.9 us -> 127 us  [swap(): return lax.ppermute(value, axis, [(i, i ^ bit) for i in range(size)])]
    ppermute x36 -> x20, starting transfers between devices: 35.4 us -> 22.9 us  [swap(): return lax.ppermute(value, axis, [(i, i ^ bit) for i in range(size)])]
    unnamed x66 -> x46, local copies, waits for them, and re-layouts: 17.3 us -> 12.6 us
  transfers between devices with their start and end apart: 36 -> 23, of which waited for: 16 -> 14; matrix products, arithmetic and copies ran while one was open for 8% -> 6% of each run, Pallas kernels for 36% -> 31%
where the time goes in v4:
time: 277 us; the launch traced here: 276 us
  waiting for transfers between devices  127 us (46%)
  Pallas kernels  86.1 us (31%)
  starting transfers between devices  22.9 us (8%)
  local copies, waits for them, and re-layouts  18.3 us (7%)
  between operations  13.4 us (5%)
  other arithmetic  8.44 us (3%)
    ppermute x20, waiting for transfers between devices, swap(): return lax.ppermute(value, axis, [(i, i ^ bit) for i in range(size)])  127 us
    pallas_call x3, Pallas kernels, x_call(): pl.pallas_call(lambda *refs: x_kernel(len(after), *refs), grid_spec=grid_...  30.9 us
    pallas_call x3, Pallas kernels, tile_call(): pl.pallas_call(lambda *refs: tile_kernel(slots, len(heard), chunks, len(a...  26 us
    ppermute x20, starting transfers between devices, swap(): return lax.ppermute(value, axis, [(i, i ^ bit) for i in range(size)])  22.9 us
    pallas_call x6, Pallas kernels, hop_call(): pl.pallas_call(lambda *refs: hop_kernel(len(others), *refs), grid_spec=gr...  18.7 us
    unnamed x46, local copies, waits for them, and re-layouts  12.6 us
    pallas_call x1, Pallas kernels, exchange_call(): pl.pallas_call(lambda *refs: exchange_kernel(len(after), *refs), grid=(po...  5.77 us
  transfers between devices with their start and end apart: 23, of which 14 were waited for; matrix products, arithmetic and copies ran while one was open for 6% of the time, Pallas kernels for 31%

profile of v4, /device:TPU:0, one launch (start us, length us, event | category | flops | bytes accessed | tf_op | source)
XLA Modules:
  0.0 276.1 jit_solution(15937065467797585994)
XLA Ops:
  12.8 4.6 %shard_map.100 = (bf16[4,3,2,72,256]{4,3,2,1,0:T(8,128)(2,1)}, bf16[4,3,2,72,256]{4,3,2,1,0:T(8,128)(2,1)}) custom-call(s32[8]{0:T(128)} %get-tuple-element.84.dest_ref, bf16[3,2,72,2048]{3,2,1,0:T(8,128)(2,1)} %bitcast.31, s32[3,1,2048]{2,1,0:T(1,128)} %reshape.133.map_ref), custom_call_target="tpu_custom_call" | custom-call | flops 7077888 | bytes 3538944 | tf_op jit(solution)/shard_map/pallas_call | solution.py:101
  17.4 3.0 %collective-permute-start = (bf16[4,3,2,72,256]{4,3,2,1,0:T(8,128)(2,1)}, bf16[4,3,2,72,256]{4,3,2,1,0:T(8,128)(2,1)S(1)}, u32[]{:S(2)}, u32[]{:S(2)}) collective-permute-start(bf16[4,3,2,72,256]{4,3,2,1,0:T(8,128)(2,1)} %get-tuple-element.39), channel_id=1, source_target_pairs={{0,4},{4,0},{8,12},{12,8},{16,20},{20,16},{24,28},{28,24},{1,5},{5... | collective-permute-start | bytes 2654216 | tf_op jit(solution)/shard_map/ppermute | solution.py:379
  22.5 17.7 %collective-permute-done.refs_6_ = bf16[4,3,2,72,256]{4,3,2,1,0:T(8,128)(2,1)S(1)} collective-permute-done((bf16[4,3,2,72,256]{4,3,2,1,0:T(8,128)(2,1)}, bf16[4,3,2,72,256]{4,3,2,1,0:T(8,128)(2,1)S(1)}, u32[]{:S(2)}, u32[]{:S(2)}) %collective-permute-start) | collective-permute-done | bytes 884768 | tf_op jit(solution)/shard_map/ppermute | solution.py:379
  45.2 10.3 %shard_map.101 = (s16[528,1024]{1,0:T(8,128)(2,1)}, f32[512,1024]{1,0:T(8,128)}, f32[8,128]{1,0:T(8,128)}) custom-call(s32[2]{0:T(128)} %pad_add_fusion.1.refs_0_, bf16[4,1,2,64,1024]{4,3,2,1,0:T(8,128)(2,1)} %bitcast.37, bf16[3,2,1024,2048]{3,2,1,0:T(8,128)(2,1)} %refs_2_.5), custom_call_target="tpu_custom_call" | custom-call | flops 4294967296 | bytes 11534336 | tf_op jit(solution)/shard_map/pallas_call | solution.py:163
  57.0 5.5 %collective-permute-done.1.refs_4_.refs_8_ = bf16[4,3,2,72,256]{4,3,2,1,0:T(8,128)(2,1)S(1)} collective-permute-done((bf16[4,3,2,72,256]{4,3,2,1,0:T(8,128)(2,1)}, bf16[4,3,2,72,256]{4,3,2,1,0:T(8,128)(2,1)S(1)}, u32[]{:S(2)}, u32[]{:S(2)}) %collective-permute-start.1) | collective-permute-done | bytes 884768 | tf_op jit(solution)/shard_map/ppermute | solution.py:379
  62.6 10.4 %shard_map.102 = (s16[528,1024]{1,0:T(8,128)(2,1)}, f32[512,1024]{1,0:T(8,128)}, f32[8,128]{1,0:T(8,128)}) custom-call(s32[2]{0:T(128)} %pad_add_fusion.1.refs_0_, bf16[4,2,2,64,1024]{4,3,2,1,0:T(8,128)(2,1)} %bitcast.29, bf16[3,2,1024,2048]{3,2,1,0:T(8,128)(2,1)} %refs_2_.5, f32[8,128]{1,0:T(8,128)} %get-tuple-element.42.refs_3_), custom_call_target="tpu_custom_call" | custom-call | flops 4294967296 | bytes 11534336 | tf_op jit(solution)/shard_map/pallas_call | solution.py:163
  78.1 10.2 %shard_map.103 = (s16[528,1024]{1,0:T(8,128)(2,1)}, f32[512,1024]{1,0:T(8,128)}, f32[8,128]{1,0:T(8,128)}) custom-call(s32[2]{0:T(128)} %pad_add_fusion.1.refs_0_, bf16[4,2,2,64,1024]{4,3,2,1,0:T(8,128)(2,1)} %bitcast.30, bf16[3,2,1024,2048]{3,2,1,0:T(8,128)(2,1)} %refs_2_.5, f32[8,128]{1,0:T(8,128)} %get-tuple-element.43.refs_3_), custom_call_target="tpu_custom_call" | custom-call | flops 4294967296 | bytes 11534336 | tf_op jit(solution)/shard_map/pallas_call | solution.py:163
  88.3 3.3 %shard_map.104 = (s16[528,512]{1,0:T(8,128)(2,1)}, f32[8,128]{1,0:T(8,128)}) custom-call(s32[2]{0:T(128)} %pad_add_fusion.2.refs_0_, f32[512,1024]{1,0:T(8,128)} %get-tuple-element.40.refs_1_.refs_10_, s16[528,1024]{1,0:T(8,128)(2,1)} %collective-permute-done.3.refs_2_.refs_11_, f32[8,128]{1,0:T(8,128)} %get-tuple-element.44.refs_3_), custom_call_target="tpu_custom_call" | custom-call | flops 5242880 | bytes 2097152 | tf_op jit(solution)/shard_map/pallas_call | solution.py:203
  99.1 5.8 %shard_map.105 = (f32[3,2,384,96]{3,2,1,0:T(8,128)}, f32[8,128]{1,0:T(8,128)}) custom-call(bf16[4,2,96,1024]{3,2,1,0:T(8,128)(2,1)} %bitcast.38, bf16[3,2,96,1024]{3,2,1,0:T(8,128)(2,1)} %bitcast.36, f32[3,1,1024]{2,1,0:T(1,128)} %reshape.134.refs_2_, f32[8,128]{1,0:T(8,128)} %get-tuple-element.46.refs_3_), custom_call_target="tpu_custom_call" | custom-call | flops 1811939328 | bytes 2359296 | tf_op jit(solution)/shard_map/pallas_call | solution.py:243
  104.9 16.9 %collective-permute-done.4.refs_3_.refs_12_ = s16[528,512]{1,0:T(8,128)(2,1)} collective-permute-done((s16[528,512]{1,0:T(8,128)(2,1)}, s16[528,512]{1,0:T(8,128)(2,1)}, u32[]{:S(2)}, u32[]{:S(2)}) %collective-permute-start.4) | collective-permute-done | bytes 540704 | tf_op jit(solution)/shard_map/ppermute | solution.py:379
  126.2 3.3 %shard_map.107 = (s16[528,512]{1,0:T(8,128)(2,1)}, f32[8,128]{1,0:T(8,128)}) custom-call(s32[2]{0:T(128)} %pad_add_fusion.2.refs_0_, f32[512,1024]{1,0:T(8,128)} %get-tuple-element.50.refs_1_.refs_10_, s16[528,1024]{1,0:T(8,128)(2,1)} %copy-done.4, f32[8,128]{1,0:T(8,128)} %get-tuple-element.52.refs_3_), custom_call_target="tpu_custom_call" | custom-call | flops 5242880 | bytes 2097152 | tf_op jit(solution)/shard_map/pallas_call | solution.py:203
  133.5 3.3 %collective-permute-done.5.refs_13_ = s16[528,256]{1,0:T(8,128)(2,1)S(1)} collective-permute-done((s16[528,256]{1,0:T(8,128)(2,1)}, s16[528,256]{1,0:T(8,128)(2,1)S(1)}, u32[]{:S(2)}, u32[]{:S(2)}) %collective-permute-start.5) | collective-permute-done | bytes 270368 | tf_op jit(solution)/shard_map/ppermute | solution.py:379
  137.5 8.5 %shard_map.108 = (f32[384,512]{1,0:T(8,128)}, f32[384,512]{1,0:T(8,128)}, f32[8,128]{1,0:T(8,128)}) custom-call(s32[8]{0:T(128)} %get-tuple-element.85.refs_0_, s32[4]{0:T(128)} %pad_add_fusion.refs_1_, bf16[4,3,2,72,256]{4,3,2,1,0:T(8,128)(2,1)} %get-tuple-element.38.refs_2_, bf16[4,3,2,72,256]{4,3,2,1,0:T(8,128)(2,1)} %copy-done, ...), custom_call_target="tpu_custom_call" | custom-call | flops 2800000000 | bytes 8000000 | tf_op jit(solution)/shard_map/pallas_call | solution.py:367
  150.9 3.3 %shard_map.110 = (s16[528,512]{1,0:T(8,128)(2,1)}, f32[8,128]{1,0:T(8,128)}) custom-call(s32[2]{0:T(128)} %pad_add_fusion.2.refs_0_, f32[512,1024]{1,0:T(8,128)} %get-tuple-element.59.refs_1_.refs_10_, s16[528,1024]{1,0:T(8,128)(2,1)} %copy-done.5, f32[8,128]{1,0:T(8,128)} %get-tuple-element.61.refs_3_), custom_call_target="tpu_custom_call" | custom-call | flops 5242880 | bytes 2097152 | tf_op jit(solution)/shard_map/pallas_call | solution.py:203
  156.5 8.3 %collective-permute-done.9.refs_13_ = s16[528,256]{1,0:T(8,128)(2,1)S(1)} collective-permute-done((s16[528,256]{1,0:T(8,128)(2,1)}, s16[528,256]{1,0:T(8,128)(2,1)S(1)}, u32[]{:S(2)}, u32[]{:S(2)}) %collective-permute-start.9) | collective-permute-done | bytes 270368 | tf_op jit(solution)/shard_map/ppermute | solution.py:379
  165.5 8.5 %shard_map.111 = (f32[384,512]{1,0:T(8,128)}, f32[384,512]{1,0:T(8,128)}, f32[8,128]{1,0:T(8,128)}) custom-call(s32[8]{0:T(128)} %get-tuple-element.85.refs_0_, s32[4]{0:T(128)} %pad_add_fusion.refs_1_, bf16[4,3,2,72,256]{4,3,2,1,0:T(8,128)(2,1)} %get-tuple-element.38.refs_2_, bf16[4,3,2,72,256]{4,3,2,1,0:T(8,128)(2,1)} %copy-done, ...), custom_call_target="tpu_custom_call" | custom-call | flops 2800000000 | bytes 8000000 | tf_op jit(solution)/shard_map/pallas_call | solution.py:367
  175.8 3.0 %shard_map.112 = (s16[528,256]{1,0:T(8,128)(2,1)}, f32[8,128]{1,0:T(8,128)}) custom-call(s32[3]{0:T(128)} %pad_add_fusion.3.refs_0_, f32[512,1024]{1,0:T(8,128)} %get-tuple-element.59.refs_1_.refs_10_, s16[528,1024]{1,0:T(8,128)(2,1)} %copy-done.5, s16[528,512]{1,0:T(8,128)(2,1)} %copy-done.7, f32[8,128]{1,0:T(8,128)} %get-tuple-element.66.refs_4_), custom_call_target="tpu_custom_call" | custom-call | flops 2621440 | bytes 1048576 | tf_op jit(solution)/shard_map/pallas_call | solution.py:203
  179.2 13.9 %collective-permute-done.14.refs_13_ = s16[528,256]{1,0:T(8,128)(2,1)S(1)} collective-permute-done((s16[528,256]{1,0:T(8,128)(2,1)}, s16[528,256]{1,0:T(8,128)(2,1)S(1)}, u32[]{:S(2)}, u32[]{:S(2)}) %collective-permute-start.14) | collective-permute-done | bytes 270368 | tf_op jit(solution)/shard_map/ppermute | solution.py:379
  193.7 9.0 %shard_map.113 = (f32[384,512]{1,0:T(8,128)}, f32[384,512]{1,0:T(8,128)}, f32[8,128]{1,0:T(8,128)}) custom-call(s32[8]{0:T(128)} %get-tuple-element.85.refs_0_, s32[4]{0:T(128)} %pad_add_fusion.refs_1_, bf16[4,3,2,72,256]{4,3,2,1,0:T(8,128)(2,1)} %get-tuple-element.38.refs_2_, bf16[4,3,2,72,256]{4,3,2,1,0:T(8,128)(2,1)} %copy-done, ...), custom_call_target="tpu_custom_call" | custom-call | flops 2800000000 | bytes 8000000 | tf_op jit(solution)/shard_map/pallas_call | solution.py:367
  207.1 16.2 %collective-permute-done.12 = f32[2,192,512]{2,1,0:T(8,128)S(1)} collective-permute-done((f32[2,192,512]{2,1,0:T(8,128)S(1)}, f32[2,192,512]{2,1,0:T(8,128)S(1)}, u32[]{:S(2)}, u32[]{:S(2)}) %collective-permute-start.12) | collective-permute-done | bytes 786464 | tf_op jit(solution)/shard_map/ppermute | solution.py:379
  223.5 7.9 %collective-permute-done.16 = f32[1,192,512]{2,1,0:T(8,128)S(1)} collective-permute-done((f32[1,192,512]{2,1,0:T(8,128)S(1)}, f32[1,192,512]{2,1,0:T(8,128)S(1)}, u32[]{:S(2)}, u32[]{:S(2)}) %collective-permute-start.16) | collective-permute-done | bytes 393248 | tf_op jit(solution)/shard_map/ppermute | solution.py:379
  232.1 14.4 %collective-permute-done.17 = f32[3,192,256]{2,1,0:T(8,128)S(1)} collective-permute-done((f32[3,192,256]{2,1,0:T(8,128)S(1)}, f32[3,192,256]{2,1,0:T(8,128)S(1)}, u32[]{:S(2)}, u32[]{:S(2)}) %collective-permute-start.17) | collective-permute-done | bytes 589856 | tf_op jit(solution)/shard_map/ppermute | solution.py:379
  246.7 7.7 %collective-permute-done.18 = f32[3,192,128]{2,1,0:T(8,128)S(1)} collective-permute-done((f32[3,192,128]{2,1,0:T(8,128)S(1)}, f32[3,192,128]{2,1,0:T(8,128)S(1)}, u32[]{:S(2)}, u32[]{:S(2)}) %collective-permute-start.18) | collective-permute-done | bytes 294944 | tf_op jit(solution)/shard_map/ppermute | solution.py:379
  255.4 13.3 %collective-permute-done.19 = f32[3,192,64]{2,1,0:T(8,128)S(1)} collective-permute-done((f32[3,192,64]{2,1,0:T(8,128)S(1)}, f32[3,192,64]{2,1,0:T(8,128)S(1)}, u32[]{:S(2)}, u32[]{:S(2)}) %collective-permute-start.19) | collective-permute-done | bytes 147488 | tf_op jit(solution)/shard_map/ppermute | solution.py:379
  (136 shorter events, 54.2 us)
Async XLA Ops:
  6.5 38.7 %all-gather.7.cloned.1.call-start = ((), (), s32[]{:S(2)}) async-start(), calls=%async_computation | async-start | bytes 1310720 | tf_op jit(solution)/shard_map/all_gather | solution.py:412
  8.6 53.9 %all-gather.9.cloned.1.call-start = ((), (), s32[]{:S(2)}) async-start(), calls=%async_computation.1 | async-start | bytes 2621440 | tf_op jit(solution)/shard_map/all_gather | solution.py:412
  9.5 89.6 %all-gather.11.cloned.1.call-start = ((), (), s32[]{:S(2)}) async-start(), calls=%async_computation.2 | async-start | bytes 1966080 | tf_op jit(solution)/shard_map/all_gather | solution.py:413
  17.4 22.9 %collective-permute-start = (bf16[4,3,2,72,256]{4,3,2,1,0:T(8,128)(2,1)}, bf16[4,3,2,72,256]{4,3,2,1,0:T(8,128)(2,1)S(1)}, u32[]{:S(2)}, u32[]{:S(2)}) collective-permute-start(bf16[4,3,2,72,256]{4,3,2,1,0:T(8,128)(2,1)} %get-tuple-element.39), channel_id=1, source_target_pairs={{0,4},{4,0},{8,12},{12,8},{16,20},{20,16},{24,28},{28,24},{1,5},{5... | collective-permute-start | bytes 2654216 | tf_op jit(solution)/shard_map/ppermute | solution.py:379
  22.5 20.8 %copy-start.20 = (s32[4]{0:T(128)S(1)}, s32[4]{0:T(128)}, u32[]{:S(2)}) copy-start(s32[4]{0:T(128)} %constant.155.clone) | copy-start | bytes 52
  41.5 21.0 %collective-permute-start.1 = (bf16[4,3,2,72,256]{4,3,2,1,0:T(8,128)(2,1)}, bf16[4,3,2,72,256]{4,3,2,1,0:T(8,128)(2,1)S(1)}, u32[]{:S(2)}, u32[]{:S(2)}) collective-permute-start(bf16[4,3,2,72,256]{4,3,2,1,0:T(8,128)(2,1)} %pad_maximum_fusion), channel_id=1, source_target_pairs={{0,8},{4,12},{8,0},{12,4},{16,24},{20,28},{24,16},{28,20},{1,9},{5... | collective-permute-start | bytes 2654216 | tf_op jit(solution)/shard_map/ppermute | solution.py:379
  55.5 32.8 %collective-permute-start.3 = (s16[528,1024]{1,0:T(8,128)(2,1)}, s16[528,1024]{1,0:T(8,128)(2,1)}, u32[]{:S(2)}, u32[]{:S(2)}) collective-permute-start(s16[528,1024]{1,0:T(8,128)(2,1)} %get-tuple-element.41), channel_id=1, source_target_pairs={{0,4},{4,0},{8,12},{12,8},{16,20},{20,16},{24,28},{28,24},{1,5},{5... | collective-permute-start | bytes 3244040 | tf_op jit(solution)/shard_map/ppermute | solution.py:379
  73.0 52.1 %collective-permute-start.6 = (s16[528,1024]{1,0:T(8,128)(2,1)}, s16[528,1024]{1,0:T(8,128)(2,1)S(1)}, u32[]{:S(2)}, u32[]{:S(2)}) collective-permute-start(s16[528,1024]{1,0:T(8,128)(2,1)} %get-tuple-element.51), channel_id=1, source_target_pairs={{0,4},{4,0},{8,12},{12,8},{16,20},{20,16},{24,28},{28,24},{1,5},{5... | collective-permute-start | bytes 3244040 | tf_op jit(solution)/shard_map/ppermute | solution.py:379
  75.5 58.0 %collective-permute-start.2 = (bf16[4,3,2,72,256]{4,3,2,1,0:T(8,128)(2,1)}, bf16[4,3,2,72,256]{4,3,2,1,0:T(8,128)(2,1)S(1)}, u32[]{:S(2)}, u32[]{:S(2)}) collective-permute-start(bf16[4,3,2,72,256]{4,3,2,1,0:T(8,128)(2,1)} %pad_maximum_fusion.1), channel_id=1, source_target_pairs={{0,16},{4,20},{8,24},{12,28},{16,0},{20,4},{24,8},{28,12},{1,17},{... | collective-permute-start | bytes 2654216 | tf_op jit(solution)/shard_map/ppermute | solution.py:379
  91.6 30.2 %collective-permute-start.4 = (s16[528,512]{1,0:T(8,128)(2,1)}, s16[528,512]{1,0:T(8,128)(2,1)}, u32[]{:S(2)}, u32[]{:S(2)}) collective-permute-start(s16[528,512]{1,0:T(8,128)(2,1)} %get-tuple-element.45), channel_id=1, source_target_pairs={{0,8},{4,12},{8,0},{12,4},{16,24},{20,28},{24,16},{28,20},{1,9},{5... | collective-permute-start | bytes 1622024 | tf_op jit(solution)/shard_map/ppermute | solution.py:379
  98.0 51.8 %collective-permute-start.10 = (s16[528,1024]{1,0:T(8,128)(2,1)}, s16[528,1024]{1,0:T(8,128)(2,1)S(1)}, u32[]{:S(2)}, u32[]{:S(2)}) collective-permute-start(s16[528,1024]{1,0:T(8,128)(2,1)} %get-tuple-element.60), channel_id=1, source_target_pairs={{0,4},{4,0},{8,12},{12,8},{16,20},{20,16},{24,28},{28,24},{1,5},{5... | collective-permute-start | bytes 3244040 | tf_op jit(solution)/shard_map/ppermute | solution.py:379
  124.7 12.1 %collective-permute-start.5 = (s16[528,256]{1,0:T(8,128)(2,1)}, s16[528,256]{1,0:T(8,128)(2,1)S(1)}, u32[]{:S(2)}, u32[]{:S(2)}) collective-permute-start(s16[528,256]{1,0:T(8,128)(2,1)} %get-tuple-element.48), channel_id=1, source_target_pairs={{0,16},{4,20},{8,24},{12,28},{16,0},{20,4},{24,8},{28,12},{1,17},{... | collective-permute-start | bytes 811016 | tf_op jit(solution)/shard_map/ppermute | solution.py:379
  129.5 16.6 %collective-permute-start.8 = (s16[528,512]{1,0:T(8,128)(2,1)}, s16[528,512]{1,0:T(8,128)(2,1)S(1)}, u32[]{:S(2)}, u32[]{:S(2)}) collective-permute-start(s16[528,512]{1,0:T(8,128)(2,1)} %get-tuple-element.56), channel_id=1, source_target_pairs={{0,8},{4,12},{8,0},{12,4},{16,24},{20,28},{24,16},{28,20},{1,9},{5... | collective-permute-start | bytes 1622024 | tf_op jit(solution)/shard_map/ppermute | solution.py:379
  146.0 33.0 %collective-permute-start.7 = (f32[384,512]{1,0:T(8,128)}, f32[384,512]{1,0:T(8,128)S(1)}, u32[]{:S(2)}, u32[]{:S(2)}) collective-permute-start(f32[384,512]{1,0:T(8,128)} %get-tuple-element.55), channel_id=1, source_target_pairs={{0,1},{1,0},{2,3},{3,2},{4,5},{5,4},{6,7},{7,6},{8,9},{9,8},{10,11... | collective-permute-start | bytes 2359304 | tf_op jit(solution)/shard_map/ppermute | solution.py:379
  149.9 14.9 %collective-permute-start.9 = (s16[528,256]{1,0:T(8,128)(2,1)}, s16[528,256]{1,0:T(8,128)(2,1)S(1)}, u32[]{:S(2)}, u32[]{:S(2)}) collective-permute-start(s16[528,256]{1,0:T(8,128)(2,1)} %get-tuple-element.58), channel_id=1, source_target_pairs={{0,16},{4,20},{8,24},{12,28},{16,0},{20,4},{24,8},{28,12},{1,17},{... | collective-permute-start | bytes 811016 | tf_op jit(solution)/shard_map/ppermute | solution.py:379
  154.2 20.8 %collective-permute-start.13 = (s16[528,512]{1,0:T(8,128)(2,1)}, s16[528,512]{1,0:T(8,128)(2,1)S(1)}, u32[]{:S(2)}, u32[]{:S(2)}) collective-permute-start(s16[528,512]{1,0:T(8,128)(2,1)} %get-tuple-element.65), channel_id=1, source_target_pairs={{0,8},{4,12},{8,0},{12,4},{16,24},{20,28},{24,16},{28,20},{1,9},{5... | collective-permute-start | bytes 1622024 | tf_op jit(solution)/shard_map/ppermute | solution.py:379
  174.0 28.7 %collective-permute-start.11 = (f32[384,512]{1,0:T(8,128)}, f32[384,512]{1,0:T(8,128)S(1)}, u32[]{:S(2)}, u32[]{:S(2)}) collective-permute-start(f32[384,512]{1,0:T(8,128)} %get-tuple-element.64), channel_id=1, source_target_pairs={{0,1},{1,0},{2,3},{3,2},{4,5},{5,4},{6,7},{7,6},{8,9},{9,8},{10,11... | collective-permute-start | bytes 2359304 | tf_op jit(solution)/shard_map/ppermute | solution.py:379
  178.8 14.2 %collective-permute-start.14 = (s16[528,256]{1,0:T(8,128)(2,1)}, s16[528,256]{1,0:T(8,128)(2,1)S(1)}, u32[]{:S(2)}, u32[]{:S(2)}) collective-permute-start(s16[528,256]{1,0:T(8,128)(2,1)} %get-tuple-element.67), channel_id=1, source_target_pairs={{0,16},{4,20},{8,24},{12,28},{16,0},{20,4},{24,8},{28,12},{1,17},{... | collective-permute-start | bytes 811016 | tf_op jit(solution)/shard_map/ppermute | solution.py:379
  202.7 2.5 collective-permute-start.15
  202.9 20.4 %collective-permute-start.12 = (f32[2,192,512]{2,1,0:T(8,128)S(1)}, f32[2,192,512]{2,1,0:T(8,128)S(1)}, u32[]{:S(2)}, u32[]{:S(2)}) collective-permute-start(f32[2,192,512]{2,1,0:T(8,128)S(1)} %pad_maximum_fusion.2), channel_id=1, source_target_pairs={{0,2},{1,3},{2,0},{3,1},{4,6},{5,7},{6,4},{7,5},{8,10},{9,11},{10,... | collective-permute-start | bytes 2359304 | tf_op jit(solution)/shard_map/ppermute | solution.py:379
  205.4 26.0 %collective-permute-start.16 = (f32[1,192,512]{2,1,0:T(8,128)S(1)}, f32[1,192,512]{2,1,0:T(8,128)S(1)}, u32[]{:S(2)}, u32[]{:S(2)}) collective-permute-start(f32[1,192,512]{2,1,0:T(8,128)S(1)} %slice.93), channel_id=1, source_target_pairs={{0,2},{1,3},{2,0},{3,1},{4,6},{5,7},{6,4},{7,5},{8,10},{9,11},{10,... | collective-permute-start | bytes 1179656 | tf_op jit(solution)/shard_map/ppermute | solution.py:379
  231.5 15.0 %collective-permute-start.17 = (f32[3,192,256]{2,1,0:T(8,128)S(1)}, f32[3,192,256]{2,1,0:T(8,128)S(1)}, u32[]{:S(2)}, u32[]{:S(2)}) collective-permute-start(f32[3,192,256]{2,1,0:T(8,128)S(1)} %pad_maximum_fusion.3), channel_id=1, source_target_pairs={{0,4},{4,0},{8,12},{12,8},{16,20},{20,16},{24,28},{28,24},{1,5},{5... | collective-permute-start | bytes 1769480 | tf_op jit(solution)/shard_map/ppermute | solution.py:379
  246.6 7.8 %collective-permute-start.18 = (f32[3,192,128]{2,1,0:T(8,128)S(1)}, f32[3,192,128]{2,1,0:T(8,128)S(1)}, u32[]{:S(2)}, u32[]{:S(2)}) collective-permute-start(f32[3,192,128]{2,1,0:T(8,128)S(1)} %slice.97), channel_id=1, source_target_pairs={{0,8},{4,12},{8,0},{12,4},{16,24},{20,28},{24,16},{28,20},{1,9},{5... | collective-permute-start | bytes 884744 | tf_op jit(solution)/shard_map/ppermute | solution.py:379
  254.6 14.1 %collective-permute-start.19 = (f32[3,192,64]{2,1,0:T(8,128)S(1)}, f32[3,192,64]{2,1,0:T(8,128)S(1)}, u32[]{:S(2)}, u32[]{:S(2)}) collective-permute-start(f32[3,192,64]{2,1,0:T(8,128)S(1)} %get-tuple-element.74), channel_id=1, source_target_pairs={{0,16},{4,20},{8,24},{12,28},{16,0},{20,4},{24,8},{28,12},{1,17},{... | collective-permute-start | bytes 442376 | tf_op jit(solution)/shard_map/ppermute | solution.py:379
  (21 other events, 76.7 us)
Sparse Core Ops, SparseCore 0:
  8.9 19.4 all-gather.6
  29.9 22.5 all-gather.8
  54.1 19.6 all-gather.10

commit v5 on v3

--- a/solution.py
+++ b/solution.py
@@ -16,11 +16,14 @@
 TOP = 32700.0
 MAGIC = 1.5 * 2.0**23
 NT_DIMS = (((1,), (1,)), ((), ()))
-VMEM = 56 * 1024 * 1024
-
-
-def params():
-    return pltpu.CompilerParams(vmem_limit_bytes=VMEM)
+MIB = 1024 * 1024
+
+
+TOKEN = jax.ShapeDtypeStruct((8, 128), jnp.float32)
+
+
+def params(mib):
+    return pltpu.CompilerParams(vmem_limit_bytes=mib * MIB)
 
 
 def cost(flops, moved):
@@ -66,11 +69,26 @@
     return (parts * factor[:, None, :]).reshape(rows, width)
 
 
-def shift_kernel(dest_ref, con_ref, map_ref, stay_ref, go_ref):
+def reversed_bits(number, count):
+    return sum(((number // (1 << b)) % 2) * (1 << (count - 1 - b)) for b in range(count))
+
+
+def block_of(me, known, stop, flip):
+    number = 0
+    for bit in range(known, stop):
+        flag = (me // (1 << bit)) % 2
+        number = 2 * number + (1 - flag if flip and bit == stop - 1 else flag)
+    return number
+
+
+def shift_kernel(order, me_ref, con_ref, map_ref, stay_ref, go_ref, token_ref):
     slots, _, _, rows, width = stay_ref.shape
+    count = len(order).bit_length() - 1
+    token_ref[...] = jnp.zeros_like(token_ref)
     for which, out_ref in enumerate((stay_ref, go_ref)):
         for slot in range(slots):
-            first = dest_ref[which * slots + slot] * width
+            dest = jnp.bitwise_xor(me_ref[0], order[which * slots + slot])
+            first = reversed_bits(dest, count) * width
             for block in range(width // GBLK):
                 cols = pl.ds(pl.multiple_of(first + block * GBLK, GBLK), GBLK)
                 within = jnp.bitwise_and(map_ref[0, 0:1, cols], GBLK - 1)
@@ -83,31 +101,35 @@
                     )
 
 
-def shift_call(con, shift_map, dests, width):
+def shift_call(con, shift_map, me, order, width):
     points, _, rows, slab = con.shape
-    slots = dests.shape[0] // 2
+    slots = len(order) // 2
     grid_spec = pltpu.PrefetchScalarGridSpec(
         num_scalar_prefetch=1,
         grid=(points,),
         in_specs=[
-            pl.BlockSpec((1, 2, rows, slab), lambda q, dest: (q, 0, 0, 0)),
-            pl.BlockSpec((1, 1, slab), lambda q, dest: (q, 0, 0)),
-        ],
-        out_specs=[pl.BlockSpec((slots, 1, 2, rows, width), lambda q, dest: (0, q, 0, 0, 0))] * 2,
+            pl.BlockSpec((1, 2, rows, slab), lambda q, me: (q, 0, 0, 0)),
+            pl.BlockSpec((1, 1, slab), lambda q, me: (q, 0, 0)),
+        ],
+        out_specs=[pl.BlockSpec((slots, 1, 2, rows, width), lambda q, me: (0, q, 0, 0, 0))] * 2
+        + [pl.BlockSpec(TOKEN.shape, lambda q, me: (0, 0))],
     )
     return pl.pallas_call(
-        shift_kernel,
+        lambda *refs: shift_kernel(order, *refs),
         grid_spec=grid_spec,
-        out_shape=[jax.ShapeDtypeStruct((slots, points, 2, rows, width), jnp.bfloat16)] * 2,
-        compiler_params=params(),
+        out_shape=[jax.ShapeDtypeStruct((slots, points, 2, rows, width), jnp.bfloat16)] * 2
+        + [TOKEN],
+        compiler_params=params(16),
         cost_estimate=cost(8 * con.size, 4 * con.size),
-    )(dests, con, shift_map.reshape(points, 1, slab))
-
-
-def x_kernel(slots, base_ref, *refs):
-    val_refs, (weight_ref, go_ref, keep_ref, left_ref) = refs[:slots], refs[slots:]
-    rows, depth = val_refs[0].shape[2], val_refs[0].shape[3]
+    )(me, con, shift_map.reshape(points, 1, slab))
+
+
+def x_kernel(slots, waits, me_ref, *refs):
+    val_refs, weight_ref = refs[:slots], refs[slots]
+    go_ref, keep_ref, token_ref, left_ref = refs[slots + 1 + waits :]
+    _, _, rows, depth = val_refs[0].shape
     half = slots * rows
+    token_ref[...] = jnp.zeros_like(token_ref)
     step = pl.program_id(0)
     halfway = pl.num_programs(0) // 2
 
@@ -133,7 +155,7 @@
         keep_ref[...] = mm(left_ref[...], weight)
 
 
-def x_call(vals, screened, place, point, side, steps):
+def x_call(vals, screened, place, point, me, steps, after):
     slots = len(vals)
     _, _, rows, depth = vals[0].shape
     height = 2 * slots * rows
@@ -144,65 +166,115 @@
         num_scalar_prefetch=1,
         grid=(steps,),
         in_specs=[
-            pl.BlockSpec((1, 2, rows, depth), lambda j, t: (place, 0, 0, 0)) for _ in vals
+            pl.BlockSpec((1, 2, rows, depth), lambda j, me: (place, 0, 0, 0)) for _ in vals
         ]
         + [
             pl.BlockSpec(
-                (1, 2, depth, width), lambda j, t: (point, 0, 0, t[j // half] * half + j % half)
+                (1, 2, depth, width),
+                lambda j, me: (point, 0, 0, ((me[0] + 1 + j // half) % 2) * half + j % half),
             )
-        ],
+        ]
+        + [pl.BlockSpec(memory_space=pl.ANY) for _ in after],
         out_specs=[
-            pl.BlockSpec((height + EXP_ROWS, width), lambda j, t: (0, jnp.minimum(j, half - 1))),
-            pl.BlockSpec((height, width), lambda j, t: (0, jnp.maximum(j - half, 0))),
+            pl.BlockSpec((height + EXP_ROWS, width), lambda j, me: (0, jnp.minimum(j, half - 1))),
+            pl.BlockSpec((height, width), lambda j, me: (0, jnp.maximum(j - half, 0))),
+            pl.BlockSpec(TOKEN.shape, lambda j, me: (0, 0)),
         ],
         scratch_shapes=[pltpu.VMEM((height, 2 * depth), jnp.bfloat16)],
     )
     return pl.pallas_call(
-        lambda *refs: x_kernel(slots, *refs),
+        lambda *refs: x_kernel(slots, len(after), *refs),
         grid_spec=grid_spec,
         out_shape=[
             jax.ShapeDtypeStruct((height + EXP_ROWS, columns), jnp.int16),
             jax.ShapeDtypeStruct((height, columns), jnp.float32),
-        ],
-        compiler_params=params(),
+            TOKEN,
+        ],
+        compiler_params=params(24),
         cost_estimate=cost(
             2 * height * 2 * depth * 2 * columns, 8 * depth * columns + 6 * height * columns
         ),
-    )(side, *vals, screened)
-
-
-def hop_kernel(heard, at_ref, keep_ref, *refs):
+    )(me, *vals, screened, *after)
+
+
+def hop_kernel(heard, me_ref, keep_ref, *refs):
     total = keep_ref[...]
     for ref in refs[:heard]:
         total = total + decode(ref)
-    encode(total, refs[-1])
-
-
-def hop_call(keep, others, at, width, after):
+    out_ref, token_ref = refs[-2:]
+    encode(total, out_ref)
+    token_ref[...] = jnp.zeros_like(token_ref)
+
+
+def hop_call(keep, others, me, stage, width, after):
     height, tall = keep.shape[0], others[0].shape[0]
+    steps = width // 128
+
+    def at(known):
+        return lambda i, me: (0, block_of(me[0], known, stage + 1, True) * steps + i)
+
+    grid_spec = pltpu.PrefetchScalarGridSpec(
+        num_scalar_prefetch=1,
+        grid=(steps,),
+        in_specs=[pl.BlockSpec((height, 128), at(1))]
+        + [pl.BlockSpec((tall, 128), at(n + 1)) for n in range(len(others))]
+        + [pl.BlockSpec(memory_space=pl.ANY) for _ in after],
+        out_specs=[
+            pl.BlockSpec((tall, 128), lambda i, me: (0, i)),
+            pl.BlockSpec(TOKEN.shape, lambda i, me: (0, 0)),
+        ],
+    )
+    return pl.pallas_call(
+        lambda *refs: hop_kernel(len(others), *refs),
+        grid_spec=grid_spec,
+        out_shape=[jax.ShapeDtypeStruct((tall, width), jnp.int16), TOKEN],
+        compiler_params=params(16),
+        cost_estimate=cost(20 * height * width, 8 * height * width),
+    )(me, keep, *others, *after)
+
+
+def fold_kernel(me_ref, own_ref, heard_ref, keep_ref, go_ref):
+    total = own_ref[...] + decode(heard_ref)
+    if go_ref.dtype == jnp.int16:
+        rows = keep_ref.shape[0]
+        keep_ref[...] = total[:rows]
+        encode(total[rows:], go_ref)
+    else:
+        cols = keep_ref.shape[1]
+        keep_ref[...] = total[:, :cols]
+        go_ref[...] = total[:, cols:]
+
+
+def fold_call(own, heard, me, by_rows):
+    rows, cols = own.shape
+    if by_rows:
+        shapes = [
+            jax.ShapeDtypeStruct((rows // 2, cols), jnp.float32),
+            jax.ShapeDtypeStruct((rows // 2 + EXP_ROWS, cols), jnp.int16),
+        ]
+    else:
+        shapes = [jax.ShapeDtypeStruct((rows, cols // 2), jnp.float32)] * 2
+    whole = lambda a: pl.BlockSpec(a.shape, lambda i, me: (0, 0))
     grid_spec = pltpu.PrefetchScalarGridSpec(
         num_scalar_prefetch=1,
         grid=(1,),
-        in_specs=[pl.BlockSpec((height, width), lambda i, at: (0, at[0]))]
-        + [
-            pl.BlockSpec((tall, width), lambda i, at, n=n: (0, at[n + 1]))
-            for n in range(len(others))
-        ]
-        + [pl.BlockSpec(memory_space=pl.ANY) for _ in after],
-        out_specs=pl.BlockSpec((tall, width), lambda i, at: (0, 0)),
+        in_specs=[whole(own), whole(heard)],
+        out_specs=[whole(a) for a in shapes],
     )
     return pl.pallas_call(
-        lambda *refs: hop_kernel(len(others), *refs),
+        fold_kernel,
         grid_spec=grid_spec,
-        out_shape=jax.ShapeDtypeStruct((tall, width), jnp.int16),
-        compiler_params=params(),
-        cost_estimate=cost(20 * height * width, 8 * height * width),
-    )(at, keep, *others, *after)
-
-
-def exchange_kernel(slots, *refs):
-    here_refs, (there_ref, coulomb_ref, out_ref, left_ref) = refs[:slots], refs[slots:]
-    rows, depth = here_refs[0].shape[1], here_refs[0].shape[2]
+        out_shape=shapes,
+        compiler_params=params(16),
+        cost_estimate=cost(20 * own.size, 10 * own.size),
+    )(me, own, heard)
+
+
+def exchange_kernel(slots, waits, *refs):
+    here_refs, (there_ref, coulomb_ref) = refs[:slots], refs[slots : slots + 2]
+    out_ref, token_ref, left_ref = refs[slots + 2 + waits :]
+    _, rows, depth = here_refs[0].shape
+    token_ref[...] = jnp.zeros_like(token_ref)
 
     @pl.when(pl.program_id(0) == 0)
     def _():
@@ -226,32 +298,39 @@
         out_ref[0, part] = both[:, part * cols : (part + 1) * cols]
 
 
-def exchange_call(heres, there, coulomb):
-    slots = len(heres)
+def exchange_call(heres, there, coulomb, after):
+    slots, rows = len(heres), heres[0].shape[1]
     points, _, cols, depth = there.shape
-    rows = heres[0].shape[1]
     height = slots * rows
     return pl.pallas_call(
-        lambda *refs: exchange_kernel(slots, *refs),
+        lambda *refs: exchange_kernel(slots, len(after), *refs),
         grid=(points,),
         in_specs=[pl.BlockSpec(h.shape, lambda q: (0, 0, 0)) for h in heres]
         + [
             pl.BlockSpec((1, 2, cols, depth), lambda q: (q, 0, 0, 0)),
             pl.BlockSpec((1, 1, depth), lambda q: (q, 0, 0)),
-        ],
-        out_specs=pl.BlockSpec((1, 2, height, cols), lambda q: (q, 0, 0, 0)),
-        out_shape=jax.ShapeDtypeStruct((points, 2, height, cols), jnp.float32),
+        ]
+        + [pl.BlockSpec(memory_space=pl.ANY) for _ in after],
+        out_specs=[
+            pl.BlockSpec((1, 2, height, cols), lambda q: (q, 0, 0, 0)),
+            pl.BlockSpec(TOKEN.shape, lambda q: (0, 0)),
+        ],
+        out_shape=[jax.ShapeDtypeStruct((points, 2, height, cols), jnp.float32), TOKEN],
         scratch_shapes=[pltpu.VMEM((height, 2 * depth), jnp.bfloat16)],
-        compiler_params=params(),
+        compiler_params=params(16),
         cost_estimate=cost(2 * points * height * 2 * cols * 2 * depth * 2, 8 * points * cols * depth),
-    )(*heres, there, coulomb.reshape(points, 1, depth))
-
-
-def tile_kernel(slots, heard, chunks, waits, index_ref, at_ref, *refs):
+    )(*heres, there, coulomb.reshape(points, 1, depth), *after)
+
+
+def tile_kernel(order, heard, chunks, waits, me_ref, *refs):
+    slots = len(order)
     con_refs, keep_ref = refs[:slots], refs[slots]
     heard_refs = refs[slots + 1 : slots + 1 + heard]
     exch_ref, row_ref, col_direct_ref, col_exch_ref = refs[slots + 1 + heard : slots + 5 + heard]
-    keep_out, go_out, con_all, direct_ref, natural_ref = refs[slots + 5 + heard + waits :]
+    keep_out, go_out, token_ref, con_all, direct_ref, natural_ref, sums_ref = refs[
+        slots + 5 + heard + waits :
+    ]
+    token_ref[...] = jnp.zeros_like(token_ref)
     total = keep_ref[...]
     for ref in heard_refs:
         total = total + decode(ref)
@@ -272,7 +351,7 @@
     direct = mm_nt(left, high) + mm_nt(left, low)
     lanes = direct_ref.shape[0]
     for slot in range(slots):
-        start = pl.multiple_of(index_ref[slot] * rows, 8)
+        start = pl.multiple_of(jnp.bitwise_xor(me_ref[0], order[slot]) * rows, 8)
         for lane in range(lanes):
             direct_ref[lane, pl.ds(start, rows), :] = direct[
                 slot * pitch : slot * pitch + rows, lane * 128 : (lane + 1) * 128
@@ -307,57 +386,65 @@
                 term = mm(moved, pick_cols[...])
                 result = term if result is None else result + term
         for chunk in range(chunks):
-            out_ref = keep_out if chunk < chunks // 2 else go_out
+            out_ref = keep_out if chunk < chunks // 2 else sums_ref
             at = (2 * (chunk % (chunks // 2)) + part) * count
             out_ref[at : at + count, :] = result[chunk * count : (chunk + 1) * count]
+    encode(sums_ref[...], go_out)
 
 
 def tile_call(
-    cons, point, keep, heard, exch, index, at, pick_rows, col_direct, col_exch, chunks, after
+    cons, point, keep, heard, exch, me, order, pick_rows, col_direct, col_exch, chunks, after
 ):
     slots = len(cons)
     _, _, _, rows, width = cons[0][0].shape
     height, tall = keep.shape[0], heard[0].shape[0]
     pitch = -(-rows // 16) * 16
     out_cols = col_direct.shape[1]
-    whole = lambda a: pl.BlockSpec(a.shape, lambda i, index, at: (0,) * a.ndim)
+    stages = len(heard)
+    whole = lambda a: pl.BlockSpec(a.shape, lambda i, me: (0,) * a.ndim)
+
+    def at(known):
+        return lambda i, me: (0, block_of(me[0], known, stages, False))
+
     grid_spec = pltpu.PrefetchScalarGridSpec(
-        num_scalar_prefetch=2,
+        num_scalar_prefetch=1,
         grid=(1,),
         in_specs=[
-            pl.BlockSpec(
-                (1, 1, 2, rows, width), lambda i, index, at, place=place: (place, point, 0, 0, 0)
-            )
+            pl.BlockSpec((1, 1, 2, rows, width), lambda i, me, place=place: (place, point, 0, 0, 0))
             for _, place in cons
         ]
-        + [pl.BlockSpec((height, width), lambda i, index, at: (0, at[0]))]
+        + [pl.BlockSpec((height, width), at(1))]
+        + [pl.BlockSpec((tall, width), at(n + 1)) for n in range(stages)]
         + [
-            pl.BlockSpec((tall, width), lambda i, index, at, n=n: (0, at[n + 1]))
-            for n in range(len(heard))
-        ]
-        + [
-            pl.BlockSpec((1,) + exch.shape[1:], lambda i, index, at: (point, 0, 0, 0)),
+            pl.BlockSpec((1,) + exch.shape[1:], lambda i, me: (point, 0, 0, 0)),
             whole(pick_rows),
             whole(col_direct),
             whole(col_exch),
         ]
         + [pl.BlockSpec(memory_space=pl.ANY) for _ in after],
-        out_specs=[pl.BlockSpec((NT, out_cols), lambda i, index, at: (0, 0))] * 2,
+        out_specs=[
+            pl.BlockSpec((NT, out_cols), lambda i, me: (0, 0)),
+            pl.BlockSpec((NT + EXP_ROWS, out_cols), lambda i, me: (0, 0)),
+            pl.BlockSpec(TOKEN.shape, lambda i, me: (0, 0)),
+        ],
         scratch_shapes=[
             pltpu.VMEM((slots * pitch, 2 * width), jnp.bfloat16),
             pltpu.VMEM((height // 128, NC * NC, 128), jnp.float32),
             pltpu.VMEM((2, NT, NT), jnp.float32),
+            pltpu.VMEM((NT, out_cols), jnp.float32),
         ],
     )
     return pl.pallas_call(
-        lambda *refs: tile_kernel(slots, len(heard), chunks, len(after), *refs),
+        lambda *refs: tile_kernel(order, stages, chunks, len(after), *refs),
         grid_spec=grid_spec,
-        out_shape=[jax.ShapeDtypeStruct((NT, out_cols), jnp.float32)] * 2,
-        compiler_params=params(),
+        out_shape=[
+            jax.ShapeDtypeStruct((NT, out_cols), jnp.float32),
+            jax.ShapeDtypeStruct((NT + EXP_ROWS, out_cols), jnp.int16),
+            TOKEN,
+        ],
+        compiler_params=params(24),
         cost_estimate=cost(2.8e9, 8e6),
-    )(
-        index, at, *[c for c, _ in cons], keep, *heard, exch, pick_rows, col_direct, col_exch, *after
-    )
+    )(me, *[c for c, _ in cons], keep, *heard, exch, pick_rows, col_direct, col_exch, *after)
 
 
 def swap(value, axis, size, bit):
@@ -381,6 +468,10 @@
     return order
 
 
+def behind(value, token):
+    return lax.optimization_barrier((value, token))[0]
+
+
 def on_device(*args):
     (val_density, con_density, screened, coulomb, trans_here, trans_there, shift_map, ordering) = args
     ga, pair = lax.axis_size("ga"), lax.axis_size("pair")
@@ -388,57 +479,50 @@
     slab = con_density.shape[3]
     width = slab // ga
     me_ga, me_pair = lax.axis_index("ga"), lax.axis_index("pair")
+    me = me_ga.astype(jnp.int32).reshape(1)
     ga_bits = [1 << b for b in range(ga.bit_length() - 1)]
     pair_bits = [1 << b for b in range(pair.bit_length() - 1)]
     ga_order = halving_order(ga_bits)
-    half = ga // 2
-    dests = me_ga ^ jnp.asarray(ga_order, jnp.int32)
-    flags = [(me_ga // bit) % 2 for bit in ga_bits]
-    blocks = sum(((dests // bit) % 2) * (half // bit) for bit in ga_bits)
-    as_index = lambda items: jnp.stack([jnp.asarray(i, jnp.int32) for i in items])
-
-    def block_at(known, chosen):
-        number = jnp.int32(0)
-        for flag in flags[known : len(flags) if chosen is None else chosen]:
-            number = 2 * number + flag
-        return number if chosen is None else 2 * number + 1 - flags[chosen]
-
-    val = jnp.transpose(val_density, (1, 2, 0, 3))
-    first, others = gather_slots(val[:1], "pair", pair), gather_slots(val[1:], "pair", pair)
+    stages, half = len(ga_bits), ga // 2
+
+    first = gather_slots(jnp.transpose(val_density[:, :1], (1, 2, 0, 3)), "pair", pair)
+    others = gather_slots(jnp.transpose(val_density[:, 1:], (1, 2, 0, 3)), "pair", pair)
 
     con = jnp.transpose(con_density, (1, 2, 0, 3))
-    stay, go = shift_call(con, shift_map, blocks, width)
+    stay, go, token = shift_call(con, shift_map, me, ga_order, width)
+    from_near = swap(go, "ga", ga, ga_bits[0])
+
+    gone, keep, tokens = [], [], [token]
+    for q in range(points):
+        vals, place = (first, 0) if q == 0 else (others, q - 1)
+        coded, own, token = x_call(vals, screened, place, q, me, 4, tokens[-1:])
+        tokens.append(token)
+        gone.append(coded)
+        keep.append(own)
+    after = tokens[-1:]
+
     cons = {}
     for p, slot in enumerate(ga_order):
         cons[slot] = (stay, p) if p < half else (go, p - half)
-    for bit in ga_bits:
+    for step, bit in enumerate(ga_bits):
         moving = [slot for slot in ga_order if slot & bit]
-        if bit == ga_bits[0]:
-            sent = go
+        if step == 0:
+            got = from_near
         else:
             sent = jnp.stack([cons[slot][0][cons[slot][1]] for slot in moving])
-        got = swap(sent, "ga", ga, bit)
+            got = swap(sent, "ga", ga, bit)
+        if step + 1 < stages:
+            got = behind(got, tokens[min(step + 2, points)])
         for place, slot in enumerate(moving):
             cons[slot] = (got, place)
     cons = [cons[slot] for slot in ga_order]
-
-    side = as_index([1 - flags[0], flags[0]])
-    gone, keep = [], []
-    for q in range(points):
-        vals, place = (first, 0) if q == 0 else (others, q - 1)
-        coded, own = x_call(vals, screened, place, q, side, 4)
-        gone.append(coded)
-        keep.append(own)
-
-    heres = gather_slots(jnp.transpose(trans_here, (1, 0, 2)), "pair", pair)
-    exch = exchange_call(heres, jnp.transpose(trans_there, (1, 2, 0, 3)), coulomb)
 
     row_count, col_count = NT // pair, NT // ga
     row_slots = jnp.asarray(halving_order(pair_bits), jnp.int32)
     row_trans = ordering.reshape(pair, row_count)[me_pair ^ row_slots].reshape(-1)
     at_row = ((row_trans // row_count) ^ me_pair) * row_count + row_trans % row_count
     pick_rows = (at_row[:, None] == jnp.arange(NT, dtype=jnp.int32)[None, :]).astype(jnp.bfloat16)
-    col_trans = ordering.reshape(ga, col_count)[dests]
+    col_trans = ordering.reshape(ga, col_count)[me_ga ^ jnp.asarray(ga_order, jnp.int32)]
     col_trans = jnp.pad(col_trans, ((0, 0), (0, 64 - col_count)), constant_values=-1).reshape(1, -1)
     real_col = col_trans >= 0
     at_direct = jnp.where(real_col, (col_trans % NC) * NV + col_trans // NC, -1)
@@ -453,29 +537,33 @@
 
     heard = [[swap(gone[q], "ga", ga, ga_bits[0])] for q in range(points)]
     outs = [None] * points
-    stages = len(ga_bits)
-    after = []
+    exch = None
     for wave in range(2 * points + stages):
         for q in reversed(range(points)):
             stage = wave - 2 * q
             if 1 <= stage < stages:
-                columns = ga >> (stage + 1)
-                at = as_index([block_at(k, stage) for k in [1] + list(range(1, stage + 1))])
-                coded = hop_call(keep[q], heard[q], at, columns * width, after)
-                after = [coded]
+                columns = (ga >> (stage + 1)) * width
+                coded, token = hop_call(keep[q], heard[q], me, stage, columns, after)
+                after = [token]
                 heard[q].append(swap(coded, "ga", ga, ga_bits[stage]))
+                if exch is None:
+                    heres = gather_slots(
+                        jnp.transpose(behind(trans_here, tokens[1]), (1, 0, 2)), "pair", pair
+                    )
+                    there = jnp.transpose(behind(trans_there, tokens[1]), (1, 2, 0, 3))
+                    exch, token = exchange_call(heres, there, coulomb, after)
+                    after = [token]
             elif stage == stages:
-                at = as_index([block_at(k, None) for k in [1] + list(range(1, stages + 1))])
-                tile, sent = tile_call(
-                    cons, q, keep[q], heard[q], exch, dests, at, pick_rows, col_direct, col_exch,
-                    pair, after,
+                tile, sent, token = tile_call(
+                    cons, q, keep[q], heard[q], exch, me, ga_order, pick_rows, col_direct,
+                    col_exch, pair, after,
                 )
-                after = [sent]
-                tile = tile + swap(sent, "pair", pair, pair_bits[0])
-                for bit in pair_bits[1:]:
-                    rows = tile.shape[0] // 2
-                    tile = tile[:rows] + swap(tile[rows:], "pair", pair, bit)
-                for bit in ga_bits:
+                after = [token]
+                for step, bit in enumerate(pair_bits):
+                    got = swap(sent, "pair", pair, bit)
+                    tile, sent = fold_call(tile, got, me, step + 1 < len(pair_bits))
+                tile = tile + swap(sent, "ga", ga, ga_bits[0])
+                for bit in ga_bits[1:]:
                     cols = tile.shape[1] // 2
                     tile = tile[:, :cols] + swap(tile[:, cols:], "ga", ga, bit)
                 outs[q] = tile[:, :col_count].reshape(2, row_count, col_count)
@@ -581,6 +669,7 @@
             and pair & (pair - 1) == 0
             and ga >= 4
             and pair >= 2
+            and NT % (pair * GROUP // 2) == 0
             and h_count % (ga * pair * GBLK) == 0
             and con_count % (8 * ga) == 0
             and args[0].shape[0] % (16 * pair) == 0

time: 243 us -> 242 us (level)
  Pallas kernels: 85.8 us -> 61.3 us
  local copies, waits for them, and re-layouts: 23.9 us -> 38.8 us
  waiting for transfers between devices: 87.9 us -> 102 us
  other arithmetic: 8.14 us -> 5.14 us
    pallas_call x8 -> x14, Pallas kernels: 67.1 us -> 49.1 us  [the longest x3 23.3 us: x_call(): pl.pallas_call(lambda *refs: x_kernel(slots, len(after), *refs), grid_spe...]
    unnamed x66 -> x65, local copies, waits for them, and re-layouts: 17.3 us -> 32.7 us
    ppermute x36, waiting for transfers between devices: 87.9 us -> 102 us  [swap(): return lax.ppermute(value, axis, [(i, i ^ bit) for i in range(size)])]
    pallas_call x6, Pallas kernels: 18.7 us -> 12.2 us  [hop_call(): pl.pallas_call(lambda *refs: hop_kernel(len(others), *refs), grid_spec=gr...]
    slice x6, local copies, waits for them, and re-layouts: 2.74 us -> 0.11 us  [on_device(): sent = jnp.stack([cons[slot][0][cons[slot][1]] for slot in moving])]
    optimization_barrier x0 -> x2, local copies, waits for them, and re-layouts: none -> 2.44 us  [behind(): return lax.optimization_barrier((value, token))[0]]
  transfers between devices with their start and end apart: 36 -> 36, of which waited for: 16 -> 16; matrix products, arithmetic and copies ran while one was open for 8% -> 5% of each run, Pallas kernels for 36% -> 25%
where the time goes in v5:
time: 242 us; the launch traced here: 241 us
  waiting for transfers between devices  102 us (42%)
  Pallas kernels  61.3 us (25%)
  local copies, waits for them, and re-layouts  38.8 us (16%)
  starting transfers between devices  33.4 us (14%)
  other arithmetic  5.14 us (2%)
    ppermute x36, waiting for transfers between devices, swap(): return lax.ppermute(value, axis, [(i, i ^ bit) for i in range(size)])  102 us
    ppermute x36, starting transfers between devices, swap(): return lax.ppermute(value, axis, [(i, i ^ bit) for i in range(size)])  33.4 us
    unnamed x65, local copies, waits for them, and re-layouts  32.7 us
    pallas_call x3, Pallas kernels, x_call(): pl.pallas_call(lambda *refs: x_kernel(slots, len(after), *refs), grid_spe...  23.3 us
    pallas_call x3, Pallas kernels, tile_call(): pl.pallas_call(lambda *refs: tile_kernel(order, stages, chunks, len(after...  17.8 us
    pallas_call x6, Pallas kernels, hop_call(): pl.pallas_call(lambda *refs: hop_kernel(len(others), *refs), grid_spec=gr...  12.2 us
    pallas_call x1, Pallas kernels, exchange_call(): pl.pallas_call(lambda *refs: exchange_kernel(slots, len(after), *refs), g...  4.88 us
  transfers between devices with their start and end apart: 36, of which 16 were waited for; matrix products, arithmetic and copies ran while one was open for 5% of the time, Pallas kernels for 25%

profile of v5, /device:TPU:0, one launch (start us, length us, event | category | flops | bytes accessed | tf_op | source)
XLA Modules:
  0.0 241.3 jit_solution(4045021791554076062)
XLA Ops:
  10.8 11.7 %collective-permute-done.5.refs_3_ = bf16[1,2,64,1024]{3,2,1,0:T(8,128)(2,1)} collective-permute-done((bf16[1,2,64,1024]{3,2,1,0:T(8,128)(2,1)}, bf16[1,2,64,1024]{3,2,1,0:T(8,128)(2,1)}, u32[]{:S(2)}, u32[]{:S(2)}) %collective-permute-start.5) | collective-permute-done | bytes 262176 | tf_op jit(solution)/shard_map/ppermute | solution.py:451
  24.4 8.2 %copy-done = bf16[3,2,1024,2048]{3,2,1,0:T(8,128)(2,1)S(1)} copy-done((bf16[3,2,1024,2048]{3,2,1,0:T(8,128)(2,1)S(1)}, bf16[3,2,1024,2048]{3,2,1,0:T(8,128)(2,1)}, u32[]{:S(2)}) %copy-start) | copy-done | bytes 25165848
  32.6 8.9 %shard_map.101 = (s16[528,1024]{1,0:T(8,128)(2,1)}, f32[512,1024]{1,0:T(8,128)S(1)}, f32[8,128]{1,0:T(8,128)S(1)}) custom-call(s32[1]{0:T(128)} %bitcast.refs_0_.me_ref, bf16[1,2,64,1024]{3,2,1,0:T(8,128)(2,1)} %bitcast.18.refs_1_, bf16[1,2,64,1024]{3,2,1,0:T(8,128)(2,1)} %collective-permute-done.4.refs_2_, ...), custom_call_target="tpu_custom_call" | custom-call | flops 4294967296 | bytes 11534336 | tf_op jit(solution)/shard_map/pallas_call | solution.py:185
  44.6 8.5 %copy-done.1 = bf16[3,2,1024,2048]{3,2,1,0:T(8,128)(2,1)S(1)} copy-done((bf16[3,2,1024,2048]{3,2,1,0:T(8,128)(2,1)S(1)}, bf16[3,2,1024,2048]{3,2,1,0:T(8,128)(2,1)}, u32[]{:S(2)}) %copy-start.1) | copy-done | bytes 25165848
  53.1 7.2 %shard_map.102 = (s16[528,1024]{1,0:T(8,128)(2,1)S(1)}, f32[512,1024]{1,0:T(8,128)S(1)}, f32[8,128]{1,0:T(8,128)S(1)}) custom-call(s32[1]{0:T(128)} %bitcast.refs_0_.me_ref, bf16[2,2,64,1024]{3,2,1,0:T(8,128)(2,1)S(1)} %bitcast.22, bf16[2,2,64,1024]{3,2,1,0:T(8,128)(2,1)S(1)} %collective-permute-done.1.refs_2_, ...), custom_call_target="tpu_custom_call" | custom-call | flops 4294967296 | bytes 11534336 | tf_op jit(solution)/shard_map/pallas_call | solution.py:185
  69.0 7.3 %collective-permute-done.12.refs_2_ = bf16[2,96,1024]{2,1,0:T(8,128)(2,1)} collective-permute-done((bf16[2,96,1024]{2,1,0:T(8,128)(2,1)}, bf16[2,96,1024]{2,1,0:T(8,128)(2,1)}, u32[]{:S(2)}, u32[]{:S(2)}) %collective-permute-start.12) | collective-permute-done | bytes 393248 | tf_op jit(solution)/shard_map/ppermute | solution.py:451
  76.9 8.2 %copy-done.2 = bf16[3,2,1024,2048]{3,2,1,0:T(8,128)(2,1)S(1)} copy-done((bf16[3,2,1024,2048]{3,2,1,0:T(8,128)(2,1)S(1)}, bf16[3,2,1024,2048]{3,2,1,0:T(8,128)(2,1)}, u32[]{:S(2)}) %copy-start.2) | copy-done | bytes 25165848
  88.2 7.2 %shard_map.103 = (s16[528,1024]{1,0:T(8,128)(2,1)S(1)}, f32[512,1024]{1,0:T(8,128)S(1)}, f32[8,128]{1,0:T(8,128)S(1)}) custom-call(s32[1]{0:T(128)} %bitcast.refs_0_.me_ref, bf16[2,2,64,1024]{3,2,1,0:T(8,128)(2,1)S(1)} %bitcast.23, bf16[2,2,64,1024]{3,2,1,0:T(8,128)(2,1)S(1)} %copy-done.14, bf16[2,2,64,1024]{3,2,1,0:T(8,128)(2,1)S(1)} %copy-done.16, ...), custom_call_target="tpu_custom_call" | custom-call | flops 4294967296 | bytes 11534336 | tf_op jit(solution)/shard_map/pallas_call | solution.py:185
  95.4 4.0 %shard_map.104 = (s16[528,512]{1,0:T(8,128)(2,1)}, f32[8,128]{1,0:T(8,128)S(1)}) custom-call(s32[1]{0:T(128)} %bitcast.refs_0_.me_ref, f32[512,1024]{1,0:T(8,128)S(1)} %copy-done.8, s16[528,1024]{1,0:T(8,128)(2,1)} %collective-permute-done.9.refs_2_.refs_10_, f32[8,128]{1,0:T(8,128)S(1)} %get-tuple-element.61.refs_3_), custom_call_target="tpu_custom_call" | custom-call | flops 5242880 | bytes 2097152 | tf_op jit(solution)/shard_map/pallas_call | solution.py:227
  107.4 4.9 %shard_map.105 = (f32[3,2,384,96]{3,2,1,0:T(8,128)S(1)}, f32[8,128]{1,0:T(8,128)S(1)}) custom-call(bf16[2,96,1024]{2,1,0:T(8,128)(2,1)} %bitcast.17.refs_0_, bf16[2,96,1024]{2,1,0:T(8,128)(2,1)} %collective-permute-done.11.refs_1_, bf16[2,96,1024]{2,1,0:T(8,128)(2,1)} %collective-permute-done.12.refs_2_, ...), custom_call_target="tpu_custom_call" | custom-call | flops 1811939328 | bytes 2359296 | tf_op jit(solution)/shard_map/pallas_call | solution.py:305
  112.3 13.4 %collective-permute-done.10.refs_3_.refs_11_ = s16[528,512]{1,0:T(8,128)(2,1)S(1)} collective-permute-done((s16[528,512]{1,0:T(8,128)(2,1)}, s16[528,512]{1,0:T(8,128)(2,1)S(1)}, u32[]{:S(2)}, u32[]{:S(2)}) %collective-permute-start.10) | collective-permute-done | bytes 540704 | tf_op jit(solution)/shard_map/ppermute | solution.py:451
  130.5 23.9 %collective-permute-done.14.refs_12_ = s16[528,256]{1,0:T(8,128)(2,1)S(1)} collective-permute-done((s16[528,256]{1,0:T(8,128)(2,1)S(1)}, s16[528,256]{1,0:T(8,128)(2,1)S(1)}, u32[]{:S(2)}, u32[]{:S(2)}) %collective-permute-start.14) | collective-permute-done | bytes 270368 | tf_op jit(solution)/shard_map/ppermute | solution.py:451
  154.5 6.1 %shard_map.108 = (f32[384,512]{1,0:T(8,128)S(1)}, s16[400,512]{1,0:T(8,128)(2,1)S(1)}, f32[8,128]{1,0:T(8,128)S(1)}) custom-call(s32[1]{0:T(128)} %bitcast.refs_0_.me_ref, bf16[4,3,2,72,256]{4,3,2,1,0:T(8,128)(2,1)S(1)} %get-tuple-element.55.refs_1_, bf16[4,3,2,72,256]{4,3,2,1,0:T(8,128)(2,1)S(1)} %collective-permute-done.8.refs_2_.refs_4_.refs_6_.refs_8_, ...), custom_call_target="tpu_custom_call" | custom-call | flops 2800000000 | bytes 8000000 | tf_op jit(solution)/shard_map/pallas_call | solution.py:437
  163.6 4.2 %collective-permute-start.29 = (s16[528,512]{1,0:T(8,128)(2,1)S(1)}, s16[528,512]{1,0:T(8,128)(2,1)S(1)}, u32[]{:S(2)}, u32[]{:S(2)}) collective-permute-start(s16[528,512]{1,0:T(8,128)(2,1)S(1)} %get-tuple-element.95), channel_id=1, source_target_pairs={{0,8},{4,12},{8,0},{12,4},{16,24},{20,28},{24,16},{28,20},{1,9},{5... | collective-permute-start | bytes 1622024 | tf_op jit(solution)/shard_map/ppermute | solution.py:451
  167.8 8.8 %collective-permute-done.22.refs_12_ = s16[528,256]{1,0:T(8,128)(2,1)S(1)} collective-permute-done((s16[528,256]{1,0:T(8,128)(2,1)S(1)}, s16[528,256]{1,0:T(8,128)(2,1)S(1)}, u32[]{:S(2)}, u32[]{:S(2)}) %collective-permute-start.22) | collective-permute-done | bytes 270368 | tf_op jit(solution)/shard_map/ppermute | solution.py:451
  176.6 6.1 %shard_map.113 = (f32[384,512]{1,0:T(8,128)S(1)}, s16[400,512]{1,0:T(8,128)(2,1)S(1)}, f32[8,128]{1,0:T(8,128)S(1)}) custom-call(s32[1]{0:T(128)} %bitcast.refs_0_.me_ref, bf16[4,3,2,72,256]{4,3,2,1,0:T(8,128)(2,1)S(1)} %get-tuple-element.55.refs_1_, bf16[4,3,2,72,256]{4,3,2,1,0:T(8,128)(2,1)S(1)} %collective-permute-done.8.refs_2_.refs_4_.refs_6_.refs_8_, ...), custom_call_target="tpu_custom_call" | custom-call | flops 2800000000 | bytes 8000000 | tf_op jit(solution)/shard_map/pallas_call | solution.py:437
  186.7 4.0 %collective-permute-done.17.heard_ref = s16[208,512]{1,0:T(8,128)(2,1)S(1)} collective-permute-done((s16[208,512]{1,0:T(8,128)(2,1)S(1)}, s16[208,512]{1,0:T(8,128)(2,1)S(1)}, u32[]{:S(2)}, u32[]{:S(2)}) %collective-permute-start.17) | collective-permute-done | bytes 213024 | tf_op jit(solution)/shard_map/ppermute | solution.py:451
  197.5 3.3 %collective-permute-done.30.refs_12_ = s16[528,256]{1,0:T(8,128)(2,1)S(1)} collective-permute-done((s16[528,256]{1,0:T(8,128)(2,1)S(1)}, s16[528,256]{1,0:T(8,128)(2,1)S(1)}, u32[]{:S(2)}, u32[]{:S(2)}) %collective-permute-start.30) | collective-permute-done | bytes 270368 | tf_op jit(solution)/shard_map/ppermute | solution.py:451
  200.9 5.6 %shard_map.117 = (f32[384,512]{1,0:T(8,128)S(1)}, s16[400,512]{1,0:T(8,128)(2,1)S(1)}, f32[8,128]{1,0:T(8,128)}) custom-call(s32[1]{0:T(128)} %bitcast.refs_0_.me_ref, bf16[4,3,2,72,256]{4,3,2,1,0:T(8,128)(2,1)S(1)} %get-tuple-element.55.refs_1_, bf16[4,3,2,72,256]{4,3,2,1,0:T(8,128)(2,1)S(1)} %collective-permute-done.8.refs_2_.refs_4_.refs_6_.refs_8_, ...), custom_call_target="tpu_custom_call" | custom-call | flops 2800000000 | bytes 8000000 | tf_op jit(solution)/shard_map/pallas_call | solution.py:437
  208.3 5.6 %collective-permute-done.26 = f32[192,256]{1,0:T(8,128)S(1)} collective-permute-done((f32[192,256]{1,0:T(8,128)S(1)}, f32[192,256]{1,0:T(8,128)S(1)}, u32[]{:S(2)}, u32[]{:S(2)}) %collective-permute-start.26) | collective-permute-done | bytes 196640 | tf_op jit(solution)/shard_map/ppermute | solution.py:451
  216.0 5.3 %collective-permute-done.32.heard_ref = s16[208,512]{1,0:T(8,128)(2,1)S(1)} collective-permute-done((s16[208,512]{1,0:T(8,128)(2,1)S(1)}, s16[208,512]{1,0:T(8,128)(2,1)S(1)}, u32[]{:S(2)}, u32[]{:S(2)}) %collective-permute-start.32) | collective-permute-done | bytes 213024 | tf_op jit(solution)/shard_map/ppermute | solution.py:451
  223.0 4.1 %collective-permute-done.33 = f32[192,256]{1,0:T(8,128)S(1)} collective-permute-done((f32[192,256]{1,0:T(8,128)S(1)}, f32[192,256]{1,0:T(8,128)S(1)}, u32[]{:S(2)}, u32[]{:S(2)}) %collective-permute-start.33) | collective-permute-done | bytes 196640 | tf_op jit(solution)/shard_map/ppermute | solution.py:451
  229.8 4.2 %collective-permute-done.34 = f32[192,128]{1,0:T(8,128)S(1)} collective-permute-done((f32[192,128]{1,0:T(8,128)S(1)}, f32[192,128]{1,0:T(8,128)S(1)}, u32[]{:S(2)}, u32[]{:S(2)}) %collective-permute-start.34) | collective-permute-done | bytes 98336 | tf_op jit(solution)/shard_map/ppermute | solution.py:451
  236.5 4.0 %collective-permute-done.35 = f32[192,64]{1,0:T(8,128)S(1)} collective-permute-done((f32[192,64]{1,0:T(8,128)S(1)}, f32[192,64]{1,0:T(8,128)S(1)}, u32[]{:S(2)}, u32[]{:S(2)}) %collective-permute-start.35) | collective-permute-done | bytes 49184 | tf_op jit(solution)/shard_map/ppermute | solution.py:451
  (194 shorter events, 65.9 us)
Async XLA Ops:
  1.2 43.3 %collective-permute-start.1 = (bf16[2,2,64,1024]{3,2,1,0:T(8,128)(2,1)S(1)}, bf16[2,2,64,1024]{3,2,1,0:T(8,128)(2,1)S(1)}, u32[]{:S(2)}, u32[]{:S(2)}) collective-permute-start(bf16[2,2,64,1024]{3,2,1,0:T(8,128)(2,1)S(1)} %bitcast.20), channel_id=1, source_target_pairs={{0,1},{1,0},{2,3},{3,2},{4,5},{5,4},{6,7},{7,6},{8,9},{9,8},{10,11... | collective-permute-start | bytes 1572872 | tf_op jit(solution)/shard_map/ppermute | solution.py:451
  1.7 21.1 %collective-permute-start.2 = (bf16[2,2,64,1024]{3,2,1,0:T(8,128)(2,1)S(1)}, bf16[2,2,64,1024]{3,2,1,0:T(8,128)(2,1)S(1)}, u32[]{:S(2)}, u32[]{:S(2)}) collective-permute-start(bf16[2,2,64,1024]{3,2,1,0:T(8,128)(2,1)S(1)} %bitcast.21), channel_id=1, source_target_pairs={{0,2},{1,3},{2,0},{3,1},{4,6},{5,7},{6,4},{7,5},{8,10},{9,11},{10,... | collective-permute-start | bytes 1572872 | tf_op jit(solution)/shard_map/ppermute | solution.py:451
  5.1 18.9 %collective-permute-start.4 = (bf16[1,2,64,1024]{3,2,1,0:T(8,128)(2,1)}, bf16[1,2,64,1024]{3,2,1,0:T(8,128)(2,1)}, u32[]{:S(2)}, u32[]{:S(2)}) collective-permute-start(bf16[1,2,64,1024]{3,2,1,0:T(8,128)(2,1)} %bitcast.18.refs_1_), channel_id=1, source_target_pairs={{0,1},{1,0},{2,3},{3,2},{4,5},{5,4},{6,7},{7,6},{8,9},{9,8},{10,11... | collective-permute-start | bytes 786440 | tf_op jit(solution)/shard_map/ppermute | solution.py:451
  5.2 17.3 %collective-permute-start.5 = (bf16[1,2,64,1024]{3,2,1,0:T(8,128)(2,1)}, bf16[1,2,64,1024]{3,2,1,0:T(8,128)(2,1)}, u32[]{:S(2)}, u32[]{:S(2)}) collective-permute-start(bf16[1,2,64,1024]{3,2,1,0:T(8,128)(2,1)} %bitcast.18.refs_1_), channel_id=1, source_target_pairs={{0,2},{1,3},{2,0},{3,1},{4,6},{5,7},{6,4},{7,5},{8,10},{9,11},{10,... | collective-permute-start | bytes 786440 | tf_op jit(solution)/shard_map/ppermute | solution.py:451
  8.4 53.0 %collective-permute-start = (bf16[4,3,2,72,256]{4,3,2,1,0:T(8,128)(2,1)}, bf16[4,3,2,72,256]{4,3,2,1,0:T(8,128)(2,1)S(1)}, u32[]{:S(2)}, u32[]{:S(2)}) collective-permute-start(bf16[4,3,2,72,256]{4,3,2,1,0:T(8,128)(2,1)} %get-tuple-element.56), channel_id=1, source_target_pairs={{0,4},{4,0},{8,12},{12,8},{16,20},{20,16},{24,28},{28,24},{1,5},{5... | collective-permute-start | bytes 2654216 | tf_op jit(solution)/shard_map/ppermute | solution.py:451
  22.8 21.8 %collective-permute-start.3 = (bf16[2,2,64,1024]{3,2,1,0:T(8,128)(2,1)S(1)}, bf16[2,2,64,1024]{3,2,1,0:T(8,128)(2,1)S(1)}, u32[]{:S(2)}, u32[]{:S(2)}) collective-permute-start(bf16[2,2,64,1024]{3,2,1,0:T(8,128)(2,1)S(1)} %collective-permute-done.2.refs_3_), channel_id=1, source_target_pairs={{0,1},{1,0},{2,3},{3,2},{4,5},{5,4},{6,7},{7,6},{8,9},{9,8},{10,11... | collective-permute-start | bytes 1572872 | tf_op jit(solution)/shard_map/ppermute | solution.py:451
  42.8 52.6 %collective-permute-start.9 = (s16[528,1024]{1,0:T(8,128)(2,1)}, s16[528,1024]{1,0:T(8,128)(2,1)}, u32[]{:S(2)}, u32[]{:S(2)}) collective-permute-start(s16[528,1024]{1,0:T(8,128)(2,1)} %get-tuple-element.64), channel_id=1, source_target_pairs={{0,4},{4,0},{8,12},{12,8},{16,20},{20,16},{24,28},{28,24},{1,5},{5... | collective-permute-start | bytes 3244040 | tf_op jit(solution)/shard_map/ppermute | solution.py:451
  63.0 36.8 %collective-permute-start.7 = (bf16[4,3,2,72,256]{4,3,2,1,0:T(8,128)(2,1)}, bf16[4,3,2,72,256]{4,3,2,1,0:T(8,128)(2,1)S(1)}, u32[]{:S(2)}, u32[]{:S(2)}) collective-permute-start(bf16[4,3,2,72,256]{4,3,2,1,0:T(8,128)(2,1)} %pad_maximum_fusion), channel_id=1, source_target_pairs={{0,8},{4,12},{8,0},{12,4},{16,24},{20,28},{24,16},{28,20},{1,9},{5... | collective-permute-start | bytes 2654216 | tf_op jit(solution)/shard_map/ppermute | solution.py:451
  65.4 10.9 %collective-permute-start.12 = (bf16[2,96,1024]{2,1,0:T(8,128)(2,1)}, bf16[2,96,1024]{2,1,0:T(8,128)(2,1)}, u32[]{:S(2)}, u32[]{:S(2)}) collective-permute-start(bf16[2,96,1024]{2,1,0:T(8,128)(2,1)} %bitcast.17.refs_0_), channel_id=1, source_target_pairs={{0,2},{1,3},{2,0},{3,1},{4,6},{5,7},{6,4},{7,5},{8,10},{9,11},{10,... | collective-permute-start | bytes 1179656 | tf_op jit(solution)/shard_map/ppermute | solution.py:451
  69.0 35.2 %collective-permute-start.11 = (bf16[2,96,1024]{2,1,0:T(8,128)(2,1)}, bf16[2,96,1024]{2,1,0:T(8,128)(2,1)}, u32[]{:S(2)}, u32[]{:S(2)}) collective-permute-start(bf16[2,96,1024]{2,1,0:T(8,128)(2,1)} %bitcast.17.refs_0_), channel_id=1, source_target_pairs={{0,1},{1,0},{2,3},{3,2},{4,5},{5,4},{6,7},{7,6},{8,9},{9,8},{10,11... | collective-permute-start | bytes 1179656 | tf_op jit(solution)/shard_map/ppermute | solution.py:451
  76.4 31.1 %collective-permute-start.13 = (bf16[2,96,1024]{2,1,0:T(8,128)(2,1)}, bf16[2,96,1024]{2,1,0:T(8,128)(2,1)}, u32[]{:S(2)}, u32[]{:S(2)}) collective-permute-start(bf16[2,96,1024]{2,1,0:T(8,128)(2,1)} %collective-permute-done.12.refs_2_), channel_id=1, source_target_pairs={{0,1},{1,0},{2,3},{3,2},{4,5},{5,4},{6,7},{7,6},{8,9},{9,8},{10,11... | collective-permute-start | bytes 1179656 | tf_op jit(solution)/shard_map/ppermute | solution.py:451
  76.4 50.9 %collective-permute-start.15 = (s16[528,1024]{1,0:T(8,128)(2,1)}, s16[528,1024]{1,0:T(8,128)(2,1)}, u32[]{:S(2)}, u32[]{:S(2)}) collective-permute-start(s16[528,1024]{1,0:T(8,128)(2,1)} %copy-done.20), channel_id=1, source_target_pairs={{0,4},{4,0},{8,12},{12,8},{16,20},{20,16},{24,28},{28,24},{1,5},{5... | collective-permute-start | bytes 3244040 | tf_op jit(solution)/shard_map/ppermute | solution.py:451
  99.5 26.2 %collective-permute-start.10 = (s16[528,512]{1,0:T(8,128)(2,1)}, s16[528,512]{1,0:T(8,128)(2,1)S(1)}, u32[]{:S(2)}, u32[]{:S(2)}) collective-permute-start(s16[528,512]{1,0:T(8,128)(2,1)} %get-tuple-element.65), channel_id=1, source_target_pairs={{0,8},{4,12},{8,0},{12,4},{16,24},{20,28},{24,16},{28,20},{1,9},{5... | collective-permute-start | bytes 1622024 | tf_op jit(solution)/shard_map/ppermute | solution.py:451
  101.0 53.5 %collective-permute-start.8 = (bf16[4,3,2,72,256]{4,3,2,1,0:T(8,128)(2,1)}, bf16[4,3,2,72,256]{4,3,2,1,0:T(8,128)(2,1)S(1)}, u32[]{:S(2)}, u32[]{:S(2)}) collective-permute-start(bf16[4,3,2,72,256]{4,3,2,1,0:T(8,128)(2,1)} %pad_maximum_fusion.1), channel_id=1, source_target_pairs={{0,16},{4,20},{8,24},{12,28},{16,0},{20,4},{24,8},{28,12},{1,17},{... | collective-permute-start | bytes 2654216 | tf_op jit(solution)/shard_map/ppermute | solution.py:451
  104.2 58.1 %collective-permute-start.23 = (s16[528,1024]{1,0:T(8,128)(2,1)}, s16[528,1024]{1,0:T(8,128)(2,1)S(1)}, u32[]{:S(2)}, u32[]{:S(2)}) collective-permute-start(s16[528,1024]{1,0:T(8,128)(2,1)} %copy-done.19), channel_id=1, source_target_pairs={{0,4},{4,0},{8,12},{12,8},{16,20},{20,16},{24,28},{28,24},{1,5},{5... | collective-permute-start | bytes 3244040 | tf_op jit(solution)/shard_map/ppermute | solution.py:451
  130.3 30.3 %collective-permute-start.21 = (s16[528,512]{1,0:T(8,128)(2,1)S(1)}, s16[528,512]{1,0:T(8,128)(2,1)S(1)}, u32[]{:S(2)}, u32[]{:S(2)}) collective-permute-start(s16[528,512]{1,0:T(8,128)(2,1)S(1)} %get-tuple-element.82), channel_id=1, source_target_pairs={{0,8},{4,12},{8,0},{12,4},{16,24},{20,28},{24,16},{28,20},{1,9},{5... | collective-permute-start | bytes 1622024 | tf_op jit(solution)/shard_map/ppermute | solution.py:451
  130.3 24.1 %collective-permute-start.14 = (s16[528,256]{1,0:T(8,128)(2,1)S(1)}, s16[528,256]{1,0:T(8,128)(2,1)S(1)}, u32[]{:S(2)}, u32[]{:S(2)}) collective-permute-start(s16[528,256]{1,0:T(8,128)(2,1)S(1)} %get-tuple-element.70), channel_id=1, source_target_pairs={{0,16},{4,20},{8,24},{12,28},{16,0},{20,4},{24,8},{28,12},{1,17},{... | collective-permute-start | bytes 811016 | tf_op jit(solution)/shard_map/ppermute | solution.py:451
  162.2 14.4 %collective-permute-start.22 = (s16[528,256]{1,0:T(8,128)(2,1)S(1)}, s16[528,256]{1,0:T(8,128)(2,1)S(1)}, u32[]{:S(2)}, u32[]{:S(2)}) collective-permute-start(s16[528,256]{1,0:T(8,128)(2,1)S(1)} %get-tuple-element.84), channel_id=1, source_target_pairs={{0,16},{4,20},{8,24},{12,28},{16,0},{20,4},{24,8},{28,12},{1,17},{... | collective-permute-start | bytes 811016 | tf_op jit(solution)/shard_map/ppermute | solution.py:451
  162.3 20.4 %collective-permute-start.16 = (s16[400,512]{1,0:T(8,128)(2,1)S(1)}, s16[400,512]{1,0:T(8,128)(2,1)S(1)}, u32[]{:S(2)}, u32[]{:S(2)}) collective-permute-start(s16[400,512]{1,0:T(8,128)(2,1)S(1)} %get-tuple-element.77), channel_id=1, source_target_pairs={{0,1},{1,0},{2,3},{3,2},{4,5},{5,4},{6,7},{7,6},{8,9},{9,8},{10,11... | collective-permute-start | bytes 1228808 | tf_op jit(solution)/shard_map/ppermute | solution.py:451
  163.6 21.8 %collective-permute-start.29 = (s16[528,512]{1,0:T(8,128)(2,1)S(1)}, s16[528,512]{1,0:T(8,128)(2,1)S(1)}, u32[]{:S(2)}, u32[]{:S(2)}) collective-permute-start(s16[528,512]{1,0:T(8,128)(2,1)S(1)} %get-tuple-element.95), channel_id=1, source_target_pairs={{0,8},{4,12},{8,0},{12,4},{16,24},{20,28},{24,16},{28,20},{1,9},{5... | collective-permute-start | bytes 1622024 | tf_op jit(solution)/shard_map/ppermute | solution.py:451
  182.6 9.7 %collective-permute-start.24 = (s16[400,512]{1,0:T(8,128)(2,1)S(1)}, s16[400,512]{1,0:T(8,128)(2,1)S(1)}, u32[]{:S(2)}, u32[]{:S(2)}) collective-permute-start(s16[400,512]{1,0:T(8,128)(2,1)S(1)} %get-tuple-element.90), channel_id=1, source_target_pairs={{0,1},{1,0},{2,3},{3,2},{4,5},{5,4},{6,7},{7,6},{8,9},{9,8},{10,11... | collective-permute-start | bytes 1228808 | tf_op jit(solution)/shard_map/ppermute | solution.py:451
  186.4 14.5 %collective-permute-start.30 = (s16[528,256]{1,0:T(8,128)(2,1)S(1)}, s16[528,256]{1,0:T(8,128)(2,1)S(1)}, u32[]{:S(2)}, u32[]{:S(2)}) collective-permute-start(s16[528,256]{1,0:T(8,128)(2,1)S(1)} %get-tuple-element.97), channel_id=1, source_target_pairs={{0,16},{4,20},{8,24},{12,28},{16,0},{20,4},{24,8},{28,12},{1,17},{... | collective-permute-start | bytes 811016 | tf_op jit(solution)/shard_map/ppermute | solution.py:451
  192.7 13.8 %collective-permute-start.25 = (s16[208,512]{1,0:T(8,128)(2,1)S(1)}, s16[208,512]{1,0:T(8,128)(2,1)S(1)}, u32[]{:S(2)}, u32[]{:S(2)}) collective-permute-start(s16[208,512]{1,0:T(8,128)(2,1)S(1)} %get-tuple-element.92), channel_id=1, source_target_pairs={{0,2},{1,3},{2,0},{3,1},{4,6},{5,7},{6,4},{7,5},{8,10},{9,11},{10,... | collective-permute-start | bytes 638984 | tf_op jit(solution)/shard_map/ppermute | solution.py:451
  197.4 10.7 %collective-permute-start.19 = (f32[192,128]{1,0:T(8,128)S(1)}, f32[192,128]{1,0:T(8,128)S(1)}, u32[]{:S(2)}, u32[]{:S(2)}) collective-permute-start(f32[192,128]{1,0:T(8,128)S(1)} %slice.101), channel_id=1, source_target_pairs={{0,8},{4,12},{8,0},{12,4},{16,24},{20,28},{24,16},{28,20},{1,9},{5... | collective-permute-start | bytes 294920 | tf_op jit(solution)/shard_map/ppermute | solution.py:451
  (46 other events, 342.7 us)

commit v6 on v5

--- a/solution.py
+++ b/solution.py
@@ -190,7 +190,7 @@
             jax.ShapeDtypeStruct((height, columns), jnp.float32),
             TOKEN,
         ],
-        compiler_params=params(24),
+        compiler_params=params(42),
         cost_estimate=cost(
             2 * height * 2 * depth * 2 * columns, 8 * depth * columns + 6 * height * columns
         ),
@@ -233,41 +233,50 @@
     )(me, keep, *others, *after)
 
 
-def fold_kernel(me_ref, own_ref, heard_ref, keep_ref, go_ref):
+def fold_kernel(*refs):
+    own_ref, heard_ref, keep_ref, go_ref = refs
     total = own_ref[...] + decode(heard_ref)
-    if go_ref.dtype == jnp.int16:
-        rows = keep_ref.shape[0]
-        keep_ref[...] = total[:rows]
-        encode(total[rows:], go_ref)
-    else:
-        cols = keep_ref.shape[1]
-        keep_ref[...] = total[:, :cols]
-        go_ref[...] = total[:, cols:]
-
-
-def fold_call(own, heard, me, by_rows):
+    rows = keep_ref.shape[0]
+    keep_ref[...] = total[:rows]
+    encode(total[rows:], go_ref)
+
+
+def fold_call(own, heard):
     rows, cols = own.shape
-    if by_rows:
-        shapes = [
-            jax.ShapeDtypeStruct((rows // 2, cols), jnp.float32),
-            jax.ShapeDtypeStruct((rows // 2 + EXP_ROWS, cols), jnp.int16),
-        ]
-    else:
-        shapes = [jax.ShapeDtypeStruct((rows, cols // 2), jnp.float32)] * 2
-    whole = lambda a: pl.BlockSpec(a.shape, lambda i, me: (0, 0))
-    grid_spec = pltpu.PrefetchScalarGridSpec(
-        num_scalar_prefetch=1,
-        grid=(1,),
-        in_specs=[whole(own), whole(heard)],
-        out_specs=[whole(a) for a in shapes],
-    )
+    shapes = [
+        jax.ShapeDtypeStruct((rows // 2, cols), jnp.float32),
+        jax.ShapeDtypeStruct((rows // 2 + EXP_ROWS, cols), jnp.int16),
+    ]
     return pl.pallas_call(
         fold_kernel,
-        grid_spec=grid_spec,
         out_shape=shapes,
         compiler_params=params(16),
         cost_estimate=cost(20 * own.size, 10 * own.size),
-    )(me, own, heard)
+    )(own, heard)
+
+
+def pack_kernel(own_ref, *refs):
+    heard_refs, out_ref = refs[:-1], refs[-1]
+    total = own_ref[...]
+    for ref in heard_refs:
+        total = total + decode(ref)
+    rows = out_ref.shape[1]
+    first = lax.broadcasted_iota(jnp.int32, (rows, 128), 1) < 64
+    for block in range(out_ref.shape[0] // 2):
+        cols = slice(block * 128, (block + 1) * 128)
+        real, imag = total[:rows, cols], total[rows:, cols]
+        out_ref[2 * block] = jnp.where(first, real, pltpu.roll(imag, 64, 1))
+        out_ref[2 * block + 1] = jnp.where(first, pltpu.roll(real, 64, 1), imag)
+
+
+def pack_call(own, heard):
+    rows, cols = own.shape
+    return pl.pallas_call(
+        pack_kernel,
+        out_shape=jax.ShapeDtypeStruct((cols // 64, rows // 2, 128), jnp.float32),
+        compiler_params=params(16),
+        cost_estimate=cost(20 * own.size, 10 * own.size),
+    )(own, *heard)
 
 
 def exchange_kernel(slots, waits, *refs):
@@ -327,7 +336,7 @@
     con_refs, keep_ref = refs[:slots], refs[slots]
     heard_refs = refs[slots + 1 : slots + 1 + heard]
     exch_ref, row_ref, col_direct_ref, col_exch_ref = refs[slots + 1 + heard : slots + 5 + heard]
-    keep_out, go_out, token_ref, con_all, direct_ref, natural_ref, sums_ref = refs[
+    keep_out, *go_outs, token_ref, con_all, direct_ref, natural_ref, sums_ref = refs[
         slots + 5 + heard + waits :
     ]
     token_ref[...] = jnp.zeros_like(token_ref)
@@ -386,14 +395,19 @@
                 term = mm(moved, pick_cols[...])
                 result = term if result is None else result + term
         for chunk in range(chunks):
-            out_ref = keep_out if chunk < chunks // 2 else sums_ref
-            at = (2 * (chunk % (chunks // 2)) + part) * count
-            out_ref[at : at + count, :] = result[chunk * count : (chunk + 1) * count]
-    encode(sums_ref[...], go_out)
+            at = (2 * chunk + part) * count
+            sums_ref[at : at + count, :] = result[chunk * count : (chunk + 1) * count]
+    stays = keep_out.shape[0]
+    keep_out[...] = sums_ref[0:stays, :]
+    at = stays
+    for out_ref in go_outs:
+        rows = out_ref.shape[0] - EXP_ROWS
+        encode(sums_ref[at : at + rows, :], out_ref)
+        at += rows
 
 
 def tile_call(
-    cons, point, keep, heard, exch, me, order, pick_rows, col_direct, col_exch, chunks, after
+    cons, point, keep, heard, exch, me, order, pick_rows, col_direct, col_exch, chunks, after, direct
 ):
     slots = len(cons)
     _, _, _, rows, width = cons[0][0].shape
@@ -401,7 +415,10 @@
     pitch = -(-rows // 16) * 16
     out_cols = col_direct.shape[1]
     stages = len(heard)
-    whole = lambda a: pl.BlockSpec(a.shape, lambda i, me: (0,) * a.ndim)
+    whole = lambda a: pl.BlockSpec(a.shape, lambda i, me: (0,) * len(a.shape))
+    each, others = (2 * NT // chunks, chunks - 1) if direct else (NT, 1)
+    shapes = [jax.ShapeDtypeStruct((each, out_cols), jnp.float32)]
+    shapes += [jax.ShapeDtypeStruct((each + EXP_ROWS, out_cols), jnp.int16)] * others + [TOKEN]
 
     def at(known):
         return lambda i, me: (0, block_of(me[0], known, stages, False))
@@ -422,26 +439,18 @@
             whole(col_exch),
         ]
         + [pl.BlockSpec(memory_space=pl.ANY) for _ in after],
-        out_specs=[
-            pl.BlockSpec((NT, out_cols), lambda i, me: (0, 0)),
-            pl.BlockSpec((NT + EXP_ROWS, out_cols), lambda i, me: (0, 0)),
-            pl.BlockSpec(TOKEN.shape, lambda i, me: (0, 0)),
-        ],
+        out_specs=[whole(a) for a in shapes],
         scratch_shapes=[
             pltpu.VMEM((slots * pitch, 2 * width), jnp.bfloat16),
             pltpu.VMEM((height // 128, NC * NC, 128), jnp.float32),
             pltpu.VMEM((2, NT, NT), jnp.float32),
-            pltpu.VMEM((NT, out_cols), jnp.float32),
+            pltpu.VMEM((2 * NT, out_cols), jnp.float32),
         ],
     )
     return pl.pallas_call(
         lambda *refs: tile_kernel(order, stages, chunks, len(after), *refs),
         grid_spec=grid_spec,
-        out_shape=[
-            jax.ShapeDtypeStruct((NT, out_cols), jnp.float32),
-            jax.ShapeDtypeStruct((NT + EXP_ROWS, out_cols), jnp.int16),
-            TOKEN,
-        ],
+        out_shape=shapes,
         compiler_params=params(24),
         cost_estimate=cost(2.8e9, 8e6),
     )(me, *[c for c, _ in cons], keep, *heard, exch, pick_rows, col_direct, col_exch, *after)
@@ -451,12 +460,13 @@
     return lax.ppermute(value, axis, [(i, i ^ bit) for i in range(size)])
 
 
-def gather_slots(value, axis, size):
+def gather_slots(value, axis, size, token=None):
     found = {0: value}
     bit = size // 2
     while bit:
         for known in sorted(found):
-            found[known ^ bit] = swap(found[known], axis, size, bit)
+            ready = found[known] if token is None or not known else behind(found[known], token)
+            found[known ^ bit] = swap(ready, axis, size, bit)
         bit //= 2
     return [found[r] for r in range(size)]
 
@@ -486,11 +496,12 @@
     stages, half = len(ga_bits), ga // 2
 
     first = gather_slots(jnp.transpose(val_density[:, :1], (1, 2, 0, 3)), "pair", pair)
-    others = gather_slots(jnp.transpose(val_density[:, 1:], (1, 2, 0, 3)), "pair", pair)
 
     con = jnp.transpose(con_density, (1, 2, 0, 3))
     stay, go, token = shift_call(con, shift_map, me, ga_order, width)
     from_near = swap(go, "ga", ga, ga_bits[0])
+    others = behind(val_density[:, 1:], first[pair // 2])
+    others = gather_slots(jnp.transpose(others, (1, 2, 0, 3)), "pair", pair)
 
     gone, keep, tokens = [], [], [token]
     for q in range(points):
@@ -504,15 +515,14 @@
     cons = {}
     for p, slot in enumerate(ga_order):
         cons[slot] = (stay, p) if p < half else (go, p - half)
-    for step, bit in enumerate(ga_bits):
+    for step, bit in enumerate(ga_bits[:1] + ga_bits[:0:-1]):
         moving = [slot for slot in ga_order if slot & bit]
         if step == 0:
             got = from_near
         else:
-            sent = jnp.stack([cons[slot][0][cons[slot][1]] for slot in moving])
-            got = swap(sent, "ga", ga, bit)
+            got = swap(jnp.stack([cons[slot][0][cons[slot][1]] for slot in moving]), "ga", ga, bit)
         if step + 1 < stages:
-            got = behind(got, tokens[min(step + 2, points)])
+            got = behind(got, tokens[min(2 * step + 1, points)])
         for place, slot in enumerate(moving):
             cons[slot] = (got, place)
     cons = [cons[slot] for slot in ga_order]
@@ -536,7 +546,7 @@
     col_direct, col_exch = pick_cols(at_direct, NT, -1.0), pick_cols(at_exch, row_count, 2.0)
 
     heard = [[swap(gone[q], "ga", ga, ga_bits[0])] for q in range(points)]
-    outs = [None] * points
+    packed = [None] * points
     exch = None
     for wave in range(2 * points + stages):
         for q in reversed(range(points)):
@@ -547,27 +557,39 @@
                 after = [token]
                 heard[q].append(swap(coded, "ga", ga, ga_bits[stage]))
                 if exch is None:
-                    heres = gather_slots(
-                        jnp.transpose(behind(trans_here, tokens[1]), (1, 0, 2)), "pair", pair
-                    )
+                    here = jnp.transpose(behind(trans_here, tokens[1]), (1, 0, 2))
+                    heres = gather_slots(here, "pair", pair, tokens[-1])
                     there = jnp.transpose(behind(trans_there, tokens[1]), (1, 2, 0, 3))
                     exch, token = exchange_call(heres, there, coulomb, after)
                     after = [token]
             elif stage == stages:
-                tile, sent, token = tile_call(
+                last = q == points - 1
+                tile, *sent, token = tile_call(
                     cons, q, keep[q], heard[q], exch, me, ga_order, pick_rows, col_direct,
-                    col_exch, pair, after,
+                    col_exch, pair, after, last,
                 )
                 after = [token]
-                for step, bit in enumerate(pair_bits):
+                if last:
+                    slots = halving_order(pair_bits)[1:]
+                    got = [swap(part, "pair", pair, slot) for slot, part in zip(slots, sent)]
+                    packed[q] = pack_call(tile, got)
+                    continue
+                got = swap(sent[0], "pair", pair, pair_bits[0])
+                for bit in pair_bits[1:]:
+                    tile, sent = fold_call(tile, got)
                     got = swap(sent, "pair", pair, bit)
-                    tile, sent = fold_call(tile, got, me, step + 1 < len(pair_bits))
-                tile = tile + swap(sent, "ga", ga, ga_bits[0])
-                for bit in ga_bits[1:]:
-                    cols = tile.shape[1] // 2
-                    tile = tile[:, :cols] + swap(tile[:, cols:], "ga", ga, bit)
-                outs[q] = tile[:, :col_count].reshape(2, row_count, col_count)
-    return jnp.stack(outs)
+                packed[q] = pack_call(tile, [got])
+    early = jnp.stack(packed[:-1], axis=1)
+    for bit in ga_bits:
+        size = early.shape[0] // 2
+        early = early[:size] + swap(early[size:], "ga", ga, bit)
+    late = packed[-1]
+    total = late[0]
+    for place, slot in enumerate(ga_order[1:]):
+        total = total + swap(late[place + 1], "ga", ga, slot)
+    out = jnp.concatenate([early[0], total[None]])
+    out = out.reshape(points, row_count, 2, 64)[..., :col_count]
+    return jnp.transpose(out, (0, 2, 1, 3))
 
 
 def contract_float(left, right):

time: 242 us -> 205 us (0.85)
  local copies, waits for them, and re-layouts: 38.8 us -> 15.5 us
  waiting for transfers between devices: 102 us -> 84.7 us
  starting transfers between devices: 33.4 us -> 41.7 us
  other arithmetic: 5.14 us -> 2.27 us
    unnamed x65 -> x42, local copies, waits for them, and re-layouts: 32.7 us -> 7.73 us
    ppermute x36 -> x38, waiting for transfers between devices: 102 us -> 84.7 us  [swap(): return lax.ppermute(value, axis, [(i, i ^ bit) for i in range(size)])]
    ppermute x36 -> x38, starting transfers between devices: 33.4 us -> 41.7 us  [swap(): return lax.ppermute(value, axis, [(i, i ^ bit) for i in range(size)])]
    pallas_call x6, Pallas kernels: 12.2 us -> 8.33 us  [hop_call(): pl.pallas_call(lambda *refs: hop_kernel(len(others), *refs), grid_spec=gr...]
  transfers between devices with their start and end apart: 36 -> 38, of which waited for: 16 -> 18; matrix products, arithmetic and copies ran while one was open for 5% -> 5% of each run, Pallas kernels for 25% -> 29%
where the time goes in v6:
time: 205 us; the launch traced here: 204 us
  waiting for transfers between devices  84.7 us (41%)
  Pallas kernels  59.2 us (29%)
  starting transfers between devices  41.7 us (20%)
  local copies, waits for them, and re-layouts  15.5 us (8%)
  other arithmetic  2.27 us (1%)
    ppermute x38, waiting for transfers between devices, swap(): return lax.ppermute(value, axis, [(i, i ^ bit) for i in range(size)])  84.7 us
    ppermute x38, starting transfers between devices, swap(): return lax.ppermute(value, axis, [(i, i ^ bit) for i in range(size)])  41.7 us
    pallas_call x3, Pallas kernels, x_call(): pl.pallas_call(lambda *refs: x_kernel(slots, len(after), *refs), grid_spe...  25.6 us
    pallas_call x3, Pallas kernels, tile_call(): pl.pallas_call(lambda *refs: tile_kernel(order, stages, chunks, len(after...  18.6 us
    pallas_call x6, Pallas kernels, hop_call(): pl.pallas_call(lambda *refs: hop_kernel(len(others), *refs), grid_spec=gr...  8.33 us
    unnamed x42, local copies, waits for them, and re-layouts  7.73 us
  transfers between devices with their start and end apart: 38, of which 18 were waited for; matrix products, arithmetic and copies ran while one was open for 5% of the time, Pallas kernels for 29%

profile of v6, /device:TPU:0, one launch (start us, length us, event | category | flops | bytes accessed | tf_op | source)
XLA Modules:
  0.0 203.9 jit_solution(18432135133445800977)
XLA Ops:
  1.7 2.6 %collective-permute-start.2 = (bf16[1,2,64,1024]{3,2,1,0:T(8,128)(2,1)S(1)}, bf16[1,2,64,1024]{3,2,1,0:T(8,128)(2,1)S(1)}, u32[]{:S(2)}, u32[]{:S(2)}) collective-permute-start(bf16[1,2,64,1024]{3,2,1,0:T(8,128)(2,1)S(1)} %bitcast.61), channel_id=1, source_target_pairs={{0,2},{1,3},{2,0},{3,1},{4,6},{5,7},{6,4},{7,5},{8,10},{9,11},{10,... | collective-permute-start | bytes 786440 | tf_op jit(solution)/shard_map/ppermute | solution.py:460
  19.3 8.8 %shard_map.101 = (s16[528,1024]{1,0:T(8,128)(2,1)}, f32[512,1024]{1,0:T(8,128)S(1)}, f32[8,128]{1,0:T(8,128)S(1)}) custom-call(s32[1]{0:T(128)} %bitcast.refs_0_, bf16[1,2,64,1024]{3,2,1,0:T(8,128)(2,1)S(1)} %bitcast.62, bf16[1,2,64,1024]{3,2,1,0:T(8,128)(2,1)S(1)} %copy-done.5, bf16[1,2,64,1024]{3,2,1,0:T(8,128)(2,1)S(1)} %copy-done.7, ...), custom_call_target="tpu_custom_call" | custom-call | flops 4294967296 | bytes 11534336 | tf_op jit(solution)/shard_map/pallas_call | solution.py:185
  33.6 2.6 %collective-permute-start.4 = (bf16[4,3,2,72,256]{4,3,2,1,0:T(8,128)(2,1)}, bf16[4,3,2,72,256]{4,3,2,1,0:T(8,128)(2,1)S(1)}, u32[]{:S(2)}, u32[]{:S(2)}) collective-permute-start(bf16[4,3,2,72,256]{4,3,2,1,0:T(8,128)(2,1)} %pad_maximum_fusion), channel_id=1, source_target_pairs={{0,16},{4,20},{8,24},{12,28},{16,0},{20,4},{24,8},{28,12},{1,17},{... | collective-permute-start | bytes 2654216 | tf_op jit(solution)/shard_map/ppermute | solution.py:460
  38.2 8.4 %shard_map.102 = (s16[528,1024]{1,0:T(8,128)(2,1)S(1)}, f32[512,1024]{1,0:T(8,128)S(1)}, f32[8,128]{1,0:T(8,128)S(1)}) custom-call(s32[1]{0:T(128)} %bitcast.refs_0_, bf16[2,2,64,1024]{3,2,1,0:T(8,128)(2,1)S(1)} %bitcast.53, bf16[2,2,64,1024]{3,2,1,0:T(8,128)(2,1)} %collective-permute-done.5.refs_2_, ...), custom_call_target="tpu_custom_call" | custom-call | flops 4294967296 | bytes 11534336 | tf_op jit(solution)/shard_map/pallas_call | solution.py:185
  48.2 8.4 %shard_map.103 = (s16[528,1024]{1,0:T(8,128)(2,1)S(1)}, f32[512,1024]{1,0:T(8,128)S(1)}, f32[8,128]{1,0:T(8,128)S(1)}) custom-call(s32[1]{0:T(128)} %bitcast.refs_0_, bf16[2,2,64,1024]{3,2,1,0:T(8,128)(2,1)S(1)} %bitcast.54, bf16[2,2,64,1024]{3,2,1,0:T(8,128)(2,1)} %collective-permute-done.5.refs_2_, ...), custom_call_target="tpu_custom_call" | custom-call | flops 4294967296 | bytes 11534336 | tf_op jit(solution)/shard_map/pallas_call | solution.py:185
  56.7 2.7 %shard_map.104 = (s16[528,512]{1,0:T(8,128)(2,1)S(1)}, f32[8,128]{1,0:T(8,128)S(1)}) custom-call(s32[1]{0:T(128)} %bitcast.refs_0_, f32[512,1024]{1,0:T(8,128)S(1)} %get-tuple-element.60.refs_1_.refs_9_, s16[528,1024]{1,0:T(8,128)(2,1)} %collective-permute-done.9.refs_2_.refs_10_, f32[8,128]{1,0:T(8,128)S(1)} %get-tuple-element.58.refs_3_), custom_call_target="tpu_custom_call" | custom-call | flops 5242880 | bytes 2097152 | tf_op jit(solution)/shard_map/pallas_call | solution.py:227
  61.1 13.8 %collective-permute-done.4.refs_2_.refs_6_ = bf16[4,3,2,72,256]{4,3,2,1,0:T(8,128)(2,1)S(1)} collective-permute-done((bf16[4,3,2,72,256]{4,3,2,1,0:T(8,128)(2,1)}, bf16[4,3,2,72,256]{4,3,2,1,0:T(8,128)(2,1)S(1)}, u32[]{:S(2)}, u32[]{:S(2)}) %collective-permute-start.4) | collective-permute-done | bytes 884768 | tf_op jit(solution)/shard_map/ppermute | solution.py:460
  77.9 3.4 %shard_map.105 = (f32[3,2,384,96]{3,2,1,0:T(8,128)S(1)}, f32[8,128]{1,0:T(8,128)S(1)}) custom-call(bf16[2,96,1024]{2,1,0:T(8,128)(2,1)S(1)} %bitcast.65, bf16[2,96,1024]{2,1,0:T(8,128)(2,1)S(1)} %collective-permute-done.11.refs_1_, bf16[2,96,1024]{2,1,0:T(8,128)(2,1)S(1)} %collective-permute-done.12.refs_2_, ...), custom_call_target="tpu_custom_call" | custom-call | flops 1811939328 | bytes 2359296 | tf_op jit(solution)/shard_map/pallas_call | solution.py:314
  81.3 5.1 %collective-permute-done.10.refs_3_.refs_11_ = s16[528,512]{1,0:T(8,128)(2,1)S(1)} collective-permute-done((s16[528,512]{1,0:T(8,128)(2,1)S(1)}, s16[528,512]{1,0:T(8,128)(2,1)S(1)}, u32[]{:S(2)}, u32[]{:S(2)}) %collective-permute-start.10) | collective-permute-done | bytes 540704 | tf_op jit(solution)/shard_map/ppermute | solution.py:460
  90.8 2.5 %collective-permute-start.18 = (s16[528,512]{1,0:T(8,128)(2,1)S(1)}, s16[528,512]{1,0:T(8,128)(2,1)S(1)}, u32[]{:S(2)}, u32[]{:S(2)}) collective-permute-start(s16[528,512]{1,0:T(8,128)(2,1)S(1)} %get-tuple-element.78), channel_id=1, source_target_pairs={{0,8},{4,12},{8,0},{12,4},{16,24},{20,28},{24,16},{28,20},{1,9},{5... | collective-permute-start | bytes 1622024 | tf_op jit(solution)/shard_map/ppermute | solution.py:460
  93.5 8.2 %collective-permute-done.14.refs_12_ = s16[528,256]{1,0:T(8,128)(2,1)S(1)} collective-permute-done((s16[528,256]{1,0:T(8,128)(2,1)S(1)}, s16[528,256]{1,0:T(8,128)(2,1)S(1)}, u32[]{:S(2)}, u32[]{:S(2)}) %collective-permute-start.14) | collective-permute-done | bytes 270368 | tf_op jit(solution)/shard_map/ppermute | solution.py:460
  101.7 9.4 %collective-permute-done.8.refs_3_.refs_4_.refs_7_.refs_8_ = bf16[4,3,2,72,256]{4,3,2,1,0:T(8,128)(2,1)S(1)} collective-permute-done((bf16[4,3,2,72,256]{4,3,2,1,0:T(8,128)(2,1)S(1)}, bf16[4,3,2,72,256]{4,3,2,1,0:T(8,128)(2,1)S(1)}, u32[]{:S(2)}, u32[]{:S(2)}) %collective-permute-start.8) | collective-permute-done | bytes 884768 | tf_op jit(solution)/shard_map/ppermute | solution.py:460
  111.1 6.1 %shard_map.108 = (f32[384,512]{1,0:T(8,128)S(1)}, s16[400,512]{1,0:T(8,128)(2,1)S(1)}, f32[8,128]{1,0:T(8,128)S(1)}) custom-call(s32[1]{0:T(128)} %bitcast.refs_0_, bf16[4,3,2,72,256]{4,3,2,1,0:T(8,128)(2,1)S(1)} %copy-done.1, bf16[4,3,2,72,256]{4,3,2,1,0:T(8,128)(2,1)S(1)} %collective-permute-done.4.refs_2_.refs_6_, ...), custom_call_target="tpu_custom_call" | custom-call | flops 2800000000 | bytes 8000000 | tf_op jit(solution)/shard_map/pallas_call | solution.py:450
  117.2 5.4 %collective-permute-done.18.refs_3_.refs_11_ = s16[528,512]{1,0:T(8,128)(2,1)S(1)} collective-permute-done((s16[528,512]{1,0:T(8,128)(2,1)S(1)}, s16[528,512]{1,0:T(8,128)(2,1)S(1)}, u32[]{:S(2)}, u32[]{:S(2)}) %collective-permute-start.18) | collective-permute-done | bytes 540704 | tf_op jit(solution)/shard_map/ppermute | solution.py:460
  128.8 10.0 %collective-permute-done.19.refs_12_ = s16[528,256]{1,0:T(8,128)(2,1)S(1)} collective-permute-done((s16[528,256]{1,0:T(8,128)(2,1)S(1)}, s16[528,256]{1,0:T(8,128)(2,1)S(1)}, u32[]{:S(2)}, u32[]{:S(2)}) %collective-permute-start.19) | collective-permute-done | bytes 270368 | tf_op jit(solution)/shard_map/ppermute | solution.py:460
  138.8 6.0 %shard_map.113 = (f32[384,512]{1,0:T(8,128)S(1)}, s16[400,512]{1,0:T(8,128)(2,1)S(1)}, f32[8,128]{1,0:T(8,128)S(1)}) custom-call(s32[1]{0:T(128)} %bitcast.refs_0_, bf16[4,3,2,72,256]{4,3,2,1,0:T(8,128)(2,1)S(1)} %copy-done.1, bf16[4,3,2,72,256]{4,3,2,1,0:T(8,128)(2,1)S(1)} %collective-permute-done.4.refs_2_.refs_6_, ...), custom_call_target="tpu_custom_call" | custom-call | flops 2800000000 | bytes 8000000 | tf_op jit(solution)/shard_map/pallas_call | solution.py:450
  148.7 4.6 %collective-permute-done.17.refs_0_ = s16[208,512]{1,0:T(8,128)(2,1)S(1)} collective-permute-done((s16[208,512]{1,0:T(8,128)(2,1)S(1)}, s16[208,512]{1,0:T(8,128)(2,1)S(1)}, u32[]{:S(2)}, u32[]{:S(2)}) %collective-permute-start.17) | collective-permute-done | bytes 213024 | tf_op jit(solution)/shard_map/ppermute | solution.py:460
  153.4 4.0 %collective-permute-done.22.refs_0_ = s16[208,512]{1,0:T(8,128)(2,1)S(1)} collective-permute-done((s16[208,512]{1,0:T(8,128)(2,1)S(1)}, s16[208,512]{1,0:T(8,128)(2,1)S(1)}, u32[]{:S(2)}, u32[]{:S(2)}) %collective-permute-start.22) | collective-permute-done | bytes 213024 | tf_op jit(solution)/shard_map/ppermute | solution.py:460
  159.1 4.4 %collective-permute-done.27.refs_12_ = s16[528,256]{1,0:T(8,128)(2,1)S(1)} collective-permute-done((s16[528,256]{1,0:T(8,128)(2,1)S(1)}, s16[528,256]{1,0:T(8,128)(2,1)S(1)}, u32[]{:S(2)}, u32[]{:S(2)}) %collective-permute-start.27) | collective-permute-done | bytes 270368 | tf_op jit(solution)/shard_map/ppermute | solution.py:460
  163.4 6.6 %shard_map.117 = (f32[192,512]{1,0:T(8,128)S(1)}, s16[208,512]{1,0:T(8,128)(2,1)S(1)}, s16[208,512]{1,0:T(8,128)(2,1)S(1)}, s16[208,512]{1,0:T(8,128)(2,1)S(1)}, f32[8,128]{1,0:T(8,128)}) custom-call(s32[1]{0:T(128)} %bitcast.refs_0_, bf16[4,3,2,72,256]{4,3,2,1,0:T(8,128)(2,1)S(1)} %copy-done.1, ...), custom_call_target="tpu_custom_call" | custom-call | flops 2800000000 | bytes 8000000 | tf_op jit(solution)/shard_map/pallas_call | solution.py:450
  172.2 6.0 %collective-permute-done.28.refs_0_ = s16[208,512]{1,0:T(8,128)(2,1)S(1)} collective-permute-done((s16[208,512]{1,0:T(8,128)(2,1)S(1)}, s16[208,512]{1,0:T(8,128)(2,1)S(1)}, u32[]{:S(2)}, u32[]{:S(2)}) %collective-permute-start.28) | collective-permute-done | bytes 213024 | tf_op jit(solution)/shard_map/ppermute | solution.py:460
  178.1 2.6 %collective-permute-done.30.refs_2_ = s16[208,512]{1,0:T(8,128)(2,1)S(1)} collective-permute-done((s16[208,512]{1,0:T(8,128)(2,1)S(1)}, s16[208,512]{1,0:T(8,128)(2,1)S(1)}, u32[]{:S(2)}, u32[]{:S(2)}) %collective-permute-start.30) | collective-permute-done | bytes 213024 | tf_op jit(solution)/shard_map/ppermute | solution.py:460
  184.7 2.7 %collective-permute-start.35 = (f32[96,128]{1,0:T(8,128)S(1)}, f32[96,128]{1,0:T(8,128)S(1)}, u32[]{:S(2)}, u32[]{:S(2)}) collective-permute-start(f32[96,128]{1,0:T(8,128)S(1)} %get-tuple-element.108), channel_id=1, source_target_pairs={{0,20},{4,16},{8,28},{12,24},{16,4},{20,0},{24,12},{28,8},{1,21},{... | collective-permute-start | bytes 147464 | tf_op jit(solution)/shard_map/ppermute | solution.py:460
  197.3 4.2 %collective-permute-done.31 = f32[96,128]{1,0:T(8,128)S(1)} collective-permute-done((f32[96,128]{1,0:T(8,128)S(1)}, f32[96,128]{1,0:T(8,128)S(1)}, u32[]{:S(2)}, u32[]{:S(2)}) %collective-permute-start.31) | collective-permute-done | bytes 49184 | tf_op jit(solution)/shard_map/ppermute | solution.py:460
  (163 shorter events, 65.0 us)
Async XLA Ops:
  1.2 12.9 %collective-permute-start.1 = (bf16[1,2,64,1024]{3,2,1,0:T(8,128)(2,1)S(1)}, bf16[1,2,64,1024]{3,2,1,0:T(8,128)(2,1)S(1)}, u32[]{:S(2)}, u32[]{:S(2)}) collective-permute-start(bf16[1,2,64,1024]{3,2,1,0:T(8,128)(2,1)S(1)} %bitcast.60), channel_id=1, source_target_pairs={{0,1},{1,0},{2,3},{3,2},{4,5},{5,4},{6,7},{7,6},{8,9},{9,8},{10,11... | collective-permute-start | bytes 786440 | tf_op jit(solution)/shard_map/ppermute | solution.py:460
  1.7 10.6 %collective-permute-start.2 = (bf16[1,2,64,1024]{3,2,1,0:T(8,128)(2,1)S(1)}, bf16[1,2,64,1024]{3,2,1,0:T(8,128)(2,1)S(1)}, u32[]{:S(2)}, u32[]{:S(2)}) collective-permute-start(bf16[1,2,64,1024]{3,2,1,0:T(8,128)(2,1)S(1)} %bitcast.61), channel_id=1, source_target_pairs={{0,2},{1,3},{2,0},{3,1},{4,6},{5,7},{6,4},{7,5},{8,10},{9,11},{10,... | collective-permute-start | bytes 786440 | tf_op jit(solution)/shard_map/ppermute | solution.py:460
  8.6 22.0 %collective-permute-start = (bf16[4,3,2,72,256]{4,3,2,1,0:T(8,128)(2,1)}, bf16[4,3,2,72,256]{4,3,2,1,0:T(8,128)(2,1)}, u32[]{:S(2)}, u32[]{:S(2)}) collective-permute-start(bf16[4,3,2,72,256]{4,3,2,1,0:T(8,128)(2,1)} %get-tuple-element.52), channel_id=1, source_target_pairs={{0,4},{4,0},{8,12},{12,8},{16,20},{20,16},{24,28},{28,24},{1,5},{5... | collective-permute-start | bytes 2654216 | tf_op jit(solution)/shard_map/ppermute | solution.py:460
  13.2 16.5 %collective-permute-start.6 = (bf16[2,2,64,1024]{3,2,1,0:T(8,128)(2,1)S(1)}, bf16[2,2,64,1024]{3,2,1,0:T(8,128)(2,1)}, u32[]{:S(2)}, u32[]{:S(2)}) collective-permute-start(bf16[2,2,64,1024]{3,2,1,0:T(8,128)(2,1)S(1)} %bitcast.51), channel_id=1, source_target_pairs={{0,2},{1,3},{2,0},{3,1},{4,6},{5,7},{6,4},{7,5},{8,10},{9,11},{10,... | collective-permute-start | bytes 1572872 | tf_op jit(solution)/shard_map/ppermute | solution.py:460
  13.9 23.8 %collective-permute-start.5 = (bf16[2,2,64,1024]{3,2,1,0:T(8,128)(2,1)S(1)}, bf16[2,2,64,1024]{3,2,1,0:T(8,128)(2,1)}, u32[]{:S(2)}, u32[]{:S(2)}) collective-permute-start(bf16[2,2,64,1024]{3,2,1,0:T(8,128)(2,1)S(1)} %bitcast.52), channel_id=1, source_target_pairs={{0,1},{1,0},{2,3},{3,2},{4,5},{5,4},{6,7},{7,6},{8,9},{9,8},{10,11... | collective-permute-start | bytes 1572872 | tf_op jit(solution)/shard_map/ppermute | solution.py:460
  28.1 28.5 %collective-permute-start.9 = (s16[528,1024]{1,0:T(8,128)(2,1)}, s16[528,1024]{1,0:T(8,128)(2,1)}, u32[]{:S(2)}, u32[]{:S(2)}) collective-permute-start(s16[528,1024]{1,0:T(8,128)(2,1)} %get-tuple-element.61), channel_id=1, source_target_pairs={{0,4},{4,0},{8,12},{12,8},{16,20},{20,16},{24,28},{28,24},{1,5},{5... | collective-permute-start | bytes 3244040 | tf_op jit(solution)/shard_map/ppermute | solution.py:460
  33.6 41.2 %collective-permute-start.4 = (bf16[4,3,2,72,256]{4,3,2,1,0:T(8,128)(2,1)}, bf16[4,3,2,72,256]{4,3,2,1,0:T(8,128)(2,1)S(1)}, u32[]{:S(2)}, u32[]{:S(2)}) collective-permute-start(bf16[4,3,2,72,256]{4,3,2,1,0:T(8,128)(2,1)} %pad_maximum_fusion), channel_id=1, source_target_pairs={{0,16},{4,20},{8,24},{12,28},{16,0},{20,4},{24,8},{28,12},{1,17},{... | collective-permute-start | bytes 2654216 | tf_op jit(solution)/shard_map/ppermute | solution.py:460
  37.5 38.9 %collective-permute-start.11 = (bf16[2,96,1024]{2,1,0:T(8,128)(2,1)S(1)}, bf16[2,96,1024]{2,1,0:T(8,128)(2,1)S(1)}, u32[]{:S(2)}, u32[]{:S(2)}) collective-permute-start(bf16[2,96,1024]{2,1,0:T(8,128)(2,1)S(1)} %bitcast.63), channel_id=1, source_target_pairs={{0,1},{1,0},{2,3},{3,2},{4,5},{5,4},{6,7},{7,6},{8,9},{9,8},{10,11... | collective-permute-start | bytes 1179656 | tf_op jit(solution)/shard_map/ppermute | solution.py:460
  37.6 19.0 %collective-permute-start.12 = (bf16[2,96,1024]{2,1,0:T(8,128)(2,1)S(1)}, bf16[2,96,1024]{2,1,0:T(8,128)(2,1)S(1)}, u32[]{:S(2)}, u32[]{:S(2)}) collective-permute-start(bf16[2,96,1024]{2,1,0:T(8,128)(2,1)S(1)} %bitcast.64), channel_id=1, source_target_pairs={{0,2},{1,3},{2,0},{3,1},{4,6},{5,7},{6,4},{7,5},{8,10},{9,11},{10,... | collective-permute-start | bytes 1179656 | tf_op jit(solution)/shard_map/ppermute | solution.py:460
  46.6 42.9 %collective-permute-start.15 = (s16[528,1024]{1,0:T(8,128)(2,1)S(1)}, s16[528,1024]{1,0:T(8,128)(2,1)S(1)}, u32[]{:S(2)}, u32[]{:S(2)}) collective-permute-start(s16[528,1024]{1,0:T(8,128)(2,1)S(1)} %get-tuple-element.71), channel_id=1, source_target_pairs={{0,4},{4,0},{8,12},{12,8},{16,20},{20,16},{24,28},{28,24},{1,5},{5... | collective-permute-start | bytes 3244040 | tf_op jit(solution)/shard_map/ppermute | solution.py:460
  56.6 21.3 %collective-permute-start.13 = (bf16[2,96,1024]{2,1,0:T(8,128)(2,1)S(1)}, bf16[2,96,1024]{2,1,0:T(8,128)(2,1)S(1)}, u32[]{:S(2)}, u32[]{:S(2)}) collective-permute-start(bf16[2,96,1024]{2,1,0:T(8,128)(2,1)S(1)} %collective-permute-done.12.refs_2_), channel_id=1, source_target_pairs={{0,1},{1,0},{2,3},{3,2},{4,5},{5,4},{6,7},{7,6},{8,9},{9,8},{10,11... | collective-permute-start | bytes 1179656 | tf_op jit(solution)/shard_map/ppermute | solution.py:460
  59.4 26.9 %collective-permute-start.10 = (s16[528,512]{1,0:T(8,128)(2,1)S(1)}, s16[528,512]{1,0:T(8,128)(2,1)S(1)}, u32[]{:S(2)}, u32[]{:S(2)}) collective-permute-start(s16[528,512]{1,0:T(8,128)(2,1)S(1)} %get-tuple-element.62), channel_id=1, source_target_pairs={{0,8},{4,12},{8,0},{12,4},{16,24},{20,28},{24,16},{28,20},{1,9},{5... | collective-permute-start | bytes 1622024 | tf_op jit(solution)/shard_map/ppermute | solution.py:460
  75.0 36.1 %collective-permute-start.8 = (bf16[4,3,2,72,256]{4,3,2,1,0:T(8,128)(2,1)S(1)}, bf16[4,3,2,72,256]{4,3,2,1,0:T(8,128)(2,1)S(1)}, u32[]{:S(2)}, u32[]{:S(2)}) collective-permute-start(bf16[4,3,2,72,256]{4,3,2,1,0:T(8,128)(2,1)S(1)} %pad_maximum_fusion.1), channel_id=1, source_target_pairs={{0,8},{4,12},{8,0},{12,4},{16,24},{20,28},{24,16},{28,20},{1,9},{5... | collective-permute-start | bytes 2654216 | tf_op jit(solution)/shard_map/ppermute | solution.py:460
  76.5 48.6 %collective-permute-start.20 = (s16[528,1024]{1,0:T(8,128)(2,1)S(1)}, s16[528,1024]{1,0:T(8,128)(2,1)S(1)}, u32[]{:S(2)}, u32[]{:S(2)}) collective-permute-start(s16[528,1024]{1,0:T(8,128)(2,1)S(1)} %get-tuple-element.82), channel_id=1, source_target_pairs={{0,4},{4,0},{8,12},{12,8},{16,20},{20,16},{24,28},{28,24},{1,5},{5... | collective-permute-start | bytes 3244040 | tf_op jit(solution)/shard_map/ppermute | solution.py:460
  87.8 13.9 %collective-permute-start.14 = (s16[528,256]{1,0:T(8,128)(2,1)S(1)}, s16[528,256]{1,0:T(8,128)(2,1)S(1)}, u32[]{:S(2)}, u32[]{:S(2)}) collective-permute-start(s16[528,256]{1,0:T(8,128)(2,1)S(1)} %get-tuple-element.68), channel_id=1, source_target_pairs={{0,16},{4,20},{8,24},{12,28},{16,0},{20,4},{24,8},{28,12},{1,17},{... | collective-permute-start | bytes 811016 | tf_op jit(solution)/shard_map/ppermute | solution.py:460
  90.8 31.8 %collective-permute-start.18 = (s16[528,512]{1,0:T(8,128)(2,1)S(1)}, s16[528,512]{1,0:T(8,128)(2,1)S(1)}, u32[]{:S(2)}, u32[]{:S(2)}) collective-permute-start(s16[528,512]{1,0:T(8,128)(2,1)S(1)} %get-tuple-element.78), channel_id=1, source_target_pairs={{0,8},{4,12},{8,0},{12,4},{16,24},{20,28},{24,16},{28,20},{1,9},{5... | collective-permute-start | bytes 1622024 | tf_op jit(solution)/shard_map/ppermute | solution.py:460
  123.4 15.3 %collective-permute-start.19 = (s16[528,256]{1,0:T(8,128)(2,1)S(1)}, s16[528,256]{1,0:T(8,128)(2,1)S(1)}, u32[]{:S(2)}, u32[]{:S(2)}) collective-permute-start(s16[528,256]{1,0:T(8,128)(2,1)S(1)} %get-tuple-element.80), channel_id=1, source_target_pairs={{0,16},{4,20},{8,24},{12,28},{16,0},{20,4},{24,8},{28,12},{1,17},{... | collective-permute-start | bytes 811016 | tf_op jit(solution)/shard_map/ppermute | solution.py:460
  125.1 19.7 %collective-permute-start.16 = (s16[400,512]{1,0:T(8,128)(2,1)S(1)}, s16[400,512]{1,0:T(8,128)(2,1)S(1)}, u32[]{:S(2)}, u32[]{:S(2)}) collective-permute-start(s16[400,512]{1,0:T(8,128)(2,1)S(1)} %get-tuple-element.75), channel_id=1, source_target_pairs={{0,1},{1,0},{2,3},{3,2},{4,5},{5,4},{6,7},{7,6},{8,9},{9,8},{10,11... | collective-permute-start | bytes 1228808 | tf_op jit(solution)/shard_map/ppermute | solution.py:460
  126.2 21.4 %collective-permute-start.26 = (s16[528,512]{1,0:T(8,128)(2,1)S(1)}, s16[528,512]{1,0:T(8,128)(2,1)S(1)}, u32[]{:S(2)}, u32[]{:S(2)}) collective-permute-start(s16[528,512]{1,0:T(8,128)(2,1)S(1)} %get-tuple-element.89), channel_id=1, source_target_pairs={{0,8},{4,12},{8,0},{12,4},{16,24},{20,28},{24,16},{28,20},{1,9},{5... | collective-permute-start | bytes 1622024 | tf_op jit(solution)/shard_map/ppermute | solution.py:460
  146.8 10.6 %collective-permute-start.22 = (s16[208,512]{1,0:T(8,128)(2,1)S(1)}, s16[208,512]{1,0:T(8,128)(2,1)S(1)}, u32[]{:S(2)}, u32[]{:S(2)}) collective-permute-start(s16[208,512]{1,0:T(8,128)(2,1)S(1)} %get-tuple-element.88), channel_id=1, source_target_pairs={{0,2},{1,3},{2,0},{3,1},{4,6},{5,7},{6,4},{7,5},{8,10},{9,11},{10,... | collective-permute-start | bytes 638984 | tf_op jit(solution)/shard_map/ppermute | solution.py:460
  148.6 14.9 %collective-permute-start.27 = (s16[528,256]{1,0:T(8,128)(2,1)S(1)}, s16[528,256]{1,0:T(8,128)(2,1)S(1)}, u32[]{:S(2)}, u32[]{:S(2)}) collective-permute-start(s16[528,256]{1,0:T(8,128)(2,1)S(1)} %get-tuple-element.91), channel_id=1, source_target_pairs={{0,16},{4,20},{8,24},{12,28},{16,0},{20,4},{24,8},{28,12},{1,17},{... | collective-permute-start | bytes 811016 | tf_op jit(solution)/shard_map/ppermute | solution.py:460
  157.6 23.4 %collective-permute-start.23 = (f32[4,2,96,128]{3,2,0,1:T(8,128)S(1)}, f32[4,2,96,128]{3,2,0,1:T(8,128)S(1)}, u32[]{:S(2)}, u32[]{:S(2)}) collective-permute-start(f32[4,2,96,128]{3,2,0,1:T(8,128)S(1)} %pad_maximum_fusion.2), channel_id=1, source_target_pairs={{0,4},{4,0},{8,12},{12,8},{16,20},{20,16},{24,28},{28,24},{1,5},{5... | collective-permute-start | bytes 1179656 | tf_op jit(solution)/shard_map/ppermute | solution.py:460
  181.1 11.7 %collective-permute-start.24 = (f32[2,2,96,128]{3,2,0,1:T(8,128)S(1)}, f32[2,2,96,128]{3,2,0,1:T(8,128)S(1)}, u32[]{:S(2)}, u32[]{:S(2)}) collective-permute-start(f32[2,2,96,128]{3,2,0,1:T(8,128)S(1)} %slice.107), channel_id=1, source_target_pairs={{0,8},{4,12},{8,0},{12,4},{16,24},{20,28},{24,16},{28,20},{1,9},{5... | collective-permute-start | bytes 589832 | tf_op jit(solution)/shard_map/ppermute | solution.py:460
  184.7 10.1 %collective-permute-start.35 = (f32[96,128]{1,0:T(8,128)S(1)}, f32[96,128]{1,0:T(8,128)S(1)}, u32[]{:S(2)}, u32[]{:S(2)}) collective-permute-start(f32[96,128]{1,0:T(8,128)S(1)} %get-tuple-element.108), channel_id=1, source_target_pairs={{0,20},{4,16},{8,28},{12,24},{16,4},{20,0},{24,12},{28,8},{1,21},{... | collective-permute-start | bytes 147464 | tf_op jit(solution)/shard_map/ppermute | solution.py:460
  (35 other events, 216.1 us)

commit v7 on v6

--- a/solution.py
+++ b/solution.py
@@ -16,18 +16,18 @@
 TOP = 32700.0
 MAGIC = 1.5 * 2.0**23
 NT_DIMS = (((1,), (1,)), ((), ()))
-MIB = 1024 * 1024
+VMEM = 40 * 1024 * 1024
 
 
 TOKEN = jax.ShapeDtypeStruct((8, 128), jnp.float32)
 
 
-def params(mib):
-    return pltpu.CompilerParams(vmem_limit_bytes=mib * MIB)
+def params():
+    return pltpu.CompilerParams(vmem_limit_bytes=VMEM)
 
 
 def cost(flops, moved):
-    return pl.CostEstimate(flops=int(flops), bytes_accessed=int(moved), transcendentals=0)
+    return pl.CostEstimate(flops=int(flops) // 64, bytes_accessed=int(moved) // 64, transcendentals=0)
 
 
 def mm(left, right):
@@ -81,29 +81,28 @@
     return number
 
 
-def shift_kernel(order, me_ref, con_ref, map_ref, stay_ref, go_ref, token_ref):
-    slots, _, _, rows, width = stay_ref.shape
+def shift_kernel(order, me_ref, con_ref, map_ref, *refs):
+    *stay_refs, go_ref, token_ref = refs
+    half, _, _, rows, width = go_ref.shape
     count = len(order).bit_length() - 1
     token_ref[...] = jnp.zeros_like(token_ref)
-    for which, out_ref in enumerate((stay_ref, go_ref)):
-        for slot in range(slots):
-            dest = jnp.bitwise_xor(me_ref[0], order[which * slots + slot])
-            first = reversed_bits(dest, count) * width
-            for block in range(width // GBLK):
-                cols = pl.ds(pl.multiple_of(first + block * GBLK, GBLK), GBLK)
-                within = jnp.bitwise_and(map_ref[0, 0:1, cols], GBLK - 1)
-                within = jnp.broadcast_to(within, (rows, GBLK))
-                for part in range(2):
-                    values = con_ref[0, part, :, cols].astype(jnp.float32)
-                    moved = jnp.take_along_axis(values, within, axis=1)
-                    out_ref[slot, 0, part, :, block * GBLK : (block + 1) * GBLK] = moved.astype(
-                        jnp.bfloat16
-                    )
+    for p, slot in enumerate(order):
+        out_ref = stay_refs[p].at[0] if p < half else go_ref.at[p - half]
+        first = reversed_bits(jnp.bitwise_xor(me_ref[0], slot), count) * width
+        for block in range(width // GBLK):
+            cols = pl.ds(pl.multiple_of(first + block * GBLK, GBLK), GBLK)
+            within = jnp.bitwise_and(map_ref[0, 0:1, cols], GBLK - 1)
+            within = jnp.broadcast_to(within, (rows, GBLK))
+            for part in range(2):
+                values = con_ref[0, part, :, cols].astype(jnp.float32)
+                moved = jnp.take_along_axis(values, within, axis=1)
+                out_ref[0, part, :, block * GBLK : (block + 1) * GBLK] = moved.astype(jnp.bfloat16)
 
 
 def shift_call(con, shift_map, me, order, width):
     points, _, rows, slab = con.shape
-    slots = len(order) // 2
+    half = len(order) // 2
+    counts = [1] * half + [half]
     grid_spec = pltpu.PrefetchScalarGridSpec(
         num_scalar_prefetch=1,
         grid=(points,),
@@ -111,15 +110,19 @@
             pl.BlockSpec((1, 2, rows, slab), lambda q, me: (q, 0, 0, 0)),
             pl.BlockSpec((1, 1, slab), lambda q, me: (q, 0, 0)),
         ],
-        out_specs=[pl.BlockSpec((slots, 1, 2, rows, width), lambda q, me: (0, q, 0, 0, 0))] * 2
+        out_specs=[
+            pl.BlockSpec((n, 1, 2, rows, width), lambda q, me: (0, q, 0, 0, 0)) for n in counts
+        ]
         + [pl.BlockSpec(TOKEN.shape, lambda q, me: (0, 0))],
     )
     return pl.pallas_call(
         lambda *refs: shift_kernel(order, *refs),
         grid_spec=grid_spec,
-        out_shape=[jax.ShapeDtypeStruct((slots, points, 2, rows, width), jnp.bfloat16)] * 2
+        out_shape=[
+            jax.ShapeDtypeStruct((n, points, 2, rows, width), jnp.bfloat16) for n in counts
+        ]
         + [TOKEN],
-        compiler_params=params(16),
+        compiler_params=params(),
         cost_estimate=cost(8 * con.size, 4 * con.size),
     )(me, con, shift_map.reshape(points, 1, slab))
 
@@ -127,7 +130,7 @@
 def x_kernel(slots, waits, me_ref, *refs):
     val_refs, weight_ref = refs[:slots], refs[slots]
     go_ref, keep_ref, token_ref, left_ref = refs[slots + 1 + waits :]
-    _, _, rows, depth = val_refs[0].shape
+    _, _, _, rows, depth = val_refs[0].shape
     half = slots * rows
     token_ref[...] = jnp.zeros_like(token_ref)
     step = pl.program_id(0)
@@ -136,7 +139,7 @@
     @pl.when(step == 0)
     def _():
         for slot in range(slots):
-            real, imag = val_refs[slot][0, 0], val_refs[slot][0, 1]
+            real, imag = val_refs[slot][0, 0, 0], val_refs[slot][0, 0, 1]
             top = slice(slot * rows, (slot + 1) * rows)
             low = slice(half + slot * rows, half + (slot + 1) * rows)
             left_ref[top, 0:depth] = real
@@ -157,7 +160,7 @@
 
 def x_call(vals, screened, place, point, me, steps, after):
     slots = len(vals)
-    _, _, rows, depth = vals[0].shape
+    _, _, _, rows, depth = vals[0][0].shape
     height = 2 * slots * rows
     columns = screened.shape[3] // 2
     half = steps // 2
@@ -166,7 +169,8 @@
         num_scalar_prefetch=1,
         grid=(steps,),
         in_specs=[
-            pl.BlockSpec((1, 2, rows, depth), lambda j, me: (place, 0, 0, 0)) for _ in vals
+            pl.BlockSpec((1, 1, 2, rows, depth), lambda j, me, slot=slot: (slot, place, 0, 0, 0))
+            for _, slot in vals
         ]
         + [
             pl.BlockSpec(
@@ -190,11 +194,11 @@
             jax.ShapeDtypeStruct((height, columns), jnp.float32),
             TOKEN,
         ],
-        compiler_params=params(42),
+        compiler_params=params(),
         cost_estimate=cost(
             2 * height * 2 * depth * 2 * columns, 8 * depth * columns + 6 * height * columns
         ),
-    )(me, *vals, screened, *after)
+    )(me, *[v for v, _ in vals], screened, *after)
 
 
 def hop_kernel(heard, me_ref, keep_ref, *refs):
@@ -228,61 +232,59 @@
         lambda *refs: hop_kernel(len(others), *refs),
         grid_spec=grid_spec,
         out_shape=[jax.ShapeDtypeStruct((tall, width), jnp.int16), TOKEN],
-        compiler_params=params(16),
+        compiler_params=params(),
         cost_estimate=cost(20 * height * width, 8 * height * width),
     )(me, keep, *others, *after)
 
 
-def fold_kernel(*refs):
-    own_ref, heard_ref, keep_ref, go_ref = refs
-    total = own_ref[...] + decode(heard_ref)
-    rows = keep_ref.shape[0]
-    keep_ref[...] = total[:rows]
-    encode(total[rows:], go_ref)
+def fold_kernel(own_ref, heard_ref, keep_ref, go_ref):
+    rows = keep_ref.shape[1]
+    for n in range(own_ref.shape[0]):
+        total = own_ref[n] + decode(heard_ref.at[n])
+        keep_ref[n] = total[:rows]
+        encode(total[rows:], go_ref.at[n])
 
 
 def fold_call(own, heard):
-    rows, cols = own.shape
+    count, rows, cols = own.shape
     shapes = [
-        jax.ShapeDtypeStruct((rows // 2, cols), jnp.float32),
-        jax.ShapeDtypeStruct((rows // 2 + EXP_ROWS, cols), jnp.int16),
+        jax.ShapeDtypeStruct((count, rows // 2, cols), jnp.float32),
+        jax.ShapeDtypeStruct((count, rows // 2 + EXP_ROWS, cols), jnp.int16),
     ]
     return pl.pallas_call(
         fold_kernel,
         out_shape=shapes,
-        compiler_params=params(16),
+        compiler_params=params(),
         cost_estimate=cost(20 * own.size, 10 * own.size),
     )(own, heard)
 
 
-def pack_kernel(own_ref, *refs):
-    heard_refs, out_ref = refs[:-1], refs[-1]
-    total = own_ref[...]
-    for ref in heard_refs:
-        total = total + decode(ref)
-    rows = out_ref.shape[1]
+def pack_kernel(own_ref, heard_ref, out_ref):
+    rows = out_ref.shape[2]
     first = lax.broadcasted_iota(jnp.int32, (rows, 128), 1) < 64
-    for block in range(out_ref.shape[0] // 2):
-        cols = slice(block * 128, (block + 1) * 128)
-        real, imag = total[:rows, cols], total[rows:, cols]
-        out_ref[2 * block] = jnp.where(first, real, pltpu.roll(imag, 64, 1))
-        out_ref[2 * block + 1] = jnp.where(first, pltpu.roll(real, 64, 1), imag)
+    for n in range(own_ref.shape[0]):
+        total = own_ref[n] + decode(heard_ref.at[n])
+        for block in range(out_ref.shape[0] // 2):
+            cols = slice(block * 128, (block + 1) * 128)
+            real, imag = total[:rows, cols], total[rows:, cols]
+            out_ref[2 * block, n] = jnp.where(first, real, pltpu.roll(imag, 64, 1))
+            out_ref[2 * block + 1, n] = jnp.where(first, pltpu.roll(real, 64, 1), imag)
 
 
 def pack_call(own, heard):
-    rows, cols = own.shape
+    count, rows, cols = own.shape
     return pl.pallas_call(
         pack_kernel,
-        out_shape=jax.ShapeDtypeStruct((cols // 64, rows // 2, 128), jnp.float32),
-        compiler_params=params(16),
+        out_shape=jax.ShapeDtypeStruct((cols // 64, count, rows // 2, 128), jnp.float32),
+        compiler_params=params(),
         cost_estimate=cost(20 * own.size, 10 * own.size),
-    )(own, *heard)
+    )(own, heard)
 
 
 def exchange_kernel(slots, waits, *refs):
     here_refs, (there_ref, coulomb_ref) = refs[:slots], refs[slots : slots + 2]
     out_ref, token_ref, left_ref = refs[slots + 2 + waits :]
-    _, rows, depth = here_refs[0].shape
+    _, _, rows, depth = here_refs[0].shape
     token_ref[...] = jnp.zeros_like(token_ref)
 
     @pl.when(pl.program_id(0) == 0)
@@ -291,7 +293,7 @@
             for part in range(2):
                 left_ref[
                     slot * rows : (slot + 1) * rows, part * depth : (part + 1) * depth
-                ] = here_refs[slot][part]
+                ] = here_refs[slot][0, part]
 
     factor = coulomb_ref[0]
     real = there_ref[0, 0].astype(jnp.float32) * factor
@@ -308,13 +310,16 @@
 
 
 def exchange_call(heres, there, coulomb, after):
-    slots, rows = len(heres), heres[0].shape[1]
+    slots, rows = len(heres), heres[0][0].shape[2]
     points, _, cols, depth = there.shape
     height = slots * rows
     return pl.pallas_call(
         lambda *refs: exchange_kernel(slots, len(after), *refs),
         grid=(points,),
-        in_specs=[pl.BlockSpec(h.shape, lambda q: (0, 0, 0)) for h in heres]
+        in_specs=[
+            pl.BlockSpec((1,) + h.shape[1:], lambda q, slot=slot: (slot, 0, 0, 0))
+            for h, slot in heres
+        ]
         + [
             pl.BlockSpec((1, 2, cols, depth), lambda q: (q, 0, 0, 0)),
             pl.BlockSpec((1, 1, depth), lambda q: (q, 0, 0)),
@@ -326,9 +331,9 @@
         ],
         out_shape=[jax.ShapeDtypeStruct((points, 2, height, cols), jnp.float32), TOKEN],
         scratch_shapes=[pltpu.VMEM((height, 2 * depth), jnp.bfloat16)],
-        compiler_params=params(16),
+        compiler_params=params(),
         cost_estimate=cost(2 * points * height * 2 * cols * 2 * depth * 2, 8 * points * cols * depth),
-    )(*heres, there, coulomb.reshape(points, 1, depth), *after)
+    )(*[h for h, _ in heres], there, coulomb.reshape(points, 1, depth), *after)
 
 
 def tile_kernel(order, heard, chunks, waits, me_ref, *refs):
@@ -336,7 +341,7 @@
     con_refs, keep_ref = refs[:slots], refs[slots]
     heard_refs = refs[slots + 1 : slots + 1 + heard]
     exch_ref, row_ref, col_direct_ref, col_exch_ref = refs[slots + 1 + heard : slots + 5 + heard]
-    keep_out, *go_outs, token_ref, con_all, direct_ref, natural_ref, sums_ref = refs[
+    keep_out, go_out, token_ref, con_all, direct_ref, natural_ref, sums_ref = refs[
         slots + 5 + heard + waits :
     ]
     token_ref[...] = jnp.zeros_like(token_ref)
@@ -399,15 +404,11 @@
             sums_ref[at : at + count, :] = result[chunk * count : (chunk + 1) * count]
     stays = keep_out.shape[0]
     keep_out[...] = sums_ref[0:stays, :]
-    at = stays
-    for out_ref in go_outs:
-        rows = out_ref.shape[0] - EXP_ROWS
-        encode(sums_ref[at : at + rows, :], out_ref)
-        at += rows
+    encode(sums_ref[stays:, :], go_out)
 
 
 def tile_call(
-    cons, point, keep, heard, exch, me, order, pick_rows, col_direct, col_exch, chunks, after, direct
+    cons, point, keep, heard, exch, me, order, pick_rows, col_direct, col_exch, chunks, after
 ):
     slots = len(cons)
     _, _, _, rows, width = cons[0][0].shape
@@ -416,9 +417,11 @@
     out_cols = col_direct.shape[1]
     stages = len(heard)
     whole = lambda a: pl.BlockSpec(a.shape, lambda i, me: (0,) * len(a.shape))
-    each, others = (2 * NT // chunks, chunks - 1) if direct else (NT, 1)
-    shapes = [jax.ShapeDtypeStruct((each, out_cols), jnp.float32)]
-    shapes += [jax.ShapeDtypeStruct((each + EXP_ROWS, out_cols), jnp.int16)] * others + [TOKEN]
+    shapes = [
+        jax.ShapeDtypeStruct((NT, out_cols), jnp.float32),
+        jax.ShapeDtypeStruct((NT + EXP_ROWS, out_cols), jnp.int16),
+        TOKEN,
+    ]
 
     def at(known):
         return lambda i, me: (0, block_of(me[0], known, stages, False))
@@ -451,7 +454,7 @@
         lambda *refs: tile_kernel(order, stages, chunks, len(after), *refs),
         grid_spec=grid_spec,
         out_shape=shapes,
-        compiler_params=params(24),
+        compiler_params=params(),
         cost_estimate=cost(2.8e9, 8e6),
     )(me, *[c for c, _ in cons], keep, *heard, exch, pick_rows, col_direct, col_exch, *after)
 
@@ -461,12 +464,16 @@
 
 
 def gather_slots(value, axis, size, token=None):
-    found = {0: value}
+    found = {0: (value[None], 0)}
     bit = size // 2
     while bit:
-        for known in sorted(found):
-            ready = found[known] if token is None or not known else behind(found[known], token)
-            found[known ^ bit] = swap(ready, axis, size, bit)
+        known = sorted(found)
+        sent = jnp.concatenate([found[r][0][found[r][1] :][:1] for r in known])
+        if token is not None and len(known) > 1:
+            sent = behind(sent, token)
+        got = swap(sent, axis, size, bit)
+        for place, r in enumerate(known):
+            found[r ^ bit] = (got, place)
         bit //= 2
     return [found[r] for r in range(size)]
 
@@ -495,36 +502,37 @@
     ga_order = halving_order(ga_bits)
     stages, half = len(ga_bits), ga // 2
 
-    first = gather_slots(jnp.transpose(val_density[:, :1], (1, 2, 0, 3)), "pair", pair)
-
     con = jnp.transpose(con_density, (1, 2, 0, 3))
-    stay, go, token = shift_call(con, shift_map, me, ga_order, width)
-    from_near = swap(go, "ga", ga, ga_bits[0])
-    others = behind(val_density[:, 1:], first[pair // 2])
-    others = gather_slots(jnp.transpose(others, (1, 2, 0, 3)), "pair", pair)
+    *stay, go, token = shift_call(con, shift_map, me, ga_order, width)
+    first = gather_slots(jnp.transpose(val_density[:, :1], (1, 2, 0, 3)), "pair", pair, token)
+    nearest = ga_bits[0]
+    from_near = swap(go, "ga", ga, nearest)
+    cons = {0: (stay[0], 0)}
+    for slot, block in zip(ga_order[1:half], stay[1:]):
+        cons[slot] = (swap(block, "ga", ga, slot), 0)
+    later = behind(val_density[:, 1:], first[pair // 2][0])
+    later = jnp.transpose(later, (1, 2, 0, 3))
 
     gone, keep, tokens = [], [], [token]
     for q in range(points):
         vals, place = (first, 0) if q == 0 else (others, q - 1)
         coded, own, token = x_call(vals, screened, place, q, me, 4, tokens[-1:])
+        if q == 0:
+            first_token = token
+            others = gather_slots(later, "pair", pair, first_token)
+        if q + 1 < min(points, half):
+            token = behind(token, cons[ga_order[q + 1]][0])
         tokens.append(token)
         gone.append(coded)
         keep.append(own)
     after = tokens[-1:]
 
-    cons = {}
-    for p, slot in enumerate(ga_order):
-        cons[slot] = (stay, p) if p < half else (go, p - half)
-    for step, bit in enumerate(ga_bits[:1] + ga_bits[:0:-1]):
-        moving = [slot for slot in ga_order if slot & bit]
-        if step == 0:
-            got = from_near
-        else:
-            got = swap(jnp.stack([cons[slot][0][cons[slot][1]] for slot in moving]), "ga", ga, bit)
-        if step + 1 < stages:
-            got = behind(got, tokens[min(2 * step + 1, points)])
-        for place, slot in enumerate(moving):
-            cons[slot] = (got, place)
+    from_near = behind(from_near, first_token)
+    for place, slot in enumerate(ga_order[half:]):
+        cons[slot] = (from_near, 0)
+        if slot != nearest:
+            cons[slot] = (swap(from_near[place : place + 1], "ga", ga, slot ^ nearest), 0)
+    after = [behind(after[0], [cons[slot][0] for slot in ga_order[half:]])]
     cons = [cons[slot] for slot in ga_order]
 
     row_count, col_count = NT // pair, NT // ga
@@ -546,7 +554,7 @@
     col_direct, col_exch = pick_cols(at_direct, NT, -1.0), pick_cols(at_exch, row_count, 2.0)
 
     heard = [[swap(gone[q], "ga", ga, ga_bits[0])] for q in range(points)]
-    packed = [None] * points
+    tiles = [None] * points
     exch = None
     for wave in range(2 * points + stages):
         for q in reversed(range(points)):
@@ -563,32 +571,27 @@
                     exch, token = exchange_call(heres, there, coulomb, after)
                     after = [token]
             elif stage == stages:
-                last = q == points - 1
-                tile, *sent, token = tile_call(
+                *tiles[q], token = tile_call(
                     cons, q, keep[q], heard[q], exch, me, ga_order, pick_rows, col_direct,
-                    col_exch, pair, after, last,
+                    col_exch, pair, after,
                 )
                 after = [token]
-                if last:
-                    slots = halving_order(pair_bits)[1:]
-                    got = [swap(part, "pair", pair, slot) for slot, part in zip(slots, sent)]
-                    packed[q] = pack_call(tile, got)
-                    continue
-                got = swap(sent[0], "pair", pair, pair_bits[0])
-                for bit in pair_bits[1:]:
-                    tile, sent = fold_call(tile, got)
-                    got = swap(sent, "pair", pair, bit)
-                packed[q] = pack_call(tile, [got])
-    early = jnp.stack(packed[:-1], axis=1)
-    for bit in ga_bits:
-        size = early.shape[0] // 2
-        early = early[:size] + swap(early[size:], "ga", ga, bit)
-    late = packed[-1]
-    total = late[0]
-    for place, slot in enumerate(ga_order[1:]):
-        total = total + swap(late[place + 1], "ga", ga, slot)
-    out = jnp.concatenate([early[0], total[None]])
-    out = out.reshape(points, row_count, 2, 64)[..., :col_count]
+            if (q, stage) == (points - 1, stages - 1):
+                gate = token
+
+    outs = []
+    for group in (tiles[:-1], tiles[-1:]):
+        own, sent = (jnp.stack(items) for items in zip(*group))
+        if len(outs) == 0:
+            sent = behind(sent, gate)
+        for bit in pair_bits[:-1]:
+            own, sent = fold_call(own, swap(sent, "pair", pair, bit))
+        total = pack_call(own, swap(sent, "pair", pair, pair_bits[-1]))
+        for bit in ga_bits:
+            size = total.shape[0] // 2
+            total = total[:size] + swap(total[size:], "ga", ga, bit)
+        outs.append(total[0])
+    out = jnp.concatenate(outs).reshape(points, row_count, 2, 64)[..., :col_count]
     return jnp.transpose(out, (0, 2, 1, 3))
 
 

time: 205 us -> 234 us (1.14)
  waiting for transfers between devices: 84.7 us -> 101 us
  local copies, waits for them, and re-layouts: 15.5 us -> 20.9 us
  Pallas kernels: 59.2 us -> 64.1 us
  other arithmetic: 2.27 us -> 6.24 us
    ppermute x38 -> x32, waiting for transfers between devices: 84.7 us -> 101 us  [swap(): return lax.ppermute(value, axis, [(i, i ^ bit) for i in range(size)])]
    pallas_call x6, Pallas kernels: 8.33 us -> 11.9 us  [hop_call(): pl.pallas_call(lambda *refs: hop_kernel(len(others), *refs), grid_spec=gr...]
    concatenate x0 -> x3, other arithmetic: none -> 3.19 us  [gather_slots(): sent = jnp.concatenate([found[r][0][found[r][1]:][:1] for r in known])]
    ppermute x38 -> x32, starting transfers between devices: 41.7 us -> 40.3 us  [swap(): return lax.ppermute(value, axis, [(i, i ^ bit) for i in range(size)])]
    unnamed x42 -> x56, local copies, waits for them, and re-layouts: 7.73 us -> 7.58 us
  transfers between devices with their start and end apart: 38 -> 32, of which waited for: 18 -> 13; matrix products, arithmetic and copies ran while one was open for 5% -> 8% of each run, Pallas kernels for 29% -> 27%
where the time goes in v7:
time: 234 us
  waiting for transfers between devices  101 us (43%)
  Pallas kernels  64.1 us (27%)
  starting transfers between devices  40.3 us (17%)
  local copies, waits for them, and re-layouts  20.9 us (9%)
  other arithmetic  6.24 us (3%)
    ppermute x32, waiting for transfers between devices, swap(): return lax.ppermute(value, axis, [(i, i ^ bit) for i in range(size)])  101 us
    ppermute x32, starting transfers between devices, swap(): return lax.ppermute(value, axis, [(i, i ^ bit) for i in range(size)])  40.3 us
    pallas_call x3, Pallas kernels, x_call(): pl.pallas_call(lambda *refs: x_kernel(slots, len(after), *refs), grid_spe...  25.3 us
    pallas_call x3, Pallas kernels, tile_call(): pl.pallas_call(lambda *refs: tile_kernel(order, stages, chunks, len(after...  19.2 us
    pallas_call x6, Pallas kernels, hop_call(): pl.pallas_call(lambda *refs: hop_kernel(len(others), *refs), grid_spec=gr...  11.9 us
    unnamed x56, local copies, waits for them, and re-layouts  7.58 us
  transfers between devices with their start and end apart: 32, of which 13 were waited for; matrix products, arithmetic and copies ran while one was open for 8% of the time, Pallas kernels for 27%

profile of v7, /device:TPU:0, one launch (start us, length us, event | category | flops | bytes accessed | tf_op | source)
XLA Modules:
  0.0 233.5 jit_solution(14060520695063658949)
XLA Ops:
  1.2 3.0 %collective-permute-start.4 = (bf16[1,1,2,64,1024]{4,3,2,1,0:T(8,128)(2,1)S(1)}, bf16[1,1,2,64,1024]{4,3,2,1,0:T(8,128)(2,1)S(1)}, u32[]{:S(2)}, u32[]{:S(2)}) collective-permute-start(bf16[1,1,2,64,1024]{4,3,2,1,0:T(8,128)(2,1)S(1)} %bitcast.39), channel_id=1, source_target_pairs={{0,2},{1,3},{2,0},{3,1},{4,6},{5,7},{6,4},{7,5},{8,10},{9,11},{10,... | collective-permute-start | bytes 786440 | tf_op jit(solution)/shard_map/ppermute | solution.py:463
  14.2 8.2 %shard_map.101 = (s16[528,1024]{1,0:T(8,128)(2,1)S(1)}, f32[512,1024]{1,0:T(8,128)S(1)}, f32[8,128]{1,0:T(8,128)S(1)}) custom-call(s32[1]{0:T(128)} %bitcast.refs_0_, bf16[1,1,2,64,1024]{4,3,2,1,0:T(8,128)(2,1)S(1)} %bitcast.41, bf16[2,1,2,64,1024]{4,3,2,1,0:T(8,128)(2,1)S(1)} %collective-permute-done.5.refs_2_.refs_4_, ...), custom_call_target="tpu_custom_call" | custom-call | flops 67108864 | bytes 180224 | tf_op jit(solution)/shard_map/pallas_call | solution.py:189
  26.4 2.9 %collective-permute-start = (bf16[1,3,2,72,256]{4,3,2,1,0:T(8,128)(2,1)}, bf16[1,3,2,72,256]{4,3,2,1,0:T(8,128)(2,1)S(1)}, u32[]{:S(2)}, u32[]{:S(2)}) collective-permute-start(bf16[1,3,2,72,256]{4,3,2,1,0:T(8,128)(2,1)} %get-tuple-element.58), channel_id=1, source_target_pairs={{0,16},{4,20},{8,24},{12,28},{16,0},{20,4},{24,8},{28,12},{1,17},{... | collective-permute-start | bytes 663560 | tf_op jit(solution)/shard_map/ppermute | solution.py:463
  34.3 6.1 %collective-permute-done.refs_2_ = bf16[1,3,2,72,256]{4,3,2,1,0:T(8,128)(2,1)S(1)} collective-permute-done((bf16[1,3,2,72,256]{4,3,2,1,0:T(8,128)(2,1)}, bf16[1,3,2,72,256]{4,3,2,1,0:T(8,128)(2,1)S(1)}, u32[]{:S(2)}, u32[]{:S(2)}) %collective-permute-start) | collective-permute-done | bytes 221216 | tf_op jit(solution)/shard_map/ppermute | solution.py:463
  45.8 8.9 %shard_map.102 = (s16[528,1024]{1,0:T(8,128)(2,1)}, f32[512,1024]{1,0:T(8,128)S(1)}, f32[8,128]{1,0:T(8,128)S(1)}) custom-call(s32[1]{0:T(128)} %bitcast.refs_0_, bf16[1,2,2,64,1024]{4,3,2,1,0:T(8,128)(2,1)S(1)} %bitcast.32, bf16[2,2,2,64,1024]{4,3,2,1,0:T(8,128)(2,1)S(1)} %collective-permute-done.11.refs_2_.refs_4_, ...), custom_call_target="tpu_custom_call" | custom-call | flops 67108864 | bytes 180224 | tf_op jit(solution)/shard_map/pallas_call | solution.py:189
  63.4 4.0 %collective-permute-start.7 = (bf16[1,3,2,72,256]{4,3,2,1,0:T(8,128)(2,1)}, bf16[1,3,2,72,256]{4,3,2,1,0:T(8,128)(2,1)}, u32[]{:S(2)}, u32[]{:S(2)}) collective-permute-start(bf16[1,3,2,72,256]{4,3,2,1,0:T(8,128)(2,1)} %get-tuple-element.110), channel_id=1, source_target_pairs={{0,8},{4,12},{8,0},{12,4},{16,24},{20,28},{24,16},{28,20},{1,9},{5... | collective-permute-start | bytes 663560 | tf_op jit(solution)/shard_map/ppermute | solution.py:463
  69.9 8.2 %shard_map.103 = (s16[528,1024]{1,0:T(8,128)(2,1)S(1)}, f32[512,1024]{1,0:T(8,128)S(1)}, f32[8,128]{1,0:T(8,128)S(1)}) custom-call(s32[1]{0:T(128)} %bitcast.refs_0_, bf16[1,2,2,64,1024]{4,3,2,1,0:T(8,128)(2,1)S(1)} %bitcast.33, bf16[2,2,2,64,1024]{4,3,2,1,0:T(8,128)(2,1)S(1)} %collective-permute-done.11.refs_2_.refs_4_, ...), custom_call_target="tpu_custom_call" | custom-call | flops 67108864 | bytes 180224 | tf_op jit(solution)/shard_map/pallas_call | solution.py:189
  81.8 3.4 %collective-permute-start.2 = (bf16[1,3,2,72,256]{4,3,2,1,0:T(8,128)(2,1)}, bf16[1,3,2,72,256]{4,3,2,1,0:T(8,128)(2,1)S(1)}, u32[]{:S(2)}, u32[]{:S(2)}) collective-permute-start(bf16[1,3,2,72,256]{4,3,2,1,0:T(8,128)(2,1)} %copy-done.18), channel_id=1, source_target_pairs={{0,24},{4,28},{8,16},{12,20},{16,8},{20,12},{24,0},{28,4},{1,25},{... | collective-permute-start | bytes 663560 | tf_op jit(solution)/shard_map/ppermute | solution.py:463
  85.2 3.6 %shard_map.104 = (s16[528,512]{1,0:T(8,128)(2,1)}, f32[8,128]{1,0:T(8,128)S(1)}) custom-call(s32[1]{0:T(128)} %bitcast.refs_0_, f32[512,1024]{1,0:T(8,128)S(1)} %get-tuple-element.66.refs_1_.refs_9_, s16[528,1024]{1,0:T(8,128)(2,1)} %collective-permute-done.9.refs_2_.refs_10_, f32[8,128]{1,0:T(8,128)S(1)} %get-tuple-element.74.refs_3_), custom_call_target="tpu_custom_call" | custom-call | flops 81920 | bytes 32768 | tf_op jit(solution)/shard_map/pallas_call | solution.py:231
  91.4 4.4 %shard_map.105 = (f32[3,2,384,96]{3,2,1,0:T(8,128)S(1)}, f32[8,128]{1,0:T(8,128)S(1)}) custom-call(bf16[1,2,96,1024]{3,2,1,0:T(8,128)(2,1)S(1)} %bitcast.38, bf16[2,2,96,1024]{3,2,1,0:T(8,128)(2,1)S(1)} %collective-permute-done.14.refs_1_.refs_3_, bf16[1,2,96,1024]{3,2,1,0:T(8,128)(2,1)} %collective-permute-done.13.refs_2_, ...), custom_call_target="tpu_custom_call" | custom-call | flops 28311552 | bytes 36864 | tf_op jit(solution)/shard_map/pallas_call | solution.py:316
  95.8 7.8 %collective-permute-done.12.refs_3_.refs_11_ = s16[528,512]{1,0:T(8,128)(2,1)} collective-permute-done((s16[528,512]{1,0:T(8,128)(2,1)}, s16[528,512]{1,0:T(8,128)(2,1)}, u32[]{:S(2)}, u32[]{:S(2)}) %collective-permute-start.12) | collective-permute-done | bytes 540704 | tf_op jit(solution)/shard_map/ppermute | solution.py:463
  112.5 14.5 %collective-permute-done.15.refs_12_ = s16[528,256]{1,0:T(8,128)(2,1)S(1)} collective-permute-done((s16[528,256]{1,0:T(8,128)(2,1)S(1)}, s16[528,256]{1,0:T(8,128)(2,1)S(1)}, u32[]{:S(2)}, u32[]{:S(2)}) %collective-permute-start.15) | collective-permute-done | bytes 270368 | tf_op jit(solution)/shard_map/ppermute | solution.py:463
  127.0 6.3 %shard_map.108 = (f32[384,512]{1,0:T(8,128)S(1)}, s16[400,512]{1,0:T(8,128)(2,1)S(1)}, f32[8,128]{1,0:T(8,128)S(1)}) custom-call(s32[1]{0:T(128)} %bitcast.refs_0_, bf16[1,3,2,72,256]{4,3,2,1,0:T(8,128)(2,1)S(1)} %copy-done.11, bf16[1,3,2,72,256]{4,3,2,1,0:T(8,128)(2,1)S(1)} %copy-done.13, bf16[1,3,2,72,256]{4,3,2,1,0:T(8,128)(2,1)} %collective-permute-done.1.refs_3_, ...), custom_call_target="tpu_custom_call" | custom-call | flops 43750000 | bytes 125000 | tf_op jit(solution)/shard_map/pallas_call | solution.py:453
  136.2 3.5 %collective-permute-start.20 = (s16[528,512]{1,0:T(8,128)(2,1)S(1)}, s16[528,512]{1,0:T(8,128)(2,1)S(1)}, u32[]{:S(2)}, u32[]{:S(2)}) collective-permute-start(s16[528,512]{1,0:T(8,128)(2,1)S(1)} %get-tuple-element.98), channel_id=1, source_target_pairs={{0,8},{4,12},{8,0},{12,4},{16,24},{20,28},{24,16},{28,20},{1,9},{5... | collective-permute-start | bytes 1622024 | tf_op jit(solution)/shard_map/ppermute | solution.py:463
  139.8 17.0 %collective-permute-done.18.refs_12_ = s16[528,256]{1,0:T(8,128)(2,1)S(1)} collective-permute-done((s16[528,256]{1,0:T(8,128)(2,1)S(1)}, s16[528,256]{1,0:T(8,128)(2,1)S(1)}, u32[]{:S(2)}, u32[]{:S(2)}) %collective-permute-start.18) | collective-permute-done | bytes 270368 | tf_op jit(solution)/shard_map/ppermute | solution.py:463
  156.8 6.2 %shard_map.111 = (f32[384,512]{1,0:T(8,128)S(1)}, s16[400,512]{1,0:T(8,128)(2,1)S(1)}, f32[8,128]{1,0:T(8,128)S(1)}) custom-call(s32[1]{0:T(128)} %bitcast.refs_0_, bf16[1,3,2,72,256]{4,3,2,1,0:T(8,128)(2,1)S(1)} %copy-done.11, bf16[1,3,2,72,256]{4,3,2,1,0:T(8,128)(2,1)S(1)} %copy-done.13, bf16[1,3,2,72,256]{4,3,2,1,0:T(8,128)(2,1)} %collective-permute-done.1.refs_3_, ...), custom_call_target="tpu_custom_call" | custom-call | flops 43750000 | bytes 125000 | tf_op jit(solution)/shard_map/pallas_call | solution.py:453
  164.2 3.4 %collective-permute-start.26 = (s16[528,256]{1,0:T(8,128)(2,1)S(1)}, s16[528,256]{1,0:T(8,128)(2,1)S(1)}, u32[]{:S(2)}, u32[]{:S(2)}) collective-permute-start(s16[528,256]{1,0:T(8,128)(2,1)S(1)} %get-tuple-element.104), channel_id=1, source_target_pairs={{0,16},{4,20},{8,24},{12,28},{16,0},{20,4},{24,8},{28,12},{1,17},{... | collective-permute-start | bytes 811016 | tf_op jit(solution)/shard_map/ppermute | solution.py:463
  167.7 12.9 %collective-permute-done.26.refs_12_ = s16[528,256]{1,0:T(8,128)(2,1)S(1)} collective-permute-done((s16[528,256]{1,0:T(8,128)(2,1)S(1)}, s16[528,256]{1,0:T(8,128)(2,1)S(1)}, u32[]{:S(2)}, u32[]{:S(2)}) %collective-permute-start.26) | collective-permute-done | bytes 270368 | tf_op jit(solution)/shard_map/ppermute | solution.py:463
  180.5 6.6 %shard_map.115 = (f32[384,512]{1,0:T(8,128)S(1)}, s16[400,512]{1,0:T(8,128)(2,1)S(1)}, f32[8,128]{1,0:T(8,128)}) custom-call(s32[1]{0:T(128)} %bitcast.refs_0_, bf16[1,3,2,72,256]{4,3,2,1,0:T(8,128)(2,1)S(1)} %copy-done.11, bf16[1,3,2,72,256]{4,3,2,1,0:T(8,128)(2,1)S(1)} %copy-done.13, bf16[1,3,2,72,256]{4,3,2,1,0:T(8,128)(2,1)} %collective-permute-done.1.refs_3_, ...), custom_call_target="tpu_custom_call" | custom-call | flops 43750000 | bytes 125000 | tf_op jit(solution)/shard_map/pallas_call | solution.py:453
  190.4 14.4 %collective-permute-done.28.heard_ref = s16[1,208,512]{2,1,0:T(8,128)(2,1)S(1)} collective-permute-done((s16[1,208,512]{2,1,0:T(8,128)(2,1)S(1)}, s16[1,208,512]{2,1,0:T(8,128)(2,1)S(1)}, u32[]{:S(2)}, u32[]{:S(2)}) %collective-permute-start.28) | collective-permute-done | bytes 213024 | tf_op jit(solution)/shard_map/ppermute | solution.py:463
  207.5 5.4 %collective-permute-done.29 = f32[4,1,96,128]{3,2,1,0:T(8,128)S(1)} collective-permute-done((f32[4,1,96,128]{3,2,1,0:T(8,128)S(1)}, f32[4,1,96,128]{3,2,1,0:T(8,128)S(1)}, u32[]{:S(2)}, u32[]{:S(2)}) %collective-permute-start.29) | collective-permute-done | bytes 196640 | tf_op jit(solution)/shard_map/ppermute | solution.py:463
  213.0 7.0 %collective-permute-done.23 = f32[4,2,96,128]{3,2,1,0:T(8,128)S(1)} collective-permute-done((f32[4,2,96,128]{3,2,1,0:T(8,128)S(1)}, f32[4,2,96,128]{3,2,1,0:T(8,128)S(1)}, u32[]{:S(2)}, u32[]{:S(2)}) %collective-permute-start.23) | collective-permute-done | bytes 393248 | tf_op jit(solution)/shard_map/ppermute | solution.py:463
  221.5 5.4 %collective-permute-done.24 = f32[2,2,96,128]{3,2,1,0:T(8,128)S(1)} collective-permute-done((f32[2,2,96,128]{3,2,1,0:T(8,128)S(1)}, f32[2,2,96,128]{3,2,1,0:T(8,128)S(1)}, u32[]{:S(2)}, u32[]{:S(2)}) %collective-permute-start.24) | collective-permute-done | bytes 196640 | tf_op jit(solution)/shard_map/ppermute | solution.py:463
  227.1 5.6 %collective-permute-done.25 = f32[1,2,96,128]{3,2,1,0:T(8,128)S(1)} collective-permute-done((f32[1,2,96,128]{3,2,1,0:T(8,128)S(1)}, f32[1,2,96,128]{3,2,1,0:T(8,128)S(1)}, u32[]{:S(2)}, u32[]{:S(2)}) %collective-permute-start.25) | collective-permute-done | bytes 98336 | tf_op jit(solution)/shard_map/ppermute | solution.py:463
  (169 shorter events, 64.1 us)
Async XLA Ops:
  10.8 14.4 %collective-permute-start.10 = (bf16[1,2,2,64,1024]{4,3,2,1,0:T(8,128)(2,1)S(1)}, bf16[1,2,2,64,1024]{4,3,2,1,0:T(8,128)(2,1)S(1)}, u32[]{:S(2)}, u32[]{:S(2)}) collective-permute-start(bf16[1,2,2,64,1024]{4,3,2,1,0:T(8,128)(2,1)S(1)} %bitcast.30), channel_id=1, source_target_pairs={{0,2},{1,3},{2,0},{3,1},{4,6},{5,7},{6,4},{7,5},{8,10},{9,11},{10,... | collective-permute-start | bytes 1572872 | tf_op jit(solution)/shard_map/ppermute | solution.py:463
  12.6 31.1 %collective-permute-start.3 = (bf16[4,3,2,72,256]{4,3,2,1,0:T(8,128)(2,1)}, bf16[4,3,2,72,256]{4,3,2,1,0:T(8,128)(2,1)}, u32[]{:S(2)}, u32[]{:S(2)}) collective-permute-start(bf16[4,3,2,72,256]{4,3,2,1,0:T(8,128)(2,1)} %get-tuple-element.61), channel_id=1, source_target_pairs={{0,4},{4,0},{8,12},{12,8},{16,20},{20,16},{24,28},{28,24},{1,5},{5... | collective-permute-start | bytes 2654216 | tf_op jit(solution)/shard_map/ppermute | solution.py:463
  26.4 19.4 %collective-permute-start.11 = (bf16[2,2,2,64,1024]{4,3,2,1,0:T(8,128)(2,1)}, bf16[2,2,2,64,1024]{4,3,2,1,0:T(8,128)(2,1)S(1)}, u32[]{:S(2)}, u32[]{:S(2)}) collective-permute-start(bf16[2,2,2,64,1024]{4,3,2,1,0:T(8,128)(2,1)} %pad_maximum_fusion.1), channel_id=1, source_target_pairs={{0,1},{1,0},{2,3},{3,2},{4,5},{5,4},{6,7},{7,6},{8,9},{9,8},{10,11... | collective-permute-start | bytes 3145736 | tf_op jit(solution)/shard_map/ppermute | solution.py:463
  26.4 14.0 %collective-permute-start = (bf16[1,3,2,72,256]{4,3,2,1,0:T(8,128)(2,1)}, bf16[1,3,2,72,256]{4,3,2,1,0:T(8,128)(2,1)S(1)}, u32[]{:S(2)}, u32[]{:S(2)}) collective-permute-start(bf16[1,3,2,72,256]{4,3,2,1,0:T(8,128)(2,1)} %get-tuple-element.58), channel_id=1, source_target_pairs={{0,16},{4,20},{8,24},{12,28},{16,0},{20,4},{24,8},{28,12},{1,17},{... | collective-permute-start | bytes 663560 | tf_op jit(solution)/shard_map/ppermute | solution.py:463
  29.3 40.1 %collective-permute-start.1 = (bf16[1,3,2,72,256]{4,3,2,1,0:T(8,128)(2,1)}, bf16[1,3,2,72,256]{4,3,2,1,0:T(8,128)(2,1)}, u32[]{:S(2)}, u32[]{:S(2)}) collective-permute-start(bf16[1,3,2,72,256]{4,3,2,1,0:T(8,128)(2,1)} %get-tuple-element.59), channel_id=1, source_target_pairs={{0,8},{4,12},{8,0},{12,4},{16,24},{20,28},{24,16},{28,20},{1,9},{5... | collective-permute-start | bytes 663560 | tf_op jit(solution)/shard_map/ppermute | solution.py:463
  31.6 53.6 %collective-permute-start.9 = (s16[528,1024]{1,0:T(8,128)(2,1)}, s16[528,1024]{1,0:T(8,128)(2,1)}, u32[]{:S(2)}, u32[]{:S(2)}) collective-permute-start(s16[528,1024]{1,0:T(8,128)(2,1)} %copy-done.17), channel_id=1, source_target_pairs={{0,4},{4,0},{8,12},{12,8},{16,20},{20,16},{24,28},{28,24},{1,5},{5... | collective-permute-start | bytes 3244040 | tf_op jit(solution)/shard_map/ppermute | solution.py:463
  42.2 21.3 %collective-permute-start.13 = (bf16[1,2,96,1024]{3,2,1,0:T(8,128)(2,1)S(1)}, bf16[1,2,96,1024]{3,2,1,0:T(8,128)(2,1)}, u32[]{:S(2)}, u32[]{:S(2)}) collective-permute-start(bf16[1,2,96,1024]{3,2,1,0:T(8,128)(2,1)S(1)} %bitcast.36), channel_id=1, source_target_pairs={{0,2},{1,3},{2,0},{3,1},{4,6},{5,7},{6,4},{7,5},{8,10},{9,11},{10,... | collective-permute-start | bytes 1179656 | tf_op jit(solution)/shard_map/ppermute | solution.py:463
  45.8 34.6 %collective-permute-start.6 = (bf16[1,3,2,72,256]{4,3,2,1,0:T(8,128)(2,1)}, bf16[1,3,2,72,256]{4,3,2,1,0:T(8,128)(2,1)}, u32[]{:S(2)}, u32[]{:S(2)}) collective-permute-start(bf16[1,3,2,72,256]{4,3,2,1,0:T(8,128)(2,1)} %get-tuple-element.111), channel_id=1, source_target_pairs={{0,16},{4,20},{8,24},{12,28},{16,0},{20,4},{24,8},{28,12},{1,17},{... | collective-permute-start | bytes 663560 | tf_op jit(solution)/shard_map/ppermute | solution.py:463
  56.6 48.7 %collective-permute-start.16 = (s16[528,1024]{1,0:T(8,128)(2,1)}, s16[528,1024]{1,0:T(8,128)(2,1)}, u32[]{:S(2)}, u32[]{:S(2)}) collective-permute-start(s16[528,1024]{1,0:T(8,128)(2,1)} %get-tuple-element.84), channel_id=1, source_target_pairs={{0,4},{4,0},{8,12},{12,8},{16,20},{20,16},{24,28},{28,24},{1,5},{5... | collective-permute-start | bytes 3244040 | tf_op jit(solution)/shard_map/ppermute | solution.py:463
  63.4 18.3 %collective-permute-start.7 = (bf16[1,3,2,72,256]{4,3,2,1,0:T(8,128)(2,1)}, bf16[1,3,2,72,256]{4,3,2,1,0:T(8,128)(2,1)}, u32[]{:S(2)}, u32[]{:S(2)}) collective-permute-start(bf16[1,3,2,72,256]{4,3,2,1,0:T(8,128)(2,1)} %get-tuple-element.110), channel_id=1, source_target_pairs={{0,8},{4,12},{8,0},{12,4},{16,24},{20,28},{24,16},{28,20},{1,9},{5... | collective-permute-start | bytes 663560 | tf_op jit(solution)/shard_map/ppermute | solution.py:463
  69.4 15.8 %collective-permute-start.8 = (bf16[1,3,2,72,256]{4,3,2,1,0:T(8,128)(2,1)}, bf16[1,3,2,72,256]{4,3,2,1,0:T(8,128)(2,1)}, u32[]{:S(2)}, u32[]{:S(2)}) collective-permute-start(bf16[1,3,2,72,256]{4,3,2,1,0:T(8,128)(2,1)} %get-tuple-element.109), channel_id=1, source_target_pairs={{0,24},{4,28},{8,16},{12,20},{16,8},{20,12},{24,0},{28,4},{1,25},{... | collective-permute-start | bytes 663560 | tf_op jit(solution)/shard_map/ppermute | solution.py:463
  80.4 11.0 %collective-permute-start.14 = (bf16[2,2,96,1024]{3,2,1,0:T(8,128)(2,1)}, bf16[2,2,96,1024]{3,2,1,0:T(8,128)(2,1)S(1)}, u32[]{:S(2)}, u32[]{:S(2)}) collective-permute-start(bf16[2,2,96,1024]{3,2,1,0:T(8,128)(2,1)} %pad_maximum_fusion.2), channel_id=1, source_target_pairs={{0,1},{1,0},{2,3},{3,2},{4,5},{5,4},{6,7},{7,6},{8,9},{9,8},{10,11... | collective-permute-start | bytes 2359304 | tf_op jit(solution)/shard_map/ppermute | solution.py:463
  81.8 30.7 %collective-permute-start.2 = (bf16[1,3,2,72,256]{4,3,2,1,0:T(8,128)(2,1)}, bf16[1,3,2,72,256]{4,3,2,1,0:T(8,128)(2,1)S(1)}, u32[]{:S(2)}, u32[]{:S(2)}) collective-permute-start(bf16[1,3,2,72,256]{4,3,2,1,0:T(8,128)(2,1)} %copy-done.18), channel_id=1, source_target_pairs={{0,24},{4,28},{8,16},{12,20},{16,8},{20,12},{24,0},{28,4},{1,25},{... | collective-permute-start | bytes 663560 | tf_op jit(solution)/shard_map/ppermute | solution.py:463
  88.8 14.9 %collective-permute-start.12 = (s16[528,512]{1,0:T(8,128)(2,1)}, s16[528,512]{1,0:T(8,128)(2,1)}, u32[]{:S(2)}, u32[]{:S(2)}) collective-permute-start(s16[528,512]{1,0:T(8,128)(2,1)} %get-tuple-element.75), channel_id=1, source_target_pairs={{0,8},{4,12},{8,0},{12,4},{16,24},{20,28},{24,16},{28,20},{1,9},{5... | collective-permute-start | bytes 1622024 | tf_op jit(solution)/shard_map/ppermute | solution.py:463
  89.2 45.8 %collective-permute-start.19 = (s16[528,1024]{1,0:T(8,128)(2,1)}, s16[528,1024]{1,0:T(8,128)(2,1)S(1)}, u32[]{:S(2)}, u32[]{:S(2)}) collective-permute-start(s16[528,1024]{1,0:T(8,128)(2,1)} %copy-done.16), channel_id=1, source_target_pairs={{0,4},{4,0},{8,12},{12,8},{16,20},{20,16},{24,28},{28,24},{1,5},{5... | collective-permute-start | bytes 3244040 | tf_op jit(solution)/shard_map/ppermute | solution.py:463
  108.4 24.9 %collective-permute-start.17 = (s16[528,512]{1,0:T(8,128)(2,1)S(1)}, s16[528,512]{1,0:T(8,128)(2,1)S(1)}, u32[]{:S(2)}, u32[]{:S(2)}) collective-permute-start(s16[528,512]{1,0:T(8,128)(2,1)S(1)} %get-tuple-element.88), channel_id=1, source_target_pairs={{0,8},{4,12},{8,0},{12,4},{16,24},{20,28},{24,16},{28,20},{1,9},{5... | collective-permute-start | bytes 1622024 | tf_op jit(solution)/shard_map/ppermute | solution.py:463
  109.8 17.2 %collective-permute-start.15 = (s16[528,256]{1,0:T(8,128)(2,1)S(1)}, s16[528,256]{1,0:T(8,128)(2,1)S(1)}, u32[]{:S(2)}, u32[]{:S(2)}) collective-permute-start(s16[528,256]{1,0:T(8,128)(2,1)S(1)} %get-tuple-element.81), channel_id=1, source_target_pairs={{0,16},{4,20},{8,24},{12,28},{16,0},{20,4},{24,8},{28,12},{1,17},{... | collective-permute-start | bytes 811016 | tf_op jit(solution)/shard_map/ppermute | solution.py:463
  136.2 26.9 %collective-permute-start.20 = (s16[528,512]{1,0:T(8,128)(2,1)S(1)}, s16[528,512]{1,0:T(8,128)(2,1)S(1)}, u32[]{:S(2)}, u32[]{:S(2)}) collective-permute-start(s16[528,512]{1,0:T(8,128)(2,1)S(1)} %get-tuple-element.98), channel_id=1, source_target_pairs={{0,8},{4,12},{8,0},{12,4},{16,24},{20,28},{24,16},{28,20},{1,9},{5... | collective-permute-start | bytes 1622024 | tf_op jit(solution)/shard_map/ppermute | solution.py:463
  139.8 17.0 %collective-permute-start.18 = (s16[528,256]{1,0:T(8,128)(2,1)S(1)}, s16[528,256]{1,0:T(8,128)(2,1)S(1)}, u32[]{:S(2)}, u32[]{:S(2)}) collective-permute-start(s16[528,256]{1,0:T(8,128)(2,1)S(1)} %get-tuple-element.90), channel_id=1, source_target_pairs={{0,16},{4,20},{8,24},{12,28},{16,0},{20,4},{24,8},{28,12},{1,17},{... | collective-permute-start | bytes 811016 | tf_op jit(solution)/shard_map/ppermute | solution.py:463
  164.1 23.2 %collective-permute-start.21 = (s16[2,400,512]{2,1,0:T(8,128)(2,1)S(1)}, s16[2,400,512]{2,1,0:T(8,128)(2,1)S(1)}, u32[]{:S(2)}, u32[]{:S(2)}) collective-permute-start(s16[2,400,512]{2,1,0:T(8,128)(2,1)S(1)} %pad_add_fusion), channel_id=1, source_target_pairs={{0,1},{1,0},{2,3},{3,2},{4,5},{5,4},{6,7},{7,6},{8,9},{9,8},{10,11... | collective-permute-start | bytes 2457608 | tf_op jit(solution)/shard_map/ppermute | solution.py:463
  164.2 16.3 %collective-permute-start.26 = (s16[528,256]{1,0:T(8,128)(2,1)S(1)}, s16[528,256]{1,0:T(8,128)(2,1)S(1)}, u32[]{:S(2)}, u32[]{:S(2)}) collective-permute-start(s16[528,256]{1,0:T(8,128)(2,1)S(1)} %get-tuple-element.104), channel_id=1, source_target_pairs={{0,16},{4,20},{8,24},{12,28},{16,0},{20,4},{24,8},{28,12},{1,17},{... | collective-permute-start | bytes 811016 | tf_op jit(solution)/shard_map/ppermute | solution.py:463
  187.9 17.6 %collective-permute-start.22 = (s16[2,208,512]{2,1,0:T(8,128)(2,1)S(1)}, s16[2,208,512]{2,1,0:T(8,128)(2,1)S(1)}, u32[]{:S(2)}, u32[]{:S(2)}) collective-permute-start(s16[2,208,512]{2,1,0:T(8,128)(2,1)S(1)} %get-tuple-element.103), channel_id=1, source_target_pairs={{0,2},{1,3},{2,0},{3,1},{4,6},{5,7},{6,4},{7,5},{8,10},{9,11},{10,... | collective-permute-start | bytes 1277960 | tf_op jit(solution)/shard_map/ppermute | solution.py:463
  189.2 15.5 %collective-permute-start.28 = (s16[1,208,512]{2,1,0:T(8,128)(2,1)S(1)}, s16[1,208,512]{2,1,0:T(8,128)(2,1)S(1)}, u32[]{:S(2)}, u32[]{:S(2)}) collective-permute-start(s16[1,208,512]{2,1,0:T(8,128)(2,1)S(1)} %get-tuple-element.108), channel_id=1, source_target_pairs={{0,2},{1,3},{2,0},{3,1},{4,6},{5,7},{6,4},{7,5},{8,10},{9,11},{10,... | collective-permute-start | bytes 638984 | tf_op jit(solution)/shard_map/ppermute | solution.py:463
  205.9 14.1 %collective-permute-start.23 = (f32[4,2,96,128]{3,2,1,0:T(8,128)S(1)}, f32[4,2,96,128]{3,2,1,0:T(8,128)S(1)}, u32[]{:S(2)}, u32[]{:S(2)}) collective-permute-start(f32[4,2,96,128]{3,2,1,0:T(8,128)S(1)} %slice.77), channel_id=1, source_target_pairs={{0,4},{4,0},{8,12},{12,8},{16,20},{20,16},{24,28},{28,24},{1,5},{5... | collective-permute-start | bytes 1179656 | tf_op jit(solution)/shard_map/ppermute | solution.py:463
  (36 other events, 231.9 us)

commit v8 on v7

--- a/solution.py
+++ b/solution.py
@@ -81,28 +81,29 @@
     return number
 
 
-def shift_kernel(order, me_ref, con_ref, map_ref, *refs):
-    *stay_refs, go_ref, token_ref = refs
-    half, _, _, rows, width = go_ref.shape
+def shift_kernel(order, me_ref, con_ref, map_ref, stay_ref, go_ref, token_ref):
+    slots, _, _, rows, width = stay_ref.shape
     count = len(order).bit_length() - 1
     token_ref[...] = jnp.zeros_like(token_ref)
-    for p, slot in enumerate(order):
-        out_ref = stay_refs[p].at[0] if p < half else go_ref.at[p - half]
-        first = reversed_bits(jnp.bitwise_xor(me_ref[0], slot), count) * width
-        for block in range(width // GBLK):
-            cols = pl.ds(pl.multiple_of(first + block * GBLK, GBLK), GBLK)
-            within = jnp.bitwise_and(map_ref[0, 0:1, cols], GBLK - 1)
-            within = jnp.broadcast_to(within, (rows, GBLK))
-            for part in range(2):
-                values = con_ref[0, part, :, cols].astype(jnp.float32)
-                moved = jnp.take_along_axis(values, within, axis=1)
-                out_ref[0, part, :, block * GBLK : (block + 1) * GBLK] = moved.astype(jnp.bfloat16)
+    for which, out_ref in enumerate((stay_ref, go_ref)):
+        for slot in range(slots):
+            dest = jnp.bitwise_xor(me_ref[0], order[which * slots + slot])
+            first = reversed_bits(dest, count) * width
+            for block in range(width // GBLK):
+                cols = pl.ds(pl.multiple_of(first + block * GBLK, GBLK), GBLK)
+                within = jnp.bitwise_and(map_ref[0, 0:1, cols], GBLK - 1)
+                within = jnp.broadcast_to(within, (rows, GBLK))
+                for part in range(2):
+                    values = con_ref[0, part, :, cols].astype(jnp.float32)
+                    moved = jnp.take_along_axis(values, within, axis=1)
+                    out_ref[slot, 0, part, :, block * GBLK : (block + 1) * GBLK] = moved.astype(
+                        jnp.bfloat16
+                    )
 
 
 def shift_call(con, shift_map, me, order, width):
     points, _, rows, slab = con.shape
-    half = len(order) // 2
-    counts = [1] * half + [half]
+    slots = len(order) // 2
     grid_spec = pltpu.PrefetchScalarGridSpec(
         num_scalar_prefetch=1,
         grid=(points,),
@@ -110,17 +111,13 @@
             pl.BlockSpec((1, 2, rows, slab), lambda q, me: (q, 0, 0, 0)),
             pl.BlockSpec((1, 1, slab), lambda q, me: (q, 0, 0)),
         ],
-        out_specs=[
-            pl.BlockSpec((n, 1, 2, rows, width), lambda q, me: (0, q, 0, 0, 0)) for n in counts
-        ]
+        out_specs=[pl.BlockSpec((slots, 1, 2, rows, width), lambda q, me: (0, q, 0, 0, 0))] * 2
         + [pl.BlockSpec(TOKEN.shape, lambda q, me: (0, 0))],
     )
     return pl.pallas_call(
         lambda *refs: shift_kernel(order, *refs),
         grid_spec=grid_spec,
-        out_shape=[
-            jax.ShapeDtypeStruct((n, points, 2, rows, width), jnp.bfloat16) for n in counts
-        ]
+        out_shape=[jax.ShapeDtypeStruct((slots, points, 2, rows, width), jnp.bfloat16)] * 2
         + [TOKEN],
         compiler_params=params(),
         cost_estimate=cost(8 * con.size, 4 * con.size),
@@ -463,21 +460,6 @@
     return lax.ppermute(value, axis, [(i, i ^ bit) for i in range(size)])
 
 
-def gather_slots(value, axis, size, token=None):
-    found = {0: (value[None], 0)}
-    bit = size // 2
-    while bit:
-        known = sorted(found)
-        sent = jnp.concatenate([found[r][0][found[r][1] :][:1] for r in known])
-        if token is not None and len(known) > 1:
-            sent = behind(sent, token)
-        got = swap(sent, axis, size, bit)
-        for place, r in enumerate(known):
-            found[r ^ bit] = (got, place)
-        bit //= 2
-    return [found[r] for r in range(size)]
-
-
 def halving_order(bits):
     order = [0]
     for bit in reversed(bits):
@@ -502,38 +484,16 @@
     ga_order = halving_order(ga_bits)
     stages, half = len(ga_bits), ga // 2
 
-    con = jnp.transpose(con_density, (1, 2, 0, 3))
-    *stay, go, token = shift_call(con, shift_map, me, ga_order, width)
-    first = gather_slots(jnp.transpose(val_density[:, :1], (1, 2, 0, 3)), "pair", pair, token)
+    val = jnp.transpose(val_density, (1, 2, 0, 3))
+    vals = {0: val}
+    for bit in reversed(pair_bits):
+        for slot in sorted(vals):
+            vals[slot ^ bit] = swap(vals[slot], "pair", pair, bit)
+
+    con = jnp.transpose(behind(con_density, val), (1, 2, 0, 3))
+    stay, go, token = shift_call(con, shift_map, me, ga_order, width)
     nearest = ga_bits[0]
     from_near = swap(go, "ga", ga, nearest)
-    cons = {0: (stay[0], 0)}
-    for slot, block in zip(ga_order[1:half], stay[1:]):
-        cons[slot] = (swap(block, "ga", ga, slot), 0)
-    later = behind(val_density[:, 1:], first[pair // 2][0])
-    later = jnp.transpose(later, (1, 2, 0, 3))
-
-    gone, keep, tokens = [], [], [token]
-    for q in range(points):
-        vals, place = (first, 0) if q == 0 else (others, q - 1)
-        coded, own, token = x_call(vals, screened, place, q, me, 4, tokens[-1:])
-        if q == 0:
-            first_token = token
-            others = gather_slots(later, "pair", pair, first_token)
-        if q + 1 < min(points, half):
-            token = behind(token, cons[ga_order[q + 1]][0])
-        tokens.append(token)
-        gone.append(coded)
-        keep.append(own)
-    after = tokens[-1:]
-
-    from_near = behind(from_near, first_token)
-    for place, slot in enumerate(ga_order[half:]):
-        cons[slot] = (from_near, 0)
-        if slot != nearest:
-            cons[slot] = (swap(from_near[place : place + 1], "ga", ga, slot ^ nearest), 0)
-    after = [behind(after[0], [cons[slot][0] for slot in ga_order[half:]])]
-    cons = [cons[slot] for slot in ga_order]
 
     row_count, col_count = NT // pair, NT // ga
     row_slots = jnp.asarray(halving_order(pair_bits), jnp.int32)
@@ -553,38 +513,64 @@
 
     col_direct, col_exch = pick_cols(at_direct, NT, -1.0), pick_cols(at_exch, row_count, 2.0)
 
+    there = jnp.transpose(trans_there, (1, 2, 0, 3))
+    here = jnp.transpose(behind(trans_here, vals[pair // 2]), (1, 0, 2))
+    heres = {0: here, pair // 2: swap(here, "pair", pair, pair // 2)}
+    token = behind(
+        token, (there, heres[pair // 2], pick_rows, col_direct, col_exch, from_near)
+    )
+    gone, keep = [], []
+    for q in range(points):
+        coded, own, token = x_call(
+            [(vals[slot][None], 0) for slot in range(pair)], screened, q, q, me, 4, [token]
+        )
+        gone.append(coded)
+        keep.append(own)
+        if q == 0:
+            stay, from_near = behind((stay, from_near), token)
+            cons = {0: (stay, 0), nearest: (from_near, 0)}
+            for place, slot in enumerate(ga_order[1:half], 1):
+                both = swap(jnp.stack([stay[place], from_near[place]]), "ga", ga, slot)
+                cons[slot], cons[slot ^ nearest] = (both, 0), (both, 1)
+    after = [behind(token, [cons[slot][0] for slot in ga_order[:half] if slot & ga_bits[-1]])]
+    cons = [cons[slot] for slot in ga_order]
+
     heard = [[swap(gone[q], "ga", ga, ga_bits[0])] for q in range(points)]
     tiles = [None] * points
     exch = None
-    for wave in range(2 * points + stages):
-        for q in reversed(range(points)):
-            stage = wave - 2 * q
-            if 1 <= stage < stages:
-                columns = (ga >> (stage + 1)) * width
-                coded, token = hop_call(keep[q], heard[q], me, stage, columns, after)
-                after = [token]
-                heard[q].append(swap(coded, "ga", ga, ga_bits[stage]))
-                if exch is None:
-                    here = jnp.transpose(behind(trans_here, tokens[1]), (1, 0, 2))
-                    heres = gather_slots(here, "pair", pair, tokens[-1])
-                    there = jnp.transpose(behind(trans_there, tokens[1]), (1, 2, 0, 3))
-                    exch, token = exchange_call(heres, there, coulomb, after)
-                    after = [token]
-            elif stage == stages:
-                *tiles[q], token = tile_call(
-                    cons, q, keep[q], heard[q], exch, me, ga_order, pick_rows, col_direct,
-                    col_exch, pair, after,
-                )
+    work = [(2 * q + stage, q, stage) for q in range(points) for stage in range(1, stages)]
+    work += [(2 * q + stages + (1.2 if q == 0 else 0.8), q, stages) for q in range(points)]
+    for _, q, stage in sorted(work):
+        if stage < stages:
+            columns = (ga >> (stage + 1)) * width
+            coded, token = hop_call(keep[q], heard[q], me, stage, columns, after)
+            after = [token]
+            heard[q].append(swap(coded, "ga", ga, ga_bits[stage]))
+            if (q, stage) == (0, 1):
+                for bit in reversed(pair_bits[:-1]):
+                    for slot in sorted(heres):
+                        heres[slot ^ bit] = swap(behind(heres[slot], token), "pair", pair, bit)
+            elif exch is None:
+                slots = [(heres[slot][None], 0) for slot in range(pair)]
+                after = [behind(token, [c for c, _ in cons])]
+                exch, token = exchange_call(slots, there, coulomb, after)
                 after = [token]
             if (q, stage) == (points - 1, stages - 1):
-                gate = token
-
+                own, sent = (jnp.stack(items) for items in zip(*tiles[:-1]))
+                early = fold_call(own, swap(behind(sent, token), "pair", pair, pair_bits[0]))
+                after = [behind(token, early[0])]
+        else:
+            *tiles[q], token = tile_call(
+                cons, q, keep[q], heard[q], exch, me, ga_order, pick_rows, col_direct,
+                col_exch, pair, after,
+            )
+            after = [token]
+
+    own, sent = (part[None] for part in tiles[-1])
+    late = fold_call(own, swap(sent, "pair", pair, pair_bits[0]))
     outs = []
-    for group in (tiles[:-1], tiles[-1:]):
-        own, sent = (jnp.stack(items) for items in zip(*group))
-        if len(outs) == 0:
-            sent = behind(sent, gate)
-        for bit in pair_bits[:-1]:
+    for own, sent in (early, late):
+        for bit in pair_bits[1:-1]:
             own, sent = fold_call(own, swap(sent, "pair", pair, bit))
         total = pack_call(own, swap(sent, "pair", pair, pair_bits[-1]))
         for bit in ga_bits:
@@ -693,7 +679,7 @@
             ga & (ga - 1) == 0
             and pair & (pair - 1) == 0
             and ga >= 4
-            and pair >= 2
+            and pair >= 4
             and NT % (pair * GROUP // 2) == 0
             and h_count % (ga * pair * GBLK) == 0
             and con_count % (8 * ga) == 0

time: 234 us -> 231 us (0.987)
  waiting for transfers between devices: 101 us -> 137 us
  local copies, waits for them, and re-layouts: 20.9 us -> 7.66 us
  starting transfers between devices: 40.3 us -> 30.4 us
  Pallas kernels: 64.1 us -> 54.2 us
  other arithmetic: 6.24 us -> 1.43 us
    ppermute x32 -> x29, waiting for transfers between devices: 101 us -> 137 us  [swap(): return lax.ppermute(value, axis, [(i, i ^ bit) for i in range(size)])]
    ppermute x32 -> x29, starting transfers between devices: 40.3 us -> 30.4 us  [swap(): return lax.ppermute(value, axis, [(i, i ^ bit) for i in range(size)])]
    pallas_call x6, Pallas kernels: 11.9 us -> 6.32 us  [hop_call(): pl.pallas_call(lambda *refs: hop_kernel(len(others), *refs), grid_spec=gr...]
    unnamed x56 -> x14, local copies, waits for them, and re-layouts: 7.58 us -> 2.98 us
    pallas_call x3, Pallas kernels: 19.2 us -> 15.8 us  [tile_call(): pl.pallas_call(lambda *refs: tile_kernel(order, stages, chunks, len(after...]
    concatenate x3 -> x0, other arithmetic: 3.19 us -> none  [gather_slots(): sent = jnp.concatenate([found[r][0][found[r][1]:][:1] for r in known])]
    slice x4 -> x1, local copies, waits for them, and re-layouts: 3.17 us -> 0.09 us  [on_device(): both = swap(jnp.stack([stay[place], from_near[place]]), 'ga', ga, slot)]
  transfers between devices with their start and end apart: 32 -> 29, of which waited for: 13 -> 15; matrix products, arithmetic and copies ran while one was open for 8% -> 3% of each run, Pallas kernels for 27% -> 16%
where the time goes in v8:
time: 231 us
  waiting for transfers between devices  137 us (59%)
  Pallas kernels  54.2 us (23%)
  starting transfers between devices  30.4 us (13%)
  local copies, waits for them, and re-layouts  7.66 us (3%)
    ppermute x29, waiting for transfers between devices, swap(): return lax.ppermute(value, axis, [(i, i ^ bit) for i in range(size)])  137 us
    ppermute x29, starting transfers between devices, swap(): return lax.ppermute(value, axis, [(i, i ^ bit) for i in range(size)])  30.4 us
    pallas_call x3, Pallas kernels, x_call(): pl.pallas_call(lambda *refs: x_kernel(slots, len(after), *refs), grid_spe...  25.3 us
    pallas_call x3, Pallas kernels, tile_call(): pl.pallas_call(lambda *refs: tile_kernel(order, stages, chunks, len(after...  15.8 us
    pallas_call x6, Pallas kernels, hop_call(): pl.pallas_call(lambda *refs: hop_kernel(len(others), *refs), grid_spec=gr...  6.32 us
  transfers between devices with their start and end apart: 29, of which 15 were waited for; matrix products, arithmetic and copies ran while one was open for 3% of the time, Pallas kernels for 16%

profile of v8, /device:TPU:0, one launch (start us, length us, event | category | flops | bytes accessed | tf_op | source)
XLA Modules:
  0.0 231.0 jit_solution(11494826896960663311)
XLA Ops:
  1.4 3.0 %collective-permute-start.2 = (bf16[3,2,64,1024]{3,2,1,0:T(8,128)(2,1)S(1)}, bf16[3,2,64,1024]{3,2,1,0:T(8,128)(2,1)S(1)}, u32[]{:S(2)}, u32[]{:S(2)}) collective-permute-start(bf16[3,2,64,1024]{3,2,1,0:T(8,128)(2,1)S(1)} %bitcast.35), channel_id=1, source_target_pairs={{0,2},{1,3},{2,0},{3,1},{4,6},{5,7},{6,4},{7,5},{8,10},{9,11},{10,... | collective-permute-start | bytes 2359304 | tf_op jit(solution)/shard_map/ppermute | solution.py:460
  12.4 9.5 %collective-permute-done.2 = bf16[3,2,64,1024]{3,2,1,0:T(8,128)(2,1)S(1)} collective-permute-done((bf16[3,2,64,1024]{3,2,1,0:T(8,128)(2,1)S(1)}, bf16[3,2,64,1024]{3,2,1,0:T(8,128)(2,1)S(1)}, u32[]{:S(2)}, u32[]{:S(2)}) %collective-permute-start.2) | collective-permute-done | bytes 786464 | tf_op jit(solution)/shard_map/ppermute | solution.py:460
  25.7 5.3 %collective-permute-done.refs_5_ = bf16[4,3,2,72,256]{4,3,2,1,0:T(8,128)(2,1)S(1)} collective-permute-done((bf16[4,3,2,72,256]{4,3,2,1,0:T(8,128)(2,1)}, bf16[4,3,2,72,256]{4,3,2,1,0:T(8,128)(2,1)S(1)}, u32[]{:S(2)}, u32[]{:S(2)}) %collective-permute-start) | collective-permute-done | bytes 884768 | tf_op jit(solution)/shard_map/ppermute | solution.py:460
  31.0 4.3 %collective-permute-done.4 = bf16[2,96,1024]{2,1,0:T(8,128)(2,1)S(1)} collective-permute-done((bf16[2,96,1024]{2,1,0:T(8,128)(2,1)S(1)}, bf16[2,96,1024]{2,1,0:T(8,128)(2,1)S(1)}, u32[]{:S(2)}, u32[]{:S(2)}) %collective-permute-start.4) | collective-permute-done | bytes 393248 | tf_op jit(solution)/shard_map/ppermute | solution.py:460
  35.3 8.2 %shard_map.101 = (s16[528,1024]{1,0:T(8,128)(2,1)S(1)}, f32[512,1024]{1,0:T(8,128)S(1)}, f32[8,128]{1,0:T(8,128)S(1)}) custom-call(s32[1]{0:T(128)} %bitcast.refs_0_, bf16[1,3,2,64,1024]{4,3,2,1,0:T(8,128)(2,1)S(1)} %bitcast.37, bf16[1,3,2,64,1024]{4,3,2,1,0:T(8,128)(2,1)} %bitcast.4.refs_2_, bf16[1,3,2,64,1024]{4,3,2,1,0:T(8,128)(2,1)S(1)} %bitcast.41, ...), custom_call_target="tpu_custom_call" | custom-call | flops 67108864 | bytes 180224 | tf_op jit(solution)/shard_map/pallas_call | solution.py:186
  45.5 3.7 %collective-permute-start.7 = (bf16[2,3,2,72,256]{4,3,2,1,0:T(8,128)(2,1)S(1)}, bf16[2,3,2,72,256]{4,3,2,1,0:T(8,128)(2,1)S(1)}, u32[]{:S(2)}, u32[]{:S(2)}) collective-permute-start(bf16[2,3,2,72,256]{4,3,2,1,0:T(8,128)(2,1)S(1)} %pad_maximum_fusion.3), channel_id=1, source_target_pairs={{0,24},{4,28},{8,16},{12,20},{16,8},{20,12},{24,0},{28,4},{1,25},{... | collective-permute-start | bytes 1327112 | tf_op jit(solution)/shard_map/ppermute | solution.py:460
  49.3 8.9 %shard_map.102 = (s16[528,1024]{1,0:T(8,128)(2,1)}, f32[512,1024]{1,0:T(8,128)S(1)}, f32[8,128]{1,0:T(8,128)S(1)}) custom-call(s32[1]{0:T(128)} %bitcast.refs_0_, bf16[1,3,2,64,1024]{4,3,2,1,0:T(8,128)(2,1)S(1)} %bitcast.38, bf16[1,3,2,64,1024]{4,3,2,1,0:T(8,128)(2,1)} %bitcast.4.refs_2_, bf16[1,3,2,64,1024]{4,3,2,1,0:T(8,128)(2,1)S(1)} %bitcast.42, ...), custom_call_target="tpu_custom_call" | custom-call | flops 67108864 | bytes 180224 | tf_op jit(solution)/shard_map/pallas_call | solution.py:186
  58.8 8.2 %shard_map.103 = (s16[528,1024]{1,0:T(8,128)(2,1)S(1)}, f32[512,1024]{1,0:T(8,128)S(1)}, f32[8,128]{1,0:T(8,128)S(1)}) custom-call(s32[1]{0:T(128)} %bitcast.refs_0_, bf16[1,3,2,64,1024]{4,3,2,1,0:T(8,128)(2,1)S(1)} %bitcast.39, bf16[1,3,2,64,1024]{4,3,2,1,0:T(8,128)(2,1)} %bitcast.4.refs_2_, bf16[1,3,2,64,1024]{4,3,2,1,0:T(8,128)(2,1)S(1)} %bitcast.43, ...), custom_call_target="tpu_custom_call" | custom-call | flops 67108864 | bytes 180224 | tf_op jit(solution)/shard_map/pallas_call | solution.py:186
  67.0 19.6 %collective-permute-done.5.refs_2_.refs_6_ = bf16[2,3,2,72,256]{4,3,2,1,0:T(8,128)(2,1)S(1)} collective-permute-done((bf16[2,3,2,72,256]{4,3,2,1,0:T(8,128)(2,1)S(1)}, bf16[2,3,2,72,256]{4,3,2,1,0:T(8,128)(2,1)S(1)}, u32[]{:S(2)}, u32[]{:S(2)}) %collective-permute-start.5) | collective-permute-done | bytes 442400 | tf_op jit(solution)/shard_map/ppermute | solution.py:460
  90.4 12.6 %collective-permute-done.9.refs_3_.refs_11_ = s16[528,512]{1,0:T(8,128)(2,1)S(1)} collective-permute-done((s16[528,512]{1,0:T(8,128)(2,1)S(1)}, s16[528,512]{1,0:T(8,128)(2,1)S(1)}, u32[]{:S(2)}, u32[]{:S(2)}) %collective-permute-start.9) | collective-permute-done | bytes 540704 | tf_op jit(solution)/shard_map/ppermute | solution.py:460
  103.8 6.7 %collective-permute-done.6.refs_3_.refs_7_ = bf16[2,3,2,72,256]{4,3,2,1,0:T(8,128)(2,1)S(1)} collective-permute-done((bf16[2,3,2,72,256]{4,3,2,1,0:T(8,128)(2,1)S(1)}, bf16[2,3,2,72,256]{4,3,2,1,0:T(8,128)(2,1)S(1)}, u32[]{:S(2)}, u32[]{:S(2)}) %collective-permute-start.6) | collective-permute-done | bytes 442400 | tf_op jit(solution)/shard_map/ppermute | solution.py:460
  110.5 3.4 %shard_map.106 = (f32[3,2,384,96]{3,2,1,0:T(8,128)S(1)}, f32[8,128]{1,0:T(8,128)S(1)}) custom-call(bf16[1,2,96,1024]{3,2,1,0:T(8,128)(2,1)S(1)} %bitcast.50, bf16[1,2,96,1024]{3,2,1,0:T(8,128)(2,1)S(1)} %bitcast.58, bf16[1,2,96,1024]{3,2,1,0:T(8,128)(2,1)S(1)} %bitcast.56, bf16[1,2,96,1024]{3,2,1,0:T(8,128)(2,1)S(1)} %bitcast.57, ...), custom_call_target="tpu_custom_call" | custom-call | flops 28311552 | bytes 36864 | tf_op jit(solution)/shard_map/pallas_call | solution.py:313
  117.6 15.7 %collective-permute-done.14.refs_3_.refs_11_ = s16[528,512]{1,0:T(8,128)(2,1)S(1)} collective-permute-done((s16[528,512]{1,0:T(8,128)(2,1)S(1)}, s16[528,512]{1,0:T(8,128)(2,1)S(1)}, u32[]{:S(2)}, u32[]{:S(2)}) %collective-permute-start.14) | collective-permute-done | bytes 540704 | tf_op jit(solution)/shard_map/ppermute | solution.py:460
  134.3 5.1 %shard_map.109 = (f32[384,512]{1,0:T(8,128)S(1)}, s16[400,512]{1,0:T(8,128)(2,1)S(1)}, f32[8,128]{1,0:T(8,128)S(1)}) custom-call(s32[1]{0:T(128)} %bitcast.refs_0_, bf16[4,3,2,72,256]{4,3,2,1,0:T(8,128)(2,1)S(1)} %get-tuple-element.61.refs_1_, bf16[2,3,2,72,256]{4,3,2,1,0:T(8,128)(2,1)S(1)} %collective-permute-done.5.refs_2_.refs_6_, ...), custom_call_target="tpu_custom_call" | custom-call | flops 43750000 | bytes 125000 | tf_op jit(solution)/shard_map/pallas_call | solution.py:450
  142.5 14.7 %collective-permute-done.15.refs_12_ = s16[528,256]{1,0:T(8,128)(2,1)S(1)} collective-permute-done((s16[528,256]{1,0:T(8,128)(2,1)S(1)}, s16[528,256]{1,0:T(8,128)(2,1)S(1)}, u32[]{:S(2)}, u32[]{:S(2)}) %collective-permute-start.15) | collective-permute-done | bytes 270368 | tf_op jit(solution)/shard_map/ppermute | solution.py:460
  157.2 5.1 %shard_map.111 = (f32[384,512]{1,0:T(8,128)S(1)}, s16[400,512]{1,0:T(8,128)(2,1)S(1)}, f32[8,128]{1,0:T(8,128)S(1)}) custom-call(s32[1]{0:T(128)} %bitcast.refs_0_, bf16[4,3,2,72,256]{4,3,2,1,0:T(8,128)(2,1)S(1)} %get-tuple-element.61.refs_1_, bf16[2,3,2,72,256]{4,3,2,1,0:T(8,128)(2,1)S(1)} %collective-permute-done.5.refs_2_.refs_6_, ...), custom_call_target="tpu_custom_call" | custom-call | flops 43750000 | bytes 125000 | tf_op jit(solution)/shard_map/pallas_call | solution.py:450
  163.5 3.4 %collective-permute-start.23 = (s16[528,256]{1,0:T(8,128)(2,1)S(1)}, s16[528,256]{1,0:T(8,128)(2,1)S(1)}, u32[]{:S(2)}, u32[]{:S(2)}) collective-permute-start(s16[528,256]{1,0:T(8,128)(2,1)S(1)} %get-tuple-element.97), channel_id=1, source_target_pairs={{0,16},{4,20},{8,24},{12,28},{16,0},{20,4},{24,8},{28,12},{1,17},{... | collective-permute-start | bytes 811016 | tf_op jit(solution)/shard_map/ppermute | solution.py:460
  167.7 12.2 %collective-permute-done.23.refs_12_ = s16[528,256]{1,0:T(8,128)(2,1)S(1)} collective-permute-done((s16[528,256]{1,0:T(8,128)(2,1)S(1)}, s16[528,256]{1,0:T(8,128)(2,1)S(1)}, u32[]{:S(2)}, u32[]{:S(2)}) %collective-permute-start.23) | collective-permute-done | bytes 270368 | tf_op jit(solution)/shard_map/ppermute | solution.py:460
  179.8 5.6 %shard_map.115 = (f32[384,512]{1,0:T(8,128)S(1)}, s16[400,512]{1,0:T(8,128)(2,1)S(1)}, f32[8,128]{1,0:T(8,128)}) custom-call(s32[1]{0:T(128)} %bitcast.refs_0_, bf16[4,3,2,72,256]{4,3,2,1,0:T(8,128)(2,1)S(1)} %get-tuple-element.61.refs_1_, bf16[2,3,2,72,256]{4,3,2,1,0:T(8,128)(2,1)S(1)} %collective-permute-done.5.refs_2_.refs_6_, ...), custom_call_target="tpu_custom_call" | custom-call | flops 43750000 | bytes 125000 | tf_op jit(solution)/shard_map/pallas_call | solution.py:450
  189.0 13.2 %collective-permute-done.25.heard_ref = s16[1,208,512]{2,1,0:T(8,128)(2,1)S(1)} collective-permute-done((s16[1,208,512]{2,1,0:T(8,128)(2,1)S(1)}, s16[1,208,512]{2,1,0:T(8,128)(2,1)S(1)}, u32[]{:S(2)}, u32[]{:S(2)}) %collective-permute-start.25) | collective-permute-done | bytes 213024 | tf_op jit(solution)/shard_map/ppermute | solution.py:460
  204.9 5.4 %collective-permute-done.26 = f32[4,1,96,128]{3,2,1,0:T(8,128)S(1)} collective-permute-done((f32[4,1,96,128]{3,2,1,0:T(8,128)S(1)}, f32[4,1,96,128]{3,2,1,0:T(8,128)S(1)}, u32[]{:S(2)}, u32[]{:S(2)}) %collective-permute-start.26) | collective-permute-done | bytes 196640 | tf_op jit(solution)/shard_map/ppermute | solution.py:460
  210.5 7.0 %collective-permute-done.20 = f32[4,2,96,128]{3,2,1,0:T(8,128)S(1)} collective-permute-done((f32[4,2,96,128]{3,2,1,0:T(8,128)S(1)}, f32[4,2,96,128]{3,2,1,0:T(8,128)S(1)}, u32[]{:S(2)}, u32[]{:S(2)}) %collective-permute-start.20) | collective-permute-done | bytes 393248 | tf_op jit(solution)/shard_map/ppermute | solution.py:460
  219.6 4.7 %collective-permute-done.21 = f32[2,2,96,128]{3,2,1,0:T(8,128)S(1)} collective-permute-done((f32[2,2,96,128]{3,2,1,0:T(8,128)S(1)}, f32[2,2,96,128]{3,2,1,0:T(8,128)S(1)}, u32[]{:S(2)}, u32[]{:S(2)}) %collective-permute-start.21) | collective-permute-done | bytes 196640 | tf_op jit(solution)/shard_map/ppermute | solution.py:460
  224.5 5.6 %collective-permute-done.22 = f32[1,2,96,128]{3,2,1,0:T(8,128)S(1)} collective-permute-done((f32[1,2,96,128]{3,2,1,0:T(8,128)S(1)}, f32[1,2,96,128]{3,2,1,0:T(8,128)S(1)}, u32[]{:S(2)}, u32[]{:S(2)}) %collective-permute-start.22) | collective-permute-done | bytes 98336 | tf_op jit(solution)/shard_map/ppermute | solution.py:460
  (117 shorter events, 39.4 us)
Async XLA Ops:
  1.4 20.5 %collective-permute-start.2 = (bf16[3,2,64,1024]{3,2,1,0:T(8,128)(2,1)S(1)}, bf16[3,2,64,1024]{3,2,1,0:T(8,128)(2,1)S(1)}, u32[]{:S(2)}, u32[]{:S(2)}) collective-permute-start(bf16[3,2,64,1024]{3,2,1,0:T(8,128)(2,1)S(1)} %bitcast.35), channel_id=1, source_target_pairs={{0,2},{1,3},{2,0},{3,1},{4,6},{5,7},{6,4},{7,5},{8,10},{9,11},{10,... | collective-permute-start | bytes 2359304 | tf_op jit(solution)/shard_map/ppermute | solution.py:460
  4.4 31.0 %collective-permute-start.1 = (bf16[3,2,64,1024]{3,2,1,0:T(8,128)(2,1)S(1)}, bf16[3,2,64,1024]{3,2,1,0:T(8,128)(2,1)}, u32[]{:S(2)}, u32[]{:S(2)}) collective-permute-start(bf16[3,2,64,1024]{3,2,1,0:T(8,128)(2,1)S(1)} %bitcast.36), channel_id=1, source_target_pairs={{0,1},{1,0},{2,3},{3,2},{4,5},{5,4},{6,7},{7,6},{8,9},{9,8},{10,11... | collective-permute-start | bytes 2359304 | tf_op jit(solution)/shard_map/ppermute | solution.py:460
  8.7 22.3 %collective-permute-start = (bf16[4,3,2,72,256]{4,3,2,1,0:T(8,128)(2,1)}, bf16[4,3,2,72,256]{4,3,2,1,0:T(8,128)(2,1)S(1)}, u32[]{:S(2)}, u32[]{:S(2)}) collective-permute-start(bf16[4,3,2,72,256]{4,3,2,1,0:T(8,128)(2,1)} %get-tuple-element.56), channel_id=1, source_target_pairs={{0,4},{4,0},{8,12},{12,8},{16,20},{20,16},{24,28},{28,24},{1,5},{5... | collective-permute-start | bytes 2654216 | tf_op jit(solution)/shard_map/ppermute | solution.py:460
  21.9 13.4 %collective-permute-start.3 = (bf16[3,2,64,1024]{3,2,1,0:T(8,128)(2,1)S(1)}, bf16[3,2,64,1024]{3,2,1,0:T(8,128)(2,1)S(1)}, u32[]{:S(2)}, u32[]{:S(2)}) collective-permute-start(bf16[3,2,64,1024]{3,2,1,0:T(8,128)(2,1)S(1)} %collective-permute-done.2), channel_id=1, source_target_pairs={{0,1},{1,0},{2,3},{3,2},{4,5},{5,4},{6,7},{7,6},{8,9},{9,8},{10,11... | collective-permute-start | bytes 2359304 | tf_op jit(solution)/shard_map/ppermute | solution.py:460
  23.7 11.6 %collective-permute-start.4 = (bf16[2,96,1024]{2,1,0:T(8,128)(2,1)S(1)}, bf16[2,96,1024]{2,1,0:T(8,128)(2,1)S(1)}, u32[]{:S(2)}, u32[]{:S(2)}) collective-permute-start(bf16[2,96,1024]{2,1,0:T(8,128)(2,1)S(1)} %bitcast.48), channel_id=1, source_target_pairs={{0,2},{1,3},{2,0},{3,1},{4,6},{5,7},{6,4},{7,5},{8,10},{9,11},{10,... | collective-permute-start | bytes 1179656 | tf_op jit(solution)/shard_map/ppermute | solution.py:460
  43.6 43.0 %collective-permute-start.8 = (s16[528,1024]{1,0:T(8,128)(2,1)S(1)}, s16[528,1024]{1,0:T(8,128)(2,1)S(1)}, u32[]{:S(2)}, u32[]{:S(2)}) collective-permute-start(s16[528,1024]{1,0:T(8,128)(2,1)S(1)} %get-tuple-element.64), channel_id=1, source_target_pairs={{0,4},{4,0},{8,12},{12,8},{16,20},{20,16},{24,28},{28,24},{1,5},{5... | collective-permute-start | bytes 3244040 | tf_op jit(solution)/shard_map/ppermute | solution.py:460
  45.5 21.4 %collective-permute-start.7 = (bf16[2,3,2,72,256]{4,3,2,1,0:T(8,128)(2,1)S(1)}, bf16[2,3,2,72,256]{4,3,2,1,0:T(8,128)(2,1)S(1)}, u32[]{:S(2)}, u32[]{:S(2)}) collective-permute-start(bf16[2,3,2,72,256]{4,3,2,1,0:T(8,128)(2,1)S(1)} %pad_maximum_fusion.3), channel_id=1, source_target_pairs={{0,24},{4,28},{8,16},{12,20},{16,8},{20,12},{24,0},{28,4},{1,25},{... | collective-permute-start | bytes 1327112 | tf_op jit(solution)/shard_map/ppermute | solution.py:460
  49.2 37.3 %collective-permute-start.5 = (bf16[2,3,2,72,256]{4,3,2,1,0:T(8,128)(2,1)S(1)}, bf16[2,3,2,72,256]{4,3,2,1,0:T(8,128)(2,1)S(1)}, u32[]{:S(2)}, u32[]{:S(2)}) collective-permute-start(bf16[2,3,2,72,256]{4,3,2,1,0:T(8,128)(2,1)S(1)} %pad_maximum_fusion.1), channel_id=1, source_target_pairs={{0,16},{4,20},{8,24},{12,28},{16,0},{20,4},{24,8},{28,12},{1,17},{... | collective-permute-start | bytes 1327112 | tf_op jit(solution)/shard_map/ppermute | solution.py:460
  58.3 55.7 %collective-permute-start.13 = (s16[528,1024]{1,0:T(8,128)(2,1)}, s16[528,1024]{1,0:T(8,128)(2,1)S(1)}, u32[]{:S(2)}, u32[]{:S(2)}) collective-permute-start(s16[528,1024]{1,0:T(8,128)(2,1)} %get-tuple-element.77), channel_id=1, source_target_pairs={{0,4},{4,0},{8,12},{12,8},{16,20},{20,16},{24,28},{28,24},{1,5},{5... | collective-permute-start | bytes 3244040 | tf_op jit(solution)/shard_map/ppermute | solution.py:460
  87.7 15.3 %collective-permute-start.9 = (s16[528,512]{1,0:T(8,128)(2,1)S(1)}, s16[528,512]{1,0:T(8,128)(2,1)S(1)}, u32[]{:S(2)}, u32[]{:S(2)}) collective-permute-start(s16[528,512]{1,0:T(8,128)(2,1)S(1)} %get-tuple-element.68), channel_id=1, source_target_pairs={{0,8},{4,12},{8,0},{12,4},{16,24},{20,28},{24,16},{28,20},{1,9},{5... | collective-permute-start | bytes 1622024 | tf_op jit(solution)/shard_map/ppermute | solution.py:460
  87.8 51.6 %collective-permute-start.16 = (s16[528,1024]{1,0:T(8,128)(2,1)S(1)}, s16[528,1024]{1,0:T(8,128)(2,1)S(1)}, u32[]{:S(2)}, u32[]{:S(2)}) collective-permute-start(s16[528,1024]{1,0:T(8,128)(2,1)S(1)} %get-tuple-element.85), channel_id=1, source_target_pairs={{0,4},{4,0},{8,12},{12,8},{16,20},{20,16},{24,28},{28,24},{1,5},{5... | collective-permute-start | bytes 3244040 | tf_op jit(solution)/shard_map/ppermute | solution.py:460
  88.4 22.1 %collective-permute-start.6 = (bf16[2,3,2,72,256]{4,3,2,1,0:T(8,128)(2,1)S(1)}, bf16[2,3,2,72,256]{4,3,2,1,0:T(8,128)(2,1)S(1)}, u32[]{:S(2)}, u32[]{:S(2)}) collective-permute-start(bf16[2,3,2,72,256]{4,3,2,1,0:T(8,128)(2,1)S(1)} %pad_maximum_fusion.2), channel_id=1, source_target_pairs={{0,8},{4,12},{8,0},{12,4},{16,24},{20,28},{24,16},{28,20},{1,9},{5... | collective-permute-start | bytes 1327112 | tf_op jit(solution)/shard_map/ppermute | solution.py:460
  90.4 20.1 %collective-permute-start.12 = (bf16[2,96,1024]{2,1,0:T(8,128)(2,1)S(1)}, bf16[2,96,1024]{2,1,0:T(8,128)(2,1)S(1)}, u32[]{:S(2)}, u32[]{:S(2)}) collective-permute-start(bf16[2,96,1024]{2,1,0:T(8,128)(2,1)S(1)} %collective-permute-done.4), channel_id=1, source_target_pairs={{0,1},{1,0},{2,3},{3,2},{4,5},{5,4},{6,7},{7,6},{8,9},{9,8},{10,11... | collective-permute-start | bytes 1179656 | tf_op jit(solution)/shard_map/ppermute | solution.py:460
  103.0 7.5 %collective-permute-start.11 = (bf16[2,96,1024]{2,1,0:T(8,128)(2,1)S(1)}, bf16[2,96,1024]{2,1,0:T(8,128)(2,1)S(1)}, u32[]{:S(2)}, u32[]{:S(2)}) collective-permute-start(bf16[2,96,1024]{2,1,0:T(8,128)(2,1)S(1)} %bitcast.49), channel_id=1, source_target_pairs={{0,1},{1,0},{2,3},{3,2},{4,5},{5,4},{6,7},{7,6},{8,9},{9,8},{10,11... | collective-permute-start | bytes 1179656 | tf_op jit(solution)/shard_map/ppermute | solution.py:460
  115.1 18.2 %collective-permute-start.14 = (s16[528,512]{1,0:T(8,128)(2,1)S(1)}, s16[528,512]{1,0:T(8,128)(2,1)S(1)}, u32[]{:S(2)}, u32[]{:S(2)}) collective-permute-start(s16[528,512]{1,0:T(8,128)(2,1)S(1)} %get-tuple-element.79), channel_id=1, source_target_pairs={{0,8},{4,12},{8,0},{12,4},{16,24},{20,28},{24,16},{28,20},{1,9},{5... | collective-permute-start | bytes 1622024 | tf_op jit(solution)/shard_map/ppermute | solution.py:460
  115.5 18.8 %collective-permute-start.10 = (s16[528,256]{1,0:T(8,128)(2,1)S(1)}, s16[528,256]{1,0:T(8,128)(2,1)S(1)}, u32[]{:S(2)}, u32[]{:S(2)}) collective-permute-start(s16[528,256]{1,0:T(8,128)(2,1)S(1)} %get-tuple-element.70), channel_id=1, source_target_pairs={{0,16},{4,20},{8,24},{12,28},{16,0},{20,4},{24,8},{28,12},{1,17},{... | collective-permute-start | bytes 811016 | tf_op jit(solution)/shard_map/ppermute | solution.py:460
  140.6 21.8 %collective-permute-start.17 = (s16[528,512]{1,0:T(8,128)(2,1)S(1)}, s16[528,512]{1,0:T(8,128)(2,1)S(1)}, u32[]{:S(2)}, u32[]{:S(2)}) collective-permute-start(s16[528,512]{1,0:T(8,128)(2,1)S(1)} %get-tuple-element.91), channel_id=1, source_target_pairs={{0,8},{4,12},{8,0},{12,4},{16,24},{20,28},{24,16},{28,20},{1,9},{5... | collective-permute-start | bytes 1622024 | tf_op jit(solution)/shard_map/ppermute | solution.py:460
  140.7 16.5 %collective-permute-start.15 = (s16[528,256]{1,0:T(8,128)(2,1)S(1)}, s16[528,256]{1,0:T(8,128)(2,1)S(1)}, u32[]{:S(2)}, u32[]{:S(2)}) collective-permute-start(s16[528,256]{1,0:T(8,128)(2,1)S(1)} %get-tuple-element.83), channel_id=1, source_target_pairs={{0,16},{4,20},{8,24},{12,28},{16,0},{20,4},{24,8},{28,12},{1,17},{... | collective-permute-start | bytes 811016 | tf_op jit(solution)/shard_map/ppermute | solution.py:460
  163.5 16.3 %collective-permute-start.23 = (s16[528,256]{1,0:T(8,128)(2,1)S(1)}, s16[528,256]{1,0:T(8,128)(2,1)S(1)}, u32[]{:S(2)}, u32[]{:S(2)}) collective-permute-start(s16[528,256]{1,0:T(8,128)(2,1)S(1)} %get-tuple-element.97), channel_id=1, source_target_pairs={{0,16},{4,20},{8,24},{12,28},{16,0},{20,4},{24,8},{28,12},{1,17},{... | collective-permute-start | bytes 811016 | tf_op jit(solution)/shard_map/ppermute | solution.py:460
  185.4 17.6 %collective-permute-start.19 = (s16[2,208,512]{2,1,0:T(8,128)(2,1)S(1)}, s16[2,208,512]{2,1,0:T(8,128)(2,1)S(1)}, u32[]{:S(2)}, u32[]{:S(2)}) collective-permute-start(s16[2,208,512]{2,1,0:T(8,128)(2,1)S(1)} %get-tuple-element.96), channel_id=1, source_target_pairs={{0,2},{1,3},{2,0},{3,1},{4,6},{5,7},{6,4},{7,5},{8,10},{9,11},{10,... | collective-permute-start | bytes 1277960 | tf_op jit(solution)/shard_map/ppermute | solution.py:460
  187.5 14.8 %collective-permute-start.25 = (s16[1,208,512]{2,1,0:T(8,128)(2,1)S(1)}, s16[1,208,512]{2,1,0:T(8,128)(2,1)S(1)}, u32[]{:S(2)}, u32[]{:S(2)}) collective-permute-start(s16[1,208,512]{2,1,0:T(8,128)(2,1)S(1)} %get-tuple-element.102), channel_id=1, source_target_pairs={{0,2},{1,3},{2,0},{3,1},{4,6},{5,7},{6,4},{7,5},{8,10},{9,11},{10,... | collective-permute-start | bytes 638984 | tf_op jit(solution)/shard_map/ppermute | solution.py:460
  202.4 7.9 %collective-permute-start.26 = (f32[4,1,96,128]{3,2,1,0:T(8,128)S(1)}, f32[4,1,96,128]{3,2,1,0:T(8,128)S(1)}, u32[]{:S(2)}, u32[]{:S(2)}) collective-permute-start(f32[4,1,96,128]{3,2,1,0:T(8,128)S(1)} %slice.87), channel_id=1, source_target_pairs={{0,4},{4,0},{8,12},{12,8},{16,20},{20,16},{24,28},{28,24},{1,5},{5... | collective-permute-start | bytes 589832 | tf_op jit(solution)/shard_map/ppermute | solution.py:460
  203.4 14.1 %collective-permute-start.20 = (f32[4,2,96,128]{3,2,1,0:T(8,128)S(1)}, f32[4,2,96,128]{3,2,1,0:T(8,128)S(1)}, u32[]{:S(2)}, u32[]{:S(2)}) collective-permute-start(f32[4,2,96,128]{3,2,1,0:T(8,128)S(1)} %slice.81), channel_id=1, source_target_pairs={{0,4},{4,0},{8,12},{12,8},{16,20},{20,16},{24,28},{28,24},{1,5},{5... | collective-permute-start | bytes 1179656 | tf_op jit(solution)/shard_map/ppermute | solution.py:460
  210.4 7.3 %collective-permute-start.27 = (f32[2,1,96,128]{3,2,1,0:T(8,128)S(1)}, f32[2,1,96,128]{3,2,1,0:T(8,128)S(1)}, u32[]{:S(2)}, u32[]{:S(2)}) collective-permute-start(f32[2,1,96,128]{3,2,1,0:T(8,128)S(1)} %slice.89), channel_id=1, source_target_pairs={{0,8},{4,12},{8,0},{12,4},{16,24},{20,28},{24,16},{28,20},{1,9},{5... | collective-permute-start | bytes 294920 | tf_op jit(solution)/shard_map/ppermute | solution.py:460
  (11 other events, 66.3 us)

commit v9 on v8

--- a/solution.py
+++ b/solution.py
@@ -81,29 +81,28 @@
     return number
 
 
-def shift_kernel(order, me_ref, con_ref, map_ref, stay_ref, go_ref, token_ref):
-    slots, _, _, rows, width = stay_ref.shape
+def shift_kernel(order, me_ref, con_ref, map_ref, *refs):
+    *stay_refs, go_ref, token_ref = refs
+    half, _, _, rows, width = go_ref.shape
     count = len(order).bit_length() - 1
     token_ref[...] = jnp.zeros_like(token_ref)
-    for which, out_ref in enumerate((stay_ref, go_ref)):
-        for slot in range(slots):
-            dest = jnp.bitwise_xor(me_ref[0], order[which * slots + slot])
-            first = reversed_bits(dest, count) * width
-            for block in range(width // GBLK):
-                cols = pl.ds(pl.multiple_of(first + block * GBLK, GBLK), GBLK)
-                within = jnp.bitwise_and(map_ref[0, 0:1, cols], GBLK - 1)
-                within = jnp.broadcast_to(within, (rows, GBLK))
-                for part in range(2):
-                    values = con_ref[0, part, :, cols].astype(jnp.float32)
-                    moved = jnp.take_along_axis(values, within, axis=1)
-                    out_ref[slot, 0, part, :, block * GBLK : (block + 1) * GBLK] = moved.astype(
-                        jnp.bfloat16
-                    )
+    for p, slot in enumerate(order):
+        out_ref = stay_refs[p].at[0] if p < half else go_ref.at[p - half]
+        first = reversed_bits(jnp.bitwise_xor(me_ref[0], slot), count) * width
+        for block in range(width // GBLK):
+            cols = pl.ds(pl.multiple_of(first + block * GBLK, GBLK), GBLK)
+            within = jnp.bitwise_and(map_ref[0, 0:1, cols], GBLK - 1)
+            within = jnp.broadcast_to(within, (rows, GBLK))
+            for part in range(2):
+                values = con_ref[0, part, :, cols].astype(jnp.float32)
+                moved = jnp.take_along_axis(values, within, axis=1)
+                out_ref[0, part, :, block * GBLK : (block + 1) * GBLK] = moved.astype(jnp.bfloat16)
 
 
 def shift_call(con, shift_map, me, order, width):
     points, _, rows, slab = con.shape
-    slots = len(order) // 2
+    half = len(order) // 2
+    counts = [1] * half + [half]
     grid_spec = pltpu.PrefetchScalarGridSpec(
         num_scalar_prefetch=1,
         grid=(points,),
@@ -111,13 +110,17 @@
             pl.BlockSpec((1, 2, rows, slab), lambda q, me: (q, 0, 0, 0)),
             pl.BlockSpec((1, 1, slab), lambda q, me: (q, 0, 0)),
         ],
-        out_specs=[pl.BlockSpec((slots, 1, 2, rows, width), lambda q, me: (0, q, 0, 0, 0))] * 2
+        out_specs=[
+            pl.BlockSpec((n, 1, 2, rows, width), lambda q, me: (0, q, 0, 0, 0)) for n in counts
+        ]
         + [pl.BlockSpec(TOKEN.shape, lambda q, me: (0, 0))],
     )
     return pl.pallas_call(
         lambda *refs: shift_kernel(order, *refs),
         grid_spec=grid_spec,
-        out_shape=[jax.ShapeDtypeStruct((slots, points, 2, rows, width), jnp.bfloat16)] * 2
+        out_shape=[
+            jax.ShapeDtypeStruct((n, points, 2, rows, width), jnp.bfloat16) for n in counts
+        ]
         + [TOKEN],
         compiler_params=params(),
         cost_estimate=cost(8 * con.size, 4 * con.size),
@@ -491,9 +494,12 @@
             vals[slot ^ bit] = swap(vals[slot], "pair", pair, bit)
 
     con = jnp.transpose(behind(con_density, val), (1, 2, 0, 3))
-    stay, go, token = shift_call(con, shift_map, me, ga_order, width)
+    *stay, go, token = shift_call(con, shift_map, me, ga_order, width)
     nearest = ga_bits[0]
     from_near = swap(go, "ga", ga, nearest)
+    cons = {0: (stay[0], 0)}
+    for slot, block in zip(ga_order[1:half], stay[1:]):
+        cons[slot] = (swap(block, "ga", ga, slot), 0)
 
     row_count, col_count = NT // pair, NT // ga
     row_slots = jnp.asarray(halving_order(pair_bits), jnp.int32)
@@ -516,9 +522,8 @@
     there = jnp.transpose(trans_there, (1, 2, 0, 3))
     here = jnp.transpose(behind(trans_here, vals[pair // 2]), (1, 0, 2))
     heres = {0: here, pair // 2: swap(here, "pair", pair, pair // 2)}
-    token = behind(
-        token, (there, heres[pair // 2], pick_rows, col_direct, col_exch, from_near)
-    )
+    arrived = [cons[slot][0] for slot in ga_order[:half]]
+    token = behind(token, (there, pick_rows, col_direct, col_exch, from_near, arrived))
     gone, keep = [], []
     for q in range(points):
         coded, own, token = x_call(
@@ -527,22 +532,27 @@
         gone.append(coded)
         keep.append(own)
         if q == 0:
-            stay, from_near = behind((stay, from_near), token)
-            cons = {0: (stay, 0), nearest: (from_near, 0)}
-            for place, slot in enumerate(ga_order[1:half], 1):
-                both = swap(jnp.stack([stay[place], from_near[place]]), "ga", ga, slot)
-                cons[slot], cons[slot ^ nearest] = (both, 0), (both, 1)
-    after = [behind(token, [cons[slot][0] for slot in ga_order[:half] if slot & ga_bits[-1]])]
+            from_near = behind(from_near, token)
+            for place, slot in enumerate(ga_order[half:]):
+                cons[slot] = (from_near, 0)
+                if slot != nearest:
+                    moved = swap(from_near[place : place + 1], "ga", ga, slot ^ nearest)
+                    cons[slot] = (moved, 0)
+        elif q == 1:
+            token = behind(token, heres[pair // 2])
+    after = [behind(token, [cons[slot][0] for slot in ga_order[half:]])]
     cons = [cons[slot] for slot in ga_order]
 
     heard = [[swap(gone[q], "ga", ga, ga_bits[0])] for q in range(points)]
     tiles = [None] * points
     exch = None
     work = [(2 * q + stage, q, stage) for q in range(points) for stage in range(1, stages)]
-    work += [(2 * q + stages + (1.2 if q == 0 else 0.8), q, stages) for q in range(points)]
+    work += [(2 * q + stages + (2.2 if q == 0 else 0.8), q, stages) for q in range(points)]
     for _, q, stage in sorted(work):
         if stage < stages:
             columns = (ga >> (stage + 1)) * width
+            if q > 0 and stage == stages - 1:
+                after = [behind(after[0], heard[q - 1][-1])]
             coded, token = hop_call(keep[q], heard[q], me, stage, columns, after)
             after = [token]
             heard[q].append(swap(coded, "ga", ga, ga_bits[stage]))

time: 231 us -> 212 us (0.918)
  waiting for transfers between devices: 137 us -> 99.4 us
  starting transfers between devices: 30.4 us -> 46.4 us
    ppermute x29 -> x32, waiting for transfers between devices: 137 us -> 99.4 us  [swap(): return lax.ppermute(value, axis, [(i, i ^ bit) for i in range(size)])]
    ppermute x29 -> x32, starting transfers between devices: 30.4 us -> 46.4 us  [swap(): return lax.ppermute(value, axis, [(i, i ^ bit) for i in range(size)])]
    pallas_call x3, Pallas kernels: 15.8 us -> 18.4 us  [tile_call(): pl.pallas_call(lambda *refs: tile_kernel(order, stages, chunks, len(after...]
  transfers between devices with their start and end apart: 29 -> 32, of which waited for: 15 -> 15; matrix products, arithmetic and copies ran while one was open for 3% -> 3% of each run, Pallas kernels for 16% -> 18%
where the time goes in v9:
time: 212 us
  waiting for transfers between devices  99.4 us (47%)
  Pallas kernels  56.1 us (26%)
  starting transfers between devices  46.4 us (22%)
  local copies, waits for them, and re-layouts  8.31 us (4%)
    ppermute x32, waiting for transfers between devices, swap(): return lax.ppermute(value, axis, [(i, i ^ bit) for i in range(size)])  99.4 us
    ppermute x32, starting transfers between devices, swap(): return lax.ppermute(value, axis, [(i, i ^ bit) for i in range(size)])  46.4 us
    pallas_call x3, Pallas kernels, x_call(): pl.pallas_call(lambda *refs: x_kernel(slots, len(after), *refs), grid_spe...  24.6 us
    pallas_call x3, Pallas kernels, tile_call(): pl.pallas_call(lambda *refs: tile_kernel(order, stages, chunks, len(after...  18.4 us
    pallas_call x6, Pallas kernels, hop_call(): pl.pallas_call(lambda *refs: hop_kernel(len(others), *refs), grid_spec=gr...  6.31 us
  transfers between devices with their start and end apart: 32, of which 15 were waited for; matrix products, arithmetic and copies ran while one was open for 3% of the time, Pallas kernels for 18%

profile of v9, /device:TPU:0, one launch (start us, length us, event | category | flops | bytes accessed | tf_op | source)
XLA Modules:
  0.0 212.0 jit_solution(16104798706648504231)
XLA Ops:
  17.3 4.6 %collective-permute-done.5 = bf16[3,2,64,1024]{3,2,1,0:T(8,128)(2,1)S(1)} collective-permute-done((bf16[3,2,64,1024]{3,2,1,0:T(8,128)(2,1)S(1)}, bf16[3,2,64,1024]{3,2,1,0:T(8,128)(2,1)S(1)}, u32[]{:S(2)}, u32[]{:S(2)}) %collective-permute-start.5) | collective-permute-done | bytes 786464 | tf_op jit(solution)/shard_map/ppermute | solution.py:463
  23.8 3.9 %collective-permute-start.2 = (bf16[1,3,2,72,256]{4,3,2,1,0:T(8,128)(2,1)S(1)}, bf16[1,3,2,72,256]{4,3,2,1,0:T(8,128)(2,1)S(1)}, u32[]{:S(2)}, u32[]{:S(2)}) collective-permute-start(bf16[1,3,2,72,256]{4,3,2,1,0:T(8,128)(2,1)S(1)} %copy-done.1), channel_id=1, source_target_pairs={{0,24},{4,28},{8,16},{12,20},{16,8},{20,12},{24,0},{28,4},{1,25},{... | collective-permute-start | bytes 663560 | tf_op jit(solution)/shard_map/ppermute | solution.py:463
  27.7 6.2 %collective-permute-done.2.refs_4_ = bf16[1,3,2,72,256]{4,3,2,1,0:T(8,128)(2,1)S(1)} collective-permute-done((bf16[1,3,2,72,256]{4,3,2,1,0:T(8,128)(2,1)S(1)}, bf16[1,3,2,72,256]{4,3,2,1,0:T(8,128)(2,1)S(1)}, u32[]{:S(2)}, u32[]{:S(2)}) %collective-permute-start.2) | collective-permute-done | bytes 221216 | tf_op jit(solution)/shard_map/ppermute | solution.py:463
  35.3 8.2 %shard_map.101 = (s16[528,1024]{1,0:T(8,128)(2,1)S(1)}, f32[512,1024]{1,0:T(8,128)S(1)}, f32[8,128]{1,0:T(8,128)S(1)}) custom-call(s32[1]{0:T(128)} %bitcast.refs_0_, bf16[1,3,2,64,1024]{4,3,2,1,0:T(8,128)(2,1)S(1)} %bitcast.37, bf16[1,3,2,64,1024]{4,3,2,1,0:T(8,128)(2,1)S(1)} %bitcast.44, bf16[1,3,2,64,1024]{4,3,2,1,0:T(8,128)(2,1)S(1)} %bitcast.41, ...), custom_call_target="tpu_custom_call" | custom-call | flops 67108864 | bytes 180224 | tf_op jit(solution)/shard_map/pallas_call | solution.py:189
  45.9 8.2 %shard_map.102 = (s16[528,1024]{1,0:T(8,128)(2,1)S(1)}, f32[512,1024]{1,0:T(8,128)S(1)}, f32[8,128]{1,0:T(8,128)S(1)}) custom-call(s32[1]{0:T(128)} %bitcast.refs_0_, bf16[1,3,2,64,1024]{4,3,2,1,0:T(8,128)(2,1)S(1)} %bitcast.38, bf16[1,3,2,64,1024]{4,3,2,1,0:T(8,128)(2,1)S(1)} %bitcast.45, bf16[1,3,2,64,1024]{4,3,2,1,0:T(8,128)(2,1)S(1)} %bitcast.42, ...), custom_call_target="tpu_custom_call" | custom-call | flops 67108864 | bytes 180224 | tf_op jit(solution)/shard_map/pallas_call | solution.py:189
  54.7 5.0 %collective-permute-start.7 = (bf16[1,3,2,72,256]{4,3,2,1,0:T(8,128)(2,1)S(1)}, bf16[1,3,2,72,256]{4,3,2,1,0:T(8,128)(2,1)S(1)}, u32[]{:S(2)}, u32[]{:S(2)}) collective-permute-start(bf16[1,3,2,72,256]{4,3,2,1,0:T(8,128)(2,1)S(1)} %get-tuple-element.115), channel_id=1, source_target_pairs={{0,16},{4,20},{8,24},{12,28},{16,0},{20,4},{24,8},{28,12},{1,17},{... | collective-permute-start | bytes 663560 | tf_op jit(solution)/shard_map/ppermute | solution.py:463
  61.2 8.2 %shard_map.103 = (s16[528,1024]{1,0:T(8,128)(2,1)S(1)}, f32[512,1024]{1,0:T(8,128)S(1)}, f32[8,128]{1,0:T(8,128)S(1)}) custom-call(s32[1]{0:T(128)} %bitcast.refs_0_, bf16[1,3,2,64,1024]{4,3,2,1,0:T(8,128)(2,1)S(1)} %bitcast.39, bf16[1,3,2,64,1024]{4,3,2,1,0:T(8,128)(2,1)S(1)} %bitcast.46, bf16[1,3,2,64,1024]{4,3,2,1,0:T(8,128)(2,1)S(1)} %bitcast.43, ...), custom_call_target="tpu_custom_call" | custom-call | flops 67108864 | bytes 180224 | tf_op jit(solution)/shard_map/pallas_call | solution.py:189
  69.3 5.5 %collective-permute-done.7.refs_6_ = bf16[1,3,2,72,256]{4,3,2,1,0:T(8,128)(2,1)S(1)} collective-permute-done((bf16[1,3,2,72,256]{4,3,2,1,0:T(8,128)(2,1)S(1)}, bf16[1,3,2,72,256]{4,3,2,1,0:T(8,128)(2,1)S(1)}, u32[]{:S(2)}, u32[]{:S(2)}) %collective-permute-start.7) | collective-permute-done | bytes 221216 | tf_op jit(solution)/shard_map/ppermute | solution.py:463
  76.0 4.1 %collective-permute-start.12 = (s16[528,512]{1,0:T(8,128)(2,1)S(1)}, s16[528,512]{1,0:T(8,128)(2,1)S(1)}, u32[]{:S(2)}, u32[]{:S(2)}) collective-permute-start(s16[528,512]{1,0:T(8,128)(2,1)S(1)} %get-tuple-element.76), channel_id=1, source_target_pairs={{0,8},{4,12},{8,0},{12,4},{16,24},{20,28},{24,16},{28,20},{1,9},{5... | collective-permute-start | bytes 1622024 | tf_op jit(solution)/shard_map/ppermute | solution.py:463
  82.1 9.3 %collective-permute-done.12.refs_3_.refs_11_ = s16[528,512]{1,0:T(8,128)(2,1)S(1)} collective-permute-done((s16[528,512]{1,0:T(8,128)(2,1)S(1)}, s16[528,512]{1,0:T(8,128)(2,1)S(1)}, u32[]{:S(2)}, u32[]{:S(2)}) %collective-permute-start.12) | collective-permute-done | bytes 540704 | tf_op jit(solution)/shard_map/ppermute | solution.py:463
  92.2 3.4 %shard_map.106 = (f32[3,2,384,96]{3,2,1,0:T(8,128)S(1)}, f32[8,128]{1,0:T(8,128)S(1)}) custom-call(bf16[1,2,96,1024]{3,2,1,0:T(8,128)(2,1)S(1)} %bitcast.53, bf16[1,2,96,1024]{3,2,1,0:T(8,128)(2,1)S(1)} %bitcast.61, bf16[1,2,96,1024]{3,2,1,0:T(8,128)(2,1)S(1)} %bitcast.59, bf16[1,2,96,1024]{3,2,1,0:T(8,128)(2,1)S(1)} %bitcast.60, ...), custom_call_target="tpu_custom_call" | custom-call | flops 28311552 | bytes 36864 | tf_op jit(solution)/shard_map/pallas_call | solution.py:316
  98.8 15.2 %collective-permute-done.13.refs_12_ = s16[528,256]{1,0:T(8,128)(2,1)S(1)} collective-permute-done((s16[528,256]{1,0:T(8,128)(2,1)S(1)}, s16[528,256]{1,0:T(8,128)(2,1)S(1)}, u32[]{:S(2)}, u32[]{:S(2)}) %collective-permute-start.13) | collective-permute-done | bytes 270368 | tf_op jit(solution)/shard_map/ppermute | solution.py:463
  120.9 6.0 %shard_map.110 = (f32[384,512]{1,0:T(8,128)S(1)}, s16[400,512]{1,0:T(8,128)(2,1)S(1)}, f32[8,128]{1,0:T(8,128)S(1)}) custom-call(s32[1]{0:T(128)} %bitcast.refs_0_, bf16[1,3,2,72,256]{4,3,2,1,0:T(8,128)(2,1)S(1)} %get-tuple-element.60.refs_1_, bf16[1,3,2,72,256]{4,3,2,1,0:T(8,128)(2,1)} %collective-permute-done.refs_2_, ...), custom_call_target="tpu_custom_call" | custom-call | flops 43750000 | bytes 125000 | tf_op jit(solution)/shard_map/pallas_call | solution.py:453
  126.9 9.3 %collective-permute-done.19.refs_12_ = s16[528,256]{1,0:T(8,128)(2,1)S(1)} collective-permute-done((s16[528,256]{1,0:T(8,128)(2,1)S(1)}, s16[528,256]{1,0:T(8,128)(2,1)S(1)}, u32[]{:S(2)}, u32[]{:S(2)}) %collective-permute-start.19) | collective-permute-done | bytes 270368 | tf_op jit(solution)/shard_map/ppermute | solution.py:463
  136.1 6.0 %shard_map.111 = (f32[384,512]{1,0:T(8,128)S(1)}, s16[400,512]{1,0:T(8,128)(2,1)S(1)}, f32[8,128]{1,0:T(8,128)S(1)}) custom-call(s32[1]{0:T(128)} %bitcast.refs_0_, bf16[1,3,2,72,256]{4,3,2,1,0:T(8,128)(2,1)S(1)} %get-tuple-element.60.refs_1_, bf16[1,3,2,72,256]{4,3,2,1,0:T(8,128)(2,1)} %collective-permute-done.refs_2_, ...), custom_call_target="tpu_custom_call" | custom-call | flops 43750000 | bytes 125000 | tf_op jit(solution)/shard_map/pallas_call | solution.py:453
  143.3 3.4 %collective-permute-start.26 = (s16[528,256]{1,0:T(8,128)(2,1)S(1)}, s16[528,256]{1,0:T(8,128)(2,1)S(1)}, u32[]{:S(2)}, u32[]{:S(2)}) collective-permute-start(s16[528,256]{1,0:T(8,128)(2,1)S(1)} %get-tuple-element.107), channel_id=1, source_target_pairs={{0,16},{4,20},{8,24},{12,28},{16,0},{20,4},{24,8},{28,12},{1,17},{... | collective-permute-start | bytes 811016 | tf_op jit(solution)/shard_map/ppermute | solution.py:463
  147.5 12.2 %collective-permute-done.26.refs_12_ = s16[528,256]{1,0:T(8,128)(2,1)S(1)} collective-permute-done((s16[528,256]{1,0:T(8,128)(2,1)S(1)}, s16[528,256]{1,0:T(8,128)(2,1)S(1)}, u32[]{:S(2)}, u32[]{:S(2)}) %collective-permute-start.26) | collective-permute-done | bytes 270368 | tf_op jit(solution)/shard_map/ppermute | solution.py:463
  159.6 6.5 %shard_map.115 = (f32[384,512]{1,0:T(8,128)S(1)}, s16[400,512]{1,0:T(8,128)(2,1)S(1)}, f32[8,128]{1,0:T(8,128)}) custom-call(s32[1]{0:T(128)} %bitcast.refs_0_, bf16[1,3,2,72,256]{4,3,2,1,0:T(8,128)(2,1)S(1)} %get-tuple-element.60.refs_1_, bf16[1,3,2,72,256]{4,3,2,1,0:T(8,128)(2,1)} %collective-permute-done.refs_2_, ...), custom_call_target="tpu_custom_call" | custom-call | flops 43750000 | bytes 125000 | tf_op jit(solution)/shard_map/pallas_call | solution.py:453
  169.7 13.2 %collective-permute-done.28.heard_ref = s16[1,208,512]{2,1,0:T(8,128)(2,1)S(1)} collective-permute-done((s16[1,208,512]{2,1,0:T(8,128)(2,1)S(1)}, s16[1,208,512]{2,1,0:T(8,128)(2,1)S(1)}, u32[]{:S(2)}, u32[]{:S(2)}) %collective-permute-start.28) | collective-permute-done | bytes 213024 | tf_op jit(solution)/shard_map/ppermute | solution.py:463
  185.6 5.4 %collective-permute-done.29 = f32[4,1,96,128]{3,2,1,0:T(8,128)S(1)} collective-permute-done((f32[4,1,96,128]{3,2,1,0:T(8,128)S(1)}, f32[4,1,96,128]{3,2,1,0:T(8,128)S(1)}, u32[]{:S(2)}, u32[]{:S(2)}) %collective-permute-start.29) | collective-permute-done | bytes 196640 | tf_op jit(solution)/shard_map/ppermute | solution.py:463
  191.1 7.0 %collective-permute-done.23 = f32[4,2,96,128]{3,2,1,0:T(8,128)S(1)} collective-permute-done((f32[4,2,96,128]{3,2,1,0:T(8,128)S(1)}, f32[4,2,96,128]{3,2,1,0:T(8,128)S(1)}, u32[]{:S(2)}, u32[]{:S(2)}) %collective-permute-start.23) | collective-permute-done | bytes 393248 | tf_op jit(solution)/shard_map/ppermute | solution.py:463
  198.3 3.1 %collective-permute-start.31 = (f32[1,1,96,128]{3,2,1,0:T(8,128)S(1)}, f32[1,1,96,128]{3,2,1,0:T(8,128)S(1)}, u32[]{:S(2)}, u32[]{:S(2)}) collective-permute-start(f32[1,1,96,128]{3,2,1,0:T(8,128)S(1)} %slice.79), channel_id=1, source_target_pairs={{0,16},{4,20},{8,24},{12,28},{16,0},{20,4},{24,8},{28,12},{1,17},{... | collective-permute-start | bytes 147464 | tf_op jit(solution)/shard_map/ppermute | solution.py:463
  201.4 3.6 %collective-permute-done.24 = f32[2,2,96,128]{3,2,1,0:T(8,128)S(1)} collective-permute-done((f32[2,2,96,128]{3,2,1,0:T(8,128)S(1)}, f32[2,2,96,128]{3,2,1,0:T(8,128)S(1)}, u32[]{:S(2)}, u32[]{:S(2)}) %collective-permute-start.24) | collective-permute-done | bytes 196640 | tf_op jit(solution)/shard_map/ppermute | solution.py:463
  205.9 5.2 %collective-permute-done.25 = f32[1,2,96,128]{3,2,1,0:T(8,128)S(1)} collective-permute-done((f32[1,2,96,128]{3,2,1,0:T(8,128)S(1)}, f32[1,2,96,128]{3,2,1,0:T(8,128)S(1)}, u32[]{:S(2)}, u32[]{:S(2)}) %collective-permute-start.25) | collective-permute-done | bytes 98336 | tf_op jit(solution)/shard_map/ppermute | solution.py:463
  (124 shorter events, 49.0 us)
Async XLA Ops:
  1.4 20.5 %collective-permute-start.5 = (bf16[3,2,64,1024]{3,2,1,0:T(8,128)(2,1)S(1)}, bf16[3,2,64,1024]{3,2,1,0:T(8,128)(2,1)S(1)}, u32[]{:S(2)}, u32[]{:S(2)}) collective-permute-start(bf16[3,2,64,1024]{3,2,1,0:T(8,128)(2,1)S(1)} %bitcast.35), channel_id=1, source_target_pairs={{0,2},{1,3},{2,0},{3,1},{4,6},{5,7},{6,4},{7,5},{8,10},{9,11},{10,... | collective-permute-start | bytes 2359304 | tf_op jit(solution)/shard_map/ppermute | solution.py:463
  4.4 31.0 %collective-permute-start.4 = (bf16[3,2,64,1024]{3,2,1,0:T(8,128)(2,1)S(1)}, bf16[3,2,64,1024]{3,2,1,0:T(8,128)(2,1)S(1)}, u32[]{:S(2)}, u32[]{:S(2)}) collective-permute-start(bf16[3,2,64,1024]{3,2,1,0:T(8,128)(2,1)S(1)} %bitcast.36), channel_id=1, source_target_pairs={{0,1},{1,0},{2,3},{3,2},{4,5},{5,4},{6,7},{7,6},{8,9},{9,8},{10,11... | collective-permute-start | bytes 2359304 | tf_op jit(solution)/shard_map/ppermute | solution.py:463
  9.4 14.3 %collective-permute-start = (bf16[1,3,2,72,256]{4,3,2,1,0:T(8,128)(2,1)}, bf16[1,3,2,72,256]{4,3,2,1,0:T(8,128)(2,1)}, u32[]{:S(2)}, u32[]{:S(2)}) collective-permute-start(bf16[1,3,2,72,256]{4,3,2,1,0:T(8,128)(2,1)} %get-tuple-element.61), channel_id=1, source_target_pairs={{0,16},{4,20},{8,24},{12,28},{16,0},{20,4},{24,8},{28,12},{1,17},{... | collective-permute-start | bytes 663560 | tf_op jit(solution)/shard_map/ppermute | solution.py:463
  12.0 15.7 %collective-permute-start.1 = (bf16[1,3,2,72,256]{4,3,2,1,0:T(8,128)(2,1)}, bf16[1,3,2,72,256]{4,3,2,1,0:T(8,128)(2,1)}, u32[]{:S(2)}, u32[]{:S(2)}) collective-permute-start(bf16[1,3,2,72,256]{4,3,2,1,0:T(8,128)(2,1)} %get-tuple-element.62), channel_id=1, source_target_pairs={{0,8},{4,12},{8,0},{12,4},{16,24},{20,28},{24,16},{28,20},{1,9},{5... | collective-permute-start | bytes 663560 | tf_op jit(solution)/shard_map/ppermute | solution.py:463
  13.6 21.7 %collective-permute-start.3 = (bf16[4,3,2,72,256]{4,3,2,1,0:T(8,128)(2,1)}, bf16[4,3,2,72,256]{4,3,2,1,0:T(8,128)(2,1)S(1)}, u32[]{:S(2)}, u32[]{:S(2)}) collective-permute-start(bf16[4,3,2,72,256]{4,3,2,1,0:T(8,128)(2,1)} %get-tuple-element.64), channel_id=1, source_target_pairs={{0,4},{4,0},{8,12},{12,8},{16,20},{20,16},{24,28},{28,24},{1,5},{5... | collective-permute-start | bytes 2654216 | tf_op jit(solution)/shard_map/ppermute | solution.py:463
  21.9 13.4 %collective-permute-start.6 = (bf16[3,2,64,1024]{3,2,1,0:T(8,128)(2,1)S(1)}, bf16[3,2,64,1024]{3,2,1,0:T(8,128)(2,1)S(1)}, u32[]{:S(2)}, u32[]{:S(2)}) collective-permute-start(bf16[3,2,64,1024]{3,2,1,0:T(8,128)(2,1)S(1)} %collective-permute-done.5), channel_id=1, source_target_pairs={{0,1},{1,0},{2,3},{3,2},{4,5},{5,4},{6,7},{7,6},{8,9},{9,8},{10,11... | collective-permute-start | bytes 2359304 | tf_op jit(solution)/shard_map/ppermute | solution.py:463
  43.6 31.2 %collective-permute-start.10 = (s16[528,1024]{1,0:T(8,128)(2,1)S(1)}, s16[528,1024]{1,0:T(8,128)(2,1)S(1)}, u32[]{:S(2)}, u32[]{:S(2)}) collective-permute-start(s16[528,1024]{1,0:T(8,128)(2,1)S(1)} %get-tuple-element.70), channel_id=1, source_target_pairs={{0,4},{4,0},{8,12},{12,8},{16,20},{20,16},{24,28},{28,24},{1,5},{5... | collective-permute-start | bytes 3244040 | tf_op jit(solution)/shard_map/ppermute | solution.py:463
  45.2 14.4 %collective-permute-start.11 = (bf16[2,96,1024]{2,1,0:T(8,128)(2,1)S(1)}, bf16[2,96,1024]{2,1,0:T(8,128)(2,1)S(1)}, u32[]{:S(2)}, u32[]{:S(2)}) collective-permute-start(bf16[2,96,1024]{2,1,0:T(8,128)(2,1)S(1)} %bitcast.51), channel_id=1, source_target_pairs={{0,2},{1,3},{2,0},{3,1},{4,6},{5,7},{6,4},{7,5},{8,10},{9,11},{10,... | collective-permute-start | bytes 1179656 | tf_op jit(solution)/shard_map/ppermute | solution.py:463
  54.0 41.6 %collective-permute-start.17 = (s16[528,1024]{1,0:T(8,128)(2,1)S(1)}, s16[528,1024]{1,0:T(8,128)(2,1)S(1)}, u32[]{:S(2)}, u32[]{:S(2)}) collective-permute-start(s16[528,1024]{1,0:T(8,128)(2,1)S(1)} %get-tuple-element.87), channel_id=1, source_target_pairs={{0,4},{4,0},{8,12},{12,8},{16,20},{20,16},{24,28},{28,24},{1,5},{5... | collective-permute-start | bytes 3244040 | tf_op jit(solution)/shard_map/ppermute | solution.py:463
  54.7 20.1 %collective-permute-start.7 = (bf16[1,3,2,72,256]{4,3,2,1,0:T(8,128)(2,1)S(1)}, bf16[1,3,2,72,256]{4,3,2,1,0:T(8,128)(2,1)S(1)}, u32[]{:S(2)}, u32[]{:S(2)}) collective-permute-start(bf16[1,3,2,72,256]{4,3,2,1,0:T(8,128)(2,1)S(1)} %get-tuple-element.115), channel_id=1, source_target_pairs={{0,16},{4,20},{8,24},{12,28},{16,0},{20,4},{24,8},{28,12},{1,17},{... | collective-permute-start | bytes 663560 | tf_op jit(solution)/shard_map/ppermute | solution.py:463
  59.6 15.2 %collective-permute-start.8 = (bf16[1,3,2,72,256]{4,3,2,1,0:T(8,128)(2,1)S(1)}, bf16[1,3,2,72,256]{4,3,2,1,0:T(8,128)(2,1)S(1)}, u32[]{:S(2)}, u32[]{:S(2)}) collective-permute-start(bf16[1,3,2,72,256]{4,3,2,1,0:T(8,128)(2,1)S(1)} %get-tuple-element.114), channel_id=1, source_target_pairs={{0,8},{4,12},{8,0},{12,4},{16,24},{20,28},{24,16},{28,20},{1,9},{5... | collective-permute-start | bytes 663560 | tf_op jit(solution)/shard_map/ppermute | solution.py:463
  59.6 15.2 %collective-permute-start.9 = (bf16[1,3,2,72,256]{4,3,2,1,0:T(8,128)(2,1)S(1)}, bf16[1,3,2,72,256]{4,3,2,1,0:T(8,128)(2,1)S(1)}, u32[]{:S(2)}, u32[]{:S(2)}) collective-permute-start(bf16[1,3,2,72,256]{4,3,2,1,0:T(8,128)(2,1)S(1)} %get-tuple-element.113), channel_id=1, source_target_pairs={{0,24},{4,28},{8,16},{12,20},{16,8},{20,12},{24,0},{28,4},{1,25},{... | collective-permute-start | bytes 663560 | tf_op jit(solution)/shard_map/ppermute | solution.py:463
  76.0 15.4 %collective-permute-start.12 = (s16[528,512]{1,0:T(8,128)(2,1)S(1)}, s16[528,512]{1,0:T(8,128)(2,1)S(1)}, u32[]{:S(2)}, u32[]{:S(2)}) collective-permute-start(s16[528,512]{1,0:T(8,128)(2,1)S(1)} %get-tuple-element.76), channel_id=1, source_target_pairs={{0,8},{4,12},{8,0},{12,4},{16,24},{20,28},{24,16},{28,20},{1,9},{5... | collective-permute-start | bytes 1622024 | tf_op jit(solution)/shard_map/ppermute | solution.py:463
  80.1 35.8 %collective-permute-start.16 = (s16[528,1024]{1,0:T(8,128)(2,1)S(1)}, s16[528,1024]{1,0:T(8,128)(2,1)S(1)}, u32[]{:S(2)}, u32[]{:S(2)}) collective-permute-start(s16[528,1024]{1,0:T(8,128)(2,1)S(1)} %get-tuple-element.85), channel_id=1, source_target_pairs={{0,4},{4,0},{8,12},{12,8},{16,20},{20,16},{24,28},{28,24},{1,5},{5... | collective-permute-start | bytes 3244040 | tf_op jit(solution)/shard_map/ppermute | solution.py:463
  81.6 10.6 %collective-permute-start.15 = (bf16[2,96,1024]{2,1,0:T(8,128)(2,1)S(1)}, bf16[2,96,1024]{2,1,0:T(8,128)(2,1)S(1)}, u32[]{:S(2)}, u32[]{:S(2)}) collective-permute-start(bf16[2,96,1024]{2,1,0:T(8,128)(2,1)S(1)} %collective-permute-done.11), channel_id=1, source_target_pairs={{0,1},{1,0},{2,3},{3,2},{4,5},{5,4},{6,7},{7,6},{8,9},{9,8},{10,11... | collective-permute-start | bytes 1179656 | tf_op jit(solution)/shard_map/ppermute | solution.py:463
  81.6 10.6 %collective-permute-start.14 = (bf16[2,96,1024]{2,1,0:T(8,128)(2,1)S(1)}, bf16[2,96,1024]{2,1,0:T(8,128)(2,1)S(1)}, u32[]{:S(2)}, u32[]{:S(2)}) collective-permute-start(bf16[2,96,1024]{2,1,0:T(8,128)(2,1)S(1)} %bitcast.52), channel_id=1, source_target_pairs={{0,1},{1,0},{2,3},{3,2},{4,5},{5,4},{6,7},{7,6},{8,9},{9,8},{10,11... | collective-permute-start | bytes 1179656 | tf_op jit(solution)/shard_map/ppermute | solution.py:463
  96.8 18.3 %collective-permute-start.18 = (s16[528,512]{1,0:T(8,128)(2,1)S(1)}, s16[528,512]{1,0:T(8,128)(2,1)S(1)}, u32[]{:S(2)}, u32[]{:S(2)}) collective-permute-start(s16[528,512]{1,0:T(8,128)(2,1)S(1)} %get-tuple-element.89), channel_id=1, source_target_pairs={{0,8},{4,12},{8,0},{12,4},{16,24},{20,28},{24,16},{28,20},{1,9},{5... | collective-permute-start | bytes 1622024 | tf_op jit(solution)/shard_map/ppermute | solution.py:463
  98.6 15.5 %collective-permute-start.13 = (s16[528,256]{1,0:T(8,128)(2,1)S(1)}, s16[528,256]{1,0:T(8,128)(2,1)S(1)}, u32[]{:S(2)}, u32[]{:S(2)}) collective-permute-start(s16[528,256]{1,0:T(8,128)(2,1)S(1)} %get-tuple-element.78), channel_id=1, source_target_pairs={{0,16},{4,20},{8,24},{12,28},{16,0},{20,4},{24,8},{28,12},{1,17},{... | collective-permute-start | bytes 811016 | tf_op jit(solution)/shard_map/ppermute | solution.py:463
  117.2 24.9 %collective-permute-start.20 = (s16[528,512]{1,0:T(8,128)(2,1)S(1)}, s16[528,512]{1,0:T(8,128)(2,1)S(1)}, u32[]{:S(2)}, u32[]{:S(2)}) collective-permute-start(s16[528,512]{1,0:T(8,128)(2,1)S(1)} %get-tuple-element.100), channel_id=1, source_target_pairs={{0,8},{4,12},{8,0},{12,4},{16,24},{20,28},{24,16},{28,20},{1,9},{5... | collective-permute-start | bytes 1622024 | tf_op jit(solution)/shard_map/ppermute | solution.py:463
  119.8 16.3 %collective-permute-start.19 = (s16[528,256]{1,0:T(8,128)(2,1)S(1)}, s16[528,256]{1,0:T(8,128)(2,1)S(1)}, u32[]{:S(2)}, u32[]{:S(2)}) collective-permute-start(s16[528,256]{1,0:T(8,128)(2,1)S(1)} %get-tuple-element.95), channel_id=1, source_target_pairs={{0,16},{4,20},{8,24},{12,28},{16,0},{20,4},{24,8},{28,12},{1,17},{... | collective-permute-start | bytes 811016 | tf_op jit(solution)/shard_map/ppermute | solution.py:463
  143.3 16.3 %collective-permute-start.26 = (s16[528,256]{1,0:T(8,128)(2,1)S(1)}, s16[528,256]{1,0:T(8,128)(2,1)S(1)}, u32[]{:S(2)}, u32[]{:S(2)}) collective-permute-start(s16[528,256]{1,0:T(8,128)(2,1)S(1)} %get-tuple-element.107), channel_id=1, source_target_pairs={{0,16},{4,20},{8,24},{12,28},{16,0},{20,4},{24,8},{28,12},{1,17},{... | collective-permute-start | bytes 811016 | tf_op jit(solution)/shard_map/ppermute | solution.py:463
  166.1 18.6 %collective-permute-start.22 = (s16[2,208,512]{2,1,0:T(8,128)(2,1)S(1)}, s16[2,208,512]{2,1,0:T(8,128)(2,1)S(1)}, u32[]{:S(2)}, u32[]{:S(2)}) collective-permute-start(s16[2,208,512]{2,1,0:T(8,128)(2,1)S(1)} %get-tuple-element.106), channel_id=1, source_target_pairs={{0,2},{1,3},{2,0},{3,1},{4,6},{5,7},{6,4},{7,5},{8,10},{9,11},{10,... | collective-permute-start | bytes 1277960 | tf_op jit(solution)/shard_map/ppermute | solution.py:463
  168.1 14.8 %collective-permute-start.28 = (s16[1,208,512]{2,1,0:T(8,128)(2,1)S(1)}, s16[1,208,512]{2,1,0:T(8,128)(2,1)S(1)}, u32[]{:S(2)}, u32[]{:S(2)}) collective-permute-start(s16[1,208,512]{2,1,0:T(8,128)(2,1)S(1)} %get-tuple-element.112), channel_id=1, source_target_pairs={{0,2},{1,3},{2,0},{3,1},{4,6},{5,7},{6,4},{7,5},{8,10},{9,11},{10,... | collective-permute-start | bytes 638984 | tf_op jit(solution)/shard_map/ppermute | solution.py:463
  185.0 13.1 %collective-permute-start.23 = (f32[4,2,96,128]{3,2,1,0:T(8,128)S(1)}, f32[4,2,96,128]{3,2,1,0:T(8,128)S(1)}, u32[]{:S(2)}, u32[]{:S(2)}) collective-permute-start(f32[4,2,96,128]{3,2,1,0:T(8,128)S(1)} %slice.69), channel_id=1, source_target_pairs={{0,4},{4,0},{8,12},{12,8},{16,20},{20,16},{24,28},{28,24},{1,5},{5... | collective-permute-start | bytes 1179656 | tf_op jit(solution)/shard_map/ppermute | solution.py:463
  (16 other events, 104.0 us)

commit v10 on v9

--- a/solution.py
+++ b/solution.py
@@ -12,6 +12,7 @@
 
 GROUP = 64
 EXP_ROWS = 16
+SMALL = 32
 STEPS = 128.0
 TOP = 32700.0
 MAGIC = 1.5 * 2.0**23
@@ -44,28 +45,35 @@
     return high, low
 
 
-def encode(value, out_ref):
+def exp_rows(rows, group):
+    return -(-(rows // group) // 16) * 16
+
+
+def encode(value, out_ref, group=GROUP):
     rows, width = value.shape
-    groups = rows // GROUP
-    parts = value.reshape(groups, GROUP, width)
+    groups = rows // group
+    parts = value.reshape(groups, group, width)
     largest = jnp.maximum(jnp.max(jnp.abs(parts), axis=1), 1e-30)
     level = jnp.ceil(jnp.log2(largest) * STEPS) + 1.0
     factor = TOP * jnp.exp2(level * (-1.0 / STEPS))
     coded = ((parts * factor[:, None, :] + MAGIC) - MAGIC).astype(jnp.int32)
     out_ref[0:rows, :] = coded.reshape(rows, width).astype(jnp.int16)
-    pad = jnp.zeros((EXP_ROWS - groups, width), jnp.int32)
-    out_ref[rows : rows + EXP_ROWS, :] = jnp.concatenate(
-        [level.astype(jnp.int32), pad], axis=0
-    ).astype(jnp.int16)
-
-
-def decode(ref):
-    rows = ref.shape[0] - EXP_ROWS
+    extra = exp_rows(rows, group)
+    level = level.astype(jnp.int32)
+    if extra > groups:
+        pad = jnp.zeros((extra - groups, width), jnp.int32)
+        level = jnp.concatenate([level, pad], axis=0)
+    out_ref[rows : rows + extra, :] = level.astype(jnp.int16)
+
+
+def decode(ref, rows=None, group=GROUP):
+    rows = ref.shape[0] - EXP_ROWS if rows is None else rows
     width = ref.shape[1]
-    groups = rows // GROUP
-    level = ref[rows : rows + EXP_ROWS, :].astype(jnp.int32).astype(jnp.float32)[0:groups]
+    groups = rows // group
+    extra = exp_rows(rows, group)
+    level = ref[rows : rows + extra, :].astype(jnp.int32).astype(jnp.float32)[0:groups]
     factor = jnp.exp2(level * (1.0 / STEPS)) * (1.0 / TOP)
-    parts = ref[0:rows, :].astype(jnp.int32).astype(jnp.float32).reshape(groups, GROUP, width)
+    parts = ref[0:rows, :].astype(jnp.int32).astype(jnp.float32).reshape(groups, group, width)
     return (parts * factor[:, None, :]).reshape(rows, width)
 
 
@@ -259,23 +267,63 @@
     )(own, heard)
 
 
-def pack_kernel(own_ref, heard_ref, out_ref):
-    rows = out_ref.shape[2]
+def split_sums(sums_ref, keep_ref, go_ref):
+    half, points, rows, width = keep_ref.shape
+    keep_ref[...] = sums_ref[0:half]
+    encode(sums_ref[half:].reshape(half * points * rows, width), go_ref, SMALL)
+
+
+def split_shapes(slots, points, rows):
+    count = slots // 2 * points * rows
+    return [
+        jax.ShapeDtypeStruct((slots // 2, points, rows, 128), jnp.float32),
+        jax.ShapeDtypeStruct((count + exp_rows(count, SMALL), 128), jnp.int16),
+    ]
+
+
+def pack_kernel(*refs):
+    *refs, keep_ref, go_ref, sums_ref = refs
+    slots, points, rows, _ = sums_ref.shape
     first = lax.broadcasted_iota(jnp.int32, (rows, 128), 1) < 64
-    for n in range(own_ref.shape[0]):
-        total = own_ref[n] + decode(heard_ref.at[n])
-        for block in range(out_ref.shape[0] // 2):
+    for n in range(points):
+        total = refs[n][...] + decode(refs[points + n])
+        for block in range(slots // 2):
             cols = slice(block * 128, (block + 1) * 128)
             real, imag = total[:rows, cols], total[rows:, cols]
-            out_ref[2 * block, n] = jnp.where(first, real, pltpu.roll(imag, 64, 1))
-            out_ref[2 * block + 1, n] = jnp.where(first, pltpu.roll(real, 64, 1), imag)
-
-
-def pack_call(own, heard):
-    count, rows, cols = own.shape
+            sums_ref[2 * block, n] = jnp.where(first, real, pltpu.roll(imag, 64, 1))
+            sums_ref[2 * block + 1, n] = jnp.where(first, pltpu.roll(real, 64, 1), imag)
+    split_sums(sums_ref, keep_ref, go_ref)
+
+
+def pack_call(owns, heards):
+    rows, cols = owns[0].shape
+    shape = (cols // 64, len(owns), rows // 2)
     return pl.pallas_call(
         pack_kernel,
-        out_shape=jax.ShapeDtypeStruct((cols // 64, count, rows // 2, 128), jnp.float32),
+        out_shape=split_shapes(*shape),
+        scratch_shapes=[pltpu.VMEM(shape + (128,), jnp.float32)],
+        compiler_params=params(),
+        cost_estimate=cost(60 * owns[0].size, 30 * owns[0].size),
+    )(*owns, *heards)
+
+
+def merge_kernel(own_ref, heard_ref, *refs):
+    slots, points, rows, width = own_ref.shape
+    count = slots * points * rows
+    sums_ref = refs[-1]
+    heard = decode(heard_ref, count, SMALL)
+    sums_ref[...] = own_ref[...] + heard.reshape(slots, points, rows, width)
+    if slots > 1:
+        split_sums(sums_ref, *refs[:-1])
+
+
+def merge_call(own, heard):
+    last = own.shape[0] == 1
+    sums = jax.ShapeDtypeStruct(own.shape, jnp.float32)
+    return pl.pallas_call(
+        merge_kernel,
+        out_shape=sums if last else split_shapes(*own.shape[:3]),
+        scratch_shapes=[] if last else [pltpu.VMEM(own.shape, jnp.float32)],
         compiler_params=params(),
         cost_estimate=cost(20 * own.size, 10 * own.size),
     )(own, heard)
@@ -547,7 +595,7 @@
     tiles = [None] * points
     exch = None
     work = [(2 * q + stage, q, stage) for q in range(points) for stage in range(1, stages)]
-    work += [(2 * q + stages + (2.2 if q == 0 else 0.8), q, stages) for q in range(points)]
+    work += [(2 * q + stages + 2.2, q, stages) for q in range(points)]
     for _, q, stage in sorted(work):
         if stage < stages:
             columns = (ga >> (stage + 1)) * width
@@ -565,29 +613,24 @@
                 after = [behind(token, [c for c, _ in cons])]
                 exch, token = exchange_call(slots, there, coulomb, after)
                 after = [token]
-            if (q, stage) == (points - 1, stages - 1):
-                own, sent = (jnp.stack(items) for items in zip(*tiles[:-1]))
-                early = fold_call(own, swap(behind(sent, token), "pair", pair, pair_bits[0]))
-                after = [behind(token, early[0])]
         else:
-            *tiles[q], token = tile_call(
+            if q == 1:
+                after = [behind(after[0], tiles[0][1])]
+            own, sent, token = tile_call(
                 cons, q, keep[q], heard[q], exch, me, ga_order, pick_rows, col_direct,
                 col_exch, pair, after,
             )
             after = [token]
-
-    own, sent = (part[None] for part in tiles[-1])
-    late = fold_call(own, swap(sent, "pair", pair, pair_bits[0]))
-    outs = []
-    for own, sent in (early, late):
-        for bit in pair_bits[1:-1]:
-            own, sent = fold_call(own, swap(sent, "pair", pair, bit))
-        total = pack_call(own, swap(sent, "pair", pair, pair_bits[-1]))
-        for bit in ga_bits:
-            size = total.shape[0] // 2
-            total = total[:size] + swap(total[size:], "ga", ga, bit)
-        outs.append(total[0])
-    out = jnp.concatenate(outs).reshape(points, row_count, 2, 64)[..., :col_count]
+            for bit in pair_bits[:-1]:
+                own, sent = fold_call(own[None], swap(sent[None], "pair", pair, bit))
+                own, sent = own[0], sent[0]
+            tiles[q] = own, swap(sent, "pair", pair, pair_bits[-1])
+
+    own, sent = pack_call(*zip(*tiles))
+    for bit in ga_bits[:-1]:
+        own, sent = merge_call(own, swap(sent, "ga", ga, bit))
+    total = merge_call(own, swap(sent, "ga", ga, ga_bits[-1]))[0]
+    out = total.reshape(points, row_count, 2, 64)[..., :col_count]
     return jnp.transpose(out, (0, 2, 1, 3))
 
 
@@ -696,6 +739,7 @@
             and args[0].shape[0] % (16 * pair) == 0
             and NT % (16 * pair) == 0
             and NT // ga <= 64
+            and args[1].shape[1] * NT % (pair * SMALL) == 0
         )
         body = on_device if suits else on_any_device
         return jax.shard_map(

time: 212 us -> 199 us (0.939)
  waiting for transfers between devices: 99.4 us -> 90.6 us
  starting transfers between devices: 46.4 us -> 41.9 us
    ppermute x32 -> x31, waiting for transfers between devices: 99.4 us -> 90.6 us  [swap(): return lax.ppermute(value, axis, [(i, i ^ bit) for i in range(size)])]
    ppermute x32 -> x31, starting transfers between devices: 46.4 us -> 41.9 us  [swap(): return lax.ppermute(value, axis, [(i, i ^ bit) for i in range(size)])]
  transfers between devices with their start and end apart: 32 -> 31, of which waited for: 15 -> 15; matrix products, arithmetic and copies ran while one was open for 3% -> 3% of each run, Pallas kernels for 18% -> 23%
where the time goes in v10:
time: 199 us; the launch traced here: 198 us
  waiting for transfers between devices  90.6 us (46%)
  Pallas kernels  56.3 us (28%)
  starting transfers between devices  41.9 us (21%)
  local copies, waits for them, and re-layouts  8.89 us (4%)
    ppermute x31, waiting for transfers between devices, swap(): return lax.ppermute(value, axis, [(i, i ^ bit) for i in range(size)])  90.6 us
    ppermute x31, starting transfers between devices, swap(): return lax.ppermute(value, axis, [(i, i ^ bit) for i in range(size)])  41.9 us
    pallas_call x3, Pallas kernels, x_call(): pl.pallas_call(lambda *refs: x_kernel(slots, len(after), *refs), grid_spe...  24.6 us
    pallas_call x3, Pallas kernels, tile_call(): pl.pallas_call(lambda *refs: tile_kernel(order, stages, chunks, len(after...  18.5 us
    pallas_call x6, Pallas kernels, hop_call(): pl.pallas_call(lambda *refs: hop_kernel(len(others), *refs), grid_spec=gr...  6.03 us
  transfers between devices with their start and end apart: 31, of which 15 were waited for; matrix products, arithmetic and copies ran while one was open for 3% of the time, Pallas kernels for 23%

profile of v10, /device:TPU:0, one launch (start us, length us, event | category | flops | bytes accessed | tf_op | source)
XLA Modules:
  0.0 198.4 jit_solution(2269031665749826959)
XLA Ops:
  1.4 3.0 %collective-permute-start.5 = (bf16[3,2,64,1024]{3,2,1,0:T(8,128)(2,1)S(1)}, bf16[3,2,64,1024]{3,2,1,0:T(8,128)(2,1)S(1)}, u32[]{:S(2)}, u32[]{:S(2)}) collective-permute-start(bf16[3,2,64,1024]{3,2,1,0:T(8,128)(2,1)S(1)} %bitcast.40), channel_id=1, source_target_pairs={{0,2},{1,3},{2,0},{3,1},{4,6},{5,7},{6,4},{7,5},{8,10},{9,11},{10,... | collective-permute-start | bytes 2359304 | tf_op jit(solution)/shard_map/ppermute | solution.py:511
  9.4 2.6 %collective-permute-start = (bf16[1,3,2,72,256]{4,3,2,1,0:T(8,128)(2,1)}, bf16[1,3,2,72,256]{4,3,2,1,0:T(8,128)(2,1)}, u32[]{:S(2)}, u32[]{:S(2)}) collective-permute-start(bf16[1,3,2,72,256]{4,3,2,1,0:T(8,128)(2,1)} %get-tuple-element.68), channel_id=1, source_target_pairs={{0,16},{4,20},{8,24},{12,28},{16,0},{20,4},{24,8},{28,12},{1,17},{... | collective-permute-start | bytes 663560 | tf_op jit(solution)/shard_map/ppermute | solution.py:511
  17.2 4.7 %collective-permute-done.5 = bf16[3,2,64,1024]{3,2,1,0:T(8,128)(2,1)S(1)} collective-permute-done((bf16[3,2,64,1024]{3,2,1,0:T(8,128)(2,1)S(1)}, bf16[3,2,64,1024]{3,2,1,0:T(8,128)(2,1)S(1)}, u32[]{:S(2)}, u32[]{:S(2)}) %collective-permute-start.5) | collective-permute-done | bytes 786464 | tf_op jit(solution)/shard_map/ppermute | solution.py:511
  23.8 3.9 %collective-permute-start.2 = (bf16[1,3,2,72,256]{4,3,2,1,0:T(8,128)(2,1)S(1)}, bf16[1,3,2,72,256]{4,3,2,1,0:T(8,128)(2,1)S(1)}, u32[]{:S(2)}, u32[]{:S(2)}) collective-permute-start(bf16[1,3,2,72,256]{4,3,2,1,0:T(8,128)(2,1)S(1)} %copy-done.1), channel_id=1, source_target_pairs={{0,24},{4,28},{8,16},{12,20},{16,8},{20,12},{24,0},{28,4},{1,25},{... | collective-permute-start | bytes 663560 | tf_op jit(solution)/shard_map/ppermute | solution.py:511
  27.8 6.2 %collective-permute-done.2.refs_4_ = bf16[1,3,2,72,256]{4,3,2,1,0:T(8,128)(2,1)S(1)} collective-permute-done((bf16[1,3,2,72,256]{4,3,2,1,0:T(8,128)(2,1)S(1)}, bf16[1,3,2,72,256]{4,3,2,1,0:T(8,128)(2,1)S(1)}, u32[]{:S(2)}, u32[]{:S(2)}) %collective-permute-start.2) | collective-permute-done | bytes 221216 | tf_op jit(solution)/shard_map/ppermute | solution.py:511
  35.3 8.2 %shard_map.101 = (s16[528,1024]{1,0:T(8,128)(2,1)S(1)}, f32[512,1024]{1,0:T(8,128)S(1)}, f32[8,128]{1,0:T(8,128)S(1)}) custom-call(s32[1]{0:T(128)} %bitcast.refs_0_, bf16[1,3,2,64,1024]{4,3,2,1,0:T(8,128)(2,1)S(1)} %bitcast.42, bf16[1,3,2,64,1024]{4,3,2,1,0:T(8,128)(2,1)S(1)} %bitcast.49, bf16[1,3,2,64,1024]{4,3,2,1,0:T(8,128)(2,1)S(1)} %bitcast.46, ...), custom_call_target="tpu_custom_call" | custom-call | flops 67108864 | bytes 180224 | tf_op jit(solution)/shard_map/pallas_call | solution.py:197
  45.8 8.2 %shard_map.102 = (s16[528,1024]{1,0:T(8,128)(2,1)S(1)}, f32[512,1024]{1,0:T(8,128)S(1)}, f32[8,128]{1,0:T(8,128)S(1)}) custom-call(s32[1]{0:T(128)} %bitcast.refs_0_, bf16[1,3,2,64,1024]{4,3,2,1,0:T(8,128)(2,1)S(1)} %bitcast.43, bf16[1,3,2,64,1024]{4,3,2,1,0:T(8,128)(2,1)S(1)} %bitcast.50, bf16[1,3,2,64,1024]{4,3,2,1,0:T(8,128)(2,1)S(1)} %bitcast.47, ...), custom_call_target="tpu_custom_call" | custom-call | flops 67108864 | bytes 180224 | tf_op jit(solution)/shard_map/pallas_call | solution.py:197
  54.6 5.1 %collective-permute-start.7 = (bf16[1,3,2,72,256]{4,3,2,1,0:T(8,128)(2,1)S(1)}, bf16[1,3,2,72,256]{4,3,2,1,0:T(8,128)(2,1)S(1)}, u32[]{:S(2)}, u32[]{:S(2)}) collective-permute-start(bf16[1,3,2,72,256]{4,3,2,1,0:T(8,128)(2,1)S(1)} %get-tuple-element.129), channel_id=1, source_target_pairs={{0,16},{4,20},{8,24},{12,28},{16,0},{20,4},{24,8},{28,12},{1,17},{... | collective-permute-start | bytes 663560 | tf_op jit(solution)/shard_map/ppermute | solution.py:511
  61.2 8.2 %shard_map.103 = (s16[528,1024]{1,0:T(8,128)(2,1)S(1)}, f32[512,1024]{1,0:T(8,128)S(1)}, f32[8,128]{1,0:T(8,128)S(1)}) custom-call(s32[1]{0:T(128)} %bitcast.refs_0_, bf16[1,3,2,64,1024]{4,3,2,1,0:T(8,128)(2,1)S(1)} %bitcast.44, bf16[1,3,2,64,1024]{4,3,2,1,0:T(8,128)(2,1)S(1)} %bitcast.51, bf16[1,3,2,64,1024]{4,3,2,1,0:T(8,128)(2,1)S(1)} %bitcast.48, ...), custom_call_target="tpu_custom_call" | custom-call | flops 67108864 | bytes 180224 | tf_op jit(solution)/shard_map/pallas_call | solution.py:197
  69.4 5.5 %collective-permute-done.7.refs_6_ = bf16[1,3,2,72,256]{4,3,2,1,0:T(8,128)(2,1)S(1)} collective-permute-done((bf16[1,3,2,72,256]{4,3,2,1,0:T(8,128)(2,1)S(1)}, bf16[1,3,2,72,256]{4,3,2,1,0:T(8,128)(2,1)S(1)}, u32[]{:S(2)}, u32[]{:S(2)}) %collective-permute-start.7) | collective-permute-done | bytes 221216 | tf_op jit(solution)/shard_map/ppermute | solution.py:511
  76.0 4.1 %collective-permute-start.12 = (s16[528,512]{1,0:T(8,128)(2,1)S(1)}, s16[528,512]{1,0:T(8,128)(2,1)S(1)}, u32[]{:S(2)}, u32[]{:S(2)}) collective-permute-start(s16[528,512]{1,0:T(8,128)(2,1)S(1)} %get-tuple-element.83), channel_id=1, source_target_pairs={{0,8},{4,12},{8,0},{12,4},{16,24},{20,28},{24,16},{28,20},{1,9},{5... | collective-permute-start | bytes 1622024 | tf_op jit(solution)/shard_map/ppermute | solution.py:511
  82.2 9.3 %collective-permute-done.12.refs_3_.refs_11_ = s16[528,512]{1,0:T(8,128)(2,1)S(1)} collective-permute-done((s16[528,512]{1,0:T(8,128)(2,1)S(1)}, s16[528,512]{1,0:T(8,128)(2,1)S(1)}, u32[]{:S(2)}, u32[]{:S(2)}) %collective-permute-start.12) | collective-permute-done | bytes 540704 | tf_op jit(solution)/shard_map/ppermute | solution.py:511
  92.2 3.4 %shard_map.106 = (f32[3,2,384,96]{3,2,1,0:T(8,128)S(1)}, f32[8,128]{1,0:T(8,128)S(1)}) custom-call(bf16[1,2,96,1024]{3,2,1,0:T(8,128)(2,1)S(1)} %bitcast.58, bf16[1,2,96,1024]{3,2,1,0:T(8,128)(2,1)S(1)} %bitcast.67, bf16[1,2,96,1024]{3,2,1,0:T(8,128)(2,1)S(1)} %bitcast.65, bf16[1,2,96,1024]{3,2,1,0:T(8,128)(2,1)S(1)} %bitcast.66, ...), custom_call_target="tpu_custom_call" | custom-call | flops 28311552 | bytes 36864 | tf_op jit(solution)/shard_map/pallas_call | solution.py:364
  98.9 15.2 %collective-permute-done.13.refs_12_ = s16[528,256]{1,0:T(8,128)(2,1)S(1)} collective-permute-done((s16[528,256]{1,0:T(8,128)(2,1)S(1)}, s16[528,256]{1,0:T(8,128)(2,1)S(1)}, u32[]{:S(2)}, u32[]{:S(2)}) %collective-permute-start.13) | collective-permute-done | bytes 270368 | tf_op jit(solution)/shard_map/ppermute | solution.py:511
  119.8 6.0 %shard_map.110 = (f32[384,512]{1,0:T(8,128)S(1)}, s16[400,512]{1,0:T(8,128)(2,1)S(1)}, f32[8,128]{1,0:T(8,128)S(1)}) custom-call(s32[1]{0:T(128)} %bitcast.refs_0_, bf16[1,3,2,72,256]{4,3,2,1,0:T(8,128)(2,1)S(1)} %get-tuple-element.67.refs_1_, bf16[1,3,2,72,256]{4,3,2,1,0:T(8,128)(2,1)} %collective-permute-done.refs_2_, ...), custom_call_target="tpu_custom_call" | custom-call | flops 43750000 | bytes 125000 | tf_op jit(solution)/shard_map/pallas_call | solution.py:501
  127.0 14.5 %collective-permute-done.20.refs_12_ = s16[528,256]{1,0:T(8,128)(2,1)S(1)} collective-permute-done((s16[528,256]{1,0:T(8,128)(2,1)S(1)}, s16[528,256]{1,0:T(8,128)(2,1)S(1)}, u32[]{:S(2)}, u32[]{:S(2)}) %collective-permute-start.20) | collective-permute-done | bytes 270368 | tf_op jit(solution)/shard_map/ppermute | solution.py:511
  144.3 5.3 %collective-permute-done.22.refs_3_ = s16[208,512]{1,0:T(8,128)(2,1)S(1)} collective-permute-done((s16[208,512]{1,0:T(8,128)(2,1)S(1)}, s16[208,512]{1,0:T(8,128)(2,1)S(1)}, u32[]{:S(2)}, u32[]{:S(2)}) %collective-permute-start.22) | collective-permute-done | bytes 213024 | tf_op jit(solution)/shard_map/ppermute | solution.py:511
  149.6 6.0 %shard_map.113 = (f32[384,512]{1,0:T(8,128)S(1)}, s16[400,512]{1,0:T(8,128)(2,1)S(1)}, f32[8,128]{1,0:T(8,128)S(1)}) custom-call(s32[1]{0:T(128)} %bitcast.refs_0_, bf16[1,3,2,72,256]{4,3,2,1,0:T(8,128)(2,1)S(1)} %get-tuple-element.67.refs_1_, bf16[1,3,2,72,256]{4,3,2,1,0:T(8,128)(2,1)} %collective-permute-done.refs_2_, ...), custom_call_target="tpu_custom_call" | custom-call | flops 43750000 | bytes 125000 | tf_op jit(solution)/shard_map/pallas_call | solution.py:501
  157.1 6.5 %shard_map.115 = (f32[384,512]{1,0:T(8,128)S(1)}, s16[400,512]{1,0:T(8,128)(2,1)S(1)}, f32[8,128]{1,0:T(8,128)}) custom-call(s32[1]{0:T(128)} %bitcast.refs_0_, bf16[1,3,2,72,256]{4,3,2,1,0:T(8,128)(2,1)S(1)} %get-tuple-element.67.refs_1_, bf16[1,3,2,72,256]{4,3,2,1,0:T(8,128)(2,1)} %collective-permute-done.refs_2_, ...), custom_call_target="tpu_custom_call" | custom-call | flops 43750000 | bytes 125000 | tf_op jit(solution)/shard_map/pallas_call | solution.py:501
  167.2 4.8 %collective-permute-done.26.refs_4_ = s16[208,512]{1,0:T(8,128)(2,1)S(1)} collective-permute-done((s16[208,512]{1,0:T(8,128)(2,1)S(1)}, s16[208,512]{1,0:T(8,128)(2,1)S(1)}, u32[]{:S(2)}, u32[]{:S(2)}) %collective-permute-start.26) | collective-permute-done | bytes 213024 | tf_op jit(solution)/shard_map/ppermute | solution.py:511
  172.0 4.2 %collective-permute-done.27.refs_5_ = s16[208,512]{1,0:T(8,128)(2,1)S(1)} collective-permute-done((s16[208,512]{1,0:T(8,128)(2,1)S(1)}, s16[208,512]{1,0:T(8,128)(2,1)S(1)}, u32[]{:S(2)}, u32[]{:S(2)}) %collective-permute-start.27) | collective-permute-done | bytes 213024 | tf_op jit(solution)/shard_map/ppermute | solution.py:511
  178.3 7.4 %collective-permute-done.28.heard_ref = s16[1200,128]{1,0:T(8,128)(2,1)S(1)} collective-permute-done((s16[1200,128]{1,0:T(8,128)(2,1)S(1)}, s16[1200,128]{1,0:T(8,128)(2,1)S(1)}, u32[]{:S(2)}, u32[]{:S(2)}) %collective-permute-start.28) | collective-permute-done | bytes 307232 | tf_op jit(solution)/shard_map/ppermute | solution.py:511
  187.0 4.3 %collective-permute-done.29.heard_ref = s16[608,128]{1,0:T(8,128)(2,1)S(1)} collective-permute-done((s16[608,128]{1,0:T(8,128)(2,1)S(1)}, s16[608,128]{1,0:T(8,128)(2,1)S(1)}, u32[]{:S(2)}, u32[]{:S(2)}) %collective-permute-start.29) | collective-permute-done | bytes 155680 | tf_op jit(solution)/shard_map/ppermute | solution.py:511
  192.1 5.4 %collective-permute-done.30.heard_ref = s16[304,128]{1,0:T(8,128)(2,1)S(1)} collective-permute-done((s16[304,128]{1,0:T(8,128)(2,1)S(1)}, s16[304,128]{1,0:T(8,128)(2,1)S(1)}, u32[]{:S(2)}, u32[]{:S(2)}) %collective-permute-start.30) | collective-permute-done | bytes 77856 | tf_op jit(solution)/shard_map/ppermute | solution.py:511
  (110 shorter events, 46.1 us)
Async XLA Ops:
  1.4 20.5 %collective-permute-start.5 = (bf16[3,2,64,1024]{3,2,1,0:T(8,128)(2,1)S(1)}, bf16[3,2,64,1024]{3,2,1,0:T(8,128)(2,1)S(1)}, u32[]{:S(2)}, u32[]{:S(2)}) collective-permute-start(bf16[3,2,64,1024]{3,2,1,0:T(8,128)(2,1)S(1)} %bitcast.40), channel_id=1, source_target_pairs={{0,2},{1,3},{2,0},{3,1},{4,6},{5,7},{6,4},{7,5},{8,10},{9,11},{10,... | collective-permute-start | bytes 2359304 | tf_op jit(solution)/shard_map/ppermute | solution.py:511
  4.4 30.9 %collective-permute-start.4 = (bf16[3,2,64,1024]{3,2,1,0:T(8,128)(2,1)S(1)}, bf16[3,2,64,1024]{3,2,1,0:T(8,128)(2,1)S(1)}, u32[]{:S(2)}, u32[]{:S(2)}) collective-permute-start(bf16[3,2,64,1024]{3,2,1,0:T(8,128)(2,1)S(1)} %bitcast.41), channel_id=1, source_target_pairs={{0,1},{1,0},{2,3},{3,2},{4,5},{5,4},{6,7},{7,6},{8,9},{9,8},{10,11... | collective-permute-start | bytes 2359304 | tf_op jit(solution)/shard_map/ppermute | solution.py:511
  9.4 14.4 %collective-permute-start = (bf16[1,3,2,72,256]{4,3,2,1,0:T(8,128)(2,1)}, bf16[1,3,2,72,256]{4,3,2,1,0:T(8,128)(2,1)}, u32[]{:S(2)}, u32[]{:S(2)}) collective-permute-start(bf16[1,3,2,72,256]{4,3,2,1,0:T(8,128)(2,1)} %get-tuple-element.68), channel_id=1, source_target_pairs={{0,16},{4,20},{8,24},{12,28},{16,0},{20,4},{24,8},{28,12},{1,17},{... | collective-permute-start | bytes 663560 | tf_op jit(solution)/shard_map/ppermute | solution.py:511
  12.0 15.8 %collective-permute-start.1 = (bf16[1,3,2,72,256]{4,3,2,1,0:T(8,128)(2,1)}, bf16[1,3,2,72,256]{4,3,2,1,0:T(8,128)(2,1)}, u32[]{:S(2)}, u32[]{:S(2)}) collective-permute-start(bf16[1,3,2,72,256]{4,3,2,1,0:T(8,128)(2,1)} %get-tuple-element.69), channel_id=1, source_target_pairs={{0,8},{4,12},{8,0},{12,4},{16,24},{20,28},{24,16},{28,20},{1,9},{5... | collective-permute-start | bytes 663560 | tf_op jit(solution)/shard_map/ppermute | solution.py:511
  13.5 21.7 %collective-permute-start.3 = (bf16[4,3,2,72,256]{4,3,2,1,0:T(8,128)(2,1)}, bf16[4,3,2,72,256]{4,3,2,1,0:T(8,128)(2,1)S(1)}, u32[]{:S(2)}, u32[]{:S(2)}) collective-permute-start(bf16[4,3,2,72,256]{4,3,2,1,0:T(8,128)(2,1)} %get-tuple-element.71), channel_id=1, source_target_pairs={{0,4},{4,0},{8,12},{12,8},{16,20},{20,16},{24,28},{28,24},{1,5},{5... | collective-permute-start | bytes 2654216 | tf_op jit(solution)/shard_map/ppermute | solution.py:511
  21.9 13.4 %collective-permute-start.6 = (bf16[3,2,64,1024]{3,2,1,0:T(8,128)(2,1)S(1)}, bf16[3,2,64,1024]{3,2,1,0:T(8,128)(2,1)S(1)}, u32[]{:S(2)}, u32[]{:S(2)}) collective-permute-start(bf16[3,2,64,1024]{3,2,1,0:T(8,128)(2,1)S(1)} %collective-permute-done.5), channel_id=1, source_target_pairs={{0,1},{1,0},{2,3},{3,2},{4,5},{5,4},{6,7},{7,6},{8,9},{9,8},{10,11... | collective-permute-start | bytes 2359304 | tf_op jit(solution)/shard_map/ppermute | solution.py:511
  23.8 10.1 %collective-permute-start.2 = (bf16[1,3,2,72,256]{4,3,2,1,0:T(8,128)(2,1)S(1)}, bf16[1,3,2,72,256]{4,3,2,1,0:T(8,128)(2,1)S(1)}, u32[]{:S(2)}, u32[]{:S(2)}) collective-permute-start(bf16[1,3,2,72,256]{4,3,2,1,0:T(8,128)(2,1)S(1)} %copy-done.1), channel_id=1, source_target_pairs={{0,24},{4,28},{8,16},{12,20},{16,8},{20,12},{24,0},{28,4},{1,25},{... | collective-permute-start | bytes 663560 | tf_op jit(solution)/shard_map/ppermute | solution.py:511
  43.5 31.3 %collective-permute-start.10 = (s16[528,1024]{1,0:T(8,128)(2,1)S(1)}, s16[528,1024]{1,0:T(8,128)(2,1)S(1)}, u32[]{:S(2)}, u32[]{:S(2)}) collective-permute-start(s16[528,1024]{1,0:T(8,128)(2,1)S(1)} %get-tuple-element.77), channel_id=1, source_target_pairs={{0,4},{4,0},{8,12},{12,8},{16,20},{20,16},{24,28},{28,24},{1,5},{5... | collective-permute-start | bytes 3244040 | tf_op jit(solution)/shard_map/ppermute | solution.py:511
  45.2 14.5 %collective-permute-start.11 = (bf16[2,96,1024]{2,1,0:T(8,128)(2,1)S(1)}, bf16[2,96,1024]{2,1,0:T(8,128)(2,1)S(1)}, u32[]{:S(2)}, u32[]{:S(2)}) collective-permute-start(bf16[2,96,1024]{2,1,0:T(8,128)(2,1)S(1)} %bitcast.56), channel_id=1, source_target_pairs={{0,2},{1,3},{2,0},{3,1},{4,6},{5,7},{6,4},{7,5},{8,10},{9,11},{10,... | collective-permute-start | bytes 1179656 | tf_op jit(solution)/shard_map/ppermute | solution.py:511
  54.0 41.7 %collective-permute-start.17 = (s16[528,1024]{1,0:T(8,128)(2,1)S(1)}, s16[528,1024]{1,0:T(8,128)(2,1)S(1)}, u32[]{:S(2)}, u32[]{:S(2)}) collective-permute-start(s16[528,1024]{1,0:T(8,128)(2,1)S(1)} %get-tuple-element.94), channel_id=1, source_target_pairs={{0,4},{4,0},{8,12},{12,8},{16,20},{20,16},{24,28},{28,24},{1,5},{5... | collective-permute-start | bytes 3244040 | tf_op jit(solution)/shard_map/ppermute | solution.py:511
  54.6 20.2 %collective-permute-start.7 = (bf16[1,3,2,72,256]{4,3,2,1,0:T(8,128)(2,1)S(1)}, bf16[1,3,2,72,256]{4,3,2,1,0:T(8,128)(2,1)S(1)}, u32[]{:S(2)}, u32[]{:S(2)}) collective-permute-start(bf16[1,3,2,72,256]{4,3,2,1,0:T(8,128)(2,1)S(1)} %get-tuple-element.129), channel_id=1, source_target_pairs={{0,16},{4,20},{8,24},{12,28},{16,0},{20,4},{24,8},{28,12},{1,17},{... | collective-permute-start | bytes 663560 | tf_op jit(solution)/shard_map/ppermute | solution.py:511
  59.6 15.2 %collective-permute-start.8 = (bf16[1,3,2,72,256]{4,3,2,1,0:T(8,128)(2,1)S(1)}, bf16[1,3,2,72,256]{4,3,2,1,0:T(8,128)(2,1)S(1)}, u32[]{:S(2)}, u32[]{:S(2)}) collective-permute-start(bf16[1,3,2,72,256]{4,3,2,1,0:T(8,128)(2,1)S(1)} %get-tuple-element.128), channel_id=1, source_target_pairs={{0,8},{4,12},{8,0},{12,4},{16,24},{20,28},{24,16},{28,20},{1,9},{5... | collective-permute-start | bytes 663560 | tf_op jit(solution)/shard_map/ppermute | solution.py:511
  59.7 15.2 %collective-permute-start.9 = (bf16[1,3,2,72,256]{4,3,2,1,0:T(8,128)(2,1)S(1)}, bf16[1,3,2,72,256]{4,3,2,1,0:T(8,128)(2,1)S(1)}, u32[]{:S(2)}, u32[]{:S(2)}) collective-permute-start(bf16[1,3,2,72,256]{4,3,2,1,0:T(8,128)(2,1)S(1)} %get-tuple-element.127), channel_id=1, source_target_pairs={{0,24},{4,28},{8,16},{12,20},{16,8},{20,12},{24,0},{28,4},{1,25},{... | collective-permute-start | bytes 663560 | tf_op jit(solution)/shard_map/ppermute | solution.py:511
  76.0 15.4 %collective-permute-start.12 = (s16[528,512]{1,0:T(8,128)(2,1)S(1)}, s16[528,512]{1,0:T(8,128)(2,1)S(1)}, u32[]{:S(2)}, u32[]{:S(2)}) collective-permute-start(s16[528,512]{1,0:T(8,128)(2,1)S(1)} %get-tuple-element.83), channel_id=1, source_target_pairs={{0,8},{4,12},{8,0},{12,4},{16,24},{20,28},{24,16},{28,20},{1,9},{5... | collective-permute-start | bytes 1622024 | tf_op jit(solution)/shard_map/ppermute | solution.py:511
  80.1 35.8 %collective-permute-start.16 = (s16[528,1024]{1,0:T(8,128)(2,1)S(1)}, s16[528,1024]{1,0:T(8,128)(2,1)S(1)}, u32[]{:S(2)}, u32[]{:S(2)}) collective-permute-start(s16[528,1024]{1,0:T(8,128)(2,1)S(1)} %get-tuple-element.92), channel_id=1, source_target_pairs={{0,4},{4,0},{8,12},{12,8},{16,20},{20,16},{24,28},{28,24},{1,5},{5... | collective-permute-start | bytes 3244040 | tf_op jit(solution)/shard_map/ppermute | solution.py:511
  81.6 10.6 %collective-permute-start.15 = (bf16[2,96,1024]{2,1,0:T(8,128)(2,1)S(1)}, bf16[2,96,1024]{2,1,0:T(8,128)(2,1)S(1)}, u32[]{:S(2)}, u32[]{:S(2)}) collective-permute-start(bf16[2,96,1024]{2,1,0:T(8,128)(2,1)S(1)} %collective-permute-done.11), channel_id=1, source_target_pairs={{0,1},{1,0},{2,3},{3,2},{4,5},{5,4},{6,7},{7,6},{8,9},{9,8},{10,11... | collective-permute-start | bytes 1179656 | tf_op jit(solution)/shard_map/ppermute | solution.py:511
  81.6 10.6 %collective-permute-start.14 = (bf16[2,96,1024]{2,1,0:T(8,128)(2,1)S(1)}, bf16[2,96,1024]{2,1,0:T(8,128)(2,1)S(1)}, u32[]{:S(2)}, u32[]{:S(2)}) collective-permute-start(bf16[2,96,1024]{2,1,0:T(8,128)(2,1)S(1)} %bitcast.57), channel_id=1, source_target_pairs={{0,1},{1,0},{2,3},{3,2},{4,5},{5,4},{6,7},{7,6},{8,9},{9,8},{10,11... | collective-permute-start | bytes 1179656 | tf_op jit(solution)/shard_map/ppermute | solution.py:511
  96.8 18.3 %collective-permute-start.18 = (s16[528,512]{1,0:T(8,128)(2,1)S(1)}, s16[528,512]{1,0:T(8,128)(2,1)S(1)}, u32[]{:S(2)}, u32[]{:S(2)}) collective-permute-start(s16[528,512]{1,0:T(8,128)(2,1)S(1)} %get-tuple-element.96), channel_id=1, source_target_pairs={{0,8},{4,12},{8,0},{12,4},{16,24},{20,28},{24,16},{28,20},{1,9},{5... | collective-permute-start | bytes 1622024 | tf_op jit(solution)/shard_map/ppermute | solution.py:511
  98.6 15.5 %collective-permute-start.13 = (s16[528,256]{1,0:T(8,128)(2,1)S(1)}, s16[528,256]{1,0:T(8,128)(2,1)S(1)}, u32[]{:S(2)}, u32[]{:S(2)}) collective-permute-start(s16[528,256]{1,0:T(8,128)(2,1)S(1)} %get-tuple-element.85), channel_id=1, source_target_pairs={{0,16},{4,20},{8,24},{12,28},{16,0},{20,4},{24,8},{28,12},{1,17},{... | collective-permute-start | bytes 811016 | tf_op jit(solution)/shard_map/ppermute | solution.py:511
  117.3 24.3 %collective-permute-start.21 = (s16[528,512]{1,0:T(8,128)(2,1)S(1)}, s16[528,512]{1,0:T(8,128)(2,1)S(1)}, u32[]{:S(2)}, u32[]{:S(2)}) collective-permute-start(s16[528,512]{1,0:T(8,128)(2,1)S(1)} %get-tuple-element.105), channel_id=1, source_target_pairs={{0,8},{4,12},{8,0},{12,4},{16,24},{20,28},{24,16},{28,20},{1,9},{5... | collective-permute-start | bytes 1622024 | tf_op jit(solution)/shard_map/ppermute | solution.py:511
  125.8 16.6 %collective-permute-start.19 = (s16[1,400,512]{2,1,0:T(8,128)(2,1)S(1)}, s16[1,400,512]{2,1,0:T(8,128)(2,1)S(1)}, u32[]{:S(2)}, u32[]{:S(2)}) collective-permute-start(s16[1,400,512]{2,1,0:T(8,128)(2,1)S(1)} %bitcast.70), channel_id=1, source_target_pairs={{0,1},{1,0},{2,3},{3,2},{4,5},{5,4},{6,7},{7,6},{8,9},{9,8},{10,11... | collective-permute-start | bytes 1228808 | tf_op jit(solution)/shard_map/ppermute | solution.py:511
  125.9 15.6 %collective-permute-start.20 = (s16[528,256]{1,0:T(8,128)(2,1)S(1)}, s16[528,256]{1,0:T(8,128)(2,1)S(1)}, u32[]{:S(2)}, u32[]{:S(2)}) collective-permute-start(s16[528,256]{1,0:T(8,128)(2,1)S(1)} %get-tuple-element.104), channel_id=1, source_target_pairs={{0,16},{4,20},{8,24},{12,28},{16,0},{20,4},{24,8},{28,12},{1,17},{... | collective-permute-start | bytes 811016 | tf_op jit(solution)/shard_map/ppermute | solution.py:511
  142.3 14.8 %collective-permute-start.24 = (s16[528,256]{1,0:T(8,128)(2,1)S(1)}, s16[528,256]{1,0:T(8,128)(2,1)S(1)}, u32[]{:S(2)}, u32[]{:S(2)}) collective-permute-start(s16[528,256]{1,0:T(8,128)(2,1)S(1)} %get-tuple-element.114), channel_id=1, source_target_pairs={{0,16},{4,20},{8,24},{12,28},{16,0},{20,4},{24,8},{28,12},{1,17},{... | collective-permute-start | bytes 811016 | tf_op jit(solution)/shard_map/ppermute | solution.py:511
  165.8 10.4 %collective-permute-start.27 = (s16[208,512]{1,0:T(8,128)(2,1)S(1)}, s16[208,512]{1,0:T(8,128)(2,1)S(1)}, u32[]{:S(2)}, u32[]{:S(2)}) collective-permute-start(s16[208,512]{1,0:T(8,128)(2,1)S(1)} %bitcast.72), channel_id=1, source_target_pairs={{0,2},{1,3},{2,0},{3,1},{4,6},{5,7},{6,4},{7,5},{8,10},{9,11},{10,... | collective-permute-start | bytes 638984 | tf_op jit(solution)/shard_map/ppermute | solution.py:511
  (15 other events, 93.4 us)

commit v11 on v10

--- a/solution.py
+++ b/solution.py
@@ -536,10 +536,14 @@
     stages, half = len(ga_bits), ga // 2
 
     val = jnp.transpose(val_density, (1, 2, 0, 3))
-    vals = {0: val}
+    vals = {0: (val[None], 0)}
     for bit in reversed(pair_bits):
-        for slot in sorted(vals):
-            vals[slot ^ bit] = swap(vals[slot], "pair", pair, bit)
+        known = sorted(vals)
+        got = swap(
+            jnp.concatenate([vals[r][0][vals[r][1] :][:1] for r in known]), "pair", pair, bit
+        )
+        for place, slot in enumerate(known):
+            vals[slot ^ bit] = (got, place)
 
     con = jnp.transpose(behind(con_density, val), (1, 2, 0, 3))
     *stay, go, token = shift_call(con, shift_map, me, ga_order, width)
@@ -547,7 +551,8 @@
     from_near = swap(go, "ga", ga, nearest)
     cons = {0: (stay[0], 0)}
     for slot, block in zip(ga_order[1:half], stay[1:]):
-        cons[slot] = (swap(block, "ga", ga, slot), 0)
+        if slot & ga_bits[-1]:
+            cons[slot] = (swap(block, "ga", ga, slot), 0)
 
     row_count, col_count = NT // pair, NT // ga
     row_slots = jnp.asarray(halving_order(pair_bits), jnp.int32)
@@ -568,59 +573,53 @@
     col_direct, col_exch = pick_cols(at_direct, NT, -1.0), pick_cols(at_exch, row_count, 2.0)
 
     there = jnp.transpose(trans_there, (1, 2, 0, 3))
-    here = jnp.transpose(behind(trans_here, vals[pair // 2]), (1, 0, 2))
-    heres = {0: here, pair // 2: swap(here, "pair", pair, pair // 2)}
-    arrived = [cons[slot][0] for slot in ga_order[:half]]
-    token = behind(token, (there, pick_rows, col_direct, col_exch, from_near, arrived))
-    gone, keep = [], []
-    for q in range(points):
-        coded, own, token = x_call(
-            [(vals[slot][None], 0) for slot in range(pair)], screened, q, q, me, 4, [token]
-        )
-        gone.append(coded)
-        keep.append(own)
-        if q == 0:
-            from_near = behind(from_near, token)
-            for place, slot in enumerate(ga_order[half:]):
-                cons[slot] = (from_near, 0)
-                if slot != nearest:
-                    moved = swap(from_near[place : place + 1], "ga", ga, slot ^ nearest)
-                    cons[slot] = (moved, 0)
-        elif q == 1:
-            token = behind(token, heres[pair // 2])
-    after = [behind(token, [cons[slot][0] for slot in ga_order[half:]])]
-    cons = [cons[slot] for slot in ga_order]
-
-    heard = [[swap(gone[q], "ga", ga, ga_bits[0])] for q in range(points)]
+    arrived = [block for block, _ in cons.values()]
+    token = behind(token, (there, pick_rows, col_direct, col_exch, arrived))
+    order = [("x", 0, 0), ("x", 1, 0), ("hop", 0, 1)] + [("x", q, 0) for q in range(2, points)]
+    hops = [(2 * q + s, q, s) for q in range(points) for s in range(1, stages)]
+    order += [("hop", q, s) for _, q, s in sorted(hops) if (q, s) != (0, 1)]
+    order += [("tile", q, stages) for q in range(points)]
+    gone, keep, heard = [], [], []
     tiles = [None] * points
-    exch = None
-    work = [(2 * q + stage, q, stage) for q in range(points) for stage in range(1, stages)]
-    work += [(2 * q + stages + 2.2, q, stages) for q in range(points)]
-    for _, q, stage in sorted(work):
-        if stage < stages:
+    for kind, q, stage in order:
+        if kind == "x":
+            if q == 2:
+                token = behind(token, [c for c, _ in cons])
+            coded, own, token = x_call(
+                [vals[slot] for slot in range(pair)], screened, q, q, me, 4, [token]
+            )
+            keep.append(own)
+            heard.append([swap(coded, "ga", ga, ga_bits[0])])
+            if q == 0:
+                stay, from_near = behind((stay, from_near), token)
+                cons[nearest] = (from_near, 0)
+                for place, slot in enumerate(ga_order[1:half], 1):
+                    sent = from_near[place : place + 1]
+                    if slot in cons:
+                        cons[slot ^ nearest] = (swap(sent, "ga", ga, slot), 0)
+                    else:
+                        both = swap(jnp.concatenate([stay[place], sent]), "ga", ga, slot)
+                        cons[slot], cons[slot ^ nearest] = (both, 0), (both, 1)
+                cons = [cons[slot] for slot in ga_order]
+        elif kind == "hop":
             columns = (ga >> (stage + 1)) * width
             if q > 0 and stage == stages - 1:
-                after = [behind(after[0], heard[q - 1][-1])]
-            coded, token = hop_call(keep[q], heard[q], me, stage, columns, after)
-            after = [token]
+                token = behind(token, heard[q - 1][-1])
+            coded, token = hop_call(keep[q], heard[q], me, stage, columns, [token])
             heard[q].append(swap(coded, "ga", ga, ga_bits[stage]))
             if (q, stage) == (0, 1):
-                for bit in reversed(pair_bits[:-1]):
+                heres = {0: jnp.transpose(behind(trans_here, token), (1, 0, 2))}
+                for bit in reversed(pair_bits):
                     for slot in sorted(heres):
-                        heres[slot ^ bit] = swap(behind(heres[slot], token), "pair", pair, bit)
-            elif exch is None:
+                        heres[slot ^ bit] = swap(heres[slot], "pair", pair, bit)
+            if (q, stage) == (1, 1):
                 slots = [(heres[slot][None], 0) for slot in range(pair)]
-                after = [behind(token, [c for c, _ in cons])]
-                exch, token = exchange_call(slots, there, coulomb, after)
-                after = [token]
+                exch, token = exchange_call(slots, there, coulomb, [token])
         else:
-            if q == 1:
-                after = [behind(after[0], tiles[0][1])]
             own, sent, token = tile_call(
                 cons, q, keep[q], heard[q], exch, me, ga_order, pick_rows, col_direct,
-                col_exch, pair, after,
+                col_exch, pair, [token],
             )
-            after = [token]
             for bit in pair_bits[:-1]:
                 own, sent = fold_call(own[None], swap(sent[None], "pair", pair, bit))
                 own, sent = own[0], sent[0]

time: 199 us -> 194 us (0.975)
  waiting for transfers between devices: 90.6 us -> 80.3 us
  starting transfers between devices: 41.9 us -> 44.9 us
    ppermute x31 -> x29, waiting for transfers between devices: 90.6 us -> 80.3 us  [swap(): return lax.ppermute(value, axis, [(i, i ^ bit) for i in range(size)])]
    ppermute x31 -> x29, starting transfers between devices: 41.9 us -> 44.9 us  [swap(): return lax.ppermute(value, axis, [(i, i ^ bit) for i in range(size)])]
  transfers between devices with their start and end apart: 31 -> 29, of which waited for: 15 -> 18; matrix products, arithmetic and copies ran while one was open for 3% -> 5% of each run, Pallas kernels for 23% -> 28%
where the time goes in v11:
time: 194 us
  waiting for transfers between devices  80.3 us (41%)
  Pallas kernels  56.6 us (29%)
  starting transfers between devices  44.9 us (23%)
  local copies, waits for them, and re-layouts  10 us (5%)
    ppermute x29, waiting for transfers between devices, swap(): return lax.ppermute(value, axis, [(i, i ^ bit) for i in range(size)])  80.3 us
    ppermute x29, starting transfers between devices, swap(): return lax.ppermute(value, axis, [(i, i ^ bit) for i in range(size)])  44.9 us
    pallas_call x3, Pallas kernels, x_call(): pl.pallas_call(lambda *refs: x_kernel(slots, len(after), *refs), grid_spe...  24.6 us
    pallas_call x3, Pallas kernels, tile_call(): pl.pallas_call(lambda *refs: tile_kernel(order, stages, chunks, len(after...  18.8 us
    pallas_call x6, Pallas kernels, hop_call(): pl.pallas_call(lambda *refs: hop_kernel(len(others), *refs), grid_spec=gr...  5.99 us
  transfers between devices with their start and end apart: 29, of which 18 were waited for; matrix products, arithmetic and copies ran while one was open for 5% of the time, Pallas kernels for 28%

profile of v11, /device:TPU:0, one launch (start us, length us, event | category | flops | bytes accessed | tf_op | source)
XLA Modules:
  0.0 193.8 jit_solution(14273533459191092359)
XLA Ops:
  1.4 3.0 %collective-permute-start.2 = (bf16[1,3,2,64,1024]{4,3,2,1,0:T(8,128)(2,1)S(1)}, bf16[1,3,2,64,1024]{4,3,2,1,0:T(8,128)(2,1)S(1)}, u32[]{:S(2)}, u32[]{:S(2)}) collective-permute-start(bf16[1,3,2,64,1024]{4,3,2,1,0:T(8,128)(2,1)S(1)} %bitcast.36), channel_id=1, source_target_pairs={{0,2},{1,3},{2,0},{3,1},{4,6},{5,7},{6,4},{7,5},{8,10},{9,11},{10,... | collective-permute-start | bytes 2359304 | tf_op jit(solution)/shard_map/ppermute | solution.py:511
  15.5 6.4 %collective-permute-done.2.refs_3_ = bf16[1,3,2,64,1024]{4,3,2,1,0:T(8,128)(2,1)S(1)} collective-permute-done((bf16[1,3,2,64,1024]{4,3,2,1,0:T(8,128)(2,1)S(1)}, bf16[1,3,2,64,1024]{4,3,2,1,0:T(8,128)(2,1)S(1)}, u32[]{:S(2)}, u32[]{:S(2)}) %collective-permute-start.2) | collective-permute-done | bytes 786464 | tf_op jit(solution)/shard_map/ppermute | solution.py:511
  28.1 8.2 %shard_map.101 = (s16[528,1024]{1,0:T(8,128)(2,1)S(1)}, f32[512,1024]{1,0:T(8,128)S(1)}, f32[8,128]{1,0:T(8,128)S(1)}) custom-call(s32[1]{0:T(128)} %bitcast.refs_0_, bf16[1,3,2,64,1024]{4,3,2,1,0:T(8,128)(2,1)S(1)} %bitcast.38, bf16[2,3,2,64,1024]{4,3,2,1,0:T(8,128)(2,1)S(1)} %collective-permute-done.3.refs_2_.refs_4_, ...), custom_call_target="tpu_custom_call" | custom-call | flops 67108864 | bytes 180224 | tf_op jit(solution)/shard_map/pallas_call | solution.py:197
  37.9 8.2 %shard_map.102 = (s16[528,1024]{1,0:T(8,128)(2,1)S(1)}, f32[512,1024]{1,0:T(8,128)S(1)}, f32[8,128]{1,0:T(8,128)S(1)}) custom-call(s32[1]{0:T(128)} %bitcast.refs_0_, bf16[1,3,2,64,1024]{4,3,2,1,0:T(8,128)(2,1)S(1)} %bitcast.39, bf16[2,3,2,64,1024]{4,3,2,1,0:T(8,128)(2,1)S(1)} %collective-permute-done.3.refs_2_.refs_4_, ...), custom_call_target="tpu_custom_call" | custom-call | flops 67108864 | bytes 180224 | tf_op jit(solution)/shard_map/pallas_call | solution.py:197
  48.0 4.3 %collective-permute-start.5 = (bf16[2,3,2,72,256]{4,3,2,1,0:T(8,128)(2,1)S(1)}, bf16[2,3,2,72,256]{4,3,2,1,0:T(8,128)(2,1)S(1)}, u32[]{:S(2)}, u32[]{:S(2)}) collective-permute-start(bf16[2,3,2,72,256]{4,3,2,1,0:T(8,128)(2,1)S(1)} %pad_maximum_fusion.1), channel_id=1, source_target_pairs={{0,8},{4,12},{8,0},{12,4},{16,24},{20,28},{24,16},{28,20},{1,9},{5... | collective-permute-start | bytes 1327112 | tf_op jit(solution)/shard_map/ppermute | solution.py:511
  52.2 3.4 %collective-permute-start.7 = (bf16[1,3,2,72,256]{4,3,2,1,0:T(8,128)(2,1)S(1)}, bf16[1,3,2,72,256]{4,3,2,1,0:T(8,128)(2,1)S(1)}, u32[]{:S(2)}, u32[]{:S(2)}) collective-permute-start(bf16[1,3,2,72,256]{4,3,2,1,0:T(8,128)(2,1)S(1)} %get-tuple-element.119), channel_id=1, source_target_pairs={{0,24},{4,28},{8,16},{12,20},{16,8},{20,12},{24,0},{28,4},{1,25},{... | collective-permute-start | bytes 663560 | tf_op jit(solution)/shard_map/ppermute | solution.py:511
  55.6 7.6 %collective-permute-done.8.refs_2_.refs_10_ = s16[528,1024]{1,0:T(8,128)(2,1)S(1)} collective-permute-done((s16[528,1024]{1,0:T(8,128)(2,1)S(1)}, s16[528,1024]{1,0:T(8,128)(2,1)S(1)}, u32[]{:S(2)}, u32[]{:S(2)}) %collective-permute-start.8) | collective-permute-done | bytes 1081376 | tf_op jit(solution)/shard_map/ppermute | solution.py:511
  64.3 7.1 %collective-permute-done.7.refs_8_ = bf16[1,3,2,72,256]{4,3,2,1,0:T(8,128)(2,1)S(1)} collective-permute-done((bf16[1,3,2,72,256]{4,3,2,1,0:T(8,128)(2,1)S(1)}, bf16[1,3,2,72,256]{4,3,2,1,0:T(8,128)(2,1)S(1)}, u32[]{:S(2)}, u32[]{:S(2)}) %collective-permute-start.7) | collective-permute-done | bytes 221216 | tf_op jit(solution)/shard_map/ppermute | solution.py:511
  71.5 3.7 %collective-permute-start.9 = (s16[528,512]{1,0:T(8,128)(2,1)S(1)}, s16[528,512]{1,0:T(8,128)(2,1)S(1)}, u32[]{:S(2)}, u32[]{:S(2)}) collective-permute-start(s16[528,512]{1,0:T(8,128)(2,1)S(1)} %get-tuple-element.76), channel_id=1, source_target_pairs={{0,8},{4,12},{8,0},{12,4},{16,24},{20,28},{24,16},{28,20},{1,9},{5... | collective-permute-start | bytes 1622024 | tf_op jit(solution)/shard_map/ppermute | solution.py:511
  75.2 8.2 %shard_map.104 = (s16[528,1024]{1,0:T(8,128)(2,1)S(1)}, f32[512,1024]{1,0:T(8,128)S(1)}, f32[8,128]{1,0:T(8,128)S(1)}) custom-call(s32[1]{0:T(128)} %bitcast.refs_0_, bf16[1,3,2,64,1024]{4,3,2,1,0:T(8,128)(2,1)S(1)} %bitcast.40, bf16[2,3,2,64,1024]{4,3,2,1,0:T(8,128)(2,1)S(1)} %collective-permute-done.3.refs_2_.refs_4_, ...), custom_call_target="tpu_custom_call" | custom-call | flops 67108864 | bytes 180224 | tf_op jit(solution)/shard_map/pallas_call | solution.py:197
  88.1 3.6 %collective-permute-start.16 = (s16[528,512]{1,0:T(8,128)(2,1)S(1)}, s16[528,512]{1,0:T(8,128)(2,1)S(1)}, u32[]{:S(2)}, u32[]{:S(2)}) collective-permute-start(s16[528,512]{1,0:T(8,128)(2,1)S(1)} %get-tuple-element.89), channel_id=1, source_target_pairs={{0,8},{4,12},{8,0},{12,4},{16,24},{20,28},{24,16},{28,20},{1,9},{5... | collective-permute-start | bytes 1622024 | tf_op jit(solution)/shard_map/ppermute | solution.py:511
  95.8 3.4 %shard_map.107 = (f32[3,2,384,96]{3,2,1,0:T(8,128)S(1)}, f32[8,128]{1,0:T(8,128)S(1)}) custom-call(bf16[1,2,96,1024]{3,2,1,0:T(8,128)(2,1)S(1)} %bitcast.45, bf16[1,2,96,1024]{3,2,1,0:T(8,128)(2,1)S(1)} %bitcast.53, bf16[1,2,96,1024]{3,2,1,0:T(8,128)(2,1)S(1)} %bitcast.52, bf16[1,2,96,1024]{3,2,1,0:T(8,128)(2,1)S(1)} %bitcast.54, ...), custom_call_target="tpu_custom_call" | custom-call | flops 28311552 | bytes 36864 | tf_op jit(solution)/shard_map/pallas_call | solution.py:364
  99.2 8.3 %collective-permute-done.10.refs_12_ = s16[528,256]{1,0:T(8,128)(2,1)S(1)} collective-permute-done((s16[528,256]{1,0:T(8,128)(2,1)S(1)}, s16[528,256]{1,0:T(8,128)(2,1)S(1)}, u32[]{:S(2)}, u32[]{:S(2)}) %collective-permute-start.10) | collective-permute-done | bytes 270368 | tf_op jit(solution)/shard_map/ppermute | solution.py:511
  110.2 3.8 %collective-permute-start.17 = (s16[528,512]{1,0:T(8,128)(2,1)S(1)}, s16[528,512]{1,0:T(8,128)(2,1)S(1)}, u32[]{:S(2)}, u32[]{:S(2)}) collective-permute-start(s16[528,512]{1,0:T(8,128)(2,1)S(1)} %get-tuple-element.93), channel_id=1, source_target_pairs={{0,8},{4,12},{8,0},{12,4},{16,24},{20,28},{24,16},{28,20},{1,9},{5... | collective-permute-start | bytes 1622024 | tf_op jit(solution)/shard_map/ppermute | solution.py:511
  115.9 14.7 %collective-permute-done.18.refs_12_ = s16[528,256]{1,0:T(8,128)(2,1)S(1)} collective-permute-done((s16[528,256]{1,0:T(8,128)(2,1)S(1)}, s16[528,256]{1,0:T(8,128)(2,1)S(1)}, u32[]{:S(2)}, u32[]{:S(2)}) %collective-permute-start.18) | collective-permute-done | bytes 270368 | tf_op jit(solution)/shard_map/ppermute | solution.py:511
  135.0 6.0 %shard_map.111 = (f32[384,512]{1,0:T(8,128)S(1)}, s16[400,512]{1,0:T(8,128)(2,1)S(1)}, f32[8,128]{1,0:T(8,128)S(1)}) custom-call(s32[1]{0:T(128)} %bitcast.refs_0_, bf16[1,3,2,72,256]{4,3,2,1,0:T(8,128)(2,1)S(1)} %get-tuple-element.63.refs_1_, bf16[1,3,2,72,256]{4,3,2,1,0:T(8,128)(2,1)} %collective-permute-done.refs_2_, ...), custom_call_target="tpu_custom_call" | custom-call | flops 43750000 | bytes 125000 | tf_op jit(solution)/shard_map/pallas_call | solution.py:501
  141.1 6.0 %shard_map.113 = (f32[384,512]{1,0:T(8,128)S(1)}, s16[400,512]{1,0:T(8,128)(2,1)S(1)}, f32[8,128]{1,0:T(8,128)S(1)}) custom-call(s32[1]{0:T(128)} %bitcast.refs_0_, bf16[1,3,2,72,256]{4,3,2,1,0:T(8,128)(2,1)S(1)} %get-tuple-element.63.refs_1_, bf16[1,3,2,72,256]{4,3,2,1,0:T(8,128)(2,1)} %collective-permute-done.refs_2_, ...), custom_call_target="tpu_custom_call" | custom-call | flops 43750000 | bytes 125000 | tf_op jit(solution)/shard_map/pallas_call | solution.py:501
  147.7 6.8 %shard_map.115 = (f32[384,512]{1,0:T(8,128)S(1)}, s16[400,512]{1,0:T(8,128)(2,1)S(1)}, f32[8,128]{1,0:T(8,128)}) custom-call(s32[1]{0:T(128)} %bitcast.refs_0_, bf16[1,3,2,72,256]{4,3,2,1,0:T(8,128)(2,1)S(1)} %get-tuple-element.63.refs_1_, bf16[1,3,2,72,256]{4,3,2,1,0:T(8,128)(2,1)} %collective-permute-done.refs_2_, ...), custom_call_target="tpu_custom_call" | custom-call | flops 43750000 | bytes 125000 | tf_op jit(solution)/shard_map/pallas_call | solution.py:501
  158.2 4.8 %collective-permute-done.23.refs_3_ = s16[208,512]{1,0:T(8,128)(2,1)S(1)} collective-permute-done((s16[208,512]{1,0:T(8,128)(2,1)S(1)}, s16[208,512]{1,0:T(8,128)(2,1)S(1)}, u32[]{:S(2)}, u32[]{:S(2)}) %collective-permute-start.23) | collective-permute-done | bytes 213024 | tf_op jit(solution)/shard_map/ppermute | solution.py:511
  162.9 4.6 %collective-permute-done.24.refs_4_ = s16[208,512]{1,0:T(8,128)(2,1)S(1)} collective-permute-done((s16[208,512]{1,0:T(8,128)(2,1)S(1)}, s16[208,512]{1,0:T(8,128)(2,1)S(1)}, u32[]{:S(2)}, u32[]{:S(2)}) %collective-permute-start.24) | collective-permute-done | bytes 213024 | tf_op jit(solution)/shard_map/ppermute | solution.py:511
  167.5 4.1 %collective-permute-done.25.refs_5_ = s16[208,512]{1,0:T(8,128)(2,1)S(1)} collective-permute-done((s16[208,512]{1,0:T(8,128)(2,1)S(1)}, s16[208,512]{1,0:T(8,128)(2,1)S(1)}, u32[]{:S(2)}, u32[]{:S(2)}) %collective-permute-start.25) | collective-permute-done | bytes 213024 | tf_op jit(solution)/shard_map/ppermute | solution.py:511
  173.8 7.3 %collective-permute-done.26.heard_ref = s16[1200,128]{1,0:T(8,128)(2,1)S(1)} collective-permute-done((s16[1200,128]{1,0:T(8,128)(2,1)S(1)}, s16[1200,128]{1,0:T(8,128)(2,1)S(1)}, u32[]{:S(2)}, u32[]{:S(2)}) %collective-permute-start.26) | collective-permute-done | bytes 307232 | tf_op jit(solution)/shard_map/ppermute | solution.py:511
  182.7 4.0 %collective-permute-done.27.heard_ref = s16[608,128]{1,0:T(8,128)(2,1)S(1)} collective-permute-done((s16[608,128]{1,0:T(8,128)(2,1)S(1)}, s16[608,128]{1,0:T(8,128)(2,1)S(1)}, u32[]{:S(2)}, u32[]{:S(2)}) %collective-permute-start.27) | collective-permute-done | bytes 155680 | tf_op jit(solution)/shard_map/ppermute | solution.py:511
  188.7 4.2 %collective-permute-done.28.heard_ref = s16[304,128]{1,0:T(8,128)(2,1)S(1)} collective-permute-done((s16[304,128]{1,0:T(8,128)(2,1)S(1)}, s16[304,128]{1,0:T(8,128)(2,1)S(1)}, u32[]{:S(2)}, u32[]{:S(2)}) %collective-permute-start.28) | collective-permute-done | bytes 77856 | tf_op jit(solution)/shard_map/ppermute | solution.py:511
  (108 shorter events, 52.1 us)
Async XLA Ops:
  1.4 20.5 %collective-permute-start.2 = (bf16[1,3,2,64,1024]{4,3,2,1,0:T(8,128)(2,1)S(1)}, bf16[1,3,2,64,1024]{4,3,2,1,0:T(8,128)(2,1)S(1)}, u32[]{:S(2)}, u32[]{:S(2)}) collective-permute-start(bf16[1,3,2,64,1024]{4,3,2,1,0:T(8,128)(2,1)S(1)} %bitcast.36), channel_id=1, source_target_pairs={{0,2},{1,3},{2,0},{3,1},{4,6},{5,7},{6,4},{7,5},{8,10},{9,11},{10,... | collective-permute-start | bytes 2359304 | tf_op jit(solution)/shard_map/ppermute | solution.py:511
  9.4 18.7 %collective-permute-start = (bf16[1,3,2,72,256]{4,3,2,1,0:T(8,128)(2,1)}, bf16[1,3,2,72,256]{4,3,2,1,0:T(8,128)(2,1)}, u32[]{:S(2)}, u32[]{:S(2)}) collective-permute-start(bf16[1,3,2,72,256]{4,3,2,1,0:T(8,128)(2,1)} %get-tuple-element.64), channel_id=1, source_target_pairs={{0,16},{4,20},{8,24},{12,28},{16,0},{20,4},{24,8},{28,12},{1,17},{... | collective-permute-start | bytes 663560 | tf_op jit(solution)/shard_map/ppermute | solution.py:511
  12.0 16.2 %collective-permute-start.4 = (bf16[1,3,2,72,256]{4,3,2,1,0:T(8,128)(2,1)}, bf16[1,3,2,72,256]{4,3,2,1,0:T(8,128)(2,1)}, u32[]{:S(2)}, u32[]{:S(2)}) collective-permute-start(bf16[1,3,2,72,256]{4,3,2,1,0:T(8,128)(2,1)} %get-tuple-element.66), channel_id=1, source_target_pairs={{0,24},{4,28},{8,16},{12,20},{16,8},{20,12},{24,0},{28,4},{1,25},{... | collective-permute-start | bytes 663560 | tf_op jit(solution)/shard_map/ppermute | solution.py:511
  13.3 24.6 %collective-permute-start.1 = (bf16[4,3,2,72,256]{4,3,2,1,0:T(8,128)(2,1)}, bf16[4,3,2,72,256]{4,3,2,1,0:T(8,128)(2,1)}, u32[]{:S(2)}, u32[]{:S(2)}) collective-permute-start(bf16[4,3,2,72,256]{4,3,2,1,0:T(8,128)(2,1)} %get-tuple-element.67), channel_id=1, source_target_pairs={{0,4},{4,0},{8,12},{12,8},{16,20},{20,16},{24,28},{28,24},{1,5},{5... | collective-permute-start | bytes 2654216 | tf_op jit(solution)/shard_map/ppermute | solution.py:511
  36.3 26.9 %collective-permute-start.8 = (s16[528,1024]{1,0:T(8,128)(2,1)S(1)}, s16[528,1024]{1,0:T(8,128)(2,1)S(1)}, u32[]{:S(2)}, u32[]{:S(2)}) collective-permute-start(s16[528,1024]{1,0:T(8,128)(2,1)S(1)} %get-tuple-element.74), channel_id=1, source_target_pairs={{0,4},{4,0},{8,12},{12,8},{16,20},{20,16},{24,28},{28,24},{1,5},{5... | collective-permute-start | bytes 3244040 | tf_op jit(solution)/shard_map/ppermute | solution.py:511
  46.1 40.8 %collective-permute-start.14 = (s16[528,1024]{1,0:T(8,128)(2,1)S(1)}, s16[528,1024]{1,0:T(8,128)(2,1)S(1)}, u32[]{:S(2)}, u32[]{:S(2)}) collective-permute-start(s16[528,1024]{1,0:T(8,128)(2,1)S(1)} %get-tuple-element.83), channel_id=1, source_target_pairs={{0,4},{4,0},{8,12},{12,8},{16,20},{20,16},{24,28},{28,24},{1,5},{5... | collective-permute-start | bytes 3244040 | tf_op jit(solution)/shard_map/ppermute | solution.py:511
  48.0 23.6 %collective-permute-start.5 = (bf16[2,3,2,72,256]{4,3,2,1,0:T(8,128)(2,1)S(1)}, bf16[2,3,2,72,256]{4,3,2,1,0:T(8,128)(2,1)S(1)}, u32[]{:S(2)}, u32[]{:S(2)}) collective-permute-start(bf16[2,3,2,72,256]{4,3,2,1,0:T(8,128)(2,1)S(1)} %pad_maximum_fusion.1), channel_id=1, source_target_pairs={{0,8},{4,12},{8,0},{12,4},{16,24},{20,28},{24,16},{28,20},{1,9},{5... | collective-permute-start | bytes 1327112 | tf_op jit(solution)/shard_map/ppermute | solution.py:511
  52.2 19.2 %collective-permute-start.7 = (bf16[1,3,2,72,256]{4,3,2,1,0:T(8,128)(2,1)S(1)}, bf16[1,3,2,72,256]{4,3,2,1,0:T(8,128)(2,1)S(1)}, u32[]{:S(2)}, u32[]{:S(2)}) collective-permute-start(bf16[1,3,2,72,256]{4,3,2,1,0:T(8,128)(2,1)S(1)} %get-tuple-element.119), channel_id=1, source_target_pairs={{0,24},{4,28},{8,16},{12,20},{16,8},{20,12},{24,0},{28,4},{1,25},{... | collective-permute-start | bytes 663560 | tf_op jit(solution)/shard_map/ppermute | solution.py:511
  55.6 15.8 %collective-permute-start.6 = (bf16[1,3,2,72,256]{4,3,2,1,0:T(8,128)(2,1)S(1)}, bf16[1,3,2,72,256]{4,3,2,1,0:T(8,128)(2,1)S(1)}, u32[]{:S(2)}, u32[]{:S(2)}) collective-permute-start(bf16[1,3,2,72,256]{4,3,2,1,0:T(8,128)(2,1)S(1)} %get-tuple-element.120), channel_id=1, source_target_pairs={{0,16},{4,20},{8,24},{12,28},{16,0},{20,4},{24,8},{28,12},{1,17},{... | collective-permute-start | bytes 663560 | tf_op jit(solution)/shard_map/ppermute | solution.py:511
  71.5 14.6 %collective-permute-start.9 = (s16[528,512]{1,0:T(8,128)(2,1)S(1)}, s16[528,512]{1,0:T(8,128)(2,1)S(1)}, u32[]{:S(2)}, u32[]{:S(2)}) collective-permute-start(s16[528,512]{1,0:T(8,128)(2,1)S(1)} %get-tuple-element.76), channel_id=1, source_target_pairs={{0,8},{4,12},{8,0},{12,4},{16,24},{20,28},{24,16},{28,20},{1,9},{5... | collective-permute-start | bytes 1622024 | tf_op jit(solution)/shard_map/ppermute | solution.py:511
  83.4 25.6 %collective-permute-start.15 = (s16[528,1024]{1,0:T(8,128)(2,1)S(1)}, s16[528,1024]{1,0:T(8,128)(2,1)S(1)}, u32[]{:S(2)}, u32[]{:S(2)}) collective-permute-start(s16[528,1024]{1,0:T(8,128)(2,1)S(1)} %get-tuple-element.88), channel_id=1, source_target_pairs={{0,4},{4,0},{8,12},{12,8},{16,20},{20,16},{24,28},{28,24},{1,5},{5... | collective-permute-start | bytes 3244040 | tf_op jit(solution)/shard_map/ppermute | solution.py:511
  85.0 9.1 %collective-permute-start.12 = (bf16[2,96,1024]{2,1,0:T(8,128)(2,1)S(1)}, bf16[2,96,1024]{2,1,0:T(8,128)(2,1)S(1)}, u32[]{:S(2)}, u32[]{:S(2)}) collective-permute-start(bf16[2,96,1024]{2,1,0:T(8,128)(2,1)S(1)} %bitcast.43), channel_id=1, source_target_pairs={{0,2},{1,3},{2,0},{3,1},{4,6},{5,7},{6,4},{7,5},{8,10},{9,11},{10,... | collective-permute-start | bytes 1179656 | tf_op jit(solution)/shard_map/ppermute | solution.py:511
  88.1 20.1 %collective-permute-start.16 = (s16[528,512]{1,0:T(8,128)(2,1)S(1)}, s16[528,512]{1,0:T(8,128)(2,1)S(1)}, u32[]{:S(2)}, u32[]{:S(2)}) collective-permute-start(s16[528,512]{1,0:T(8,128)(2,1)S(1)} %get-tuple-element.89), channel_id=1, source_target_pairs={{0,8},{4,12},{8,0},{12,4},{16,24},{20,28},{24,16},{28,20},{1,9},{5... | collective-permute-start | bytes 1622024 | tf_op jit(solution)/shard_map/ppermute | solution.py:511
  94.1 13.4 %collective-permute-start.10 = (s16[528,256]{1,0:T(8,128)(2,1)S(1)}, s16[528,256]{1,0:T(8,128)(2,1)S(1)}, u32[]{:S(2)}, u32[]{:S(2)}) collective-permute-start(s16[528,256]{1,0:T(8,128)(2,1)S(1)} %get-tuple-element.80), channel_id=1, source_target_pairs={{0,16},{4,20},{8,24},{12,28},{16,0},{20,4},{24,8},{28,12},{1,17},{... | collective-permute-start | bytes 811016 | tf_op jit(solution)/shard_map/ppermute | solution.py:511
  110.2 21.2 %collective-permute-start.17 = (s16[528,512]{1,0:T(8,128)(2,1)S(1)}, s16[528,512]{1,0:T(8,128)(2,1)S(1)}, u32[]{:S(2)}, u32[]{:S(2)}) collective-permute-start(s16[528,512]{1,0:T(8,128)(2,1)S(1)} %get-tuple-element.93), channel_id=1, source_target_pairs={{0,8},{4,12},{8,0},{12,4},{16,24},{20,28},{24,16},{28,20},{1,9},{5... | collective-permute-start | bytes 1622024 | tf_op jit(solution)/shard_map/ppermute | solution.py:511
  114.0 16.7 %collective-permute-start.18 = (s16[528,256]{1,0:T(8,128)(2,1)S(1)}, s16[528,256]{1,0:T(8,128)(2,1)S(1)}, u32[]{:S(2)}, u32[]{:S(2)}) collective-permute-start(s16[528,256]{1,0:T(8,128)(2,1)S(1)} %get-tuple-element.95), channel_id=1, source_target_pairs={{0,16},{4,20},{8,24},{12,28},{16,0},{20,4},{24,8},{28,12},{1,17},{... | collective-permute-start | bytes 811016 | tf_op jit(solution)/shard_map/ppermute | solution.py:511
  132.3 15.4 %collective-permute-start.21 = (s16[528,256]{1,0:T(8,128)(2,1)S(1)}, s16[528,256]{1,0:T(8,128)(2,1)S(1)}, u32[]{:S(2)}, u32[]{:S(2)}) collective-permute-start(s16[528,256]{1,0:T(8,128)(2,1)S(1)} %get-tuple-element.105), channel_id=1, source_target_pairs={{0,16},{4,20},{8,24},{12,28},{16,0},{20,4},{24,8},{28,12},{1,17},{... | collective-permute-start | bytes 811016 | tf_op jit(solution)/shard_map/ppermute | solution.py:511
  141.1 13.5 %collective-permute-start.19 = (s16[1,400,512]{2,1,0:T(8,128)(2,1)S(1)}, s16[1,400,512]{2,1,0:T(8,128)(2,1)S(1)}, u32[]{:S(2)}, u32[]{:S(2)}) collective-permute-start(s16[1,400,512]{2,1,0:T(8,128)(2,1)S(1)} %bitcast.56), channel_id=1, source_target_pairs={{0,1},{1,0},{2,3},{3,2},{4,5},{5,4},{6,7},{7,6},{8,9},{9,8},{10,11... | collective-permute-start | bytes 1228808 | tf_op jit(solution)/shard_map/ppermute | solution.py:511
  147.2 8.2 %collective-permute-start.20 = (s16[1,400,512]{2,1,0:T(8,128)(2,1)S(1)}, s16[1,400,512]{2,1,0:T(8,128)(2,1)S(1)}, u32[]{:S(2)}, u32[]{:S(2)}) collective-permute-start(s16[1,400,512]{2,1,0:T(8,128)(2,1)S(1)} %bitcast.55), channel_id=1, source_target_pairs={{0,1},{1,0},{2,3},{3,2},{4,5},{5,4},{6,7},{7,6},{8,9},{9,8},{10,11... | collective-permute-start | bytes 1228808 | tf_op jit(solution)/shard_map/ppermute | solution.py:511
  154.8 8.1 %collective-permute-start.23 = (s16[208,512]{1,0:T(8,128)(2,1)S(1)}, s16[208,512]{1,0:T(8,128)(2,1)S(1)}, u32[]{:S(2)}, u32[]{:S(2)}) collective-permute-start(s16[208,512]{1,0:T(8,128)(2,1)S(1)} %bitcast.58), channel_id=1, source_target_pairs={{0,2},{1,3},{2,0},{3,1},{4,6},{5,7},{6,4},{7,5},{8,10},{9,11},{10,... | collective-permute-start | bytes 638984 | tf_op jit(solution)/shard_map/ppermute | solution.py:511
  155.7 11.8 %collective-permute-start.24 = (s16[208,512]{1,0:T(8,128)(2,1)S(1)}, s16[208,512]{1,0:T(8,128)(2,1)S(1)}, u32[]{:S(2)}, u32[]{:S(2)}) collective-permute-start(s16[208,512]{1,0:T(8,128)(2,1)S(1)} %bitcast.59), channel_id=1, source_target_pairs={{0,2},{1,3},{2,0},{3,1},{4,6},{5,7},{6,4},{7,5},{8,10},{9,11},{10,... | collective-permute-start | bytes 638984 | tf_op jit(solution)/shard_map/ppermute | solution.py:511
  157.6 14.1 %collective-permute-start.25 = (s16[208,512]{1,0:T(8,128)(2,1)S(1)}, s16[208,512]{1,0:T(8,128)(2,1)S(1)}, u32[]{:S(2)}, u32[]{:S(2)}) collective-permute-start(s16[208,512]{1,0:T(8,128)(2,1)S(1)} %bitcast.60), channel_id=1, source_target_pairs={{0,2},{1,3},{2,0},{3,1},{4,6},{5,7},{6,4},{7,5},{8,10},{9,11},{10,... | collective-permute-start | bytes 638984 | tf_op jit(solution)/shard_map/ppermute | solution.py:511
  172.2 8.9 %collective-permute-start.26 = (s16[1200,128]{1,0:T(8,128)(2,1)S(1)}, s16[1200,128]{1,0:T(8,128)(2,1)S(1)}, u32[]{:S(2)}, u32[]{:S(2)}) collective-permute-start(s16[1200,128]{1,0:T(8,128)(2,1)S(1)} %get-tuple-element.114), channel_id=1, source_target_pairs={{0,4},{4,0},{8,12},{12,8},{16,20},{20,16},{24,28},{28,24},{1,5},{5... | collective-permute-start | bytes 921608 | tf_op jit(solution)/shard_map/ppermute | solution.py:511
  186.8 6.2 %collective-permute-start.28 = (s16[304,128]{1,0:T(8,128)(2,1)S(1)}, s16[304,128]{1,0:T(8,128)(2,1)S(1)}, u32[]{:S(2)}, u32[]{:S(2)}) collective-permute-start(s16[304,128]{1,0:T(8,128)(2,1)S(1)} %get-tuple-element.118), channel_id=1, source_target_pairs={{0,16},{4,20},{8,24},{12,28},{16,0},{20,4},{24,8},{28,12},{1,17},{... | collective-permute-start | bytes 233480 | tf_op jit(solution)/shard_map/ppermute | solution.py:511
  (13 other events, 77.9 us)

commit v12 on v11

--- a/solution.py
+++ b/solution.py
@@ -284,20 +284,25 @@
 def pack_kernel(*refs):
     *refs, keep_ref, go_ref, sums_ref = refs
     slots, points, rows, _ = sums_ref.shape
+    width = refs[0].shape[1]
+    count = width // slots
     first = lax.broadcasted_iota(jnp.int32, (rows, 128), 1) < 64
     for n in range(points):
         total = refs[n][...] + decode(refs[points + n])
-        for block in range(slots // 2):
-            cols = slice(block * 128, (block + 1) * 128)
-            real, imag = total[:rows, cols], total[rows:, cols]
-            sums_ref[2 * block, n] = jnp.where(first, real, pltpu.roll(imag, 64, 1))
-            sums_ref[2 * block + 1, n] = jnp.where(first, pltpu.roll(real, 64, 1), imag)
+        for slot in range(slots):
+            tile, lane = divmod(slot * count, 128)
+            reach = min(width, (tile + (1 if lane + count <= 128 else 2)) * 128)
+            piece = total[:, tile * 128 : reach]
+            if lane:
+                piece = pltpu.roll(piece, reach - tile * 128 - lane, 1)
+            real, imag = piece[:rows, :128], piece[rows:, :128]
+            sums_ref[slot, n] = jnp.where(first, real, pltpu.roll(imag, 64, 1))
     split_sums(sums_ref, keep_ref, go_ref)
 
 
-def pack_call(owns, heards):
+def pack_call(owns, heards, slots):
     rows, cols = owns[0].shape
-    shape = (cols // 64, len(owns), rows // 2)
+    shape = (slots, len(owns), rows // 2)
     return pl.pallas_call(
         pack_kernel,
         out_shape=split_shapes(*shape),
@@ -560,11 +565,9 @@
     at_row = ((row_trans // row_count) ^ me_pair) * row_count + row_trans % row_count
     pick_rows = (at_row[:, None] == jnp.arange(NT, dtype=jnp.int32)[None, :]).astype(jnp.bfloat16)
     col_trans = ordering.reshape(ga, col_count)[me_ga ^ jnp.asarray(ga_order, jnp.int32)]
-    col_trans = jnp.pad(col_trans, ((0, 0), (0, 64 - col_count)), constant_values=-1).reshape(1, -1)
-    real_col = col_trans >= 0
-    at_direct = jnp.where(real_col, (col_trans % NC) * NV + col_trans // NC, -1)
-    own_col = real_col & (col_trans // row_count == me_pair)
-    at_exch = jnp.where(own_col, col_trans % row_count, -1)
+    col_trans = col_trans.reshape(1, -1)
+    at_direct = (col_trans % NC) * NV + col_trans // NC
+    at_exch = jnp.where(col_trans // row_count == me_pair, col_trans % row_count, -1)
 
     def pick_cols(at, size, scale):
         hot = at == jnp.arange(size, dtype=jnp.int32)[:, None]
@@ -575,16 +578,14 @@
     there = jnp.transpose(trans_there, (1, 2, 0, 3))
     arrived = [block for block, _ in cons.values()]
     token = behind(token, (there, pick_rows, col_direct, col_exch, arrived))
-    order = [("x", 0, 0), ("x", 1, 0), ("hop", 0, 1)] + [("x", q, 0) for q in range(2, points)]
+    order = [("x", q, 0) for q in range(points)]
     hops = [(2 * q + s, q, s) for q in range(points) for s in range(1, stages)]
-    order += [("hop", q, s) for _, q, s in sorted(hops) if (q, s) != (0, 1)]
+    order += [("hop", q, s) for _, q, s in sorted(hops)]
     order += [("tile", q, stages) for q in range(points)]
     gone, keep, heard = [], [], []
     tiles = [None] * points
     for kind, q, stage in order:
         if kind == "x":
-            if q == 2:
-                token = behind(token, [c for c, _ in cons])
             coded, own, token = x_call(
                 [vals[slot] for slot in range(pair)], screened, q, q, me, 4, [token]
             )
@@ -603,6 +604,8 @@
                 cons = [cons[slot] for slot in ga_order]
         elif kind == "hop":
             columns = (ga >> (stage + 1)) * width
+            if (q, stage) == (0, 1):
+                token = behind(token, [c for c, _ in cons])
             if q > 0 and stage == stages - 1:
                 token = behind(token, heard[q - 1][-1])
             coded, token = hop_call(keep[q], heard[q], me, stage, columns, [token])
@@ -625,7 +628,7 @@
                 own, sent = own[0], sent[0]
             tiles[q] = own, swap(sent, "pair", pair, pair_bits[-1])
 
-    own, sent = pack_call(*zip(*tiles))
+    own, sent = pack_call(*zip(*tiles), ga)
     for bit in ga_bits[:-1]:
         own, sent = merge_call(own, swap(sent, "ga", ga, bit))
     total = merge_call(own, swap(sent, "ga", ga, ga_bits[-1]))[0]

time: 194 us -> 191 us (0.985)
  waiting for transfers between devices: 80.3 us -> 75.3 us
    ppermute x29, waiting for transfers between devices: 80.3 us -> 75.3 us  [swap(): return lax.ppermute(value, axis, [(i, i ^ bit) for i in range(size)])]
  transfers between devices with their start and end apart: 29 -> 29, of which waited for: 18 -> 15; matrix products, arithmetic and copies ran while one was open for 5% -> 5% of each run, Pallas kernels for 28% -> 28%
where the time goes in v12:
time: 191 us
  waiting for transfers between devices  75.3 us (39%)
  Pallas kernels  57.8 us (30%)
  starting transfers between devices  45.9 us (24%)
  local copies, waits for them, and re-layouts  9.94 us (5%)
    ppermute x29, waiting for transfers between devices, swap(): return lax.ppermute(value, axis, [(i, i ^ bit) for i in range(size)])  75.3 us
    ppermute x29, starting transfers between devices, swap(): return lax.ppermute(value, axis, [(i, i ^ bit) for i in range(size)])  45.9 us
    pallas_call x3, Pallas kernels, x_call(): pl.pallas_call(lambda *refs: x_kernel(slots, len(after), *refs), grid_spe...  24.6 us
    pallas_call x3, Pallas kernels, tile_call(): pl.pallas_call(lambda *refs: tile_kernel(order, stages, chunks, len(after...  18.7 us
    pallas_call x6, Pallas kernels, hop_call(): pl.pallas_call(lambda *refs: hop_kernel(len(others), *refs), grid_spec=gr...  5.99 us
  transfers between devices with their start and end apart: 29, of which 15 were waited for; matrix products, arithmetic and copies ran while one was open for 5% of the time, Pallas kernels for 28%

profile of v12, /device:TPU:0, one launch (start us, length us, event | category | flops | bytes accessed | tf_op | source)
XLA Modules:
  0.0 191.0 jit_solution(7812777818617433862)
XLA Ops:
  1.4 3.0 %collective-permute-start.2 = (bf16[1,3,2,64,1024]{4,3,2,1,0:T(8,128)(2,1)S(1)}, bf16[1,3,2,64,1024]{4,3,2,1,0:T(8,128)(2,1)S(1)}, u32[]{:S(2)}, u32[]{:S(2)}) collective-permute-start(bf16[1,3,2,64,1024]{4,3,2,1,0:T(8,128)(2,1)S(1)} %bitcast.36), channel_id=1, source_target_pairs={{0,2},{1,3},{2,0},{3,1},{4,6},{5,7},{6,4},{7,5},{8,10},{9,11},{10,... | collective-permute-start | bytes 2359304 | tf_op jit(solution)/shard_map/ppermute | solution.py:516
  16.5 5.4 %collective-permute-done.2.refs_3_ = bf16[1,3,2,64,1024]{4,3,2,1,0:T(8,128)(2,1)S(1)} collective-permute-done((bf16[1,3,2,64,1024]{4,3,2,1,0:T(8,128)(2,1)S(1)}, bf16[1,3,2,64,1024]{4,3,2,1,0:T(8,128)(2,1)S(1)}, u32[]{:S(2)}, u32[]{:S(2)}) %collective-permute-start.2) | collective-permute-done | bytes 786464 | tf_op jit(solution)/shard_map/ppermute | solution.py:516
  28.1 8.2 %shard_map.101 = (s16[528,1024]{1,0:T(8,128)(2,1)S(1)}, f32[512,1024]{1,0:T(8,128)S(1)}, f32[8,128]{1,0:T(8,128)S(1)}) custom-call(s32[1]{0:T(128)} %bitcast.refs_0_, bf16[1,3,2,64,1024]{4,3,2,1,0:T(8,128)(2,1)S(1)} %bitcast.38, bf16[2,3,2,64,1024]{4,3,2,1,0:T(8,128)(2,1)S(1)} %collective-permute-done.3.refs_2_.refs_4_, ...), custom_call_target="tpu_custom_call" | custom-call | flops 67108864 | bytes 180224 | tf_op jit(solution)/shard_map/pallas_call | solution.py:197
  37.9 8.2 %shard_map.102 = (s16[528,1024]{1,0:T(8,128)(2,1)S(1)}, f32[512,1024]{1,0:T(8,128)S(1)}, f32[8,128]{1,0:T(8,128)S(1)}) custom-call(s32[1]{0:T(128)} %bitcast.refs_0_, bf16[1,3,2,64,1024]{4,3,2,1,0:T(8,128)(2,1)S(1)} %bitcast.39, bf16[2,3,2,64,1024]{4,3,2,1,0:T(8,128)(2,1)S(1)} %collective-permute-done.3.refs_2_.refs_4_, ...), custom_call_target="tpu_custom_call" | custom-call | flops 67108864 | bytes 180224 | tf_op jit(solution)/shard_map/pallas_call | solution.py:197
  48.0 4.3 %collective-permute-start.5 = (bf16[2,3,2,72,256]{4,3,2,1,0:T(8,128)(2,1)S(1)}, bf16[2,3,2,72,256]{4,3,2,1,0:T(8,128)(2,1)S(1)}, u32[]{:S(2)}, u32[]{:S(2)}) collective-permute-start(bf16[2,3,2,72,256]{4,3,2,1,0:T(8,128)(2,1)S(1)} %pad_maximum_fusion.1), channel_id=1, source_target_pairs={{0,8},{4,12},{8,0},{12,4},{16,24},{20,28},{24,16},{28,20},{1,9},{5... | collective-permute-start | bytes 1327112 | tf_op jit(solution)/shard_map/ppermute | solution.py:516
  52.3 3.4 %collective-permute-start.7 = (bf16[1,3,2,72,256]{4,3,2,1,0:T(8,128)(2,1)S(1)}, bf16[1,3,2,72,256]{4,3,2,1,0:T(8,128)(2,1)S(1)}, u32[]{:S(2)}, u32[]{:S(2)}) collective-permute-start(bf16[1,3,2,72,256]{4,3,2,1,0:T(8,128)(2,1)S(1)} %get-tuple-element.119), channel_id=1, source_target_pairs={{0,24},{4,28},{8,16},{12,20},{16,8},{20,12},{24,0},{28,4},{1,25},{... | collective-permute-start | bytes 663560 | tf_op jit(solution)/shard_map/ppermute | solution.py:516
  55.6 8.2 %shard_map.103 = (s16[528,1024]{1,0:T(8,128)(2,1)S(1)}, f32[512,1024]{1,0:T(8,128)S(1)}, f32[8,128]{1,0:T(8,128)S(1)}) custom-call(s32[1]{0:T(128)} %bitcast.refs_0_, bf16[1,3,2,64,1024]{4,3,2,1,0:T(8,128)(2,1)S(1)} %bitcast.40, bf16[2,3,2,64,1024]{4,3,2,1,0:T(8,128)(2,1)S(1)} %collective-permute-done.3.refs_2_.refs_4_, ...), custom_call_target="tpu_custom_call" | custom-call | flops 67108864 | bytes 180224 | tf_op jit(solution)/shard_map/pallas_call | solution.py:197
  63.8 7.6 %collective-permute-done.7.refs_8_ = bf16[1,3,2,72,256]{4,3,2,1,0:T(8,128)(2,1)S(1)} collective-permute-done((bf16[1,3,2,72,256]{4,3,2,1,0:T(8,128)(2,1)S(1)}, bf16[1,3,2,72,256]{4,3,2,1,0:T(8,128)(2,1)S(1)}, u32[]{:S(2)}, u32[]{:S(2)}) %collective-permute-start.7) | collective-permute-done | bytes 221216 | tf_op jit(solution)/shard_map/ppermute | solution.py:516
  72.7 3.8 %collective-permute-start.9 = (s16[528,512]{1,0:T(8,128)(2,1)S(1)}, s16[528,512]{1,0:T(8,128)(2,1)S(1)}, u32[]{:S(2)}, u32[]{:S(2)}) collective-permute-start(s16[528,512]{1,0:T(8,128)(2,1)S(1)} %get-tuple-element.78), channel_id=1, source_target_pairs={{0,8},{4,12},{8,0},{12,4},{16,24},{20,28},{24,16},{28,20},{1,9},{5... | collective-permute-start | bytes 1622024 | tf_op jit(solution)/shard_map/ppermute | solution.py:516
  78.6 8.8 %collective-permute-done.9.refs_3_.refs_11_ = s16[528,512]{1,0:T(8,128)(2,1)S(1)} collective-permute-done((s16[528,512]{1,0:T(8,128)(2,1)S(1)}, s16[528,512]{1,0:T(8,128)(2,1)S(1)}, u32[]{:S(2)}, u32[]{:S(2)}) %collective-permute-start.9) | collective-permute-done | bytes 540704 | tf_op jit(solution)/shard_map/ppermute | solution.py:516
  94.3 3.4 %shard_map.107 = (f32[3,2,384,96]{3,2,1,0:T(8,128)S(1)}, f32[8,128]{1,0:T(8,128)S(1)}) custom-call(bf16[1,2,96,1024]{3,2,1,0:T(8,128)(2,1)S(1)} %bitcast.45, bf16[1,2,96,1024]{3,2,1,0:T(8,128)(2,1)S(1)} %bitcast.50, bf16[1,2,96,1024]{3,2,1,0:T(8,128)(2,1)S(1)} %bitcast.49, bf16[1,2,96,1024]{3,2,1,0:T(8,128)(2,1)S(1)} %bitcast.51, ...), custom_call_target="tpu_custom_call" | custom-call | flops 28311552 | bytes 36864 | tf_op jit(solution)/shard_map/pallas_call | solution.py:369
  97.6 9.8 %collective-permute-done.10.refs_12_ = s16[528,256]{1,0:T(8,128)(2,1)S(1)} collective-permute-done((s16[528,256]{1,0:T(8,128)(2,1)S(1)}, s16[528,256]{1,0:T(8,128)(2,1)S(1)}, u32[]{:S(2)}, u32[]{:S(2)}) %collective-permute-start.10) | collective-permute-done | bytes 270368 | tf_op jit(solution)/shard_map/ppermute | solution.py:516
  110.2 3.8 %collective-permute-start.17 = (s16[528,512]{1,0:T(8,128)(2,1)S(1)}, s16[528,512]{1,0:T(8,128)(2,1)S(1)}, u32[]{:S(2)}, u32[]{:S(2)}) collective-permute-start(s16[528,512]{1,0:T(8,128)(2,1)S(1)} %get-tuple-element.93), channel_id=1, source_target_pairs={{0,8},{4,12},{8,0},{12,4},{16,24},{20,28},{24,16},{28,20},{1,9},{5... | collective-permute-start | bytes 1622024 | tf_op jit(solution)/shard_map/ppermute | solution.py:516
  115.9 14.7 %collective-permute-done.18.refs_12_ = s16[528,256]{1,0:T(8,128)(2,1)S(1)} collective-permute-done((s16[528,256]{1,0:T(8,128)(2,1)S(1)}, s16[528,256]{1,0:T(8,128)(2,1)S(1)}, u32[]{:S(2)}, u32[]{:S(2)}) %collective-permute-start.18) | collective-permute-done | bytes 270368 | tf_op jit(solution)/shard_map/ppermute | solution.py:516
  132.3 2.7 %collective-permute-start.21 = (s16[528,256]{1,0:T(8,128)(2,1)S(1)}, s16[528,256]{1,0:T(8,128)(2,1)S(1)}, u32[]{:S(2)}, u32[]{:S(2)}) collective-permute-start(s16[528,256]{1,0:T(8,128)(2,1)S(1)} %get-tuple-element.105), channel_id=1, source_target_pairs={{0,16},{4,20},{8,24},{12,28},{16,0},{20,4},{24,8},{28,12},{1,17},{... | collective-permute-start | bytes 811016 | tf_op jit(solution)/shard_map/ppermute | solution.py:516
  135.0 6.0 %shard_map.111 = (f32[384,384]{1,0:T(8,128)S(1)}, s16[400,384]{1,0:T(8,128)(2,1)S(1)}, f32[8,128]{1,0:T(8,128)S(1)}) custom-call(s32[1]{0:T(128)} %bitcast.refs_0_, bf16[1,3,2,72,256]{4,3,2,1,0:T(8,128)(2,1)S(1)} %get-tuple-element.63.refs_1_, bf16[1,3,2,72,256]{4,3,2,1,0:T(8,128)(2,1)} %collective-permute-done.refs_2_, ...), custom_call_target="tpu_custom_call" | custom-call | flops 43750000 | bytes 125000 | tf_op jit(solution)/shard_map/pallas_call | solution.py:506
  141.1 6.0 %shard_map.113 = (f32[384,384]{1,0:T(8,128)S(1)}, s16[400,384]{1,0:T(8,128)(2,1)S(1)}, f32[8,128]{1,0:T(8,128)S(1)}) custom-call(s32[1]{0:T(128)} %bitcast.refs_0_, bf16[1,3,2,72,256]{4,3,2,1,0:T(8,128)(2,1)S(1)} %get-tuple-element.63.refs_1_, bf16[1,3,2,72,256]{4,3,2,1,0:T(8,128)(2,1)} %collective-permute-done.refs_2_, ...), custom_call_target="tpu_custom_call" | custom-call | flops 43750000 | bytes 125000 | tf_op jit(solution)/shard_map/pallas_call | solution.py:506
  147.6 6.7 %shard_map.115 = (f32[384,384]{1,0:T(8,128)S(1)}, s16[400,384]{1,0:T(8,128)(2,1)S(1)}, f32[8,128]{1,0:T(8,128)}) custom-call(s32[1]{0:T(128)} %bitcast.refs_0_, bf16[1,3,2,72,256]{4,3,2,1,0:T(8,128)(2,1)S(1)} %get-tuple-element.63.refs_1_, bf16[1,3,2,72,256]{4,3,2,1,0:T(8,128)(2,1)} %collective-permute-done.refs_2_, ...), custom_call_target="tpu_custom_call" | custom-call | flops 43750000 | bytes 125000 | tf_op jit(solution)/shard_map/pallas_call | solution.py:506
  157.8 3.8 %collective-permute-done.23.refs_3_ = s16[208,384]{1,0:T(8,128)(2,1)S(1)} collective-permute-done((s16[208,384]{1,0:T(8,128)(2,1)S(1)}, s16[208,384]{1,0:T(8,128)(2,1)S(1)}, u32[]{:S(2)}, u32[]{:S(2)}) %collective-permute-start.23) | collective-permute-done | bytes 159776 | tf_op jit(solution)/shard_map/ppermute | solution.py:516
  161.6 3.4 %collective-permute-done.24.refs_4_ = s16[208,384]{1,0:T(8,128)(2,1)S(1)} collective-permute-done((s16[208,384]{1,0:T(8,128)(2,1)S(1)}, s16[208,384]{1,0:T(8,128)(2,1)S(1)}, u32[]{:S(2)}, u32[]{:S(2)}) %collective-permute-start.24) | collective-permute-done | bytes 159776 | tf_op jit(solution)/shard_map/ppermute | solution.py:516
  165.0 3.0 %collective-permute-done.25.refs_5_ = s16[208,384]{1,0:T(8,128)(2,1)S(1)} collective-permute-done((s16[208,384]{1,0:T(8,128)(2,1)S(1)}, s16[208,384]{1,0:T(8,128)(2,1)S(1)}, u32[]{:S(2)}, u32[]{:S(2)}) %collective-permute-start.25) | collective-permute-done | bytes 159776 | tf_op jit(solution)/shard_map/ppermute | solution.py:516
  171.7 7.4 %collective-permute-done.26.heard_ref = s16[1200,128]{1,0:T(8,128)(2,1)S(1)} collective-permute-done((s16[1200,128]{1,0:T(8,128)(2,1)S(1)}, s16[1200,128]{1,0:T(8,128)(2,1)S(1)}, u32[]{:S(2)}, u32[]{:S(2)}) %collective-permute-start.26) | collective-permute-done | bytes 307232 | tf_op jit(solution)/shard_map/ppermute | solution.py:516
  180.7 3.9 %collective-permute-done.27.heard_ref = s16[608,128]{1,0:T(8,128)(2,1)S(1)} collective-permute-done((s16[608,128]{1,0:T(8,128)(2,1)S(1)}, s16[608,128]{1,0:T(8,128)(2,1)S(1)}, u32[]{:S(2)}, u32[]{:S(2)}) %collective-permute-start.27) | collective-permute-done | bytes 155680 | tf_op jit(solution)/shard_map/ppermute | solution.py:516
  186.7 3.4 %collective-permute-done.28.heard_ref = s16[304,128]{1,0:T(8,128)(2,1)S(1)} collective-permute-done((s16[304,128]{1,0:T(8,128)(2,1)S(1)}, s16[304,128]{1,0:T(8,128)(2,1)S(1)}, u32[]{:S(2)}, u32[]{:S(2)}) %collective-permute-start.28) | collective-permute-done | bytes 77856 | tf_op jit(solution)/shard_map/ppermute | solution.py:516
  (107 shorter events, 51.9 us)
Async XLA Ops:
  1.4 20.5 %collective-permute-start.2 = (bf16[1,3,2,64,1024]{4,3,2,1,0:T(8,128)(2,1)S(1)}, bf16[1,3,2,64,1024]{4,3,2,1,0:T(8,128)(2,1)S(1)}, u32[]{:S(2)}, u32[]{:S(2)}) collective-permute-start(bf16[1,3,2,64,1024]{4,3,2,1,0:T(8,128)(2,1)S(1)} %bitcast.36), channel_id=1, source_target_pairs={{0,2},{1,3},{2,0},{3,1},{4,6},{5,7},{6,4},{7,5},{8,10},{9,11},{10,... | collective-permute-start | bytes 2359304 | tf_op jit(solution)/shard_map/ppermute | solution.py:516
  9.4 18.7 %collective-permute-start = (bf16[1,3,2,72,256]{4,3,2,1,0:T(8,128)(2,1)}, bf16[1,3,2,72,256]{4,3,2,1,0:T(8,128)(2,1)}, u32[]{:S(2)}, u32[]{:S(2)}) collective-permute-start(bf16[1,3,2,72,256]{4,3,2,1,0:T(8,128)(2,1)} %get-tuple-element.64), channel_id=1, source_target_pairs={{0,16},{4,20},{8,24},{12,28},{16,0},{20,4},{24,8},{28,12},{1,17},{... | collective-permute-start | bytes 663560 | tf_op jit(solution)/shard_map/ppermute | solution.py:516
  12.0 16.2 %collective-permute-start.4 = (bf16[1,3,2,72,256]{4,3,2,1,0:T(8,128)(2,1)}, bf16[1,3,2,72,256]{4,3,2,1,0:T(8,128)(2,1)}, u32[]{:S(2)}, u32[]{:S(2)}) collective-permute-start(bf16[1,3,2,72,256]{4,3,2,1,0:T(8,128)(2,1)} %get-tuple-element.66), channel_id=1, source_target_pairs={{0,24},{4,28},{8,16},{12,20},{16,8},{20,12},{24,0},{28,4},{1,25},{... | collective-permute-start | bytes 663560 | tf_op jit(solution)/shard_map/ppermute | solution.py:516
  13.3 24.6 %collective-permute-start.1 = (bf16[4,3,2,72,256]{4,3,2,1,0:T(8,128)(2,1)}, bf16[4,3,2,72,256]{4,3,2,1,0:T(8,128)(2,1)}, u32[]{:S(2)}, u32[]{:S(2)}) collective-permute-start(bf16[4,3,2,72,256]{4,3,2,1,0:T(8,128)(2,1)} %get-tuple-element.67), channel_id=1, source_target_pairs={{0,4},{4,0},{8,12},{12,8},{16,20},{20,16},{24,28},{28,24},{1,5},{5... | collective-permute-start | bytes 2654216 | tf_op jit(solution)/shard_map/ppermute | solution.py:516
  36.3 35.2 %collective-permute-start.8 = (s16[528,1024]{1,0:T(8,128)(2,1)S(1)}, s16[528,1024]{1,0:T(8,128)(2,1)S(1)}, u32[]{:S(2)}, u32[]{:S(2)}) collective-permute-start(s16[528,1024]{1,0:T(8,128)(2,1)S(1)} %get-tuple-element.74), channel_id=1, source_target_pairs={{0,4},{4,0},{8,12},{12,8},{16,20},{20,16},{24,28},{28,24},{1,5},{5... | collective-permute-start | bytes 3244040 | tf_op jit(solution)/shard_map/ppermute | solution.py:516
  46.1 42.1 %collective-permute-start.14 = (s16[528,1024]{1,0:T(8,128)(2,1)S(1)}, s16[528,1024]{1,0:T(8,128)(2,1)S(1)}, u32[]{:S(2)}, u32[]{:S(2)}) collective-permute-start(s16[528,1024]{1,0:T(8,128)(2,1)S(1)} %get-tuple-element.83), channel_id=1, source_target_pairs={{0,4},{4,0},{8,12},{12,8},{16,20},{20,16},{24,28},{28,24},{1,5},{5... | collective-permute-start | bytes 3244040 | tf_op jit(solution)/shard_map/ppermute | solution.py:516
  48.0 23.5 %collective-permute-start.5 = (bf16[2,3,2,72,256]{4,3,2,1,0:T(8,128)(2,1)S(1)}, bf16[2,3,2,72,256]{4,3,2,1,0:T(8,128)(2,1)S(1)}, u32[]{:S(2)}, u32[]{:S(2)}) collective-permute-start(bf16[2,3,2,72,256]{4,3,2,1,0:T(8,128)(2,1)S(1)} %pad_maximum_fusion.1), channel_id=1, source_target_pairs={{0,8},{4,12},{8,0},{12,4},{16,24},{20,28},{24,16},{28,20},{1,9},{5... | collective-permute-start | bytes 1327112 | tf_op jit(solution)/shard_map/ppermute | solution.py:516
  52.3 19.2 %collective-permute-start.7 = (bf16[1,3,2,72,256]{4,3,2,1,0:T(8,128)(2,1)S(1)}, bf16[1,3,2,72,256]{4,3,2,1,0:T(8,128)(2,1)S(1)}, u32[]{:S(2)}, u32[]{:S(2)}) collective-permute-start(bf16[1,3,2,72,256]{4,3,2,1,0:T(8,128)(2,1)S(1)} %get-tuple-element.119), channel_id=1, source_target_pairs={{0,24},{4,28},{8,16},{12,20},{16,8},{20,12},{24,0},{28,4},{1,25},{... | collective-permute-start | bytes 663560 | tf_op jit(solution)/shard_map/ppermute | solution.py:516
  55.6 15.8 %collective-permute-start.6 = (bf16[1,3,2,72,256]{4,3,2,1,0:T(8,128)(2,1)S(1)}, bf16[1,3,2,72,256]{4,3,2,1,0:T(8,128)(2,1)S(1)}, u32[]{:S(2)}, u32[]{:S(2)}) collective-permute-start(bf16[1,3,2,72,256]{4,3,2,1,0:T(8,128)(2,1)S(1)} %get-tuple-element.120), channel_id=1, source_target_pairs={{0,16},{4,20},{8,24},{12,28},{16,0},{20,4},{24,8},{28,12},{1,17},{... | collective-permute-start | bytes 663560 | tf_op jit(solution)/shard_map/ppermute | solution.py:516
  72.7 14.7 %collective-permute-start.9 = (s16[528,512]{1,0:T(8,128)(2,1)S(1)}, s16[528,512]{1,0:T(8,128)(2,1)S(1)}, u32[]{:S(2)}, u32[]{:S(2)}) collective-permute-start(s16[528,512]{1,0:T(8,128)(2,1)S(1)} %get-tuple-element.78), channel_id=1, source_target_pairs={{0,8},{4,12},{8,0},{12,4},{16,24},{20,28},{24,16},{28,20},{1,9},{5... | collective-permute-start | bytes 1622024 | tf_op jit(solution)/shard_map/ppermute | solution.py:516
  76.4 32.5 %collective-permute-start.15 = (s16[528,1024]{1,0:T(8,128)(2,1)S(1)}, s16[528,1024]{1,0:T(8,128)(2,1)S(1)}, u32[]{:S(2)}, u32[]{:S(2)}) collective-permute-start(s16[528,1024]{1,0:T(8,128)(2,1)S(1)} %get-tuple-element.88), channel_id=1, source_target_pairs={{0,4},{4,0},{8,12},{12,8},{16,20},{20,16},{24,28},{28,24},{1,5},{5... | collective-permute-start | bytes 3244040 | tf_op jit(solution)/shard_map/ppermute | solution.py:516
  78.0 13.7 %collective-permute-start.12 = (bf16[2,96,1024]{2,1,0:T(8,128)(2,1)S(1)}, bf16[2,96,1024]{2,1,0:T(8,128)(2,1)S(1)}, u32[]{:S(2)}, u32[]{:S(2)}) collective-permute-start(bf16[2,96,1024]{2,1,0:T(8,128)(2,1)S(1)} %bitcast.43), channel_id=1, source_target_pairs={{0,2},{1,3},{2,0},{3,1},{4,6},{5,7},{6,4},{7,5},{8,10},{9,11},{10,... | collective-permute-start | bytes 1179656 | tf_op jit(solution)/shard_map/ppermute | solution.py:516
  89.4 18.8 %collective-permute-start.16 = (s16[528,512]{1,0:T(8,128)(2,1)S(1)}, s16[528,512]{1,0:T(8,128)(2,1)S(1)}, u32[]{:S(2)}, u32[]{:S(2)}) collective-permute-start(s16[528,512]{1,0:T(8,128)(2,1)S(1)} %get-tuple-element.89), channel_id=1, source_target_pairs={{0,8},{4,12},{8,0},{12,4},{16,24},{20,28},{24,16},{28,20},{1,9},{5... | collective-permute-start | bytes 1622024 | tf_op jit(solution)/shard_map/ppermute | solution.py:516
  92.2 15.2 %collective-permute-start.10 = (s16[528,256]{1,0:T(8,128)(2,1)S(1)}, s16[528,256]{1,0:T(8,128)(2,1)S(1)}, u32[]{:S(2)}, u32[]{:S(2)}) collective-permute-start(s16[528,256]{1,0:T(8,128)(2,1)S(1)} %get-tuple-element.80), channel_id=1, source_target_pairs={{0,16},{4,20},{8,24},{12,28},{16,0},{20,4},{24,8},{28,12},{1,17},{... | collective-permute-start | bytes 811016 | tf_op jit(solution)/shard_map/ppermute | solution.py:516
  110.2 21.2 %collective-permute-start.17 = (s16[528,512]{1,0:T(8,128)(2,1)S(1)}, s16[528,512]{1,0:T(8,128)(2,1)S(1)}, u32[]{:S(2)}, u32[]{:S(2)}) collective-permute-start(s16[528,512]{1,0:T(8,128)(2,1)S(1)} %get-tuple-element.93), channel_id=1, source_target_pairs={{0,8},{4,12},{8,0},{12,4},{16,24},{20,28},{24,16},{28,20},{1,9},{5... | collective-permute-start | bytes 1622024 | tf_op jit(solution)/shard_map/ppermute | solution.py:516
  114.0 16.7 %collective-permute-start.18 = (s16[528,256]{1,0:T(8,128)(2,1)S(1)}, s16[528,256]{1,0:T(8,128)(2,1)S(1)}, u32[]{:S(2)}, u32[]{:S(2)}) collective-permute-start(s16[528,256]{1,0:T(8,128)(2,1)S(1)} %get-tuple-element.95), channel_id=1, source_target_pairs={{0,16},{4,20},{8,24},{12,28},{16,0},{20,4},{24,8},{28,12},{1,17},{... | collective-permute-start | bytes 811016 | tf_op jit(solution)/shard_map/ppermute | solution.py:516
  132.3 15.3 %collective-permute-start.21 = (s16[528,256]{1,0:T(8,128)(2,1)S(1)}, s16[528,256]{1,0:T(8,128)(2,1)S(1)}, u32[]{:S(2)}, u32[]{:S(2)}) collective-permute-start(s16[528,256]{1,0:T(8,128)(2,1)S(1)} %get-tuple-element.105), channel_id=1, source_target_pairs={{0,16},{4,20},{8,24},{12,28},{16,0},{20,4},{24,8},{28,12},{1,17},{... | collective-permute-start | bytes 811016 | tf_op jit(solution)/shard_map/ppermute | solution.py:516
  141.0 13.4 %collective-permute-start.19 = (s16[1,400,384]{2,1,0:T(8,128)(2,1)S(1)}, s16[1,400,384]{2,1,0:T(8,128)(2,1)S(1)}, u32[]{:S(2)}, u32[]{:S(2)}) collective-permute-start(s16[1,400,384]{2,1,0:T(8,128)(2,1)S(1)} %bitcast.56), channel_id=1, source_target_pairs={{0,1},{1,0},{2,3},{3,2},{4,5},{5,4},{6,7},{7,6},{8,9},{9,8},{10,11... | collective-permute-start | bytes 921608 | tf_op jit(solution)/shard_map/ppermute | solution.py:516
  147.0 8.2 %collective-permute-start.20 = (s16[1,400,384]{2,1,0:T(8,128)(2,1)S(1)}, s16[1,400,384]{2,1,0:T(8,128)(2,1)S(1)}, u32[]{:S(2)}, u32[]{:S(2)}) collective-permute-start(s16[1,400,384]{2,1,0:T(8,128)(2,1)S(1)} %bitcast.55), channel_id=1, source_target_pairs={{0,1},{1,0},{2,3},{3,2},{4,5},{5,4},{6,7},{7,6},{8,9},{9,8},{10,11... | collective-permute-start | bytes 921608 | tf_op jit(solution)/shard_map/ppermute | solution.py:516
  154.6 7.0 %collective-permute-start.23 = (s16[208,384]{1,0:T(8,128)(2,1)S(1)}, s16[208,384]{1,0:T(8,128)(2,1)S(1)}, u32[]{:S(2)}, u32[]{:S(2)}) collective-permute-start(s16[208,384]{1,0:T(8,128)(2,1)S(1)} %bitcast.58), channel_id=1, source_target_pairs={{0,2},{1,3},{2,0},{3,1},{4,6},{5,7},{6,4},{7,5},{8,10},{9,11},{10,... | collective-permute-start | bytes 479240 | tf_op jit(solution)/shard_map/ppermute | solution.py:516
  155.4 9.6 %collective-permute-start.24 = (s16[208,384]{1,0:T(8,128)(2,1)S(1)}, s16[208,384]{1,0:T(8,128)(2,1)S(1)}, u32[]{:S(2)}, u32[]{:S(2)}) collective-permute-start(s16[208,384]{1,0:T(8,128)(2,1)S(1)} %bitcast.59), channel_id=1, source_target_pairs={{0,2},{1,3},{2,0},{3,1},{4,6},{5,7},{6,4},{7,5},{8,10},{9,11},{10,... | collective-permute-start | bytes 479240 | tf_op jit(solution)/shard_map/ppermute | solution.py:516
  157.2 10.8 %collective-permute-start.25 = (s16[208,384]{1,0:T(8,128)(2,1)S(1)}, s16[208,384]{1,0:T(8,128)(2,1)S(1)}, u32[]{:S(2)}, u32[]{:S(2)}) collective-permute-start(s16[208,384]{1,0:T(8,128)(2,1)S(1)} %bitcast.60), channel_id=1, source_target_pairs={{0,2},{1,3},{2,0},{3,1},{4,6},{5,7},{6,4},{7,5},{8,10},{9,11},{10,... | collective-permute-start | bytes 479240 | tf_op jit(solution)/shard_map/ppermute | solution.py:516
  170.1 8.9 %collective-permute-start.26 = (s16[1200,128]{1,0:T(8,128)(2,1)S(1)}, s16[1200,128]{1,0:T(8,128)(2,1)S(1)}, u32[]{:S(2)}, u32[]{:S(2)}) collective-permute-start(s16[1200,128]{1,0:T(8,128)(2,1)S(1)} %get-tuple-element.114), channel_id=1, source_target_pairs={{0,4},{4,0},{8,12},{12,8},{16,20},{20,16},{24,28},{28,24},{1,5},{5... | collective-permute-start | bytes 921608 | tf_op jit(solution)/shard_map/ppermute | solution.py:516
  184.7 5.4 %collective-permute-start.28 = (s16[304,128]{1,0:T(8,128)(2,1)S(1)}, s16[304,128]{1,0:T(8,128)(2,1)S(1)}, u32[]{:S(2)}, u32[]{:S(2)}) collective-permute-start(s16[304,128]{1,0:T(8,128)(2,1)S(1)} %get-tuple-element.118), channel_id=1, source_target_pairs={{0,16},{4,20},{8,24},{12,28},{16,0},{20,4},{24,8},{28,12},{1,17},{... | collective-permute-start | bytes 233480 | tf_op jit(solution)/shard_map/ppermute | solution.py:516
  (13 other events, 71.2 us)

commit v13 on v12

--- a/solution.py
+++ b/solution.py
@@ -281,35 +281,50 @@
     ]
 
 
-def pack_kernel(*refs):
-    *refs, keep_ref, go_ref, sums_ref = refs
-    slots, points, rows, _ = sums_ref.shape
-    width = refs[0].shape[1]
+def pack_point(own_ref, heard_ref, out_ref):
+    slots, rows, _ = out_ref.shape
+    width = own_ref.shape[1]
     count = width // slots
     first = lax.broadcasted_iota(jnp.int32, (rows, 128), 1) < 64
-    for n in range(points):
-        total = refs[n][...] + decode(refs[points + n])
-        for slot in range(slots):
-            tile, lane = divmod(slot * count, 128)
-            reach = min(width, (tile + (1 if lane + count <= 128 else 2)) * 128)
-            piece = total[:, tile * 128 : reach]
-            if lane:
-                piece = pltpu.roll(piece, reach - tile * 128 - lane, 1)
-            real, imag = piece[:rows, :128], piece[rows:, :128]
-            sums_ref[slot, n] = jnp.where(first, real, pltpu.roll(imag, 64, 1))
+    total = own_ref[...] + decode(heard_ref)
+    for slot in range(slots):
+        tile, lane = divmod(slot * count, 128)
+        reach = min(width, (tile + (1 if lane + count <= 128 else 2)) * 128)
+        piece = total[:, tile * 128 : reach]
+        if lane:
+            piece = pltpu.roll(piece, reach - tile * 128 - lane, 1)
+        real, imag = piece[:rows, :128], piece[rows:, :128]
+        out_ref[slot] = jnp.where(first, real, pltpu.roll(imag, 64, 1))
+
+
+def pack_call(own, heard, slots):
+    rows, cols = own.shape
+    return pl.pallas_call(
+        pack_point,
+        out_shape=jax.ShapeDtypeStruct((slots, rows // 2, 128), jnp.float32),
+        compiler_params=params(),
+        cost_estimate=cost(20 * own.size, 10 * own.size),
+    )(own, heard)
+
+
+def gather_kernel(own_ref, heard_ref, *refs):
+    *packed_refs, keep_ref, go_ref, sums_ref = refs
+    for n, ref in enumerate(packed_refs):
+        sums_ref[:, n] = ref[...]
+    pack_point(own_ref, heard_ref, sums_ref.at[:, len(packed_refs)])
     split_sums(sums_ref, keep_ref, go_ref)
 
 
-def pack_call(owns, heards, slots):
-    rows, cols = owns[0].shape
-    shape = (slots, len(owns), rows // 2)
-    return pl.pallas_call(
-        pack_kernel,
+def gather_call(own, heard, packed):
+    slots, rows, _ = packed[0].shape
+    shape = (slots, len(packed) + 1, rows)
+    return pl.pallas_call(
+        gather_kernel,
         out_shape=split_shapes(*shape),
         scratch_shapes=[pltpu.VMEM(shape + (128,), jnp.float32)],
         compiler_params=params(),
-        cost_estimate=cost(60 * owns[0].size, 30 * owns[0].size),
-    )(*owns, *heards)
+        cost_estimate=cost(60 * own.size, 30 * own.size),
+    )(own, heard, *packed)
 
 
 def merge_kernel(own_ref, heard_ref, *refs):
@@ -628,7 +643,7 @@
                 own, sent = own[0], sent[0]
             tiles[q] = own, swap(sent, "pair", pair, pair_bits[-1])
 
-    own, sent = pack_call(*zip(*tiles), ga)
+    own, sent = gather_call(*tiles[-1], [pack_call(*tile, ga) for tile in tiles[:-1]])
     for bit in ga_bits[:-1]:
         own, sent = merge_call(own, swap(sent, "ga", ga, bit))
     total = merge_call(own, swap(sent, "ga", ga, ga_bits[-1]))[0]

time: 191 us -> 190 us (level)
  transfers between devices with their start and end apart: 29 -> 29, of which waited for: 15 -> 15; matrix products, arithmetic and copies ran while one was open for 5% -> 5% of each run, Pallas kernels for 28% -> 29%
where the time goes in v13:
time: 190 us
  waiting for transfers between devices  73.9 us (39%)
  Pallas kernels  57.8 us (30%)
  starting transfers between devices  45.9 us (24%)
  local copies, waits for them, and re-layouts  9.94 us (5%)
    ppermute x29, waiting for transfers between devices, swap(): return lax.ppermute(value, axis, [(i, i ^ bit) for i in range(size)])  73.9 us
    ppermute x29, starting transfers between devices, swap(): return lax.ppermute(value, axis, [(i, i ^ bit) for i in range(size)])  45.9 us
    pallas_call x3, Pallas kernels, x_call(): pl.pallas_call(lambda *refs: x_kernel(slots, len(after), *refs), grid_spe...  24.6 us
    pallas_call x3, Pallas kernels, tile_call(): pl.pallas_call(lambda *refs: tile_kernel(order, stages, chunks, len(after...  18.7 us
    pallas_call x6, Pallas kernels, hop_call(): pl.pallas_call(lambda *refs: hop_kernel(len(others), *refs), grid_spec=gr...  5.99 us
  transfers between devices with their start and end apart: 29, of which 15 were waited for; matrix products, arithmetic and copies ran while one was open for 5% of the time, Pallas kernels for 29%

profile of v13, /device:TPU:0, one launch (start us, length us, event | category | flops | bytes accessed | tf_op | source)
XLA Modules:
  0.0 189.5 jit_solution(1330218121492585800)
XLA Ops:
  1.4 3.0 %collective-permute-start.2 = (bf16[1,3,2,64,1024]{4,3,2,1,0:T(8,128)(2,1)S(1)}, bf16[1,3,2,64,1024]{4,3,2,1,0:T(8,128)(2,1)S(1)}, u32[]{:S(2)}, u32[]{:S(2)}) collective-permute-start(bf16[1,3,2,64,1024]{4,3,2,1,0:T(8,128)(2,1)S(1)} %bitcast.36), channel_id=1, source_target_pairs={{0,2},{1,3},{2,0},{3,1},{4,6},{5,7},{6,4},{7,5},{8,10},{9,11},{10,... | collective-permute-start | bytes 2359304 | tf_op jit(solution)/shard_map/ppermute | solution.py:531
  16.5 5.4 %collective-permute-done.2.refs_3_ = bf16[1,3,2,64,1024]{4,3,2,1,0:T(8,128)(2,1)S(1)} collective-permute-done((bf16[1,3,2,64,1024]{4,3,2,1,0:T(8,128)(2,1)S(1)}, bf16[1,3,2,64,1024]{4,3,2,1,0:T(8,128)(2,1)S(1)}, u32[]{:S(2)}, u32[]{:S(2)}) %collective-permute-start.2) | collective-permute-done | bytes 786464 | tf_op jit(solution)/shard_map/ppermute | solution.py:531
  25.5 2.6 %collective-permute-done.refs_2_ = bf16[1,3,2,72,256]{4,3,2,1,0:T(8,128)(2,1)} collective-permute-done((bf16[1,3,2,72,256]{4,3,2,1,0:T(8,128)(2,1)}, bf16[1,3,2,72,256]{4,3,2,1,0:T(8,128)(2,1)}, u32[]{:S(2)}, u32[]{:S(2)}) %collective-permute-start) | collective-permute-done | bytes 221216 | tf_op jit(solution)/shard_map/ppermute | solution.py:531
  28.1 8.2 %shard_map.101 = (s16[528,1024]{1,0:T(8,128)(2,1)S(1)}, f32[512,1024]{1,0:T(8,128)S(1)}, f32[8,128]{1,0:T(8,128)S(1)}) custom-call(s32[1]{0:T(128)} %bitcast.refs_0_, bf16[1,3,2,64,1024]{4,3,2,1,0:T(8,128)(2,1)S(1)} %bitcast.38, bf16[2,3,2,64,1024]{4,3,2,1,0:T(8,128)(2,1)S(1)} %collective-permute-done.3.refs_2_.refs_4_, ...), custom_call_target="tpu_custom_call" | custom-call | flops 67108864 | bytes 180224 | tf_op jit(solution)/shard_map/pallas_call | solution.py:197
  37.9 8.2 %shard_map.102 = (s16[528,1024]{1,0:T(8,128)(2,1)S(1)}, f32[512,1024]{1,0:T(8,128)S(1)}, f32[8,128]{1,0:T(8,128)S(1)}) custom-call(s32[1]{0:T(128)} %bitcast.refs_0_, bf16[1,3,2,64,1024]{4,3,2,1,0:T(8,128)(2,1)S(1)} %bitcast.39, bf16[2,3,2,64,1024]{4,3,2,1,0:T(8,128)(2,1)S(1)} %collective-permute-done.3.refs_2_.refs_4_, ...), custom_call_target="tpu_custom_call" | custom-call | flops 67108864 | bytes 180224 | tf_op jit(solution)/shard_map/pallas_call | solution.py:197
  48.0 4.3 %collective-permute-start.5 = (bf16[2,3,2,72,256]{4,3,2,1,0:T(8,128)(2,1)S(1)}, bf16[2,3,2,72,256]{4,3,2,1,0:T(8,128)(2,1)S(1)}, u32[]{:S(2)}, u32[]{:S(2)}) collective-permute-start(bf16[2,3,2,72,256]{4,3,2,1,0:T(8,128)(2,1)S(1)} %pad_maximum_fusion.1), channel_id=1, source_target_pairs={{0,8},{4,12},{8,0},{12,4},{16,24},{20,28},{24,16},{28,20},{1,9},{5... | collective-permute-start | bytes 1327112 | tf_op jit(solution)/shard_map/ppermute | solution.py:531
  52.3 3.4 %collective-permute-start.7 = (bf16[1,3,2,72,256]{4,3,2,1,0:T(8,128)(2,1)S(1)}, bf16[1,3,2,72,256]{4,3,2,1,0:T(8,128)(2,1)S(1)}, u32[]{:S(2)}, u32[]{:S(2)}) collective-permute-start(bf16[1,3,2,72,256]{4,3,2,1,0:T(8,128)(2,1)S(1)} %get-tuple-element.119), channel_id=1, source_target_pairs={{0,24},{4,28},{8,16},{12,20},{16,8},{20,12},{24,0},{28,4},{1,25},{... | collective-permute-start | bytes 663560 | tf_op jit(solution)/shard_map/ppermute | solution.py:531
  55.6 8.2 %shard_map.103 = (s16[528,1024]{1,0:T(8,128)(2,1)S(1)}, f32[512,1024]{1,0:T(8,128)S(1)}, f32[8,128]{1,0:T(8,128)S(1)}) custom-call(s32[1]{0:T(128)} %bitcast.refs_0_, bf16[1,3,2,64,1024]{4,3,2,1,0:T(8,128)(2,1)S(1)} %bitcast.40, bf16[2,3,2,64,1024]{4,3,2,1,0:T(8,128)(2,1)S(1)} %collective-permute-done.3.refs_2_.refs_4_, ...), custom_call_target="tpu_custom_call" | custom-call | flops 67108864 | bytes 180224 | tf_op jit(solution)/shard_map/pallas_call | solution.py:197
  63.8 7.6 %collective-permute-done.7.refs_8_ = bf16[1,3,2,72,256]{4,3,2,1,0:T(8,128)(2,1)S(1)} collective-permute-done((bf16[1,3,2,72,256]{4,3,2,1,0:T(8,128)(2,1)S(1)}, bf16[1,3,2,72,256]{4,3,2,1,0:T(8,128)(2,1)S(1)}, u32[]{:S(2)}, u32[]{:S(2)}) %collective-permute-start.7) | collective-permute-done | bytes 221216 | tf_op jit(solution)/shard_map/ppermute | solution.py:531
  72.7 3.8 %collective-permute-start.11 = (s16[528,512]{1,0:T(8,128)(2,1)S(1)}, s16[528,512]{1,0:T(8,128)(2,1)S(1)}, u32[]{:S(2)}, u32[]{:S(2)}) collective-permute-start(s16[528,512]{1,0:T(8,128)(2,1)S(1)} %get-tuple-element.82), channel_id=1, source_target_pairs={{0,8},{4,12},{8,0},{12,4},{16,24},{20,28},{24,16},{28,20},{1,9},{5... | collective-permute-start | bytes 1622024 | tf_op jit(solution)/shard_map/ppermute | solution.py:531
  78.6 8.8 %collective-permute-done.11.refs_3_.refs_11_ = s16[528,512]{1,0:T(8,128)(2,1)S(1)} collective-permute-done((s16[528,512]{1,0:T(8,128)(2,1)S(1)}, s16[528,512]{1,0:T(8,128)(2,1)S(1)}, u32[]{:S(2)}, u32[]{:S(2)}) %collective-permute-start.11) | collective-permute-done | bytes 540704 | tf_op jit(solution)/shard_map/ppermute | solution.py:531
  94.3 3.4 %shard_map.107 = (f32[3,2,384,96]{3,2,1,0:T(8,128)S(1)}, f32[8,128]{1,0:T(8,128)S(1)}) custom-call(bf16[1,2,96,1024]{3,2,1,0:T(8,128)(2,1)S(1)} %bitcast.45, bf16[1,2,96,1024]{3,2,1,0:T(8,128)(2,1)S(1)} %bitcast.50, bf16[1,2,96,1024]{3,2,1,0:T(8,128)(2,1)S(1)} %bitcast.49, bf16[1,2,96,1024]{3,2,1,0:T(8,128)(2,1)S(1)} %bitcast.51, ...), custom_call_target="tpu_custom_call" | custom-call | flops 28311552 | bytes 36864 | tf_op jit(solution)/shard_map/pallas_call | solution.py:384
  97.6 9.8 %collective-permute-done.16.refs_12_ = s16[528,256]{1,0:T(8,128)(2,1)S(1)} collective-permute-done((s16[528,256]{1,0:T(8,128)(2,1)S(1)}, s16[528,256]{1,0:T(8,128)(2,1)S(1)}, u32[]{:S(2)}, u32[]{:S(2)}) %collective-permute-start.16) | collective-permute-done | bytes 270368 | tf_op jit(solution)/shard_map/ppermute | solution.py:531
  110.2 3.8 %collective-permute-start.17 = (s16[528,512]{1,0:T(8,128)(2,1)S(1)}, s16[528,512]{1,0:T(8,128)(2,1)S(1)}, u32[]{:S(2)}, u32[]{:S(2)}) collective-permute-start(s16[528,512]{1,0:T(8,128)(2,1)S(1)} %get-tuple-element.92), channel_id=1, source_target_pairs={{0,8},{4,12},{8,0},{12,4},{16,24},{20,28},{24,16},{28,20},{1,9},{5... | collective-permute-start | bytes 1622024 | tf_op jit(solution)/shard_map/ppermute | solution.py:531
  115.9 14.7 %collective-permute-done.18.refs_12_ = s16[528,256]{1,0:T(8,128)(2,1)S(1)} collective-permute-done((s16[528,256]{1,0:T(8,128)(2,1)S(1)}, s16[528,256]{1,0:T(8,128)(2,1)S(1)}, u32[]{:S(2)}, u32[]{:S(2)}) %collective-permute-start.18) | collective-permute-done | bytes 270368 | tf_op jit(solution)/shard_map/ppermute | solution.py:531
  132.3 2.7 %collective-permute-start.19 = (s16[528,256]{1,0:T(8,128)(2,1)S(1)}, s16[528,256]{1,0:T(8,128)(2,1)S(1)}, u32[]{:S(2)}, u32[]{:S(2)}) collective-permute-start(s16[528,256]{1,0:T(8,128)(2,1)S(1)} %get-tuple-element.96), channel_id=1, source_target_pairs={{0,16},{4,20},{8,24},{12,28},{16,0},{20,4},{24,8},{28,12},{1,17},{... | collective-permute-start | bytes 811016 | tf_op jit(solution)/shard_map/ppermute | solution.py:531
  135.0 6.0 %shard_map.111 = (f32[384,384]{1,0:T(8,128)S(1)}, s16[400,384]{1,0:T(8,128)(2,1)S(1)}, f32[8,128]{1,0:T(8,128)S(1)}) custom-call(s32[1]{0:T(128)} %bitcast.refs_0_, bf16[1,3,2,72,256]{4,3,2,1,0:T(8,128)(2,1)S(1)} %get-tuple-element.63.refs_1_, bf16[1,3,2,72,256]{4,3,2,1,0:T(8,128)(2,1)} %collective-permute-done.refs_2_, ...), custom_call_target="tpu_custom_call" | custom-call | flops 43750000 | bytes 125000 | tf_op jit(solution)/shard_map/pallas_call | solution.py:521
  141.0 6.0 %shard_map.112 = (f32[384,384]{1,0:T(8,128)S(1)}, s16[400,384]{1,0:T(8,128)(2,1)S(1)}, f32[8,128]{1,0:T(8,128)S(1)}) custom-call(s32[1]{0:T(128)} %bitcast.refs_0_, bf16[1,3,2,72,256]{4,3,2,1,0:T(8,128)(2,1)S(1)} %get-tuple-element.63.refs_1_, bf16[1,3,2,72,256]{4,3,2,1,0:T(8,128)(2,1)} %collective-permute-done.refs_2_, ...), custom_call_target="tpu_custom_call" | custom-call | flops 43750000 | bytes 125000 | tf_op jit(solution)/shard_map/pallas_call | solution.py:521
  147.6 6.7 %shard_map.113 = (f32[384,384]{1,0:T(8,128)S(1)}, s16[400,384]{1,0:T(8,128)(2,1)S(1)}, f32[8,128]{1,0:T(8,128)}) custom-call(s32[1]{0:T(128)} %bitcast.refs_0_, bf16[1,3,2,72,256]{4,3,2,1,0:T(8,128)(2,1)S(1)} %get-tuple-element.63.refs_1_, bf16[1,3,2,72,256]{4,3,2,1,0:T(8,128)(2,1)} %collective-permute-done.refs_2_, ...), custom_call_target="tpu_custom_call" | custom-call | flops 43750000 | bytes 125000 | tf_op jit(solution)/shard_map/pallas_call | solution.py:521
  157.8 3.8 %collective-permute-done.25.heard_ref = s16[208,384]{1,0:T(8,128)(2,1)S(1)} collective-permute-done((s16[208,384]{1,0:T(8,128)(2,1)S(1)}, s16[208,384]{1,0:T(8,128)(2,1)S(1)}, u32[]{:S(2)}, u32[]{:S(2)}) %collective-permute-start.25) | collective-permute-done | bytes 159776 | tf_op jit(solution)/shard_map/ppermute | solution.py:531
  162.3 2.7 %collective-permute-done.23.heard_ref = s16[208,384]{1,0:T(8,128)(2,1)S(1)} collective-permute-done((s16[208,384]{1,0:T(8,128)(2,1)S(1)}, s16[208,384]{1,0:T(8,128)(2,1)S(1)}, u32[]{:S(2)}, u32[]{:S(2)}) %collective-permute-start.23) | collective-permute-done | bytes 159776 | tf_op jit(solution)/shard_map/ppermute | solution.py:531
  170.3 7.3 %collective-permute-done.26.heard_ref = s16[1200,128]{1,0:T(8,128)(2,1)S(1)} collective-permute-done((s16[1200,128]{1,0:T(8,128)(2,1)S(1)}, s16[1200,128]{1,0:T(8,128)(2,1)S(1)}, u32[]{:S(2)}, u32[]{:S(2)}) %collective-permute-start.26) | collective-permute-done | bytes 307232 | tf_op jit(solution)/shard_map/ppermute | solution.py:531
  179.2 3.9 %collective-permute-done.27.heard_ref = s16[608,128]{1,0:T(8,128)(2,1)S(1)} collective-permute-done((s16[608,128]{1,0:T(8,128)(2,1)S(1)}, s16[608,128]{1,0:T(8,128)(2,1)S(1)}, u32[]{:S(2)}, u32[]{:S(2)}) %collective-permute-start.27) | collective-permute-done | bytes 155680 | tf_op jit(solution)/shard_map/ppermute | solution.py:531
  185.3 3.4 %collective-permute-done.28.heard_ref = s16[304,128]{1,0:T(8,128)(2,1)S(1)} collective-permute-done((s16[304,128]{1,0:T(8,128)(2,1)S(1)}, s16[304,128]{1,0:T(8,128)(2,1)S(1)}, u32[]{:S(2)}, u32[]{:S(2)}) %collective-permute-start.28) | collective-permute-done | bytes 77856 | tf_op jit(solution)/shard_map/ppermute | solution.py:531
  (109 shorter events, 51.5 us)
Async XLA Ops:
  1.4 20.5 %collective-permute-start.2 = (bf16[1,3,2,64,1024]{4,3,2,1,0:T(8,128)(2,1)S(1)}, bf16[1,3,2,64,1024]{4,3,2,1,0:T(8,128)(2,1)S(1)}, u32[]{:S(2)}, u32[]{:S(2)}) collective-permute-start(bf16[1,3,2,64,1024]{4,3,2,1,0:T(8,128)(2,1)S(1)} %bitcast.36), channel_id=1, source_target_pairs={{0,2},{1,3},{2,0},{3,1},{4,6},{5,7},{6,4},{7,5},{8,10},{9,11},{10,... | collective-permute-start | bytes 2359304 | tf_op jit(solution)/shard_map/ppermute | solution.py:531
  9.4 18.7 %collective-permute-start = (bf16[1,3,2,72,256]{4,3,2,1,0:T(8,128)(2,1)}, bf16[1,3,2,72,256]{4,3,2,1,0:T(8,128)(2,1)}, u32[]{:S(2)}, u32[]{:S(2)}) collective-permute-start(bf16[1,3,2,72,256]{4,3,2,1,0:T(8,128)(2,1)} %get-tuple-element.64), channel_id=1, source_target_pairs={{0,16},{4,20},{8,24},{12,28},{16,0},{20,4},{24,8},{28,12},{1,17},{... | collective-permute-start | bytes 663560 | tf_op jit(solution)/shard_map/ppermute | solution.py:531
  12.0 16.2 %collective-permute-start.4 = (bf16[1,3,2,72,256]{4,3,2,1,0:T(8,128)(2,1)}, bf16[1,3,2,72,256]{4,3,2,1,0:T(8,128)(2,1)}, u32[]{:S(2)}, u32[]{:S(2)}) collective-permute-start(bf16[1,3,2,72,256]{4,3,2,1,0:T(8,128)(2,1)} %get-tuple-element.66), channel_id=1, source_target_pairs={{0,24},{4,28},{8,16},{12,20},{16,8},{20,12},{24,0},{28,4},{1,25},{... | collective-permute-start | bytes 663560 | tf_op jit(solution)/shard_map/ppermute | solution.py:531
  13.3 24.6 %collective-permute-start.1 = (bf16[4,3,2,72,256]{4,3,2,1,0:T(8,128)(2,1)}, bf16[4,3,2,72,256]{4,3,2,1,0:T(8,128)(2,1)}, u32[]{:S(2)}, u32[]{:S(2)}) collective-permute-start(bf16[4,3,2,72,256]{4,3,2,1,0:T(8,128)(2,1)} %get-tuple-element.67), channel_id=1, source_target_pairs={{0,4},{4,0},{8,12},{12,8},{16,20},{20,16},{24,28},{28,24},{1,5},{5... | collective-permute-start | bytes 2654216 | tf_op jit(solution)/shard_map/ppermute | solution.py:531
  36.3 35.2 %collective-permute-start.10 = (s16[528,1024]{1,0:T(8,128)(2,1)S(1)}, s16[528,1024]{1,0:T(8,128)(2,1)S(1)}, u32[]{:S(2)}, u32[]{:S(2)}) collective-permute-start(s16[528,1024]{1,0:T(8,128)(2,1)S(1)} %get-tuple-element.79), channel_id=1, source_target_pairs={{0,4},{4,0},{8,12},{12,8},{16,20},{20,16},{24,28},{28,24},{1,5},{5... | collective-permute-start | bytes 3244040 | tf_op jit(solution)/shard_map/ppermute | solution.py:531
  46.1 42.1 %collective-permute-start.9 = (s16[528,1024]{1,0:T(8,128)(2,1)S(1)}, s16[528,1024]{1,0:T(8,128)(2,1)S(1)}, u32[]{:S(2)}, u32[]{:S(2)}) collective-permute-start(s16[528,1024]{1,0:T(8,128)(2,1)S(1)} %get-tuple-element.77), channel_id=1, source_target_pairs={{0,4},{4,0},{8,12},{12,8},{16,20},{20,16},{24,28},{28,24},{1,5},{5... | collective-permute-start | bytes 3244040 | tf_op jit(solution)/shard_map/ppermute | solution.py:531
  48.0 23.5 %collective-permute-start.5 = (bf16[2,3,2,72,256]{4,3,2,1,0:T(8,128)(2,1)S(1)}, bf16[2,3,2,72,256]{4,3,2,1,0:T(8,128)(2,1)S(1)}, u32[]{:S(2)}, u32[]{:S(2)}) collective-permute-start(bf16[2,3,2,72,256]{4,3,2,1,0:T(8,128)(2,1)S(1)} %pad_maximum_fusion.1), channel_id=1, source_target_pairs={{0,8},{4,12},{8,0},{12,4},{16,24},{20,28},{24,16},{28,20},{1,9},{5... | collective-permute-start | bytes 1327112 | tf_op jit(solution)/shard_map/ppermute | solution.py:531
  52.3 19.2 %collective-permute-start.7 = (bf16[1,3,2,72,256]{4,3,2,1,0:T(8,128)(2,1)S(1)}, bf16[1,3,2,72,256]{4,3,2,1,0:T(8,128)(2,1)S(1)}, u32[]{:S(2)}, u32[]{:S(2)}) collective-permute-start(bf16[1,3,2,72,256]{4,3,2,1,0:T(8,128)(2,1)S(1)} %get-tuple-element.119), channel_id=1, source_target_pairs={{0,24},{4,28},{8,16},{12,20},{16,8},{20,12},{24,0},{28,4},{1,25},{... | collective-permute-start | bytes 663560 | tf_op jit(solution)/shard_map/ppermute | solution.py:531
  55.6 15.8 %collective-permute-start.6 = (bf16[1,3,2,72,256]{4,3,2,1,0:T(8,128)(2,1)S(1)}, bf16[1,3,2,72,256]{4,3,2,1,0:T(8,128)(2,1)S(1)}, u32[]{:S(2)}, u32[]{:S(2)}) collective-permute-start(bf16[1,3,2,72,256]{4,3,2,1,0:T(8,128)(2,1)S(1)} %get-tuple-element.120), channel_id=1, source_target_pairs={{0,16},{4,20},{8,24},{12,28},{16,0},{20,4},{24,8},{28,12},{1,17},{... | collective-permute-start | bytes 663560 | tf_op jit(solution)/shard_map/ppermute | solution.py:531
  72.7 14.7 %collective-permute-start.11 = (s16[528,512]{1,0:T(8,128)(2,1)S(1)}, s16[528,512]{1,0:T(8,128)(2,1)S(1)}, u32[]{:S(2)}, u32[]{:S(2)}) collective-permute-start(s16[528,512]{1,0:T(8,128)(2,1)S(1)} %get-tuple-element.82), channel_id=1, source_target_pairs={{0,8},{4,12},{8,0},{12,4},{16,24},{20,28},{24,16},{28,20},{1,9},{5... | collective-permute-start | bytes 1622024 | tf_op jit(solution)/shard_map/ppermute | solution.py:531
  76.4 32.5 %collective-permute-start.8 = (s16[528,1024]{1,0:T(8,128)(2,1)S(1)}, s16[528,1024]{1,0:T(8,128)(2,1)S(1)}, u32[]{:S(2)}, u32[]{:S(2)}) collective-permute-start(s16[528,1024]{1,0:T(8,128)(2,1)S(1)} %get-tuple-element.75), channel_id=1, source_target_pairs={{0,4},{4,0},{8,12},{12,8},{16,20},{20,16},{24,28},{28,24},{1,5},{5... | collective-permute-start | bytes 3244040 | tf_op jit(solution)/shard_map/ppermute | solution.py:531
  78.1 13.7 %collective-permute-start.14 = (bf16[2,96,1024]{2,1,0:T(8,128)(2,1)S(1)}, bf16[2,96,1024]{2,1,0:T(8,128)(2,1)S(1)}, u32[]{:S(2)}, u32[]{:S(2)}) collective-permute-start(bf16[2,96,1024]{2,1,0:T(8,128)(2,1)S(1)} %bitcast.43), channel_id=1, source_target_pairs={{0,2},{1,3},{2,0},{3,1},{4,6},{5,7},{6,4},{7,5},{8,10},{9,11},{10,... | collective-permute-start | bytes 1179656 | tf_op jit(solution)/shard_map/ppermute | solution.py:531
  89.4 18.8 %collective-permute-start.12 = (s16[528,512]{1,0:T(8,128)(2,1)S(1)}, s16[528,512]{1,0:T(8,128)(2,1)S(1)}, u32[]{:S(2)}, u32[]{:S(2)}) collective-permute-start(s16[528,512]{1,0:T(8,128)(2,1)S(1)} %get-tuple-element.85), channel_id=1, source_target_pairs={{0,8},{4,12},{8,0},{12,4},{16,24},{20,28},{24,16},{28,20},{1,9},{5... | collective-permute-start | bytes 1622024 | tf_op jit(solution)/shard_map/ppermute | solution.py:531
  92.2 15.2 %collective-permute-start.16 = (s16[528,256]{1,0:T(8,128)(2,1)S(1)}, s16[528,256]{1,0:T(8,128)(2,1)S(1)}, u32[]{:S(2)}, u32[]{:S(2)}) collective-permute-start(s16[528,256]{1,0:T(8,128)(2,1)S(1)} %get-tuple-element.89), channel_id=1, source_target_pairs={{0,16},{4,20},{8,24},{12,28},{16,0},{20,4},{24,8},{28,12},{1,17},{... | collective-permute-start | bytes 811016 | tf_op jit(solution)/shard_map/ppermute | solution.py:531
  110.2 21.2 %collective-permute-start.17 = (s16[528,512]{1,0:T(8,128)(2,1)S(1)}, s16[528,512]{1,0:T(8,128)(2,1)S(1)}, u32[]{:S(2)}, u32[]{:S(2)}) collective-permute-start(s16[528,512]{1,0:T(8,128)(2,1)S(1)} %get-tuple-element.92), channel_id=1, source_target_pairs={{0,8},{4,12},{8,0},{12,4},{16,24},{20,28},{24,16},{28,20},{1,9},{5... | collective-permute-start | bytes 1622024 | tf_op jit(solution)/shard_map/ppermute | solution.py:531
  114.0 16.7 %collective-permute-start.18 = (s16[528,256]{1,0:T(8,128)(2,1)S(1)}, s16[528,256]{1,0:T(8,128)(2,1)S(1)}, u32[]{:S(2)}, u32[]{:S(2)}) collective-permute-start(s16[528,256]{1,0:T(8,128)(2,1)S(1)} %get-tuple-element.94), channel_id=1, source_target_pairs={{0,16},{4,20},{8,24},{12,28},{16,0},{20,4},{24,8},{28,12},{1,17},{... | collective-permute-start | bytes 811016 | tf_op jit(solution)/shard_map/ppermute | solution.py:531
  132.3 15.3 %collective-permute-start.19 = (s16[528,256]{1,0:T(8,128)(2,1)S(1)}, s16[528,256]{1,0:T(8,128)(2,1)S(1)}, u32[]{:S(2)}, u32[]{:S(2)}) collective-permute-start(s16[528,256]{1,0:T(8,128)(2,1)S(1)} %get-tuple-element.96), channel_id=1, source_target_pairs={{0,16},{4,20},{8,24},{12,28},{16,0},{20,4},{24,8},{28,12},{1,17},{... | collective-permute-start | bytes 811016 | tf_op jit(solution)/shard_map/ppermute | solution.py:531
  147.0 7.4 %collective-permute-start.24 = (s16[1,400,384]{2,1,0:T(8,128)(2,1)S(1)}, s16[1,400,384]{2,1,0:T(8,128)(2,1)S(1)}, u32[]{:S(2)}, u32[]{:S(2)}) collective-permute-start(s16[1,400,384]{2,1,0:T(8,128)(2,1)S(1)} %bitcast.57), channel_id=1, source_target_pairs={{0,1},{1,0},{2,3},{3,2},{4,5},{5,4},{6,7},{7,6},{8,9},{9,8},{10,11... | collective-permute-start | bytes 921608 | tf_op jit(solution)/shard_map/ppermute | solution.py:531
  147.1 8.2 %collective-permute-start.22 = (s16[1,400,384]{2,1,0:T(8,128)(2,1)S(1)}, s16[1,400,384]{2,1,0:T(8,128)(2,1)S(1)}, u32[]{:S(2)}, u32[]{:S(2)}) collective-permute-start(s16[1,400,384]{2,1,0:T(8,128)(2,1)S(1)} %bitcast.55), channel_id=1, source_target_pairs={{0,1},{1,0},{2,3},{3,2},{4,5},{5,4},{6,7},{7,6},{8,9},{9,8},{10,11... | collective-permute-start | bytes 921608 | tf_op jit(solution)/shard_map/ppermute | solution.py:531
  154.6 7.0 %collective-permute-start.25 = (s16[208,384]{1,0:T(8,128)(2,1)S(1)}, s16[208,384]{1,0:T(8,128)(2,1)S(1)}, u32[]{:S(2)}, u32[]{:S(2)}) collective-permute-start(s16[208,384]{1,0:T(8,128)(2,1)S(1)} %bitcast.58), channel_id=1, source_target_pairs={{0,2},{1,3},{2,0},{3,1},{4,6},{5,7},{6,4},{7,5},{8,10},{9,11},{10,... | collective-permute-start | bytes 479240 | tf_op jit(solution)/shard_map/ppermute | solution.py:531
  155.5 9.6 %collective-permute-start.23 = (s16[208,384]{1,0:T(8,128)(2,1)S(1)}, s16[208,384]{1,0:T(8,128)(2,1)S(1)}, u32[]{:S(2)}, u32[]{:S(2)}) collective-permute-start(s16[208,384]{1,0:T(8,128)(2,1)S(1)} %bitcast.59), channel_id=1, source_target_pairs={{0,2},{1,3},{2,0},{3,1},{4,6},{5,7},{6,4},{7,5},{8,10},{9,11},{10,... | collective-permute-start | bytes 479240 | tf_op jit(solution)/shard_map/ppermute | solution.py:531
  157.2 10.8 %collective-permute-start.21 = (s16[208,384]{1,0:T(8,128)(2,1)S(1)}, s16[208,384]{1,0:T(8,128)(2,1)S(1)}, u32[]{:S(2)}, u32[]{:S(2)}) collective-permute-start(s16[208,384]{1,0:T(8,128)(2,1)S(1)} %bitcast.60), channel_id=1, source_target_pairs={{0,2},{1,3},{2,0},{3,1},{4,6},{5,7},{6,4},{7,5},{8,10},{9,11},{10,... | collective-permute-start | bytes 479240 | tf_op jit(solution)/shard_map/ppermute | solution.py:531
  168.7 8.9 %collective-permute-start.26 = (s16[1200,128]{1,0:T(8,128)(2,1)S(1)}, s16[1200,128]{1,0:T(8,128)(2,1)S(1)}, u32[]{:S(2)}, u32[]{:S(2)}) collective-permute-start(s16[1200,128]{1,0:T(8,128)(2,1)S(1)} %get-tuple-element.114), channel_id=1, source_target_pairs={{0,4},{4,0},{8,12},{12,8},{16,20},{20,16},{24,28},{28,24},{1,5},{5... | collective-permute-start | bytes 921608 | tf_op jit(solution)/shard_map/ppermute | solution.py:531
  183.3 5.4 %collective-permute-start.28 = (s16[304,128]{1,0:T(8,128)(2,1)S(1)}, s16[304,128]{1,0:T(8,128)(2,1)S(1)}, u32[]{:S(2)}, u32[]{:S(2)}) collective-permute-start(s16[304,128]{1,0:T(8,128)(2,1)S(1)} %get-tuple-element.118), channel_id=1, source_target_pairs={{0,16},{4,20},{8,24},{12,28},{16,0},{20,4},{24,8},{28,12},{1,17},{... | collective-permute-start | bytes 233480 | tf_op jit(solution)/shard_map/ppermute | solution.py:531
  (13 other events, 71.2 us)
